TPU v7x, 32 devices: a whole 2x2x4 slice. The times are simulated.
32 devices in a mesh: rows: 8 (over y, x, core), cols: 4 (over z).
Axes of the slice: x: 2, y: 2, z: 4, core: 2. Of those that a mesh axis runs over, the one named last changes fastest.
Arguments:
- known_inverse: bfloat16 [4, 8, 32, 1024], P(None, 'rows', None, 'cols'), may hold values from -6 to 6
- lower_panel: bfloat16 [4, 4, 8, 32, 512], P(None, 'cols'), may hold values from -0.1875 to 0.1875
- chain_panel: bfloat16 [4, 512, 512], replicated, may hold values from -0.25 to 0.25
- diag_inverse: float32 [4, 512, 512], P(None, 'rows'), may hold values from -6 to 6
- top_cols: bfloat16 [4, 8, 32, 512], P('cols', 'rows'), may hold values from -6 to 6
- top_diag: float32 [512, 512], P('rows'), may hold values from -6 to 6
- pattern: int32 [4, 32], replicated, may hold values from 0 to 1, as said below
Outputs:
- inverse_cols: bfloat16 [4, 4, 8, 32, 512], P(None, 'cols', 'rows')
- inverse_diag: float32 [4, 512, 512], P(None, 'rows')
- inverse_sub: float32 [4, 512, 512], P(None, 'rows')
Inputs may be any that keep to these rules, and one draw needn't show every extreme that they name: `pattern`: row k marks exactly (32 * (5 + k)) // 9 block rows, and every block row marked in row k is marked in row k + 1.
All inputs are finite; a program needn't handle non-finite values.
Results may differ from a plain program's by a relative error of at most 0.025.
Values may be sent and summed in bfloat16 or wider, within the bound.
No kernel may reach another device: no remote copies, remote signals or barrier semaphores. Data moves between devices by JAX's collectives and lax.ppermute only.
A program may use at most 128 MiB of HBM per device.

v0:
```python
import jax
import jax.numpy as jnp
from jax import lax
from jax.sharding import PartitionSpec as P


def local(known_inverse, lower_panel, chain_panel, diag_inverse, top_cols, top_diag, pattern):
    n_rows = lax.axis_size("rows")
    n_cols = lax.axis_size("cols")
    row_id = lax.axis_index("rows")
    col_id = lax.axis_index("cols")
    supers = lower_panel.shape[0]
    piece_rows = known_inverse.shape[2]
    panel_width = lower_panel.shape[-1]
    diag_count = panel_width // n_rows
    known_rows = known_inverse.reshape(n_cols * piece_rows, -1)
    group_mask = lax.dynamic_slice_in_dim(pattern, col_id * n_rows, n_rows, 1)
    panels = lower_panel[:, 0] * group_mask[:, :, None, None].astype(jnp.bfloat16)
    panel_slab = panels.reshape(supers, n_rows * piece_rows, panel_width)
    own_pieces = lax.dynamic_index_in_dim(panels, row_id, 1, keepdims=False)
    own_mask = lax.dynamic_index_in_dim(group_mask, row_id, 1, keepdims=False).astype(jnp.float32)
    first_col = jnp.where(col_id == 0, 1.0, 0.0).astype(jnp.float32)
    prev_cols = top_cols.reshape(piece_rows, panel_width)
    prev_diag = top_diag
    cols_list = [None] * supers
    diag_list = [None] * supers
    sub_list = [None] * supers
    for section in reversed(range(supers)):
        link_block = chain_panel[section]
        link_wide = link_block.astype(jnp.float32)
        own_panel = own_pieces[section]
        link_rows = lax.dynamic_slice_in_dim(link_wide, row_id * diag_count, diag_count, 0)
        diag_link = jnp.dot(prev_diag, link_wide, precision=lax.Precision.HIGHEST)
        carried = jnp.dot(prev_cols, link_block, preferred_element_type=jnp.float32)
        sub_term = -jnp.einsum(
            "pi,pj->ij", prev_cols, own_panel, preferred_element_type=jnp.float32
        )
        product = lax.psum_scatter(
            jnp.dot(known_rows, panel_slab[section], preferred_element_type=jnp.float32).astype(
                jnp.bfloat16
            ),
            "cols",
            scatter_dimension=0,
            tiled=True,
        ).astype(jnp.float32)
        new_cols = (-(product + carried) * own_mask[section]).astype(jnp.bfloat16)
        diag_term = (
            -jnp.einsum("pi,pj->ij", own_panel, new_cols, preferred_element_type=jnp.float32)
            + jnp.einsum(
                "pi,pj->ij", carried, own_panel.astype(jnp.float32), precision=lax.Precision.HIGHEST
            )
            + first_col
            * jnp.einsum("mi,mj->ij", link_rows, diag_link, precision=lax.Precision.HIGHEST)
        )
        joined = jnp.stack([sub_term, diag_term], axis=1)
        reduced = lax.psum_scatter(joined, "rows", scatter_dimension=0, tiled=True)
        reduced = lax.psum(reduced.astype(jnp.bfloat16), "cols").astype(jnp.float32)
        sub_sum = reduced[:, 0]
        diag_sum = reduced[:, 1]
        sub_block = sub_sum - diag_link
        diag_block = diag_inverse[section] + diag_sum
        cols_list[section] = new_cols
        diag_list[section] = diag_block
        sub_list[section] = sub_block
        prev_cols = new_cols
        prev_diag = diag_block
    cols_out = jnp.stack(cols_list).reshape(supers, 1, 1, piece_rows, panel_width)
    return (cols_out, jnp.stack(diag_list), jnp.stack(sub_list))


def solution(mesh):
    in_specs = (
        P(None, "rows", None, "cols"),
        P(None, "cols", None, None, None),
        P(),
        P(None, "rows", None),
        P("cols", "rows", None, None),
        P("rows", None),
        P(),
    )
    out_specs = (P(None, "cols", "rows", None, None), P(None, "rows", None), P(None, "rows", None))
    return jax.shard_map(local, mesh=mesh, in_specs=in_specs, out_specs=out_specs, check_vma=False)
```

profile of v0, /device:TPU:0, one launch (start us, length us, event | category | flops | bytes accessed | tf_op | source)
XLA Modules:
  0.0 434.8 jit_solution(9207028200780825592)
XLA Ops:
  7.2 0.8 fusion.73
  8.0 1.4 bitcast_multiply_fusion
  9.4 0.9 fusion.84
  10.6 0.8 copy.29
  11.4 1.2 fusion.14
  12.6 0.8 copy.27
  13.6 0.6 fusion.85
  14.2 1.4 fusion.83
  16.0 1.4 fusion.2
  17.3 2.4 convolution_multiply_fusion.3
  19.8 13.7 %reduce-scatter.31.cloned.1.call-done = bf16[32,512]{1,0:T(8,128)(2,1)} async-done(((bf16[128,512]{1,0:T(8,128)(2,1)}), bf16[32,512]{1,0:T(8,128)(2,1)}) %reduce-scatter.31.cloned.1.call-update) | async-done | bytes 32784 | tf_op jit(solution)/shard_map/reduce_scatter | solution.py:38
  33.4 1.7 multiply_convert_fusion.3
  35.5 0.7 fusion.1
  36.3 1.5 pad_maximum_fusion
  37.9 15.2 %reduce-scatter.29.cloned.1.call-done = bf16[32,512]{1,0:T(8,128)(2,1)} async-done(((bf16[128,512]{1,0:T(8,128)(2,1)}), bf16[32,512]{1,0:T(8,128)(2,1)}) %reduce-scatter.29.cloned.1.call-update) | async-done | bytes 32784 | tf_op jit(solution)/shard_map/reduce_scatter | solution.py:38
  53.1 2.2 multiply_convert_fusion.2
  55.3 40.5 %reduce-scatter.17.cloned.1.call-done = f32[64,2,512]{2,0,1:T(8,128)} async-done(((f32[512,2,512]{2,0,1:T(8,128)}), f32[64,2,512]{2,0,1:T(8,128)}) %reduce-scatter.17.cloned.1.call-update) | async-done | bytes 262160 | tf_op jit(solution)/shard_map/reduce_scatter | solution.py:56
  95.8 1.6 convert_element_type.106
  97.5 1.3 convolution_negate_fusion.2
  98.8 1.3 fusion.5
  100.2 33.0 %all-reduce.5.cloned.1.call-done = bf16[64,2,512]{2,0,1:T(8,128)(2,1)} async-done(((bf16[64,2,512]{2,0,1:T(8,128)(2,1)}), bf16[64,2,512]{2,0,1:T(8,128)(2,1)}) %all-reduce.5.cloned.1.call-update) | async-done | bytes 131088 | tf_op jit(solution)/shard_map/psum | solution.py:57
  133.2 1.0 convert_element_type.107
  134.2 1.0 fusion.43
  135.7 1.6 convolution_multiply_fusion.2
  137.2 1.5 fusion.4
  138.8 1.5 pad_maximum_fusion.1
  140.4 1.9 fusion.13
  142.3 1.7 copy.25
  144.0 37.3 %reduce-scatter.19.cloned.1.call-done = f32[64,2,512]{2,0,1:T(8,128)} async-done(((f32[512,2,512]{2,0,1:T(8,128)}), f32[64,2,512]{2,0,1:T(8,128)}) %reduce-scatter.19.cloned.1.call-update) | async-done | bytes 262160 | tf_op jit(solution)/shard_map/reduce_scatter | solution.py:56
  181.3 1.6 convert_element_type.108
  183.0 1.9 fusion.12
  184.9 1.7 copy.23
  186.6 1.3 fusion.8
  188.0 15.3 %reduce-scatter.27.cloned.1.call-done = bf16[32,512]{1,0:T(8,128)(2,1)} async-done(((bf16[128,512]{1,0:T(8,128)(2,1)}), bf16[32,512]{1,0:T(8,128)(2,1)}) %reduce-scatter.27.cloned.1.call-update) | async-done | bytes 32784 | tf_op jit(solution)/shard_map/reduce_scatter | solution.py:38
  203.3 2.2 multiply_convert_fusion.1
  205.5 1.3 convolution_negate_fusion.4
  206.8 31.5 %all-reduce.7.cloned.1.call-done = bf16[64,2,512]{2,0,1:T(8,128)(2,1)} async-done(((bf16[64,2,512]{2,0,1:T(8,128)(2,1)}), bf16[64,2,512]{2,0,1:T(8,128)(2,1)}) %all-reduce.7.cloned.1.call-update) | async-done | bytes 131088 | tf_op jit(solution)/shard_map/psum | solution.py:57
  238.3 1.0 convert_element_type.109
  239.3 1.0 fusion.42
  240.4 0.4 fusion.20
  240.8 1.6 convolution_multiply_fusion.1
  242.4 0.7 fusion.7
  243.1 1.5 pad_maximum_fusion.2
  244.7 14.8 %reduce-scatter.25.cloned.1.call-done = bf16[32,512]{1,0:T(8,128)(2,1)} async-done(((bf16[128,512]{1,0:T(8,128)(2,1)}), bf16[32,512]{1,0:T(8,128)(2,1)}) %reduce-scatter.25.cloned.1.call-update) | async-done | bytes 32784 | tf_op jit(solution)/shard_map/reduce_scatter | solution.py:38
  259.5 2.2 multiply_convert_fusion
  261.7 40.5 %reduce-scatter.21.cloned.1.call-done = f32[64,2,512]{2,0,1:T(8,128)} async-done(((f32[512,2,512]{2,0,1:T(8,128)}), f32[64,2,512]{2,0,1:T(8,128)}) %reduce-scatter.21.cloned.1.call-update) | async-done | bytes 262160 | tf_op jit(solution)/shard_map/reduce_scatter | solution.py:56
  302.2 1.6 convert_element_type.110
  303.9 2.1 convolution_negate_fusion.6
  305.9 2.1 fusion.11
  308.0 31.5 %all-reduce.9.cloned.1.call-done = bf16[64,2,512]{2,0,1:T(8,128)(2,1)} async-done(((bf16[64,2,512]{2,0,1:T(8,128)(2,1)}), bf16[64,2,512]{2,0,1:T(8,128)(2,1)}) %all-reduce.9.cloned.1.call-update) | async-done | bytes 131088 | tf_op jit(solution)/shard_map/psum | solution.py:57
  339.6 1.0 convert_element_type.111
  340.6 0.7 copy-done.25
  341.3 0.9 fusion.41
  342.6 1.6 convolution_multiply_fusion
  344.3 0.7 fusion.10
  345.0 1.6 pad_maximum_fusion.3
  346.7 0.6 copy-done.28
  347.3 0.7 maximum_bitcast_fusion
  348.1 39.5 %reduce-scatter.23.cloned.1.call-done = f32[64,2,512]{2,0,1:T(8,128)} async-done(((f32[512,2,512]{2,0,1:T(8,128)}), f32[64,2,512]{2,0,1:T(8,128)}) %reduce-scatter.23.cloned.1.call-update) | async-done | bytes 262160 | tf_op jit(solution)/shard_map/reduce_scatter | solution.py:56
  387.6 1.6 convert_element_type.112
  389.3 35.6 %all-reduce.11.cloned.1.call-done = bf16[64,2,512]{2,0,1:T(8,128)(2,1)} async-done(((bf16[64,2,512]{2,0,1:T(8,128)(2,1)}), bf16[64,2,512]{2,0,1:T(8,128)(2,1)}) %all-reduce.11.cloned.1.call-update) | async-done | bytes 131088 | tf_op jit(solution)/shard_map/psum | solution.py:57
  425.0 0.9 convert_element_type.113
  425.9 0.9 fusion.40
  426.9 1.1 pad_maximum_fusion.4
  (108 shorter events, 3.0 us)
Async XLA Ops:
  7.2 8.4 %copy-start = (f32[64,512]{1,0:T(8,128)S(1)}, f32[64,512]{1,0:T(8,128)}, u32[]{:S(2)}) copy-start(f32[64,512]{1,0:T(8,128)} %param.12) | copy-start | bytes 393220
  7.2 26.2 %reduce-scatter.31.cloned.1.call-start = ((), (), s32[]{:S(2)}) async-start(), calls=%async_computation.19 | async-start | bytes 163840 | tf_op jit(solution)/shard_map/reduce_scatter | solution.py:38
  8.0 2.3 copy-start.20
  9.4 4.1 copy-start.37
  9.4 4.8 %copy-start.1 = (bf16[4,512,512]{2,1,0:T(8,128)(2,1)S(1)}, bf16[4,512,512]{2,1,0:T(8,128)(2,1)}, u32[]{:S(2)}) copy-start(bf16[4,512,512]{2,1,0:T(8,128)(2,1)} %param.9) | copy-start | bytes 6291460
  11.4 41.8 %reduce-scatter.29.cloned.1.call-start = ((), (), s32[]{:S(2)}) async-start(), calls=%async_computation.18 | async-start | bytes 163840 | tf_op jit(solution)/shard_map/reduce_scatter | solution.py:38
  13.5 82.4 %reduce-scatter.17.cloned.1.call-start = ((), (), s32[]{:S(2)}) async-start(), calls=%async_computation.8 | async-start | bytes 2359296 | tf_op jit(solution)/shard_map/reduce_scatter | solution.py:56
  14.2 1.8 copy-start.36
  15.9 20.2 %copy-start.12 = (f32[64,512]{1,0:T(8,128)}, f32[64,512]{1,0:T(8,128)S(1)}, u32[]{:S(2)}) copy-start(f32[64,512]{1,0:T(8,128)S(1)} %fusion.28) | copy-start | bytes 393220
  33.4 2.0 copy-start.5
  35.1 63.7 %copy-start.27 = (bf16[32,512]{1,0:T(8,128)(2,1)}, bf16[32,512]{1,0:T(8,128)(2,1)S(1)}, u32[]{:S(2)}) copy-start(bf16[32,512]{1,0:T(8,128)(2,1)S(1)} %get-tuple-element.21) | copy-start | bytes 98308
  35.1 1.2 copy-start.7
  37.9 95.3 %all-reduce.5.cloned.1.call-start = ((), (), s32[]{:S(2)}) async-start(), calls=%async_computation.9 | async-start | bytes 262144 | tf_op jit(solution)/shard_map/psum | solution.py:57
  55.3 148.0 %copy-start.29 = (bf16[32,512]{1,0:T(8,128)(2,1)}, bf16[32,512]{1,0:T(8,128)(2,1)S(1)}, u32[]{:S(2)}) copy-start(bf16[32,512]{1,0:T(8,128)(2,1)S(1)} %get-tuple-element.23) | copy-start | bytes 98308
  97.5 83.8 %reduce-scatter.19.cloned.1.call-start = ((), (), s32[]{:S(2)}) async-start(), calls=%async_computation.10 | async-start | bytes 2359296 | tf_op jit(solution)/shard_map/reduce_scatter | solution.py:56
  133.2 4.1 copy-start.2
  134.2 3.0 copy-start.21
  135.6 1.6 copy-start.14
  135.6 3.1 copy-start.8
  140.3 63.0 %reduce-scatter.27.cloned.1.call-start = ((), (), s32[]{:S(2)}) async-start(), calls=%async_computation.17 | async-start | bytes 163840 | tf_op jit(solution)/shard_map/reduce_scatter | solution.py:38
  143.9 94.4 %all-reduce.7.cloned.1.call-start = ((), (), s32[]{:S(2)}) async-start(), calls=%async_computation.11 | async-start | bytes 262144 | tf_op jit(solution)/shard_map/psum | solution.py:57
  183.0 76.5 %reduce-scatter.25.cloned.1.call-start = ((), (), s32[]{:S(2)}) async-start(), calls=%async_computation.16 | async-start | bytes 163840 | tf_op jit(solution)/shard_map/reduce_scatter | solution.py:38
  186.6 115.6 %reduce-scatter.21.cloned.1.call-start = ((), (), s32[]{:S(2)}) async-start(), calls=%async_computation.12 | async-start | bytes 2359296 | tf_op jit(solution)/shard_map/reduce_scatter | solution.py:56
  205.5 32.8 %copy-start.31 = (bf16[32,512]{1,0:T(8,128)(2,1)}, bf16[32,512]{1,0:T(8,128)(2,1)S(1)}, u32[]{:S(2)}) copy-start(bf16[32,512]{1,0:T(8,128)(2,1)S(1)} %get-tuple-element.25) | copy-start | bytes 98308
  238.3 4.1 copy-start.3
  238.3 4.1 copy-start.35
  239.3 3.0 copy-start.23
  240.8 1.6 copy-start.16
  240.8 2.3 copy-start.6
  244.6 94.9 %all-reduce.9.cloned.1.call-start = ((), (), s32[]{:S(2)}) async-start(), calls=%async_computation.13 | async-start | bytes 262144 | tf_op jit(solution)/shard_map/psum | solution.py:57
  303.8 83.8 %reduce-scatter.23.cloned.1.call-start = ((), (), s32[]{:S(2)}) async-start(), calls=%async_computation.14 | async-start | bytes 2359296 | tf_op jit(solution)/shard_map/reduce_scatter | solution.py:56
  339.6 4.7 %copy-start.4 = (f32[512,512]{1,0:T(8,128)S(1)}, f32[512,512]{1,0:T(8,128)}, u32[]{:S(2)}) copy-start(f32[512,512]{1,0:T(8,128)} %convolution_negate_fusion.6) | copy-start | bytes 3145732
  339.6 4.7 %copy-start.34 = (f32[32,512]{1,0:T(8,128)S(1)}, f32[32,512]{1,0:T(8,128)}, u32[]{:S(2)}) copy-start(f32[32,512]{1,0:T(8,128)} %get-tuple-element.28) | copy-start | bytes 196612
  340.6 0.7 copy-start.25
  342.2 2.0 copy-start.10
  342.6 1.6 copy-start.18
  342.6 2.3 copy-start.9
  346.5 0.8 copy-start.28
  346.5 0.8 copy-start.30
  346.5 0.8 copy-start.32
  346.5 0.8 copy-start.33
  346.5 1.5 copy-start.13
  346.5 1.5 copy-start.22
  346.6 1.5 copy-start.15
  346.6 1.5 copy-start.24
  346.6 42.7 %copy-start.17 = (f32[64,512]{1,0:T(8,128)S(1)}, f32[64,512]{1,0:T(8,128)}, u32[]{:S(2)}) copy-start(f32[64,512]{1,0:T(8,128)} %copy-done.16) | copy-start | bytes 393220
  346.6 42.7 %copy-start.26 = (f32[64,2,512]{2,0,1:T(8,128)S(1)}, f32[64,2,512]{2,0,1:T(8,128)}, u32[]{:S(2)}) copy-start(f32[64,2,512]{2,0,1:T(8,128)} %copy-done.25) | copy-start | bytes 786436
  346.6 80.2 %copy-start.19 = (f32[64,512]{1,0:T(8,128)S(1)}, f32[64,512]{1,0:T(8,128)}, u32[]{:S(2)}) copy-start(f32[64,512]{1,0:T(8,128)} %copy-done.18) | copy-start | bytes 393220
  346.6 80.2 %copy-start.11 = (f32[1,64,512]{2,1,0:T(8,128)S(1)}, f32[1,64,512]{2,1,0:T(8,128)}, u32[]{:S(2)}) copy-start(f32[1,64,512]{2,1,0:T(8,128)} %copy-done.10) | copy-start | bytes 393220
  346.6 78.3 %all-reduce.11.cloned.1.call-start = ((), (), s32[]{:S(2)}) async-start(), calls=%async_computation.15 | async-start | bytes 262144 | tf_op jit(solution)/shard_map/psum | solution.py:57
Sparse Core Ops, SparseCore 0:
  11.5 21.8 reduce-scatter.30
  35.7 17.3 reduce-scatter.28
  56.4 39.3 reduce-scatter.16
  98.7 34.4 all-reduce.4
  140.4 40.8 reduce-scatter.18
  184.1 19.1 reduce-scatter.26
  205.6 32.6 all-reduce.6
  240.6 18.7 reduce-scatter.24
  262.8 39.3 reduce-scatter.20
  305.0 34.4 all-reduce.8
  346.8 40.8 reduce-scatter.22
  390.5 34.4 all-reduce.10
where the time goes:
time: 436 us; the launch traced here: 435 us
  waiting for transfers between devices  349 us (80%)
  matrix products  36.9 us (8%)
  other arithmetic  24.5 us (6%)
  between operations  14.8 us (3%)
  local copies, waits for them, and re-layouts  9.36 us (2%)
    reduce_scatter x4, waiting for transfers between devices, local(): reduced = lax.psum_scatter(joined, 'rows', scatter_dimension=0, tiled=True)  158 us
    psum x4, waiting for transfers between devices, local(): reduced = lax.psum(reduced.astype(jnp.bfloat16), 'cols').astype(jnp.float32)  132 us
    reduce_scatter x4, waiting for transfers between devices, local(): lax.psum_scatter(jnp.dot(known_rows, panel_slab[section], preferred_eleme...  59 us
    convert_element_type x8, other arithmetic, local(): reduced = lax.psum(reduced.astype(jnp.bfloat16), 'cols').astype(jnp.float32)  10.4 us
  transfers between devices with their start and end apart: 12, of which 12 were waited for; matrix products, arithmetic and copies ran while one was open for 10% of the time, Pallas kernels for 0%

commit v1 on v0

v1 whole, which is shorter than its diff:
```python
import jax
import jax.numpy as jnp
from jax import lax
from jax.sharding import PartitionSpec as P

BF = jnp.bfloat16
F32 = jnp.float32


def dot(a, b):
    return jnp.dot(a, b, preferred_element_type=F32)


def dot_nt(a, b):
    return lax.dot_general(a, b, (((1,), (1,)), ((), ())), preferred_element_type=F32)


def pow2(n):
    return n & (n - 1) == 0


def target(i, j, n):
    return i ^ j if pow2(n) else (i + j) % n


def source(i, j, n):
    return i ^ j if pow2(n) else (i - j) % n


def hop(x, axis, j):
    n = lax.axis_size(axis)
    return lax.ppermute(x, axis, [(i, target(i, j, n)) for i in range(n)])


def gather_rows(x):
    n = lax.axis_size("rows")
    me = lax.axis_index("rows")
    if n == 8:
        parts = [x] + [hop(x, "rows", j) for j in (6, 4, 2)]
        offsets = [0, 6, 4, 2]
        here = jnp.stack(parts)
        there = hop(here, "rows", 1)
        whole = jnp.concatenate([here, there], 0)
        offsets = offsets + [o ^ 1 for o in offsets]
        return whole, [source(me, o, n) for o in offsets]
    if pow2(n):
        whole, offsets, bit = x[None], [0], n // 2
        while bit:
            whole = jnp.concatenate([whole, hop(whole, "rows", bit)], 0)
            offsets = offsets + [o ^ bit for o in offsets]
            bit //= 2
        return whole, [source(me, o, n) for o in offsets]
    return lax.all_gather(x, "rows"), list(range(n))


def scatter_cols(pieces):
    n = lax.axis_size("cols")
    me = lax.axis_index("cols")
    total = lax.dynamic_index_in_dim(pieces, me, 0, False).astype(F32)
    for j in reversed(range(1, n)):
        sent = lax.dynamic_index_in_dim(pieces, target(me, j, n), 0, False)
        total = total + hop(sent, "cols", j).astype(F32)
    return total


def gather_cols(x):
    n = lax.axis_size("cols")
    me = lax.axis_index("cols")
    whole = jnp.zeros((n,) + x.shape, x.dtype)
    got = [(me, x)] + [(source(me, j, n), hop(x, "cols", j)) for j in reversed(range(1, n))]
    for at, piece in got:
        whole = lax.dynamic_update_index_in_dim(whole, piece, at, 0)
    return whole


def local(known_inverse, lower_panel, chain_panel, diag_inverse, top_cols, top_diag, pattern):
    n_rows = lax.axis_size("rows")
    n_cols = lax.axis_size("cols")
    row_id = lax.axis_index("rows")
    col_id = lax.axis_index("cols")
    supers = lower_panel.shape[0]
    piece = known_inverse.shape[2]
    width = lower_panel.shape[-1]
    share = width // n_rows
    known = known_inverse.reshape(n_cols * piece, -1)
    group_mask = lax.dynamic_slice_in_dim(pattern, col_id * n_rows, n_rows, 1).astype(BF)
    panels = lower_panel[:, 0] * group_mask[:, :, None, None]
    own_mask = lax.dynamic_index_in_dim(group_mask, row_id, 1, keepdims=False).astype(F32)

    slabs = panels.reshape(supers, n_rows * piece, width)
    partial = jnp.stack([dot(known, slabs[k]).astype(BF).reshape(n_cols, piece, width) for k in range(supers)], 1)
    product = scatter_cols(partial)

    start = [top_diag] + [diag_inverse[k] for k in reversed(range(1, supers))]
    level_of = lambda c: supers - c
    mine = jnp.zeros((share, width), F32)
    for i, s in enumerate(start):
        mine = jnp.where(col_id % len(start) == i, s, mine) if n_cols <= len(start) else jnp.where(col_id == i, s, mine)
    joined = jnp.concatenate([mine.astype(BF), top_cols.reshape(piece, width)], 0)
    gathered, order = gather_rows(joined)
    shares = gathered[:, :share].reshape(width, width)
    tops = gathered[:, share:].reshape(n_rows * piece, width)
    order = jnp.stack([jnp.asarray(o, jnp.int32) for o in order])
    panel_rel = [p[order].reshape(n_rows * piece, width) for p in panels]
    own_rows = (lax.broadcasted_iota(jnp.int32, (share, width), 1) == row_id * share + lax.broadcasted_iota(jnp.int32, (share, width), 0)).astype(BF)
    stacks = [own_rows]
    for k in range(supers):
        stacks.append(jnp.concatenate([dot_nt(stacks[k], chain_panel[k]).astype(BF), own_rows], 0))
    begins = []
    for k in range(supers + 1):
        rel = stacks[k].reshape(-1, n_rows, share)[:, order].reshape(-1, width)
        begins.append(dot(rel, shares))
    reach = [dot_nt(stacks[k], panel_rel[k]).astype(BF) for k in range(supers)]

    prev = top_cols.reshape(piece, width)
    cols_list = [None] * supers
    for k in reversed(range(supers)):
        carried = dot(prev, chain_panel[k])
        prev = (-(product[k] + carried) * own_mask[k]).astype(BF)
        cols_list[k] = prev
    cols_out = jnp.stack(cols_list)
    all_cols, _ = gather_rows(cols_out)
    slab_cols = [all_cols[:, k].reshape(n_rows * piece, width) for k in range(supers)] + [tops]

    acc = jnp.where(col_id == 0, begins[supers], 0.0)
    diag_list = [None] * supers
    sub_list = [None] * supers
    for k in reversed(range(supers)):
        across = dot_nt(stacks[k + 1], slab_cols[k + 1]).astype(BF)
        full = dot(acc.astype(BF), chain_panel[k]) + dot(across, panel_rel[k])
        sub_list[k] = -full[(k + 1) * share:]
        acc = full[: (k + 1) * share] - dot(reach[k], slab_cols[k])
        diag_list[k] = acc[k * share :]
        if k:
            acc = acc + jnp.where(col_id == level_of(k), begins[k], 0.0)
    done = jnp.stack(diag_list + sub_list)
    if share % n_cols == 0:
        part = share // n_cols
        pieces = jnp.swapaxes(done.astype(BF).reshape(2 * supers, n_cols, part, width), 0, 1)
        summed = gather_cols(scatter_cols(pieces).astype(BF))
        summed = jnp.swapaxes(summed, 0, 1).reshape(2 * supers, share, width)
    else:
        summed = lax.psum(done.astype(BF), "cols")
    summed = summed.astype(F32)
    return (
        cols_out.reshape(supers, 1, 1, piece, width),
        diag_inverse + summed[:supers],
        summed[supers:],
    )


def solution(mesh):
    in_specs = (
        P(None, "rows", None, "cols"),
        P(None, "cols", None, None, None),
        P(),
        P(None, "rows", None),
        P("cols", "rows", None, None),
        P("rows", None),
        P(),
    )
    out_specs = (P(None, "cols", "rows", None, None), P(None, "rows", None), P(None, "rows", None))
    return jax.shard_map(local, mesh=mesh, in_specs=in_specs, out_specs=out_specs, check_vma=False)
```

time: 436 us -> 134 us (0.31)
  waiting for transfers between devices: 349 us -> 25.1 us
  local copies, waits for them, and re-layouts: 9.36 us -> 30.5 us
  starting transfers between devices: 0.5 us -> 21.5 us
  between operations: 14.8 us -> 1.23 us
    reduce_scatter x8 -> x0, waiting for transfers between devices: 217 us -> none  [the longest x4 158 us: local(): reduced = lax.psum_scatter(joined, 'rows', scatter_dimension=0, tiled=True)]
    psum x4 -> x0, waiting for transfers between devices: 132 us -> none  [local(): reduced = lax.psum(reduced.astype(jnp.bfloat16), 'cols').astype(jnp.float32)]
    ppermute x0 -> x17, waiting for transfers between devices: none -> 25.1 us  [hop(): return lax.ppermute(x, axis, [(i, target(i, j, n)) for i in range(n)])]
    ppermute x0 -> x17, starting transfers between devices: none -> 21.5 us  [hop(): return lax.ppermute(x, axis, [(i, target(i, j, n)) for i in range(n)])]
    convert_element_type x10 -> x5, other arithmetic: 11.3 us -> 2.16 us  [the longest x1 1.14 us: local(): mine.astype(BF)]
    gather x0 -> x8, local copies, waits for them, and re-layouts: none -> 8.09 us  [the longest x4 5.12 us: local(): rel = stacks[k].reshape(-1, n_rows, share)[:, order].reshape(-1, width)]
    concatenate x0 -> x6, local copies, waits for them, and re-layouts: none -> 5.41 us  [the longest x4 3.48 us: local(): jnp.concatenate([dot_nt(stacks[k], chain_panel[k]).astype(BF), own_rows], 0)]
    slice x3 -> x7, local copies, waits for them, and re-layouts: 2.82 us -> 8.03 us  [the longest x3 3.75 us: local(): diag_list[k] = acc[k * share:]]
  transfers between devices with their start and end apart: 12 -> 17, of which waited for: 12 -> 7; matrix products, arithmetic and copies ran while one was open for 10% -> 36% of each run, Pallas kernels for 0% -> 0%
where the time goes in v1:
time: 134 us; the launch traced here: 132 us
  matrix products  32.8 us (24%)
  local copies, waits for them, and re-layouts  30.5 us (23%)
  waiting for transfers between devices  25.1 us (19%)
  starting transfers between devices  21.5 us (16%)
  other arithmetic  21.3 us (16%)
    dot_general x20, matrix products, dot(): return jnp.dot(a, b, preferred_element_type=F32)  30.8 us
    ppermute x17, waiting for transfers between devices, hop(): return lax.ppermute(x, axis, [(i, target(i, j, n)) for i in range(n)])  25.1 us
    ppermute x17, starting transfers between devices, hop(): return lax.ppermute(x, axis, [(i, target(i, j, n)) for i in range(n)])  21.5 us
    unnamed x63, local copies, waits for them, and re-layouts  7.8 us
    gather x4, local copies, waits for them, and re-layouts, local(): rel = stacks[k].reshape(-1, n_rows, share)[:, order].reshape(-1, width)  5.12 us
    another operation x4, other arithmetic  4.64 us
    another operation x4, other arithmetic, gather_rows(): here = jnp.stack(parts)  4.04 us
    concatenate x4, other arithmetic, local(): jnp.concatenate([dot_nt(stacks[k], chain_panel[k]).astype(BF), own_rows], 0)  3.78 us
  transfers between devices with their start and end apart: 17, of which 7 were waited for; matrix products, arithmetic and copies ran while one was open for 36% of the time, Pallas kernels for 0%

profile of v1, /device:TPU:0, one launch (start us, length us, event | category | flops | bytes accessed | tf_op | source)
XLA Modules:
  0.0 132.5 jit_solution(15088546399019383992)
XLA Ops:
  0.7 1.1 fusion.77
  1.8 1.4 %fusion.113 = (bf16[1,96,512]{2,1,0:T(8,128)(2,1)}, bf16[96,512]{1,0:T(8,128)(2,1)}) fusion(bf16[32,512]{1,0:T(8,128)(2,1)} %bitcast.355, bf16[64,512]{1,0:T(8,128)(2,1)S(1)} %fusion.77), kind=kLoop, calls=%fused_computation.200 | loop fusion | flops 196608 | bytes 294912 | tf_op jit(solution)/shard_map/stack | solution.py:41
  3.3 3.9 %collective-permute-start.3 = (bf16[96,512]{1,0:T(8,128)(2,1)}, bf16[96,512]{1,0:T(8,128)(2,1)}, u32[]{:S(2)}, u32[]{:S(2)}) collective-permute-start(bf16[96,512]{1,0:T(8,128)(2,1)} %get-tuple-element.35), channel_id=1, source_target_pairs={{0,24},{4,28},{8,16},{12,20},{16,8},{20,12},{24,0},{28,4},{1,25},{... | collective-permute-start | bytes 294920 | tf_op jit(solution)/shard_map/ppermute | solution.py:32
  8.5 1.4 %bitcast_multiply_fusion = bf16[4,8,32,512]{3,2,1,0:T(8,128)(2,1)S(1)} fusion(bf16[4,1,8,32,512]{4,3,2,1,0:T(8,128)(2,1)} %param.8, bf16[4,8]{1,0:T(4,128)(2,1)S(1)} %fusion.101), kind=kLoop, calls=%fused_computation.52 | loop fusion | flops 524288 | bytes 2097216 | tf_op jit(solution)/shard_map/mul | solution.py:87
  10.1 0.8 convolution_convert_fusion.6
  10.9 0.8 convolution_convert_fusion.7
  11.8 0.8 convolution_convert_fusion.8
  12.6 0.8 convolution_convert_fusion.9
  13.4 1.2 pad_maximum_fusion
  16.1 2.0 %collective-permute-start.2 = (bf16[4,32,512]{2,1,0:T(8,128)(2,1)}, bf16[4,32,512]{2,1,0:T(8,128)(2,1)}, u32[]{:S(2)}, u32[]{:S(2)}) collective-permute-start(bf16[4,32,512]{2,1,0:T(8,128)(2,1)} %get-tuple-element.29), channel_id=1, source_target_pairs={{0,1},{1,0},{2,3},{3,2},{4,5},{5,4},{6,7},{7,6},{8,9},{9,8},{10,11... | collective-permute-start | bytes 393224 | tf_op jit(solution)/shard_map/ppermute | solution.py:32
  18.1 2.6 %collective-permute-start.1 = (bf16[4,32,512]{2,1,0:T(8,128)(2,1)}, bf16[4,32,512]{2,1,0:T(8,128)(2,1)}, u32[]{:S(2)}, u32[]{:S(2)}) collective-permute-start(bf16[4,32,512]{2,1,0:T(8,128)(2,1)} %get-tuple-element.30), channel_id=1, source_target_pairs={{0,2},{1,3},{2,0},{3,1},{4,6},{5,7},{6,4},{7,5},{8,10},{9,11},{10,... | collective-permute-start | bytes 393224 | tf_op jit(solution)/shard_map/ppermute | solution.py:32
  20.7 1.4 %constant_dynamic-update-slice_fusion.4 = bf16[8,96,512]{2,1,0:T(8,128)(2,1)} fusion(bf16[32,512]{1,0:T(8,128)(2,1)} %bitcast.356, bf16[64,512]{1,0:T(8,128)(2,1)S(1)} %fusion.77), kind=kLoop, calls=%fused_computation.168 | loop fusion | flops 196607 | bytes 196608
  23.2 1.0 convolution_convert_fusion
  27.1 1.3 gather_fusion.5
  29.5 1.7 %pad_maximum_fusion.3 = bf16[320,512]{1,0:T(8,128)(2,1)} fusion(bf16[64,512]{1,0:T(8,128)(2,1)S(1)} %fusion.79, bf16[256,512]{1,0:T(8,128)(2,1)} %convolution_convert_fusion), kind=kLoop, calls=%fused_computation.91 | loop fusion | flops 655360 | bytes 655360 | tf_op jit(solution)/shard_map/concatenate | solution.py:108
  31.2 1.2 copy.23
  32.4 1.3 %gather_fusion = bf16[8,320,64]{1,2,0:T(8,128)(2,1)} fusion(bf16[320,8,64]{0,2,1:T(8,128)(2,1)S(1)} %bitcast.317, s32[1024]{0:T(1024)S(1)} %pad_clamp_fusion), kind=kCustom, calls=%fused_computation | custom fusion | bytes 655392 | tf_op jit(solution)/shard_map/gather | solution.py:111
  33.7 1.1 copy.24
  34.9 1.3 gather_fusion.2
  36.1 1.1 copy.25
  37.2 1.3 gather_fusion.4
  38.6 1.2 gather_fusion.6
  40.5 1.0 pad_maximum_fusion.2
  41.6 1.5 %constant_dynamic-update-slice_fusion.3 = bf16[8,96,512]{2,1,0:T(8,128)(2,1)} fusion(bf16[8,96,512]{2,1,0:T(8,128)(2,1)} %constant_dynamic-update-slice_fusion.4, bf16[96,512]{1,0:T(8,128)(2,1)} %collective-permute-done.3), kind=kLoop, calls=%fused_computation.167 | loop fusion | bytes 196608
  43.1 1.5 %constant_dynamic-update-slice_fusion.2 = bf16[8,96,512]{2,1,0:T(8,128)(2,1)} fusion(bf16[8,96,512]{2,1,0:T(8,128)(2,1)} %constant_dynamic-update-slice_fusion.3, bf16[96,512]{1,0:T(8,128)(2,1)} %collective-permute-done.4), kind=kLoop, calls=%fused_computation.166 | loop fusion | bytes 196608
  44.7 2.8 %collective-permute-done = bf16[4,32,512]{2,1,0:T(8,128)(2,1)S(1)} collective-permute-done((bf16[4,32,512]{2,1,0:T(8,128)(2,1)}, bf16[4,32,512]{2,1,0:T(8,128)(2,1)S(1)}, u32[]{:S(2)}, u32[]{:S(2)}) %collective-permute-start) | collective-permute-done | bytes 131104 | tf_op jit(solution)/shard_map/ppermute | solution.py:32
  47.5 1.1 fusion.60
  49.4 0.8 fusion.88
  50.2 0.8 fusion.92
  52.5 2.4 %collective-permute-start.7 = (bf16[4,32,512]{2,1,0:T(8,128)(2,1)S(1)}, bf16[4,32,512]{2,1,0:T(8,128)(2,1)S(1)}, u32[]{:S(2)}, u32[]{:S(2)}) collective-permute-start(bf16[4,32,512]{2,1,0:T(8,128)(2,1)S(1)} %get-tuple-element.33), channel_id=1, source_target_pairs={{0,24},{4,28},{8,16},{12,20},{16,8},{20,12},{24,0},{28,4},{1,25},{... | collective-permute-start | bytes 393224 | tf_op jit(solution)/shard_map/ppermute | solution.py:32
  56.0 0.9 constant_dynamic-update-slice_fusion.1
  57.5 1.8 %collective-permute-done.7 = bf16[4,32,512]{2,1,0:T(8,128)(2,1)S(1)} collective-permute-done((bf16[4,32,512]{2,1,0:T(8,128)(2,1)S(1)}, bf16[4,32,512]{2,1,0:T(8,128)(2,1)S(1)}, u32[]{:S(2)}, u32[]{:S(2)}) %collective-permute-start.7) | collective-permute-done | bytes 131104 | tf_op jit(solution)/shard_map/ppermute | solution.py:32
  59.3 1.1 collective-permute-done.8
  60.5 0.9 pad_maximum_fusion.1
  63.4 0.9 copy-done.12
  65.0 2.4 %fusion.13 = f32[320,512]{1,0:T(8,128)} fusion(bf16[256,512]{1,0:T(8,128)(2,1)S(1)} %bitcast.320, bf16[256,512]{1,0:T(8,128)(2,1)} %bitcast.339, bf16[64,512]{1,0:T(8,128)(2,1)S(1)} %fusion.79, bf16[256,512]{1,0:T(8,128)(2,1)} %convolution_convert_fusion), kind=kOutput, calls=%fused_computation.42 | convolution fusion | flops 168509440 | bytes 1507328 | tf_op jit(solution)/shard_map/dot_general | solution.py:11
  67.4 2.7 %convolution_add_fusion = f32[320,512]{1,0:T(8,128)} fusion(f32[320,512]{1,0:T(8,128)} %fusion.13, bf16[4,512,512]{2,1,0:T(8,128)(2,1)S(1)} %copy-done.1, bf16[8,320,64]{1,2,0:T(8,128)(2,1)S(1)} %copy-done.10, bf16[8,96,512]{2,1,0:T(8,128)(2,1)} %copy-done.12, pred[]{:T(512)S(6)} %eq.32), kind=kOutput, calls=%fused_computation.8 | convolution fusion | flops 336035840 | bytes 2752513 | tf_op jit(solution)/shard_map/dot_general | solution.py:11
  70.1 1.5 %fusion.69 = bf16[64,512]{1,0:T(8,128)(2,1)} fusion(f32[320,512]{1,0:T(8,128)} %convolution_add_fusion), kind=kLoop, calls=%fused_computation.110 | loop fusion | flops 65536 | bytes 196608 | tf_op jit(solution)/shard_map/convert.11
  71.7 1.9 %constant_dynamic-update-slice_fusion.5 = bf16[8,4,32,512]{3,2,1,0:T(8,128)(2,1)} fusion(bf16[8,4,32,512]{3,2,1,0:T(8,128)(2,1)} %constant_dynamic-update-slice_fusion.6, bf16[4,4,32,512]{3,2,1,0:T(8,128)(2,1)} %collective-permute-done.10), kind=kLoop, calls=%fused_computation.169 | loop fusion | bytes 1048576 | tf_op jit(solution)/shard_map/concatenate | solution.py:43
  73.6 2.1 %fusion.118 = (bf16[8,1,32,512]{3,2,1,0:T(8,128)(2,1)S(1)}, bf16[8,1,32,512]{3,2,1,0:T(8,128)(2,1)}, bf16[8,1,32,512]{3,2,1,0:T(8,128)(2,1)}, bf16[8,1,32,512]{3,2,1,0:T(8,128)(2,1)S(1)}) fusion(bf16[8,4,32,512]{3,2,1,0:T(8,128)(2,1)} %constant_dynamic-update-slice_fusion.5), kind=kLoop, calls=%fused_computation.204 | loop fusion | bytes 2097152 | tf_op jit(solution)/shard_map/slice | solution.py:123
  75.6 2.4 %convolution_subtract_fusion = f32[256,512]{1,0:T(8,128)} fusion(bf16[256,512]{1,0:T(8,128)(2,1)S(1)} %bitcast.326, bf16[256,512]{1,0:T(8,128)(2,1)S(1)} %bitcast.321, f32[320,512]{1,0:T(8,128)} %convolution_add_fusion, bf16[64,512]{1,0:T(8,128)(2,1)S(1)} %fusion.79, bf16[192,512]{1,0:T(8,128)(2,1)} %copy-done.5), kind=kOutput, calls=%fused_computation.12 | convolution fusion | flops 134938624 | bytes 1835008 | tf_op jit(solution)/shard_map/dot_general | solution.py:11
  78.1 1.6 %slice.348 = bf16[64,512]{1,0:T(8,128)(2,1)} slice(f32[256,512]{1,0:T(8,128)} %convolution_subtract_fusion), slice={[192:256], [0:512]} | slice | bytes 131072 | tf_op jit(solution)/shard_map/slice | solution.py:133
  79.7 2.6 %fusion.8 = f32[256,512]{1,0:T(8,128)} fusion(f32[256,512]{1,0:T(8,128)} %convolution_subtract_fusion, bf16[4,512,512]{2,1,0:T(8,128)(2,1)S(1)} %copy-done.1, bf16[8,96,512]{2,1,0:T(8,128)(2,1)} %copy-done.12, bf16[8,256,64]{1,2,0:T(8,128)(2,1)} %gather_fusion.2, pred[]{:T(512)S(6)} %eq.38), kind=kOutput, calls=%fused_computation.29 | convolution fusion | flops 268828672 | bytes 2359297 | tf_op jit(solution)/shard_map/dot_general | solution.py:11
  82.3 2.3 %convolution_add_fusion.1 = f32[256,512]{1,0:T(8,128)} fusion(f32[256,512]{1,0:T(8,128)} %fusion.8, bf16[256,512]{1,0:T(8,128)(2,1)S(1)} %bitcast.318, bf16[256,512]{1,0:T(8,128)(2,1)S(1)} %bitcast.327, bf16[64,512]{1,0:T(8,128)(2,1)S(1)} %fusion.79, bf16[192,512]{1,0:T(8,128)(2,1)S(1)} %copy-done.6), kind=kOutput, calls=%fused_computation.11 | convolution fusion | flops 134938624 | bytes 1835008 | tf_op jit(solution)/shard_map/dot_general | solution.py:11
  84.6 1.5 %fusion.70 = bf16[64,512]{1,0:T(8,128)(2,1)} fusion(f32[256,512]{1,0:T(8,128)} %convolution_add_fusion.1), kind=kLoop, calls=%fused_computation.112 | loop fusion | flops 65536 | bytes 196608 | tf_op jit(solution)/shard_map/convert.12
  86.2 2.3 %convolution_subtract_fusion.1 = f32[192,512]{1,0:T(8,128)} fusion(bf16[256,512]{1,0:T(8,128)(2,1)S(1)} %bitcast.331, bf16[256,512]{1,0:T(8,128)(2,1)S(1)} %bitcast.319, f32[256,512]{1,0:T(8,128)} %convolution_add_fusion.1, bf16[64,512]{1,0:T(8,128)(2,1)S(1)} %fusion.79, bf16[128,512]{1,0:T(8,128)(2,1)} %copy-done.7), kind=kOutput, calls=%fused_computation.20 | convolution fusion | flops 101203968 | bytes 1507328 | tf_op jit(solution)/shard_map/dot_general | solution.py:11
  88.5 1.5 %slice.349 = bf16[64,512]{1,0:T(8,128)(2,1)} slice(f32[192,512]{1,0:T(8,128)} %convolution_subtract_fusion.1), slice={[128:192], [0:512]} | slice | bytes 131072 | tf_op jit(solution)/shard_map/slice | solution.py:133
  90.0 2.5 %fusion.12 = f32[192,512]{1,0:T(8,128)} fusion(f32[192,512]{1,0:T(8,128)} %convolution_subtract_fusion.1, bf16[4,512,512]{2,1,0:T(8,128)(2,1)S(1)} %copy-done.1, bf16[8,96,512]{2,1,0:T(8,128)(2,1)} %copy-done.12, bf16[8,192,64]{1,2,0:T(8,128)(2,1)} %gather_fusion.4, pred[]{:T(512)S(6)} %eq.39), kind=kOutput, calls=%fused_computation.41 | convolution fusion | flops 201621504 | bytes 2097153 | tf_op jit(solution)/shard_map/dot_general | solution.py:11
  92.5 2.3 %convolution_add_fusion.2 = f32[192,512]{1,0:T(8,128)} fusion(f32[192,512]{1,0:T(8,128)} %fusion.12, bf16[256,512]{1,0:T(8,128)(2,1)S(1)} %bitcast.324, bf16[256,512]{1,0:T(8,128)(2,1)S(1)} %bitcast.332, bf16[64,512]{1,0:T(8,128)(2,1)S(1)} %fusion.79, bf16[128,512]{1,0:T(8,128)(2,1)S(1)} %copy-done.8), kind=kOutput, calls=%fused_computation.18 | convolution fusion | flops 101203968 | bytes 1507328 | tf_op jit(solution)/shard_map/dot_general | solution.py:11
  94.8 1.6 %fusion.71 = bf16[64,512]{1,0:T(8,128)(2,1)} fusion(f32[192,512]{1,0:T(8,128)} %convolution_add_fusion.2), kind=kLoop, calls=%fused_computation.114 | loop fusion | flops 65536 | bytes 196608 | tf_op jit(solution)/shard_map/convert.13
  96.4 1.4 %convolution_subtract_fusion.2 = f32[128,512]{1,0:T(8,128)S(1)} fusion(bf16[256,512]{1,0:T(8,128)(2,1)S(1)} %bitcast.329, bf16[256,512]{1,0:T(8,128)(2,1)S(1)} %bitcast.325, f32[192,512]{1,0:T(8,128)} %convolution_add_fusion.2, bf16[64,512]{1,0:T(8,128)(2,1)S(1)} %fusion.79, bf16[64,512]{1,0:T(8,128)(2,1)} %copy-done.14), kind=kOutput, calls=%fused_computation.28 | convolution fusion | flops 67469312 | bytes 1179648 | tf_op jit(solution)/shard_map/dot_general | solution.py:11
  98.4 1.5 %fusion.14 = f32[128,512]{1,0:T(8,128)S(1)} fusion(f32[128,512]{1,0:T(8,128)S(1)} %convolution_subtract_fusion.2, bf16[4,512,512]{2,1,0:T(8,128)(2,1)S(1)} %copy-done.1, bf16[8,96,512]{2,1,0:T(8,128)(2,1)} %copy-done.12, bf16[8,128,64]{1,2,0:T(8,128)(2,1)S(1)} %copy-done.9, pred[]{:T(512)S(6)} %eq.40), kind=kOutput, calls=%fused_computation.45 | convolution fusion | flops 134414336 | bytes 1703937 | tf_op jit(solution)/shard_map/dot_general | solution.py:11
  100.5 1.4 %fusion.15 = bf16[64,512]{1,0:T(8,128)(2,1)S(1)} fusion(bf16[256,512]{1,0:T(8,128)(2,1)} %bitcast.340, bf16[256,512]{1,0:T(8,128)(2,1)S(1)} %bitcast.323, f32[128,512]{1,0:T(8,128)S(1)} %convolution_add_fusion.3, s32[64]{0:T(128)S(1)} %iota_add_fusion), kind=kOutput, calls=%fused_computation.47 | convolution fusion | flops 33669120 | bytes 721152 | tf_op jit(solution)/shard_map/dot_general | solution.py:11
  102.1 0.8 collective-permute-start.13
  102.9 2.6 %collective-permute-start.12 = (bf16[8,16,512]{2,1,0:T(8,128)(2,1)S(1)}, bf16[8,16,512]{2,1,0:T(8,128)(2,1)S(1)}, u32[]{:S(2)}, u32[]{:S(2)}) collective-permute-start(bf16[8,16,512]{2,1,0:T(8,128)(2,1)S(1)} %get-tuple-element.27), channel_id=1, source_target_pairs={{0,2},{1,3},{2,0},{3,1},{4,6},{5,7},{6,4},{7,5},{8,10},{9,11},{10,... | collective-permute-start | bytes 393224 | tf_op jit(solution)/shard_map/ppermute | solution.py:32
  105.4 1.1 collective-permute-start.11
  106.5 3.8 %collective-permute-done.13 = bf16[8,16,512]{2,1,0:T(8,128)(2,1)S(1)} collective-permute-done((bf16[8,16,512]{2,1,0:T(8,128)(2,1)S(1)}, bf16[8,16,512]{2,1,0:T(8,128)(2,1)S(1)}, u32[]{:S(2)}, u32[]{:S(2)}) %collective-permute-start.13) | collective-permute-done | bytes 131104 | tf_op jit(solution)/shard_map/ppermute | solution.py:32
  110.4 5.4 %collective-permute-done.12 = bf16[8,16,512]{2,1,0:T(8,128)(2,1)S(1)} collective-permute-done((bf16[8,16,512]{2,1,0:T(8,128)(2,1)S(1)}, bf16[8,16,512]{2,1,0:T(8,128)(2,1)S(1)}, u32[]{:S(2)}, u32[]{:S(2)}) %collective-permute-start.12) | collective-permute-done | bytes 131104 | tf_op jit(solution)/shard_map/ppermute | solution.py:32
  115.9 2.1 %collective-permute-start.14 = (bf16[8,16,512]{2,1,0:T(8,128)(2,1)S(1)}, bf16[8,16,512]{2,1,0:T(8,128)(2,1)S(1)}, u32[]{:S(2)}, u32[]{:S(2)}) collective-permute-start(bf16[8,16,512]{2,1,0:T(8,128)(2,1)S(1)} %get-tuple-element.10), channel_id=1, source_target_pairs={{0,3},{1,2},{2,1},{3,0},{4,7},{5,6},{6,5},{7,4},{8,11},{9,10},{10,... | collective-permute-start | bytes 393224 | tf_op jit(solution)/shard_map/ppermute | solution.py:32
  118.0 2.1 %collective-permute-start.15 = (bf16[8,16,512]{2,1,0:T(8,128)(2,1)S(1)}, bf16[8,16,512]{2,1,0:T(8,128)(2,1)S(1)}, u32[]{:S(2)}, u32[]{:S(2)}) collective-permute-start(bf16[8,16,512]{2,1,0:T(8,128)(2,1)S(1)} %get-tuple-element.10), channel_id=1, source_target_pairs={{0,2},{1,3},{2,0},{3,1},{4,6},{5,7},{6,4},{7,5},{8,10},{9,11},{10,... | collective-permute-start | bytes 393224 | tf_op jit(solution)/shard_map/ppermute | solution.py:32
  120.4 2.7 %collective-permute-done.14 = bf16[8,16,512]{2,1,0:T(8,128)(2,1)S(1)} collective-permute-done((bf16[8,16,512]{2,1,0:T(8,128)(2,1)S(1)}, bf16[8,16,512]{2,1,0:T(8,128)(2,1)S(1)}, u32[]{:S(2)}, u32[]{:S(2)}) %collective-permute-start.14) | collective-permute-done | bytes 131104 | tf_op jit(solution)/shard_map/ppermute | solution.py:32
  123.1 7.4 %collective-permute-done.15 = bf16[8,16,512]{2,1,0:T(8,128)(2,1)S(1)} collective-permute-done((bf16[8,16,512]{2,1,0:T(8,128)(2,1)S(1)}, bf16[8,16,512]{2,1,0:T(8,128)(2,1)S(1)}, u32[]{:S(2)}, u32[]{:S(2)}) %collective-permute-start.15) | collective-permute-done | bytes 131104 | tf_op jit(solution)/shard_map/ppermute | solution.py:32
  130.7 0.9 fusion.117
  131.6 0.9 bitcast_add_fusion
  (114 shorter events, 17.3 us)
Async XLA Ops:
  0.6 9.4 %copy-start = (bf16[4,1,32,256]{3,2,1,0:T(8,128)(2,1)S(1)}, bf16[4,1,32,256]{3,2,1,0:T(8,128)(2,1)}, u32[]{:S(2)}) copy-start(bf16[4,1,32,256]{3,2,1,0:T(8,128)(2,1)} %param.7) | copy-start | bytes 196612
  3.3 37.2 %collective-permute-start.3 = (bf16[96,512]{1,0:T(8,128)(2,1)}, bf16[96,512]{1,0:T(8,128)(2,1)}, u32[]{:S(2)}, u32[]{:S(2)}) collective-permute-start(bf16[96,512]{1,0:T(8,128)(2,1)} %get-tuple-element.35), channel_id=1, source_target_pairs={{0,24},{4,28},{8,16},{12,20},{16,8},{20,12},{24,0},{28,4},{1,25},{... | collective-permute-start | bytes 294920 | tf_op jit(solution)/shard_map/ppermute | solution.py:32
  7.1 33.3 %collective-permute-start.4 = (bf16[96,512]{1,0:T(8,128)(2,1)}, bf16[96,512]{1,0:T(8,128)(2,1)}, u32[]{:S(2)}, u32[]{:S(2)}) collective-permute-start(bf16[96,512]{1,0:T(8,128)(2,1)} %get-tuple-element.35), channel_id=1, source_target_pairs={{0,16},{4,20},{8,24},{12,28},{16,0},{20,4},{24,8},{28,12},{1,17},{... | collective-permute-start | bytes 294920 | tf_op jit(solution)/shard_map/ppermute | solution.py:32
  7.7 32.8 %collective-permute-start.5 = (bf16[96,512]{1,0:T(8,128)(2,1)}, bf16[96,512]{1,0:T(8,128)(2,1)}, u32[]{:S(2)}, u32[]{:S(2)}) collective-permute-start(bf16[96,512]{1,0:T(8,128)(2,1)} %get-tuple-element.35), channel_id=1, source_target_pairs={{0,8},{4,12},{8,0},{12,4},{16,24},{20,28},{24,16},{28,20},{1,9},{5... | collective-permute-start | bytes 294920 | tf_op jit(solution)/shard_map/ppermute | solution.py:32
  10.1 12.2 %copy-start.1 = (bf16[4,512,512]{2,1,0:T(8,128)(2,1)S(1)}, bf16[4,512,512]{2,1,0:T(8,128)(2,1)}, u32[]{:S(2)}) copy-start(bf16[4,512,512]{2,1,0:T(8,128)(2,1)} %param.9) | copy-start | bytes 6291460
  14.6 0.8 copy-start.4
  16.1 28.5 %collective-permute-start.2 = (bf16[4,32,512]{2,1,0:T(8,128)(2,1)}, bf16[4,32,512]{2,1,0:T(8,128)(2,1)}, u32[]{:S(2)}, u32[]{:S(2)}) collective-permute-start(bf16[4,32,512]{2,1,0:T(8,128)(2,1)} %get-tuple-element.29), channel_id=1, source_target_pairs={{0,1},{1,0},{2,3},{3,2},{4,5},{5,4},{6,7},{7,6},{8,9},{9,8},{10,11... | collective-permute-start | bytes 393224 | tf_op jit(solution)/shard_map/ppermute | solution.py:32
  18.1 26.5 %collective-permute-start.1 = (bf16[4,32,512]{2,1,0:T(8,128)(2,1)}, bf16[4,32,512]{2,1,0:T(8,128)(2,1)}, u32[]{:S(2)}, u32[]{:S(2)}) collective-permute-start(bf16[4,32,512]{2,1,0:T(8,128)(2,1)} %get-tuple-element.30), channel_id=1, source_target_pairs={{0,2},{1,3},{2,0},{3,1},{4,6},{5,7},{6,4},{7,5},{8,10},{9,11},{10,... | collective-permute-start | bytes 393224 | tf_op jit(solution)/shard_map/ppermute | solution.py:32
  22.5 3.1 %copy-start.14 = (bf16[64,512]{1,0:T(8,128)(2,1)}, bf16[64,512]{1,0:T(8,128)(2,1)S(1)}, u32[]{:S(2)}) copy-start(bf16[64,512]{1,0:T(8,128)(2,1)S(1)} %convolution_convert_fusion.14) | copy-start | bytes 196612
  22.8 3.7 %copy-start.7 = (bf16[128,512]{1,0:T(8,128)(2,1)}, bf16[128,512]{1,0:T(8,128)(2,1)S(1)}, u32[]{:S(2)}) copy-start(bf16[128,512]{1,0:T(8,128)(2,1)S(1)} %convolution_convert_fusion.5) | copy-start | bytes 393220
  23.2 1.0 copy-start.5
  32.4 6.1 %copy-start.16 = (bf16[128,512]{1,0:T(8,128)(2,1)S(1)}, bf16[128,512]{1,0:T(8,128)(2,1)}, u32[]{:S(2)}) copy-start(bf16[128,512]{1,0:T(8,128)(2,1)} %pad_maximum_fusion.7) | copy-start | bytes 393220
  33.7 6.7 %copy-start.17 = (bf16[1,96,512]{2,1,0:T(8,128)(2,1)S(1)}, bf16[1,96,512]{2,1,0:T(8,128)(2,1)}, u32[]{:S(2)}) copy-start(bf16[1,96,512]{2,1,0:T(8,128)(2,1)} %get-tuple-element.34) | copy-start | bytes 294916
  36.1 12.5 %copy-start.18 = (bf16[1,1,32,512]{3,2,1,0:T(8,128)(2,1)S(1)}, bf16[1,1,32,512]{3,2,1,0:T(8,128)(2,1)}, u32[]{:S(2)}) copy-start(bf16[1,1,32,512]{3,2,1,0:T(8,128)(2,1)} %param.11) | copy-start | bytes 98308
  40.4 7.1 %collective-permute-start = (bf16[4,32,512]{2,1,0:T(8,128)(2,1)}, bf16[4,32,512]{2,1,0:T(8,128)(2,1)S(1)}, u32[]{:S(2)}, u32[]{:S(2)}) collective-permute-start(bf16[4,32,512]{2,1,0:T(8,128)(2,1)} %get-tuple-element.28), channel_id=1, source_target_pairs={{0,3},{1,2},{2,1},{3,0},{4,7},{5,6},{6,5},{7,4},{8,11},{9,10},{10,... | collective-permute-start | bytes 393224 | tf_op jit(solution)/shard_map/ppermute | solution.py:32
  41.5 21.9 %collective-permute-start.6 = (bf16[4,96,512]{2,1,0:T(8,128)(2,1)S(1)}, bf16[4,96,512]{2,1,0:T(8,128)(2,1)S(1)}, u32[]{:S(2)}, u32[]{:S(2)}) collective-permute-start(bf16[4,96,512]{2,1,0:T(8,128)(2,1)S(1)} %pad_maximum_fusion.2), channel_id=1, source_target_pairs={{0,4},{4,0},{8,12},{12,8},{16,20},{20,16},{24,28},{28,24},{1,5},{5... | collective-permute-start | bytes 1179656 | tf_op jit(solution)/shard_map/ppermute | solution.py:32
  44.7 11.3 %copy-start.11 = (bf16[8,96,512]{2,1,0:T(8,128)(2,1)S(1)}, bf16[8,96,512]{2,1,0:T(8,128)(2,1)}, u32[]{:S(2)}) copy-start(bf16[8,96,512]{2,1,0:T(8,128)(2,1)} %constant_dynamic-update-slice_fusion.2) | copy-start | bytes 2359300
  52.5 6.9 %collective-permute-start.7 = (bf16[4,32,512]{2,1,0:T(8,128)(2,1)S(1)}, bf16[4,32,512]{2,1,0:T(8,128)(2,1)S(1)}, u32[]{:S(2)}, u32[]{:S(2)}) collective-permute-start(bf16[4,32,512]{2,1,0:T(8,128)(2,1)S(1)} %get-tuple-element.33), channel_id=1, source_target_pairs={{0,24},{4,28},{8,16},{12,20},{16,8},{20,12},{24,0},{28,4},{1,25},{... | collective-permute-start | bytes 393224 | tf_op jit(solution)/shard_map/ppermute | solution.py:32
  54.9 5.6 %collective-permute-start.8 = (bf16[4,32,512]{2,1,0:T(8,128)(2,1)S(1)}, bf16[4,32,512]{2,1,0:T(8,128)(2,1)S(1)}, u32[]{:S(2)}, u32[]{:S(2)}) collective-permute-start(bf16[4,32,512]{2,1,0:T(8,128)(2,1)S(1)} %get-tuple-element.33), channel_id=1, source_target_pairs={{0,16},{4,20},{8,24},{12,28},{16,0},{20,4},{24,8},{28,12},{1,17},{... | collective-permute-start | bytes 393224 | tf_op jit(solution)/shard_map/ppermute | solution.py:32
  55.4 5.0 %collective-permute-start.9 = (bf16[4,32,512]{2,1,0:T(8,128)(2,1)S(1)}, bf16[4,32,512]{2,1,0:T(8,128)(2,1)S(1)}, u32[]{:S(2)}, u32[]{:S(2)}) collective-permute-start(bf16[4,32,512]{2,1,0:T(8,128)(2,1)S(1)} %get-tuple-element.33), channel_id=1, source_target_pairs={{0,8},{4,12},{8,0},{12,4},{16,24},{20,28},{24,16},{28,20},{1,9},{5... | collective-permute-start | bytes 393224 | tf_op jit(solution)/shard_map/ppermute | solution.py:32
  60.5 7.0 %copy-start.10 = (bf16[8,320,64]{1,2,0:T(8,128)(2,1)S(1)}, bf16[8,320,64]{1,2,0:T(8,128)(2,1)}, u32[]{:S(2)}) copy-start(bf16[8,320,64]{1,2,0:T(8,128)(2,1)} %gather_fusion) | copy-start | bytes 983044
  61.3 10.3 %collective-permute-start.10 = (bf16[4,4,32,512]{3,2,1,0:T(8,128)(2,1)}, bf16[4,4,32,512]{3,2,1,0:T(8,128)(2,1)}, u32[]{:S(2)}, u32[]{:S(2)}) collective-permute-start(bf16[4,4,32,512]{3,2,1,0:T(8,128)(2,1)} %pad_maximum_fusion.1), channel_id=1, source_target_pairs={{0,4},{4,0},{8,12},{12,8},{16,20},{20,16},{24,28},{28,24},{1,5},{5... | collective-permute-start | bytes 1572872 | tf_op jit(solution)/shard_map/ppermute | solution.py:32
  63.4 0.9 copy-start.12
  78.1 4.2 %copy-start.6 = (bf16[192,512]{1,0:T(8,128)(2,1)S(1)}, bf16[192,512]{1,0:T(8,128)(2,1)}, u32[]{:S(2)}) copy-start(bf16[192,512]{1,0:T(8,128)(2,1)} %copy-done.5) | copy-start | bytes 589828
  86.2 6.4 %copy-start.2 = (bf16[8,32,512]{2,1,0:T(8,128)(2,1)S(1)}, bf16[8,32,512]{2,1,0:T(8,128)(2,1)}, u32[]{:S(2)}) copy-start(bf16[8,32,512]{2,1,0:T(8,128)(2,1)} %gather_fusion.5) | copy-start | bytes 786436
  86.2 6.4 %copy-start.8 = (bf16[128,512]{1,0:T(8,128)(2,1)S(1)}, bf16[128,512]{1,0:T(8,128)(2,1)}, u32[]{:S(2)}) copy-start(bf16[128,512]{1,0:T(8,128)(2,1)} %copy-done.7) | copy-start | bytes 393220
  90.0 6.3 %copy-start.3 = (bf16[8,1,32,512]{3,2,1,0:T(8,128)(2,1)S(1)}, bf16[8,1,32,512]{3,2,1,0:T(8,128)(2,1)}, u32[]{:S(2)}) copy-start(bf16[8,1,32,512]{3,2,1,0:T(8,128)(2,1)} %get-tuple-element.23) | copy-start | bytes 786436
  92.5 5.9 %copy-start.9 = (bf16[8,128,64]{1,2,0:T(8,128)(2,1)S(1)}, bf16[8,128,64]{1,2,0:T(8,128)(2,1)}, u32[]{:S(2)}) copy-start(bf16[8,128,64]{1,2,0:T(8,128)(2,1)} %gather_fusion.6) | copy-start | bytes 393220
  94.8 5.2 %copy-start.15 = (bf16[64,512]{1,0:T(8,128)(2,1)S(1)}, bf16[64,512]{1,0:T(8,128)(2,1)}, u32[]{:S(2)}) copy-start(bf16[64,512]{1,0:T(8,128)(2,1)} %copy-done.14) | copy-start | bytes 196612
  98.4 3.6 %copy-start.19 = (bf16[64,512]{1,0:T(8,128)(2,1)S(1)}, bf16[64,512]{1,0:T(8,128)(2,1)}, u32[]{:S(2)}) copy-start(bf16[64,512]{1,0:T(8,128)(2,1)} %fusion.69) | copy-start | bytes 196612
  99.9 1.9 %copy-start.24 = (bf16[64,512]{1,0:T(8,128)(2,1)S(1)}, bf16[64,512]{1,0:T(8,128)(2,1)}, u32[]{:S(2)}) copy-start(bf16[64,512]{1,0:T(8,128)(2,1)} %slice.350) | copy-start | bytes 196612
  99.9 1.9 %copy-start.23 = (bf16[64,512]{1,0:T(8,128)(2,1)S(1)}, bf16[64,512]{1,0:T(8,128)(2,1)}, u32[]{:S(2)}) copy-start(bf16[64,512]{1,0:T(8,128)(2,1)} %slice.349) | copy-start | bytes 196612
  100.0 1.9 %copy-start.22 = (bf16[64,512]{1,0:T(8,128)(2,1)S(1)}, bf16[64,512]{1,0:T(8,128)(2,1)}, u32[]{:S(2)}) copy-start(bf16[64,512]{1,0:T(8,128)(2,1)} %slice.348) | copy-start | bytes 196612
  100.0 2.0 %copy-start.21 = (bf16[64,512]{1,0:T(8,128)(2,1)S(1)}, bf16[64,512]{1,0:T(8,128)(2,1)}, u32[]{:S(2)}) copy-start(bf16[64,512]{1,0:T(8,128)(2,1)} %fusion.71) | copy-start | bytes 196612
  100.0 2.0 %copy-start.20 = (bf16[64,512]{1,0:T(8,128)(2,1)S(1)}, bf16[64,512]{1,0:T(8,128)(2,1)}, u32[]{:S(2)}) copy-start(bf16[64,512]{1,0:T(8,128)(2,1)} %fusion.70) | copy-start | bytes 196612
  102.1 8.3 %collective-permute-start.13 = (bf16[8,16,512]{2,1,0:T(8,128)(2,1)S(1)}, bf16[8,16,512]{2,1,0:T(8,128)(2,1)S(1)}, u32[]{:S(2)}, u32[]{:S(2)}) collective-permute-start(bf16[8,16,512]{2,1,0:T(8,128)(2,1)S(1)} %get-tuple-element.26), channel_id=1, source_target_pairs={{0,1},{1,0},{2,3},{3,2},{4,5},{5,4},{6,7},{7,6},{8,9},{9,8},{10,11... | collective-permute-start | bytes 393224 | tf_op jit(solution)/shard_map/ppermute | solution.py:32
  102.9 12.9 %collective-permute-start.12 = (bf16[8,16,512]{2,1,0:T(8,128)(2,1)S(1)}, bf16[8,16,512]{2,1,0:T(8,128)(2,1)S(1)}, u32[]{:S(2)}, u32[]{:S(2)}) collective-permute-start(bf16[8,16,512]{2,1,0:T(8,128)(2,1)S(1)} %get-tuple-element.27), channel_id=1, source_target_pairs={{0,2},{1,3},{2,0},{3,1},{4,6},{5,7},{6,4},{7,5},{8,10},{9,11},{10,... | collective-permute-start | bytes 393224 | tf_op jit(solution)/shard_map/ppermute | solution.py:32
  105.4 10.3 %collective-permute-start.11 = (bf16[8,16,512]{2,1,0:T(8,128)(2,1)S(1)}, bf16[8,16,512]{2,1,0:T(8,128)(2,1)S(1)}, u32[]{:S(2)}, u32[]{:S(2)}) collective-permute-start(bf16[8,16,512]{2,1,0:T(8,128)(2,1)S(1)} %get-tuple-element.25), channel_id=1, source_target_pairs={{0,3},{1,2},{2,1},{3,0},{4,7},{5,6},{6,5},{7,4},{8,11},{9,10},{10,... | collective-permute-start | bytes 393224 | tf_op jit(solution)/shard_map/ppermute | solution.py:32
  115.9 7.2 %collective-permute-start.14 = (bf16[8,16,512]{2,1,0:T(8,128)(2,1)S(1)}, bf16[8,16,512]{2,1,0:T(8,128)(2,1)S(1)}, u32[]{:S(2)}, u32[]{:S(2)}) collective-permute-start(bf16[8,16,512]{2,1,0:T(8,128)(2,1)S(1)} %get-tuple-element.10), channel_id=1, source_target_pairs={{0,3},{1,2},{2,1},{3,0},{4,7},{5,6},{6,5},{7,4},{8,11},{9,10},{10,... | collective-permute-start | bytes 393224 | tf_op jit(solution)/shard_map/ppermute | solution.py:32
  118.0 12.5 %collective-permute-start.15 = (bf16[8,16,512]{2,1,0:T(8,128)(2,1)S(1)}, bf16[8,16,512]{2,1,0:T(8,128)(2,1)S(1)}, u32[]{:S(2)}, u32[]{:S(2)}) collective-permute-start(bf16[8,16,512]{2,1,0:T(8,128)(2,1)S(1)} %get-tuple-element.10), channel_id=1, source_target_pairs={{0,2},{1,3},{2,0},{3,1},{4,6},{5,7},{6,4},{7,5},{8,10},{9,11},{10,... | collective-permute-start | bytes 393224 | tf_op jit(solution)/shard_map/ppermute | solution.py:32
  120.1 10.4 %collective-permute-start.16 = (bf16[8,16,512]{2,1,0:T(8,128)(2,1)S(1)}, bf16[8,16,512]{2,1,0:T(8,128)(2,1)S(1)}, u32[]{:S(2)}, u32[]{:S(2)}) collective-permute-start(bf16[8,16,512]{2,1,0:T(8,128)(2,1)S(1)} %get-tuple-element.10), channel_id=1, source_target_pairs={{0,1},{1,0},{2,3},{3,2},{4,5},{5,4},{6,7},{7,6},{8,9},{9,8},{10,11... | collective-permute-start | bytes 393224 | tf_op jit(solution)/shard_map/ppermute | solution.py:32
  123.1 8.5 %copy-start.13 = (f32[4,64,512]{2,1,0:T(8,128)S(1)}, f32[4,64,512]{2,1,0:T(8,128)}, u32[]{:S(2)}) copy-start(f32[4,64,512]{2,1,0:T(8,128)} %param.10) | copy-start | bytes 1572868

commit v2 on v1

--- a/solution.py
+++ b/solution.py
@@ -1,10 +1,16 @@
+import functools
+
 import jax
 import jax.numpy as jnp
 from jax import lax
+from jax.experimental import pallas as pl
+from jax.experimental.pallas import tpu as pltpu
 from jax.sharding import PartitionSpec as P
 
 BF = jnp.bfloat16
 F32 = jnp.float32
+ROW_ORDER = (0, 6, 4, 2, 1, 7, 5, 3)
+VMEM_BYTES = 32 << 20
 
 
 def dot(a, b):
@@ -73,7 +79,7 @@
     return whole
 
 
-def local(known_inverse, lower_panel, chain_panel, diag_inverse, top_cols, top_diag, pattern):
+def general(known_inverse, lower_panel, chain_panel, diag_inverse, top_cols, top_diag, pattern):
     n_rows = lax.axis_size("rows")
     n_cols = lax.axis_size("cols")
     row_id = lax.axis_index("rows")
@@ -149,6 +155,210 @@
     )
 
 
+def first_kernel(n_cols, n_rows, g_ref, m_ref, pattern_ref, diag_ref, top_ref, tops_ref, panel_ref, joined_ref, *piece_refs):
+    col = lax.axis_index("cols")
+    supers, _, piece, width = m_ref.shape
+    share = top_ref.shape[0]
+    for k in range(supers):
+        for r in range(n_rows):
+            on = pattern_ref[k, col * n_rows + r].astype(F32)
+            panel_ref[k, pl.ds(r * piece, piece)] = (m_ref[k, r].astype(F32) * on).astype(BF)
+    for j, out in enumerate(piece_refs):
+        rows = g_ref[col ^ j]
+        for k in range(supers):
+            out[k] = dot(rows, panel_ref[k]).astype(BF)
+    mine = jnp.zeros((share, width), F32)
+    for i in range(supers):
+        begin = top_ref[...] if i == 0 else diag_ref[supers - i]
+        mine = jnp.where(col == i, begin, mine)
+    joined_ref[pl.ds(0, share)] = mine.astype(BF)
+    joined_ref[pl.ds(share, piece)] = tops_ref[...]
+
+
+def chain_kernel(n_cols, n_rows, l_ref, tops_ref, pattern_ref, own_ref, *refs):
+    *got_refs, cols_ref = refs
+    supers = own_ref.shape[0]
+    at = lax.axis_index("cols") * n_rows + lax.axis_index("rows")
+    prev = tops_ref[...]
+    for k in reversed(range(supers)):
+        total = own_ref[k].astype(F32)
+        for got in got_refs:
+            total = total + got[k].astype(F32)
+        total = total + dot(prev, l_ref[k])
+        prev = (-(total * pattern_ref[k, at].astype(F32))).astype(BF)
+        cols_ref[k] = prev
+
+
+def place(refs, order, write):
+    me = lax.axis_index("rows")
+    for ref, offset in zip(refs, order):
+        write(me ^ offset, ref)
+
+
+def ready_kernel(n_cols, n_rows, order, l_ref, panel_ref, *refs):
+    got = refs[: len(order)]
+    stacks_ref, reach_ref, begin_ref, ahead_ref, x_ref, y_ref, all_ref = refs[len(order) :]
+    supers, width, _ = l_ref.shape
+    share = width // n_rows
+    piece = y_ref.shape[0] // n_rows
+    col, row = lax.axis_index("cols"), lax.axis_index("rows")
+
+    def write(at, ref):
+        x_ref[pl.ds(pl.multiple_of(at * share, share), share)] = ref[pl.ds(0, share)]
+        y_ref[pl.ds(pl.multiple_of(at * piece, piece), piece)] = ref[pl.ds(share, piece)]
+
+    place(got, order, write)
+    lane = lax.broadcasted_iota(jnp.int32, (share, width), 1)
+    sub = lax.broadcasted_iota(jnp.int32, (share, width), 0)
+    unit = jnp.where(lane == row * share + sub, 1.0, 0.0).astype(BF)
+    stack = unit
+    all_ref[...] = jnp.zeros_like(all_ref)
+    all_ref[0, pl.ds(0, share)] = unit
+    at = 0
+    for k in range(supers):
+        reach_ref[pl.ds(at, (k + 1) * share)] = dot_nt(stack, panel_ref[k]).astype(BF)
+        at += (k + 1) * share
+        stack = jnp.concatenate([dot_nt(stack, l_ref[k]).astype(BF), unit], 0)
+        all_ref[k + 1, pl.ds(0, (k + 2) * share)] = stack
+    at = 0
+    for k in range(1, supers):
+        stacks_ref[pl.ds(at, (k + 1) * share)] = all_ref[k, pl.ds(0, (k + 1) * share)]
+        at += (k + 1) * share
+    begin = dot(all_ref[jnp.maximum(supers - col, 0)], x_ref[...])
+    begin_ref[...] = begin
+    first = jnp.where(col == 0, begin, 0.0).astype(BF)
+    across = dot_nt(stack, y_ref[...]).astype(BF)
+    ahead_ref[...] = dot(first, l_ref[supers - 1]) + dot(across, panel_ref[supers - 1])
+
+
+def rows_kernel(n_cols, n_rows, order, l_ref, panel_ref, stacks_ref, reach_ref, begin_ref, ahead_ref, *refs):
+    got = refs[: len(order)]
+    pieces = refs[len(order) : len(order) + n_cols]
+    y_ref, done_ref = refs[len(order) + n_cols :]
+    supers, width, _ = l_ref.shape
+    share = width // n_rows
+    piece = y_ref.shape[1] // n_rows
+    part = share // n_cols
+    col = lax.axis_index("cols")
+
+    def write(at, ref):
+        for k in range(supers):
+            y_ref[k, pl.ds(pl.multiple_of(at * piece, piece), piece)] = ref[k]
+
+    place(got, order, write)
+    full = ahead_ref[...]
+    stack_at = sum((k + 1) * share for k in range(1, supers))
+    reach_at = sum((k + 1) * share for k in range(supers))
+    for k in reversed(range(supers)):
+        here = (k + 1) * share
+        if k < supers - 1:
+            stack_at -= here + share
+            across = dot_nt(stacks_ref[pl.ds(stack_at, here + share)], y_ref[k + 1]).astype(BF)
+            full = dot(acc.astype(BF), l_ref[k]) + dot(across, panel_ref[k])
+        reach_at -= here
+        acc = full[:here] - dot(reach_ref[pl.ds(reach_at, here)], y_ref[k])
+        done_ref[supers + k] = -full[here:]
+        done_ref[k] = acc[k * share :]
+        if k:
+            acc = acc + jnp.where(col == supers - k, begin_ref[pl.ds(0, here)], 0.0)
+    for j, out in enumerate(pieces):
+        at = pl.multiple_of((col ^ j) * part, part)
+        for i in range(2 * supers):
+            out[i] = done_ref[i, pl.ds(at, part)].astype(BF)
+
+
+def sum_kernel(own_ref, *refs):
+    *got_refs, out_ref = refs
+    for i in range(own_ref.shape[0]):
+        total = own_ref[i].astype(F32)
+        for got in got_refs:
+            total = total + got[i].astype(F32)
+        out_ref[i] = total.astype(BF)
+
+
+def last_kernel(n_cols, diag_ref, *refs):
+    *got_refs, diag_out, sub_out = refs
+    supers = diag_ref.shape[0]
+    part = got_refs[0].shape[1]
+    col = lax.axis_index("cols")
+    for j, got in enumerate(got_refs):
+        rows = pl.ds(pl.multiple_of((col ^ j) * part, part), part)
+        for k in range(supers):
+            diag_out[k, rows] = diag_ref[k, rows] + got[k].astype(F32)
+            sub_out[k, rows] = got[supers + k].astype(F32)
+
+
+def call(kernel, outs, *args, scratch=(), smem=(), flops=0, moved=0):
+    vmem = pl.BlockSpec(memory_space=pltpu.VMEM)
+    return pl.pallas_call(
+        kernel,
+        out_shape=tuple(jax.ShapeDtypeStruct(s, d) for s, d in outs),
+        in_specs=[pl.BlockSpec(memory_space=pltpu.SMEM) if i in smem else vmem for i in range(len(args))],
+        out_specs=tuple(vmem for _ in outs),
+        scratch_shapes=[pltpu.VMEM(s, d) for s, d in scratch],
+        compiler_params=pltpu.CompilerParams(vmem_limit_bytes=VMEM_BYTES),
+        cost_estimate=pl.CostEstimate(flops=flops, bytes_accessed=moved, transcendentals=0),
+    )(*args)
+
+
+def exchange_rows(x):
+    near = [x] + [hop(x, "rows", j) for j in ROW_ORDER[1:4]]
+    return near + [hop(p, "rows", 1) for p in near]
+
+
+def local(known_inverse, lower_panel, chain_panel, diag_inverse, top_cols, top_diag, pattern):
+    n_rows = lax.axis_size("rows")
+    n_cols = lax.axis_size("cols")
+    supers = lower_panel.shape[0]
+    piece = known_inverse.shape[2]
+    width = lower_panel.shape[-1]
+    share = width // n_rows
+    if n_rows != len(ROW_ORDER) or not pow2(n_cols) or n_cols < supers or share % (16 * n_cols) or piece % 16:
+        return general(known_inverse, lower_panel, chain_panel, diag_inverse, top_cols, top_diag, pattern)
+    known = known_inverse[:, 0]
+    tops = top_cols[0, 0]
+    block = n_rows * piece
+    ways = range(1, n_cols)
+    rows_of = [(k + 1) * share for k in range(supers + 1)]
+    panel, joined, own, *sent = call(
+        functools.partial(first_kernel, n_cols, n_rows),
+        [((supers, block, width), BF), ((share + piece, width), BF)] + [((supers, piece, width), BF)] * n_cols,
+        known, lower_panel[:, 0], pattern, diag_inverse, top_diag, tops, smem=(2,),
+        flops=2 * known.size * supers * width, moved=4 * block * width * supers,
+    )
+    got = [hop(sent[j - 1], "cols", j) for j in reversed(ways)]
+    around = exchange_rows(joined)
+    stacks, reach, begin, ahead = call(
+        functools.partial(ready_kernel, n_cols, n_rows, ROW_ORDER),
+        [((sum(rows_of[1:supers]), width), BF), ((sum(rows_of[:supers]), block), BF), ((rows_of[supers], width), F32), ((rows_of[supers], width), F32)],
+        chain_panel, panel, *around,
+        scratch=[((width, width), BF), ((block, width), BF), ((supers + 1, rows_of[supers], width), BF)],
+        flops=2 * 8 * share * width * width * 4, moved=4 * width * width * supers,
+    )
+    (cols,) = call(
+        functools.partial(chain_kernel, n_cols, n_rows),
+        [((supers, piece, width), BF)],
+        chain_panel, tops, pattern, own, *got, smem=(2,),
+        flops=2 * piece * width * width * supers, moved=2 * width * width * supers,
+    )
+    pieces = call(
+        functools.partial(rows_kernel, n_cols, n_rows, ROW_ORDER),
+        [((2 * supers, share // n_cols, width), BF)] * n_cols,
+        chain_panel, panel, stacks, reach, begin, ahead, *exchange_rows(cols),
+        scratch=[((supers, block, width), BF), ((2 * supers, share, width), F32)],
+        flops=2 * 20 * share * width * width, moved=4 * width * width * supers,
+    )
+    got = [hop(pieces[j], "cols", j) for j in reversed(ways)]
+    (summed,) = call(sum_kernel, [(pieces[0].shape, BF)], pieces[0], *got)
+    there = {j: hop(summed, "cols", j) for j in reversed(ways)}
+    diag, sub = call(
+        functools.partial(last_kernel, n_cols),
+        [(diag_inverse.shape, F32)] * 2,
+        diag_inverse, summed, *[there[j] for j in ways],
+    )
+    return cols.reshape(supers, 1, 1, piece, width), diag, sub
+
+
 def solution(mesh):
     in_specs = (
         P(None, "rows", None, "cols"),

time: 134 us -> 71.4 us (0.53)
  matrix products: 32.8 us -> 0 us
  local copies, waits for them, and re-layouts: 30.5 us -> 8.48 us
  other arithmetic: 21.3 us -> 0 us
  Pallas kernels: 0 us -> 8.41 us
  waiting for transfers between devices: 25.1 us -> 29.4 us
  starting transfers between devices: 21.5 us -> 23.8 us
    dot_general x24 -> x0, matrix products: 32.8 us -> none  [the longest x20 30.8 us: dot(): return jnp.dot(a, b, preferred_element_type=F32)]
    another operation x9 -> x0, other arithmetic: 9.84 us -> none
    pallas_call x0 -> x6, Pallas kernels: none -> 8.41 us  [call(): pl.pallas_call(kernel, out_shape=tuple((jax.ShapeDtypeStruct(s, d) for s,...]
    gather x8 -> x0, local copies, waits for them, and re-layouts: 8.09 us -> none  [the longest x4 5.12 us: local(): rel = stacks[k].reshape(-1, n_rows, share)[:, order].reshape(-1, width)]
    slice x7 -> x0, local copies, waits for them, and re-layouts: 8.03 us -> none  [the longest x3 3.75 us: local(): diag_list[k] = acc[k * share:]]
    concatenate x6 -> x0, local copies, waits for them, and re-layouts: 5.41 us -> none  [the longest x4 3.48 us: local(): jnp.concatenate([dot_nt(stacks[k], chain_panel[k]).astype(BF), own_rows], 0)]
    ppermute x17 -> x23, waiting for transfers between devices: 25.1 us -> 29.4 us  [hop(): return lax.ppermute(x, axis, [(i, target(i, j, n)) for i in range(n)])]
    concatenate x4 -> x0, other arithmetic: 3.78 us -> none  [local(): jnp.concatenate([dot_nt(stacks[k], chain_panel[k]).astype(BF), own_rows], 0)]
  transfers between devices with their start and end apart: 17 -> 23, of which waited for: 7 -> 10; matrix products, arithmetic and copies ran while one was open for 36% -> 0% of each run, Pallas kernels for 0% -> 6%
where the time goes in v2:
time: 71.4 us; the launch traced here: 70.9 us
  waiting for transfers between devices  29.4 us (41%)
  starting transfers between devices  23.8 us (33%)
  local copies, waits for them, and re-layouts  8.48 us (12%)
  Pallas kernels  8.41 us (12%)
  between operations  0.75 us (1%)
    ppermute x23, waiting for transfers between devices, hop(): return lax.ppermute(x, axis, [(i, target(i, j, n)) for i in range(n)])  29.4 us
    ppermute x23, starting transfers between devices, hop(): return lax.ppermute(x, axis, [(i, target(i, j, n)) for i in range(n)])  23.8 us
    unnamed x24, local copies, waits for them, and re-layouts  8.48 us
    pallas_call x6, Pallas kernels, call(): pl.pallas_call(kernel, out_shape=tuple((jax.ShapeDtypeStruct(s, d) for s,...  8.41 us
  transfers between devices with their start and end apart: 23, of which 10 were waited for; matrix products, arithmetic and copies ran while one was open for 0% of the time, Pallas kernels for 6%

profile of v2, /device:TPU:0, one launch (start us, length us, event | category | flops | bytes accessed | tf_op | source)
XLA Modules:
  0.0 70.9 jit_solution(5138550138577776522)
XLA Ops:
  0.6 0.0 copy-start.2
  0.6 1.0 %copy-done.2 = f32[4,64,512]{2,1,0:T(8,128)S(1)} copy-done((f32[4,64,512]{2,1,0:T(8,128)S(1)}, f32[4,64,512]{2,1,0:T(8,128)}, u32[]{:S(2)}) %copy-start.2) | copy-done | bytes 524312
  1.7 1.2 %copy-done.4 = bf16[4,1,8,32,512]{4,3,2,1,0:T(8,128)(2,1)S(1)} copy-done((bf16[4,1,8,32,512]{4,3,2,1,0:T(8,128)(2,1)S(1)}, bf16[4,1,8,32,512]{4,3,2,1,0:T(8,128)(2,1)}, u32[]{:S(2)}) %copy-start.4) | copy-done | bytes 1048600
  2.9 0.8 %copy-done.6 = bf16[1,1,32,512]{3,2,1,0:T(8,128)(2,1)S(1)} copy-done((bf16[1,1,32,512]{3,2,1,0:T(8,128)(2,1)S(1)}, bf16[1,1,32,512]{3,2,1,0:T(8,128)(2,1)}, u32[]{:S(2)}) %copy-start.6) | copy-done | bytes 32792
  3.7 0.9 %copy-done.8 = f32[64,512]{1,0:T(8,128)S(1)} copy-done((f32[64,512]{1,0:T(8,128)S(1)}, f32[64,512]{1,0:T(8,128)}, u32[]{:S(2)}) %copy-start.8) | copy-done | bytes 131096
  4.6 0.8 %copy-done.9 = bf16[4,1,32,256]{3,2,1,0:T(8,128)(2,1)S(1)} copy-done((bf16[4,1,32,256]{3,2,1,0:T(8,128)(2,1)S(1)}, bf16[4,1,32,256]{3,2,1,0:T(8,128)(2,1)}, u32[]{:S(2)}) %copy-start.9) | copy-done | bytes 65560
  5.4 0.7 copy-done.10
  6.1 1.5 %shard_map.94 = (bf16[4,256,512]{2,1,0:T(8,128)(2,1)S(1)}, bf16[96,512]{1,0:T(8,128)(2,1)S(1)}, bf16[4,32,512]{2,1,0:T(8,128)(2,1)S(1)}, bf16[4,32,512]{2,1,0:T(...) custom-call(bf16[4,32,256]{2,1,0:T(8,128)(2,1)S(1)} %bitcast.10, ...), custom_call_target="tpu_custom_call" | custom-call | flops 134217728 | bytes 2097152 | tf_op jit(solution)/shard_map/pallas_call | solution.py:293
  7.6 5.1 %collective-permute-start = (bf16[4,32,512]{2,1,0:T(8,128)(2,1)S(1)}, bf16[4,32,512]{2,1,0:T(8,128)(2,1)S(1)}, u32[]{:S(2)}, u32[]{:S(2)}) collective-permute-start(bf16[4,32,512]{2,1,0:T(8,128)(2,1)S(1)} %get-tuple-element.20), channel_id=1, source_target_pairs={{0,3},{1,2},{2,1},{3,0},{4,7},{5,6},{6,5},{7,4},{8,11},{9,10},{10,... | collective-permute-start | bytes 393224 | tf_op jit(solution)/shard_map/ppermute | solution.py:38
  12.7 2.4 %collective-permute-start.3 = (bf16[96,512]{1,0:T(8,128)(2,1)S(1)}, bf16[96,512]{1,0:T(8,128)(2,1)S(1)}, u32[]{:S(2)}, u32[]{:S(2)}) collective-permute-start(bf16[96,512]{1,0:T(8,128)(2,1)S(1)} %get-tuple-element.24.refs_0_), channel_id=1, source_target_pairs={{0,24},{4,28},{8,16},{12,20},{16,8},{20,12},{24,0},{28,4},{1,25},{... | collective-permute-start | bytes 294920 | tf_op jit(solution)/shard_map/ppermute | solution.py:38
  15.1 0.0 collective-permute-start.1
  15.1 0.8 %collective-permute-start.2 = (bf16[4,32,512]{2,1,0:T(8,128)(2,1)S(1)}, bf16[4,32,512]{2,1,0:T(8,128)(2,1)S(1)}, u32[]{:S(2)}, u32[]{:S(2)}) collective-permute-start(bf16[4,32,512]{2,1,0:T(8,128)(2,1)S(1)} %get-tuple-element.22), channel_id=1, source_target_pairs={{0,1},{1,0},{2,3},{3,2},{4,5},{5,4},{6,7},{7,6},{8,9},{9,8},{10,11... | collective-permute-start | bytes 393224 | tf_op jit(solution)/shard_map/ppermute | solution.py:38
  15.9 0.5 collective-permute-start.4
  16.4 1.9 %collective-permute-done.3.refs_1_ = bf16[96,512]{1,0:T(8,128)(2,1)S(1)} collective-permute-done((bf16[96,512]{1,0:T(8,128)(2,1)S(1)}, bf16[96,512]{1,0:T(8,128)(2,1)S(1)}, u32[]{:S(2)}, u32[]{:S(2)}) %collective-permute-start.3) | collective-permute-done | bytes 98336 | tf_op jit(solution)/shard_map/ppermute | solution.py:38
  18.3 1.5 %collective-permute-start.5 = (bf16[96,512]{1,0:T(8,128)(2,1)S(1)}, bf16[96,512]{1,0:T(8,128)(2,1)S(1)}, u32[]{:S(2)}, u32[]{:S(2)}) collective-permute-start(bf16[96,512]{1,0:T(8,128)(2,1)S(1)} %get-tuple-element.24.refs_0_), channel_id=1, source_target_pairs={{0,8},{4,12},{8,0},{12,4},{16,24},{20,28},{24,16},{28,20},{1,9},{5... | collective-permute-start | bytes 294920 | tf_op jit(solution)/shard_map/ppermute | solution.py:38
  19.8 0.0 collective-permute-done.refs_0_
  19.8 0.0 collective-permute-start.6
  19.8 4.0 %collective-permute-done.1.refs_1_ = bf16[4,32,512]{2,1,0:T(8,128)(2,1)S(1)} collective-permute-done((bf16[4,32,512]{2,1,0:T(8,128)(2,1)S(1)}, bf16[4,32,512]{2,1,0:T(8,128)(2,1)S(1)}, u32[]{:S(2)}, u32[]{:S(2)}) %collective-permute-start.1) | collective-permute-done | bytes 131104 | tf_op jit(solution)/shard_map/ppermute | solution.py:38
  23.8 0.0 collective-permute-start.7
  23.8 0.0 collective-permute-done.2.refs_2_
  23.8 1.6 %copy-done = bf16[4,512,512]{2,1,0:T(8,128)(2,1)S(1)} copy-done((bf16[4,512,512]{2,1,0:T(8,128)(2,1)S(1)}, bf16[4,512,512]{2,1,0:T(8,128)(2,1)}, u32[]{:S(2)}) %copy-start) | copy-done | bytes 2097176
  25.4 0.8 %copy-done.7 = bf16[1,1,32,512]{3,2,1,0:T(8,128)(2,1)S(1)} copy-done((bf16[1,1,32,512]{3,2,1,0:T(8,128)(2,1)S(1)}, bf16[1,1,32,512]{3,2,1,0:T(8,128)(2,1)}, u32[]{:S(2)}) %copy-start.7) | copy-done | bytes 32792
  26.1 0.7 copy-done.11
  26.8 1.9 %shard_map.95.refs_0_ = bf16[4,32,512]{2,1,0:T(8,128)(2,1)} custom-call(bf16[4,512,512]{2,1,0:T(8,128)(2,1)S(1)} %copy-done, bf16[32,512]{1,0:T(8,128)(2,1)S(1)} %bitcast.9, s32[4,32]{1,0:T(4,128)S(1)} %copy-done.11, bf16[4,32,512]{2,1,0:T(8,128)(2,1)S(1)} %get-tuple-element.19.own_ref, bf16[4,32,512]{2,1,0:T(8,128)(2,1)S(1)} %collective-permute-done.refs_0_, ...), custom_call_target="tpu_custom_call" | custom-call | flops 67108864 | bytes 2097152 | tf_op jit(solution)/shard_map/pallas_call | solution.py:293
  28.7 2.4 %collective-permute-start.10 = (bf16[4,32,512]{2,1,0:T(8,128)(2,1)}, bf16[4,32,512]{2,1,0:T(8,128)(2,1)S(1)}, u32[]{:S(2)}, u32[]{:S(2)}) collective-permute-start(bf16[4,32,512]{2,1,0:T(8,128)(2,1)} %shard_map.95.refs_0_), channel_id=1, source_target_pairs={{0,24},{4,28},{8,16},{12,20},{16,8},{20,12},{24,0},{28,4},{1,25},{... | collective-permute-start | bytes 393224 | tf_op jit(solution)/shard_map/ppermute | solution.py:38
  31.2 0.0 collective-permute-done.4.refs_2_
  31.2 0.5 collective-permute-start.11
  31.7 0.0 collective-permute-done.5.refs_3_
  31.7 0.5 collective-permute-start.12
  32.2 0.0 collective-permute-done.6.refs_4_
  32.2 0.0 collective-permute-start.8
  32.2 0.0 collective-permute-done.7.refs_5_
  32.2 0.5 collective-permute-start.9
  32.8 0.8 %collective-permute-done.8.refs_6_ = bf16[96,512]{1,0:T(8,128)(2,1)S(1)} collective-permute-done((bf16[96,512]{1,0:T(8,128)(2,1)S(1)}, bf16[96,512]{1,0:T(8,128)(2,1)S(1)}, u32[]{:S(2)}, u32[]{:S(2)}) %collective-permute-start.8) | collective-permute-done | bytes 98336 | tf_op jit(solution)/shard_map/ppermute | solution.py:38
  33.5 0.2 collective-permute-start.13
  33.7 2.3 %collective-permute-done.10.refs_1_ = bf16[4,32,512]{2,1,0:T(8,128)(2,1)S(1)} collective-permute-done((bf16[4,32,512]{2,1,0:T(8,128)(2,1)}, bf16[4,32,512]{2,1,0:T(8,128)(2,1)S(1)}, u32[]{:S(2)}, u32[]{:S(2)}) %collective-permute-start.10) | collective-permute-done | bytes 131104 | tf_op jit(solution)/shard_map/ppermute | solution.py:38
  36.0 0.0 collective-permute-start.14
  36.0 2.5 %collective-permute-done.11.refs_2_ = bf16[4,32,512]{2,1,0:T(8,128)(2,1)S(1)} collective-permute-done((bf16[4,32,512]{2,1,0:T(8,128)(2,1)}, bf16[4,32,512]{2,1,0:T(8,128)(2,1)S(1)}, u32[]{:S(2)}, u32[]{:S(2)}) %collective-permute-start.11) | collective-permute-done | bytes 131104 | tf_op jit(solution)/shard_map/ppermute | solution.py:38
  38.6 0.0 collective-permute-start.15
  38.6 0.1 collective-permute-done.12.refs_3_
  38.7 0.4 collective-permute-start.16
  39.1 0.0 collective-permute-done.9.refs_7_
  39.1 2.3 %shard_map.96 = (bf16[576,512]{1,0:T(8,128)(2,1)S(1)}, bf16[640,256]{1,0:T(8,128)(2,1)S(1)}, f32[320,512]{1,0:T(8,128)S(1)}, f32[320,512]{1,0:T(8,128)S(1)}) custom-call(bf16[4,512,512]{2,1,0:T(8,128)(2,1)S(1)} %copy-done.1, bf16[4,256,512]{2,1,0:T(8,128)(2,1)S(1)} %get-tuple-element.23.panel_ref, bf16[96,512]{1,0:T(8,128)(2,1)S(1)} %get-tuple-element.24.refs_0_, ...), custom_call_target="tpu_custom_call" | custom-call | flops 1073741824 | bytes 4194304 | tf_op jit(solution)/shard_map/pallas_call | solution.py:293
  41.4 0.0 collective-permute-done.13.refs_4_
  41.4 0.0 collective-permute-done.14.refs_5_
  41.4 0.0 collective-permute-done.15.refs_6_
  41.5 0.0 collective-permute-done.16.refs_7_
  41.5 0.0 copy-start.3
  41.5 1.6 %shard_map.97 = (bf16[8,16,512]{2,1,0:T(8,128)(2,1)S(1)}, bf16[8,16,512]{2,1,0:T(8,128)(2,1)S(1)}, bf16[8,16,512]{2,1,0:T(8,128)(2,1)S(1)}, bf16[8,16,512]{2,1,0:T(8,128)(2,1)S(1)}) custom-call(bf16[4,512,512]{2,1,0:T(8,128)(2,1)S(1)} %copy-done.1, bf16[4,256,512]{2,1,0:T(8,128)(2,1)S(1)} %get-tuple-element.23.panel_ref, ...), custom_call_target="tpu_custom_call" | custom-call | flops 671088640 | bytes 4194304 | tf_op jit(solution)/shard_map/pallas_call | solution.py:293
  43.1 2.5 %collective-permute-start.17 = (bf16[8,16,512]{2,1,0:T(8,128)(2,1)S(1)}, bf16[8,16,512]{2,1,0:T(8,128)(2,1)S(1)}, u32[]{:S(2)}, u32[]{:S(2)}) collective-permute-start(bf16[8,16,512]{2,1,0:T(8,128)(2,1)S(1)} %get-tuple-element.30), channel_id=1, source_target_pairs={{0,3},{1,2},{2,1},{3,0},{4,7},{5,6},{6,5},{7,4},{8,11},{9,10},{10,... | collective-permute-start | bytes 393224 | tf_op jit(solution)/shard_map/ppermute | solution.py:38
  45.6 0.0 collective-permute-start.18
  45.6 1.9 %collective-permute-start.19 = (bf16[8,16,512]{2,1,0:T(8,128)(2,1)S(1)}, bf16[8,16,512]{2,1,0:T(8,128)(2,1)S(1)}, u32[]{:S(2)}, u32[]{:S(2)}) collective-permute-start(bf16[8,16,512]{2,1,0:T(8,128)(2,1)S(1)} %get-tuple-element.32), channel_id=1, source_target_pairs={{0,1},{1,0},{2,3},{3,2},{4,5},{5,4},{6,7},{7,6},{8,9},{9,8},{10,11... | collective-permute-start | bytes 393224 | tf_op jit(solution)/shard_map/ppermute | solution.py:38
  47.5 3.9 %collective-permute-done.17.refs_0_ = bf16[8,16,512]{2,1,0:T(8,128)(2,1)S(1)} collective-permute-done((bf16[8,16,512]{2,1,0:T(8,128)(2,1)S(1)}, bf16[8,16,512]{2,1,0:T(8,128)(2,1)S(1)}, u32[]{:S(2)}, u32[]{:S(2)}) %collective-permute-start.17) | collective-permute-done | bytes 131104 | tf_op jit(solution)/shard_map/ppermute | solution.py:38
  51.4 4.8 %collective-permute-done.18.refs_1_ = bf16[8,16,512]{2,1,0:T(8,128)(2,1)S(1)} collective-permute-done((bf16[8,16,512]{2,1,0:T(8,128)(2,1)S(1)}, bf16[8,16,512]{2,1,0:T(8,128)(2,1)S(1)}, u32[]{:S(2)}, u32[]{:S(2)}) %collective-permute-start.18) | collective-permute-done | bytes 131104 | tf_op jit(solution)/shard_map/ppermute | solution.py:38
  56.1 0.0 collective-permute-done.19.refs_2_
  56.1 0.1 shard_map.98.refs_0_
  56.2 0.7 collective-permute-start.20
  56.9 2.3 %collective-permute-start.21 = (bf16[8,16,512]{2,1,0:T(8,128)(2,1)S(1)}, bf16[8,16,512]{2,1,0:T(8,128)(2,1)S(1)}, u32[]{:S(2)}, u32[]{:S(2)}) collective-permute-start(bf16[8,16,512]{2,1,0:T(8,128)(2,1)S(1)} %shard_map.98.refs_0_), channel_id=1, source_target_pairs={{0,2},{1,3},{2,0},{3,1},{4,6},{5,7},{6,4},{7,5},{8,10},{9,11},{10,... | collective-permute-start | bytes 393224 | tf_op jit(solution)/shard_map/ppermute | solution.py:38
  59.2 1.4 %collective-permute-start.22 = (bf16[8,16,512]{2,1,0:T(8,128)(2,1)S(1)}, bf16[8,16,512]{2,1,0:T(8,128)(2,1)S(1)}, u32[]{:S(2)}, u32[]{:S(2)}) collective-permute-start(bf16[8,16,512]{2,1,0:T(8,128)(2,1)S(1)} %shard_map.98.refs_0_), channel_id=1, source_target_pairs={{0,3},{1,2},{2,1},{3,0},{4,7},{5,6},{6,5},{7,4},{8,11},{9,10},{10,... | collective-permute-start | bytes 393224 | tf_op jit(solution)/shard_map/ppermute | solution.py:38
  60.7 3.0 %collective-permute-done.20.refs_1_ = bf16[8,16,512]{2,1,0:T(8,128)(2,1)S(1)} collective-permute-done((bf16[8,16,512]{2,1,0:T(8,128)(2,1)S(1)}, bf16[8,16,512]{2,1,0:T(8,128)(2,1)S(1)}, u32[]{:S(2)}, u32[]{:S(2)}) %collective-permute-start.20) | collective-permute-done | bytes 131104 | tf_op jit(solution)/shard_map/ppermute | solution.py:38
  63.7 6.1 %collective-permute-done.21.refs_2_ = bf16[8,16,512]{2,1,0:T(8,128)(2,1)S(1)} collective-permute-done((bf16[8,16,512]{2,1,0:T(8,128)(2,1)S(1)}, bf16[8,16,512]{2,1,0:T(8,128)(2,1)S(1)}, u32[]{:S(2)}, u32[]{:S(2)}) %collective-permute-start.21) | collective-permute-done | bytes 131104 | tf_op jit(solution)/shard_map/ppermute | solution.py:38
  69.8 0.0 collective-permute-done.22.refs_3_
  69.8 0.0 copy-done.3
  69.8 1.0 %shard_map.99 = (f32[4,64,512]{2,1,0:T(8,128)}, f32[4,64,512]{2,1,0:T(8,128)}) custom-call(f32[4,64,512]{2,1,0:T(8,128)S(1)} %copy-done.3, bf16[8,16,512]{2,1,0:T(8,128)(2,1)S(1)} %shard_map.98.refs_0_, bf16[8,16,512]{2,1,0:T(8,128)(2,1)S(1)} %collective-permute-done.20.refs_1_, bf16[8,16,512]{2,1,0:T(8,128)(2,1)S(1)} %collective-permute-done.21.refs_2_, ...), custom_call_target="tpu_custom_call" | custom-call | tf_op jit(solution)/shard_map/pallas_call | solution.py:293
  (12 shorter events, 0.0 us)
Async XLA Ops:
  0.6 1.0 %copy-start.2 = (f32[4,64,512]{2,1,0:T(8,128)S(1)}, f32[4,64,512]{2,1,0:T(8,128)}, u32[]{:S(2)}) copy-start(f32[4,64,512]{2,1,0:T(8,128)} %diag_ref.3) | copy-start | bytes 1572868
  1.7 1.2 %copy-start.4 = (bf16[4,1,8,32,512]{4,3,2,1,0:T(8,128)(2,1)S(1)}, bf16[4,1,8,32,512]{4,3,2,1,0:T(8,128)(2,1)}, u32[]{:S(2)}) copy-start(bf16[4,1,8,32,512]{4,3,2,1,0:T(8,128)(2,1)} %param.8) | copy-start | bytes 3145732
  2.9 0.8 %copy-start.6 = (bf16[1,1,32,512]{3,2,1,0:T(8,128)(2,1)S(1)}, bf16[1,1,32,512]{3,2,1,0:T(8,128)(2,1)}, u32[]{:S(2)}) copy-start(bf16[1,1,32,512]{3,2,1,0:T(8,128)(2,1)} %param.11) | copy-start | bytes 98308
  3.7 0.9 %copy-start.8 = (f32[64,512]{1,0:T(8,128)S(1)}, f32[64,512]{1,0:T(8,128)}, u32[]{:S(2)}) copy-start(f32[64,512]{1,0:T(8,128)} %top_ref.1) | copy-start | bytes 393220
  4.6 0.8 %copy-start.9 = (bf16[4,1,32,256]{3,2,1,0:T(8,128)(2,1)S(1)}, bf16[4,1,32,256]{3,2,1,0:T(8,128)(2,1)}, u32[]{:S(2)}) copy-start(bf16[4,1,32,256]{3,2,1,0:T(8,128)(2,1)} %param.7) | copy-start | bytes 196612
  5.4 0.7 copy-start.10
  7.6 12.2 %collective-permute-start = (bf16[4,32,512]{2,1,0:T(8,128)(2,1)S(1)}, bf16[4,32,512]{2,1,0:T(8,128)(2,1)S(1)}, u32[]{:S(2)}, u32[]{:S(2)}) collective-permute-start(bf16[4,32,512]{2,1,0:T(8,128)(2,1)S(1)} %get-tuple-element.20), channel_id=1, source_target_pairs={{0,3},{1,2},{2,1},{3,0},{4,7},{5,6},{6,5},{7,4},{8,11},{9,10},{10,... | collective-permute-start | bytes 393224 | tf_op jit(solution)/shard_map/ppermute | solution.py:38
  12.7 5.6 %collective-permute-start.3 = (bf16[96,512]{1,0:T(8,128)(2,1)S(1)}, bf16[96,512]{1,0:T(8,128)(2,1)S(1)}, u32[]{:S(2)}, u32[]{:S(2)}) collective-permute-start(bf16[96,512]{1,0:T(8,128)(2,1)S(1)} %get-tuple-element.24.refs_0_), channel_id=1, source_target_pairs={{0,24},{4,28},{8,16},{12,20},{16,8},{20,12},{24,0},{28,4},{1,25},{... | collective-permute-start | bytes 294920 | tf_op jit(solution)/shard_map/ppermute | solution.py:38
  15.1 8.6 %collective-permute-start.1 = (bf16[4,32,512]{2,1,0:T(8,128)(2,1)S(1)}, bf16[4,32,512]{2,1,0:T(8,128)(2,1)S(1)}, u32[]{:S(2)}, u32[]{:S(2)}) collective-permute-start(bf16[4,32,512]{2,1,0:T(8,128)(2,1)S(1)} %get-tuple-element.21), channel_id=1, source_target_pairs={{0,2},{1,3},{2,0},{3,1},{4,6},{5,7},{6,4},{7,5},{8,10},{9,11},{10,... | collective-permute-start | bytes 393224 | tf_op jit(solution)/shard_map/ppermute | solution.py:38
  15.1 8.6 %collective-permute-start.2 = (bf16[4,32,512]{2,1,0:T(8,128)(2,1)S(1)}, bf16[4,32,512]{2,1,0:T(8,128)(2,1)S(1)}, u32[]{:S(2)}, u32[]{:S(2)}) collective-permute-start(bf16[4,32,512]{2,1,0:T(8,128)(2,1)S(1)} %get-tuple-element.22), channel_id=1, source_target_pairs={{0,1},{1,0},{2,3},{3,2},{4,5},{5,4},{6,7},{7,6},{8,9},{9,8},{10,11... | collective-permute-start | bytes 393224 | tf_op jit(solution)/shard_map/ppermute | solution.py:38
  15.9 15.3 %collective-permute-start.4 = (bf16[96,512]{1,0:T(8,128)(2,1)S(1)}, bf16[96,512]{1,0:T(8,128)(2,1)S(1)}, u32[]{:S(2)}, u32[]{:S(2)}) collective-permute-start(bf16[96,512]{1,0:T(8,128)(2,1)S(1)} %get-tuple-element.24.refs_0_), channel_id=1, source_target_pairs={{0,16},{4,20},{8,24},{12,28},{16,0},{20,4},{24,8},{28,12},{1,17},{... | collective-permute-start | bytes 294920 | tf_op jit(solution)/shard_map/ppermute | solution.py:38
  18.3 13.4 %collective-permute-start.5 = (bf16[96,512]{1,0:T(8,128)(2,1)S(1)}, bf16[96,512]{1,0:T(8,128)(2,1)S(1)}, u32[]{:S(2)}, u32[]{:S(2)}) collective-permute-start(bf16[96,512]{1,0:T(8,128)(2,1)S(1)} %get-tuple-element.24.refs_0_), channel_id=1, source_target_pairs={{0,8},{4,12},{8,0},{12,4},{16,24},{20,28},{24,16},{28,20},{1,9},{5... | collective-permute-start | bytes 294920 | tf_op jit(solution)/shard_map/ppermute | solution.py:38
  19.8 12.5 %collective-permute-start.6 = (bf16[96,512]{1,0:T(8,128)(2,1)S(1)}, bf16[96,512]{1,0:T(8,128)(2,1)S(1)}, u32[]{:S(2)}, u32[]{:S(2)}) collective-permute-start(bf16[96,512]{1,0:T(8,128)(2,1)S(1)} %get-tuple-element.24.refs_0_), channel_id=1, source_target_pairs={{0,4},{4,0},{8,12},{12,8},{16,20},{20,16},{24,28},{28,24},{1,5},{5... | collective-permute-start | bytes 294920 | tf_op jit(solution)/shard_map/ppermute | solution.py:38
  23.8 8.5 %collective-permute-start.7 = (bf16[96,512]{1,0:T(8,128)(2,1)S(1)}, bf16[96,512]{1,0:T(8,128)(2,1)S(1)}, u32[]{:S(2)}, u32[]{:S(2)}) collective-permute-start(bf16[96,512]{1,0:T(8,128)(2,1)S(1)} %collective-permute-done.3.refs_1_), channel_id=1, source_target_pairs={{0,4},{4,0},{8,12},{12,8},{16,20},{20,16},{24,28},{28,24},{1,5},{5... | collective-permute-start | bytes 294920 | tf_op jit(solution)/shard_map/ppermute | solution.py:38
  23.8 1.6 %copy-start = (bf16[4,512,512]{2,1,0:T(8,128)(2,1)S(1)}, bf16[4,512,512]{2,1,0:T(8,128)(2,1)}, u32[]{:S(2)}) copy-start(bf16[4,512,512]{2,1,0:T(8,128)(2,1)} %l_ref.5) | copy-start | bytes 6291460
  25.4 0.8 %copy-start.7 = (bf16[1,1,32,512]{3,2,1,0:T(8,128)(2,1)S(1)}, bf16[1,1,32,512]{3,2,1,0:T(8,128)(2,1)}, u32[]{:S(2)}) copy-start(bf16[1,1,32,512]{3,2,1,0:T(8,128)(2,1)} %param.11) | copy-start | bytes 98308
  26.1 0.7 copy-start.11
  26.8 12.3 %copy-start.1 = (bf16[4,512,512]{2,1,0:T(8,128)(2,1)S(1)}, bf16[4,512,512]{2,1,0:T(8,128)(2,1)}, u32[]{:S(2)}) copy-start(bf16[4,512,512]{2,1,0:T(8,128)(2,1)} %l_ref.5) | copy-start | bytes 6291460
  28.7 12.7 %copy-start.5 = (bf16[4,32,512]{2,1,0:T(8,128)(2,1)S(1)}, bf16[4,32,512]{2,1,0:T(8,128)(2,1)}, u32[]{:S(2)}) copy-start(bf16[4,32,512]{2,1,0:T(8,128)(2,1)} %shard_map.95.refs_0_) | copy-start | bytes 393220
  28.7 7.3 %collective-permute-start.10 = (bf16[4,32,512]{2,1,0:T(8,128)(2,1)}, bf16[4,32,512]{2,1,0:T(8,128)(2,1)S(1)}, u32[]{:S(2)}, u32[]{:S(2)}) collective-permute-start(bf16[4,32,512]{2,1,0:T(8,128)(2,1)} %shard_map.95.refs_0_), channel_id=1, source_target_pairs={{0,24},{4,28},{8,16},{12,20},{16,8},{20,12},{24,0},{28,4},{1,25},{... | collective-permute-start | bytes 393224 | tf_op jit(solution)/shard_map/ppermute | solution.py:38
  31.2 7.4 %collective-permute-start.11 = (bf16[4,32,512]{2,1,0:T(8,128)(2,1)}, bf16[4,32,512]{2,1,0:T(8,128)(2,1)S(1)}, u32[]{:S(2)}, u32[]{:S(2)}) collective-permute-start(bf16[4,32,512]{2,1,0:T(8,128)(2,1)} %shard_map.95.refs_0_), channel_id=1, source_target_pairs={{0,16},{4,20},{8,24},{12,28},{16,0},{20,4},{24,8},{28,12},{1,17},{... | collective-permute-start | bytes 393224 | tf_op jit(solution)/shard_map/ppermute | solution.py:38
  31.7 7.0 %collective-permute-start.12 = (bf16[4,32,512]{2,1,0:T(8,128)(2,1)}, bf16[4,32,512]{2,1,0:T(8,128)(2,1)S(1)}, u32[]{:S(2)}, u32[]{:S(2)}) collective-permute-start(bf16[4,32,512]{2,1,0:T(8,128)(2,1)} %shard_map.95.refs_0_), channel_id=1, source_target_pairs={{0,8},{4,12},{8,0},{12,4},{16,24},{20,28},{24,16},{28,20},{1,9},{5... | collective-permute-start | bytes 393224 | tf_op jit(solution)/shard_map/ppermute | solution.py:38
  32.2 1.3 %collective-permute-start.8 = (bf16[96,512]{1,0:T(8,128)(2,1)S(1)}, bf16[96,512]{1,0:T(8,128)(2,1)S(1)}, u32[]{:S(2)}, u32[]{:S(2)}) collective-permute-start(bf16[96,512]{1,0:T(8,128)(2,1)S(1)} %collective-permute-done.4.refs_2_), channel_id=1, source_target_pairs={{0,4},{4,0},{8,12},{12,8},{16,20},{20,16},{24,28},{28,24},{1,5},{5... | collective-permute-start | bytes 294920 | tf_op jit(solution)/shard_map/ppermute | solution.py:38
  32.2 6.8 %collective-permute-start.9 = (bf16[96,512]{1,0:T(8,128)(2,1)S(1)}, bf16[96,512]{1,0:T(8,128)(2,1)S(1)}, u32[]{:S(2)}, u32[]{:S(2)}) collective-permute-start(bf16[96,512]{1,0:T(8,128)(2,1)S(1)} %collective-permute-done.5.refs_3_), channel_id=1, source_target_pairs={{0,4},{4,0},{8,12},{12,8},{16,20},{20,16},{24,28},{28,24},{1,5},{5... | collective-permute-start | bytes 294920 | tf_op jit(solution)/shard_map/ppermute | solution.py:38
  33.5 7.9 %collective-permute-start.13 = (bf16[4,32,512]{2,1,0:T(8,128)(2,1)}, bf16[4,32,512]{2,1,0:T(8,128)(2,1)S(1)}, u32[]{:S(2)}, u32[]{:S(2)}) collective-permute-start(bf16[4,32,512]{2,1,0:T(8,128)(2,1)} %shard_map.95.refs_0_), channel_id=1, source_target_pairs={{0,4},{4,0},{8,12},{12,8},{16,20},{20,16},{24,28},{28,24},{1,5},{5... | collective-permute-start | bytes 393224 | tf_op jit(solution)/shard_map/ppermute | solution.py:38
  36.0 5.4 %collective-permute-start.14 = (bf16[4,32,512]{2,1,0:T(8,128)(2,1)S(1)}, bf16[4,32,512]{2,1,0:T(8,128)(2,1)S(1)}, u32[]{:S(2)}, u32[]{:S(2)}) collective-permute-start(bf16[4,32,512]{2,1,0:T(8,128)(2,1)S(1)} %collective-permute-done.10.refs_1_), channel_id=1, source_target_pairs={{0,4},{4,0},{8,12},{12,8},{16,20},{20,16},{24,28},{28,24},{1,5},{5... | collective-permute-start | bytes 393224 | tf_op jit(solution)/shard_map/ppermute | solution.py:38
  38.6 2.9 %collective-permute-start.15 = (bf16[4,32,512]{2,1,0:T(8,128)(2,1)S(1)}, bf16[4,32,512]{2,1,0:T(8,128)(2,1)S(1)}, u32[]{:S(2)}, u32[]{:S(2)}) collective-permute-start(bf16[4,32,512]{2,1,0:T(8,128)(2,1)S(1)} %collective-permute-done.11.refs_2_), channel_id=1, source_target_pairs={{0,4},{4,0},{8,12},{12,8},{16,20},{20,16},{24,28},{28,24},{1,5},{5... | collective-permute-start | bytes 393224 | tf_op jit(solution)/shard_map/ppermute | solution.py:38
  38.7 2.8 %collective-permute-start.16 = (bf16[4,32,512]{2,1,0:T(8,128)(2,1)S(1)}, bf16[4,32,512]{2,1,0:T(8,128)(2,1)S(1)}, u32[]{:S(2)}, u32[]{:S(2)}) collective-permute-start(bf16[4,32,512]{2,1,0:T(8,128)(2,1)S(1)} %collective-permute-done.12.refs_3_), channel_id=1, source_target_pairs={{0,4},{4,0},{8,12},{12,8},{16,20},{20,16},{24,28},{28,24},{1,5},{5... | collective-permute-start | bytes 393224 | tf_op jit(solution)/shard_map/ppermute | solution.py:38
  41.5 28.4 %copy-start.3 = (f32[4,64,512]{2,1,0:T(8,128)S(1)}, f32[4,64,512]{2,1,0:T(8,128)}, u32[]{:S(2)}) copy-start(f32[4,64,512]{2,1,0:T(8,128)} %diag_ref.3) | copy-start | bytes 1572868
  43.1 8.3 %collective-permute-start.17 = (bf16[8,16,512]{2,1,0:T(8,128)(2,1)S(1)}, bf16[8,16,512]{2,1,0:T(8,128)(2,1)S(1)}, u32[]{:S(2)}, u32[]{:S(2)}) collective-permute-start(bf16[8,16,512]{2,1,0:T(8,128)(2,1)S(1)} %get-tuple-element.30), channel_id=1, source_target_pairs={{0,3},{1,2},{2,1},{3,0},{4,7},{5,6},{6,5},{7,4},{8,11},{9,10},{10,... | collective-permute-start | bytes 393224 | tf_op jit(solution)/shard_map/ppermute | solution.py:38
  45.6 10.6 %collective-permute-start.18 = (bf16[8,16,512]{2,1,0:T(8,128)(2,1)S(1)}, bf16[8,16,512]{2,1,0:T(8,128)(2,1)S(1)}, u32[]{:S(2)}, u32[]{:S(2)}) collective-permute-start(bf16[8,16,512]{2,1,0:T(8,128)(2,1)S(1)} %get-tuple-element.31), channel_id=1, source_target_pairs={{0,2},{1,3},{2,0},{3,1},{4,6},{5,7},{6,4},{7,5},{8,10},{9,11},{10,... | collective-permute-start | bytes 393224 | tf_op jit(solution)/shard_map/ppermute | solution.py:38
  45.6 10.6 %collective-permute-start.19 = (bf16[8,16,512]{2,1,0:T(8,128)(2,1)S(1)}, bf16[8,16,512]{2,1,0:T(8,128)(2,1)S(1)}, u32[]{:S(2)}, u32[]{:S(2)}) collective-permute-start(bf16[8,16,512]{2,1,0:T(8,128)(2,1)S(1)} %get-tuple-element.32), channel_id=1, source_target_pairs={{0,1},{1,0},{2,3},{3,2},{4,5},{5,4},{6,7},{7,6},{8,9},{9,8},{10,11... | collective-permute-start | bytes 393224 | tf_op jit(solution)/shard_map/ppermute | solution.py:38
  56.2 7.5 %collective-permute-start.20 = (bf16[8,16,512]{2,1,0:T(8,128)(2,1)S(1)}, bf16[8,16,512]{2,1,0:T(8,128)(2,1)S(1)}, u32[]{:S(2)}, u32[]{:S(2)}) collective-permute-start(bf16[8,16,512]{2,1,0:T(8,128)(2,1)S(1)} %shard_map.98.refs_0_), channel_id=1, source_target_pairs={{0,1},{1,0},{2,3},{3,2},{4,5},{5,4},{6,7},{7,6},{8,9},{9,8},{10,11... | collective-permute-start | bytes 393224 | tf_op jit(solution)/shard_map/ppermute | solution.py:38
  56.9 12.9 %collective-permute-start.21 = (bf16[8,16,512]{2,1,0:T(8,128)(2,1)S(1)}, bf16[8,16,512]{2,1,0:T(8,128)(2,1)S(1)}, u32[]{:S(2)}, u32[]{:S(2)}) collective-permute-start(bf16[8,16,512]{2,1,0:T(8,128)(2,1)S(1)} %shard_map.98.refs_0_), channel_id=1, source_target_pairs={{0,2},{1,3},{2,0},{3,1},{4,6},{5,7},{6,4},{7,5},{8,10},{9,11},{10,... | collective-permute-start | bytes 393224 | tf_op jit(solution)/shard_map/ppermute | solution.py:38
  59.2 10.6 %collective-permute-start.22 = (bf16[8,16,512]{2,1,0:T(8,128)(2,1)S(1)}, bf16[8,16,512]{2,1,0:T(8,128)(2,1)S(1)}, u32[]{:S(2)}, u32[]{:S(2)}) collective-permute-start(bf16[8,16,512]{2,1,0:T(8,128)(2,1)S(1)} %shard_map.98.refs_0_), channel_id=1, source_target_pairs={{0,3},{1,2},{2,1},{3,0},{4,7},{5,6},{6,5},{7,4},{8,11},{9,10},{10,... | collective-permute-start | bytes 393224 | tf_op jit(solution)/shard_map/ppermute | solution.py:38

commit v3 on v2

--- a/solution.py
+++ b/solution.py
@@ -155,38 +155,46 @@
     )
 
 
-def first_kernel(n_cols, n_rows, g_ref, m_ref, pattern_ref, diag_ref, top_ref, tops_ref, panel_ref, joined_ref, *piece_refs):
-    col = lax.axis_index("cols")
-    supers, _, piece, width = m_ref.shape
-    share = top_ref.shape[0]
+def fetch(source, into, sem):
+    copy = pltpu.make_async_copy(source, into, sem)
+    copy.start()
+    return copy
+
+
+def first_kernel(n_cols, n_rows, g_any, m_any, pattern_any, *refs):
+    panel_ref, mask_ref = refs[:2]
+    piece_refs = refs[2 : 2 + n_cols]
+    g_ref, m_ref, pattern_ref, sems = refs[2 + n_cols :]
+    col, row = lax.axis_index("cols"), lax.axis_index("rows")
+    supers, _, piece, _ = m_ref.shape
+    pattern_copy = fetch(pattern_any, pattern_ref, sems.at[0])
+    panel_copies = [fetch(m_any.at[k], m_ref.at[k], sems.at[1 + k]) for k in range(supers)]
+    g_copy = fetch(g_any, g_ref, sems.at[1 + supers])
+    pattern_copy.wait()
     for k in range(supers):
+        mask_ref[k] = jnp.full(mask_ref.shape[1:], pattern_ref[k, col * n_rows + row].astype(F32))
+        panel_copies[k].wait()
+        if k == 0:
+            g_copy.wait()
         for r in range(n_rows):
             on = pattern_ref[k, col * n_rows + r].astype(F32)
             panel_ref[k, pl.ds(r * piece, piece)] = (m_ref[k, r].astype(F32) * on).astype(BF)
-    for j, out in enumerate(piece_refs):
-        rows = g_ref[col ^ j]
-        for k in range(supers):
-            out[k] = dot(rows, panel_ref[k]).astype(BF)
-    mine = jnp.zeros((share, width), F32)
-    for i in range(supers):
-        begin = top_ref[...] if i == 0 else diag_ref[supers - i]
-        mine = jnp.where(col == i, begin, mine)
-    joined_ref[pl.ds(0, share)] = mine.astype(BF)
-    joined_ref[pl.ds(share, piece)] = tops_ref[...]
-
-
-def chain_kernel(n_cols, n_rows, l_ref, tops_ref, pattern_ref, own_ref, *refs):
-    *got_refs, cols_ref = refs
-    supers = own_ref.shape[0]
-    at = lax.axis_index("cols") * n_rows + lax.axis_index("rows")
-    prev = tops_ref[...]
+        for j, out in enumerate(piece_refs):
+            out[k] = dot(g_ref[col ^ j], panel_ref[k]).astype(BF)
+
+
+def chain_kernel(l_ref, joined_ref, mask_ref, own_ref, *refs):
+    *got_refs, cols_ref, copy_ref = refs
+    supers, piece, _ = own_ref.shape
+    prev = joined_ref[pl.ds(joined_ref.shape[0] - piece, piece)]
     for k in reversed(range(supers)):
         total = own_ref[k].astype(F32)
         for got in got_refs:
             total = total + got[k].astype(F32)
         total = total + dot(prev, l_ref[k])
-        prev = (-(total * pattern_ref[k, at].astype(F32))).astype(BF)
+        prev = (-(total * mask_ref[k, pl.ds(0, 1)])).astype(BF)
         cols_ref[k] = prev
+        copy_ref[k] = prev
 
 
 def place(refs, order, write):
@@ -195,39 +203,65 @@
         write(me ^ offset, ref)
 
 
-def ready_kernel(n_cols, n_rows, order, l_ref, panel_ref, *refs):
+def ready_kernel(n_cols, n_rows, l_any, diag_any, top_any, tops_any, panel_ref, *refs):
+    l_ref, stacks_ref, reach_ref, joined_ref, begin_ref, tops_ref, sems = refs
+    supers, width, _ = l_ref.shape
+    share, piece = width // n_rows, tops_ref.shape[0]
+    col, row = lax.axis_index("cols"), lax.axis_index("rows")
+    copies = [fetch(l_any.at[k], l_ref.at[k], sems.at[k]) for k in range(supers)]
+    tops_copy = fetch(tops_any, tops_ref, sems.at[supers])
+
+    @pl.when(col == 0)
+    def _():
+        fetch(top_any, begin_ref, sems.at[supers + 1]).wait()
+
+    @pl.when(jnp.logical_and(col > 0, col < supers))
+    def _():
+        fetch(diag_any.at[jnp.clip(supers - col, 1, supers - 1)], begin_ref, sems.at[supers + 1]).wait()
+
+    @pl.when(col >= supers)
+    def _():
+        begin_ref[...] = jnp.zeros_like(begin_ref)
+
+    tops_copy.wait()
+    joined_ref[pl.ds(0, share)] = begin_ref[...].astype(BF)
+    joined_ref[pl.ds(share, piece)] = tops_ref[...]
+    lane = lax.broadcasted_iota(jnp.int32, (share, width), 1)
+    sub = lax.broadcasted_iota(jnp.int32, (share, width), 0)
+    unit = jnp.where(lane == row * share + sub, 1.0, 0.0).astype(BF)
+    stacks_ref[...] = jnp.zeros_like(stacks_ref)
+    stacks_ref[0, pl.ds(0, share)] = unit
+    stack, at = unit, 0
+    for k in range(supers):
+        reach_ref[pl.ds(at, (k + 1) * share)] = dot_nt(stack, panel_ref[k]).astype(BF)
+        at += (k + 1) * share
+        copies[k].wait()
+        stack = jnp.concatenate([dot_nt(stack, l_ref[k]).astype(BF), unit], 0)
+        stacks_ref[k + 1, pl.ds(0, (k + 2) * share)] = stack
+
+
+def place(refs, order, write):
+    me = lax.axis_index("rows")
+    for ref, offset in zip(refs, order):
+        write(me ^ offset, ref)
+
+
+def begin_kernel(n_cols, n_rows, order, l_ref, panel_ref, stacks_ref, *refs):
     got = refs[: len(order)]
-    stacks_ref, reach_ref, begin_ref, ahead_ref, x_ref, y_ref, all_ref = refs[len(order) :]
+    begin_ref, ahead_ref, x_ref, y_ref = refs[len(order) :]
     supers, width, _ = l_ref.shape
-    share = width // n_rows
-    piece = y_ref.shape[0] // n_rows
-    col, row = lax.axis_index("cols"), lax.axis_index("rows")
+    share, piece = width // n_rows, y_ref.shape[0] // n_rows
+    col = lax.axis_index("cols")
 
     def write(at, ref):
         x_ref[pl.ds(pl.multiple_of(at * share, share), share)] = ref[pl.ds(0, share)]
         y_ref[pl.ds(pl.multiple_of(at * piece, piece), piece)] = ref[pl.ds(share, piece)]
 
     place(got, order, write)
-    lane = lax.broadcasted_iota(jnp.int32, (share, width), 1)
-    sub = lax.broadcasted_iota(jnp.int32, (share, width), 0)
-    unit = jnp.where(lane == row * share + sub, 1.0, 0.0).astype(BF)
-    stack = unit
-    all_ref[...] = jnp.zeros_like(all_ref)
-    all_ref[0, pl.ds(0, share)] = unit
-    at = 0
-    for k in range(supers):
-        reach_ref[pl.ds(at, (k + 1) * share)] = dot_nt(stack, panel_ref[k]).astype(BF)
-        at += (k + 1) * share
-        stack = jnp.concatenate([dot_nt(stack, l_ref[k]).astype(BF), unit], 0)
-        all_ref[k + 1, pl.ds(0, (k + 2) * share)] = stack
-    at = 0
-    for k in range(1, supers):
-        stacks_ref[pl.ds(at, (k + 1) * share)] = all_ref[k, pl.ds(0, (k + 1) * share)]
-        at += (k + 1) * share
-    begin = dot(all_ref[jnp.maximum(supers - col, 0)], x_ref[...])
+    begin = dot(stacks_ref[jnp.maximum(supers - col, 0)], x_ref[...])
     begin_ref[...] = begin
     first = jnp.where(col == 0, begin, 0.0).astype(BF)
-    across = dot_nt(stack, y_ref[...]).astype(BF)
+    across = dot_nt(stacks_ref[supers], y_ref[...]).astype(BF)
     ahead_ref[...] = dot(first, l_ref[supers - 1]) + dot(across, panel_ref[supers - 1])
 
 
@@ -247,13 +281,11 @@
 
     place(got, order, write)
     full = ahead_ref[...]
-    stack_at = sum((k + 1) * share for k in range(1, supers))
     reach_at = sum((k + 1) * share for k in range(supers))
     for k in reversed(range(supers)):
         here = (k + 1) * share
         if k < supers - 1:
-            stack_at -= here + share
-            across = dot_nt(stacks_ref[pl.ds(stack_at, here + share)], y_ref[k + 1]).astype(BF)
+            across = dot_nt(stacks_ref[k + 1, pl.ds(0, here + share)], y_ref[k + 1]).astype(BF)
             full = dot(acc.astype(BF), l_ref[k]) + dot(across, panel_ref[k])
         reach_at -= here
         acc = full[:here] - dot(reach_ref[pl.ds(reach_at, here)], y_ref[k])
@@ -288,14 +320,14 @@
             sub_out[k, rows] = got[supers + k].astype(F32)
 
 
-def call(kernel, outs, *args, scratch=(), smem=(), flops=0, moved=0):
-    vmem = pl.BlockSpec(memory_space=pltpu.VMEM)
+def call(kernel, outs, *args, scratch=(), away=(), flops=0, moved=0):
+    vmem, hbm = pl.BlockSpec(memory_space=pltpu.VMEM), pl.BlockSpec(memory_space=pltpu.HBM)
     return pl.pallas_call(
         kernel,
         out_shape=tuple(jax.ShapeDtypeStruct(s, d) for s, d in outs),
-        in_specs=[pl.BlockSpec(memory_space=pltpu.SMEM) if i in smem else vmem for i in range(len(args))],
+        in_specs=[hbm if i in away else vmem for i in range(len(args))],
         out_specs=tuple(vmem for _ in outs),
-        scratch_shapes=[pltpu.VMEM(s, d) for s, d in scratch],
+        scratch_shapes=scratch,
         compiler_params=pltpu.CompilerParams(vmem_limit_bytes=VMEM_BYTES),
         cost_estimate=pl.CostEstimate(flops=flops, bytes_accessed=moved, transcendentals=0),
     )(*args)
@@ -320,32 +352,42 @@
     block = n_rows * piece
     ways = range(1, n_cols)
     rows_of = [(k + 1) * share for k in range(supers + 1)]
-    panel, joined, own, *sent = call(
+    panel, mask, own, *sent = call(
         functools.partial(first_kernel, n_cols, n_rows),
-        [((supers, block, width), BF), ((share + piece, width), BF)] + [((supers, piece, width), BF)] * n_cols,
-        known, lower_panel[:, 0], pattern, diag_inverse, top_diag, tops, smem=(2,),
+        [((supers, block, width), BF), ((supers, 8, width), F32)] + [((supers, piece, width), BF)] * n_cols,
+        known, lower_panel[:, 0], pattern, away=range(3),
+        scratch=[
+            pltpu.VMEM(known.shape, BF), pltpu.VMEM((supers, n_rows, piece, width), BF),
+            pltpu.SMEM(pattern.shape, jnp.int32), pltpu.SemaphoreType.DMA((2 + supers,)),
+        ],
         flops=2 * known.size * supers * width, moved=4 * block * width * supers,
     )
     got = [hop(sent[j - 1], "cols", j) for j in reversed(ways)]
-    around = exchange_rows(joined)
-    stacks, reach, begin, ahead = call(
-        functools.partial(ready_kernel, n_cols, n_rows, ROW_ORDER),
-        [((sum(rows_of[1:supers]), width), BF), ((sum(rows_of[:supers]), block), BF), ((rows_of[supers], width), F32), ((rows_of[supers], width), F32)],
-        chain_panel, panel, *around,
-        scratch=[((width, width), BF), ((block, width), BF), ((supers + 1, rows_of[supers], width), BF)],
-        flops=2 * 8 * share * width * width * 4, moved=4 * width * width * supers,
-    )
-    (cols,) = call(
-        functools.partial(chain_kernel, n_cols, n_rows),
-        [((supers, piece, width), BF)],
-        chain_panel, tops, pattern, own, *got, smem=(2,),
+    links, stacks, reach, joined = call(
+        functools.partial(ready_kernel, n_cols, n_rows),
+        [(chain_panel.shape, BF), ((supers + 1, rows_of[supers], width), BF), ((sum(rows_of[:supers]), block), BF), ((share + piece, width), BF)],
+        chain_panel, diag_inverse, top_diag, tops, panel, away=range(4),
+        scratch=[pltpu.VMEM((share, width), F32), pltpu.VMEM((piece, width), BF), pltpu.SemaphoreType.DMA((supers + 2,))],
+        flops=2 * 12 * share * width * width, moved=4 * width * width * supers,
+    )
+    begin, ahead = call(
+        functools.partial(begin_kernel, n_cols, n_rows, ROW_ORDER),
+        [((rows_of[supers], width), F32)] * 2,
+        links, panel, stacks, *exchange_rows(joined),
+        scratch=[pltpu.VMEM((width, width), BF), pltpu.VMEM((block, width), BF)],
+        flops=2 * 15 * share * width * width, moved=4 * width * width,
+    )
+    cols, cols_out = call(
+        chain_kernel,
+        [((supers, piece, width), BF)] * 2,
+        links, joined, mask, own, *got,
         flops=2 * piece * width * width * supers, moved=2 * width * width * supers,
     )
     pieces = call(
         functools.partial(rows_kernel, n_cols, n_rows, ROW_ORDER),
         [((2 * supers, share // n_cols, width), BF)] * n_cols,
-        chain_panel, panel, stacks, reach, begin, ahead, *exchange_rows(cols),
-        scratch=[((supers, block, width), BF), ((2 * supers, share, width), F32)],
+        links, panel, stacks, reach, begin, ahead, *exchange_rows(cols),
+        scratch=[pltpu.VMEM((supers, block, width), BF), pltpu.VMEM((2 * supers, share, width), F32)],
         flops=2 * 20 * share * width * width, moved=4 * width * width * supers,
     )
     got = [hop(pieces[j], "cols", j) for j in reversed(ways)]
@@ -356,7 +398,7 @@
         [(diag_inverse.shape, F32)] * 2,
         diag_inverse, summed, *[there[j] for j in ways],
     )
-    return cols.reshape(supers, 1, 1, piece, width), diag, sub
+    return cols_out.reshape(supers, 1, 1, piece, width), diag, sub
 
 
 def solution(mesh):

time: 71.4 us -> 65 us (0.910)
  waiting for transfers between devices: 29.4 us -> 23.3 us
  local copies, waits for them, and re-layouts: 8.48 us -> 7.04 us
  Pallas kernels: 8.41 us -> 9.73 us
    ppermute x23, waiting for transfers between devices: 29.4 us -> 23.3 us  [hop(): return lax.ppermute(x, axis, [(i, target(i, j, n)) for i in range(n)])]
    unnamed x24 -> x16, local copies, waits for them, and re-layouts: 8.48 us -> 7.04 us
    pallas_call x6 -> x7, Pallas kernels: 8.41 us -> 9.73 us  [call(): pl.pallas_call(kernel, out_shape=tuple((jax.ShapeDtypeStruct(s, d) for s,...]
  transfers between devices with their start and end apart: 23 -> 23, of which waited for: 10 -> 8; matrix products, arithmetic and copies ran while one was open for 0% -> 0% of each run, Pallas kernels for 6% -> 8%
where the time goes in v3:
time: 65 us; the launch traced here: 64.6 us
  starting transfers between devices  23.8 us (37%)
  waiting for transfers between devices  23.3 us (36%)
  Pallas kernels  9.73 us (15%)
  local copies, waits for them, and re-layouts  7.04 us (11%)
  between operations  0.75 us (1%)
    ppermute x23, starting transfers between devices, hop(): return lax.ppermute(x, axis, [(i, target(i, j, n)) for i in range(n)])  23.8 us
    ppermute x23, waiting for transfers between devices, hop(): return lax.ppermute(x, axis, [(i, target(i, j, n)) for i in range(n)])  23.3 us
    pallas_call x7, Pallas kernels, call(): pl.pallas_call(kernel, out_shape=tuple((jax.ShapeDtypeStruct(s, d) for s,...  9.73 us
    unnamed x16, local copies, waits for them, and re-layouts  7.04 us
  transfers between devices with their start and end apart: 23, of which 8 were waited for; matrix products, arithmetic and copies ran while one was open for 0% of the time, Pallas kernels for 8%

profile of v3, /device:TPU:0, one launch (start us, length us, event | category | flops | bytes accessed | tf_op | source)
XLA Modules:
  0.0 64.6 jit_solution(7467375434569412799)
XLA Ops:
  0.6 0.0 copy-start.3
  0.6 1.2 %copy-done.3 = bf16[4,1,8,32,512]{4,3,2,1,0:T(8,128)(2,1)S(1)} copy-done((bf16[4,1,8,32,512]{4,3,2,1,0:T(8,128)(2,1)S(1)}, bf16[4,1,8,32,512]{4,3,2,1,0:T(8,128)(2,1)}, u32[]{:S(2)}) %copy-start.3) | copy-done | bytes 1048600
  1.9 0.8 %copy-done.5 = bf16[4,1,32,256]{3,2,1,0:T(8,128)(2,1)S(1)} copy-done((bf16[4,1,32,256]{3,2,1,0:T(8,128)(2,1)S(1)}, bf16[4,1,32,256]{3,2,1,0:T(8,128)(2,1)}, u32[]{:S(2)}) %copy-start.5) | copy-done | bytes 65560
  2.7 0.7 %copy-done.7 = s32[4,32]{1,0:T(4,128)S(1)} copy-done((s32[4,32]{1,0:T(4,128)S(1)}, s32[4,32]{1,0:T(4,128)}, u32[]{:S(2)}) %copy-start.7) | copy-done | bytes 536
  3.4 1.9 %shard_map.94 = (bf16[4,256,512]{2,1,0:T(8,128)(2,1)S(1)}, f32[4,8,512]{2,1,0:T(8,128)S(1)}, bf16[4,32,512]{2,1,0:T(8,128)(2,1)S(1)}, bf16[4,32,512]{2,1,0:T(8,1...) custom-call(bf16[4,32,256]{2,1,0:T(8,128)(2,1)S(1)} %bitcast.7, ...), custom_call_target="tpu_custom_call" | custom-call | flops 134217728 | bytes 2097152 | tf_op jit(solution)/shard_map/pallas_call | solution.py:325
  5.3 5.1 %collective-permute-start = (bf16[4,32,512]{2,1,0:T(8,128)(2,1)S(1)}, bf16[4,32,512]{2,1,0:T(8,128)(2,1)S(1)}, u32[]{:S(2)}, u32[]{:S(2)}) collective-permute-start(bf16[4,32,512]{2,1,0:T(8,128)(2,1)S(1)} %get-tuple-element.28), channel_id=1, source_target_pairs={{0,3},{1,2},{2,1},{3,0},{4,7},{5,6},{6,5},{7,4},{8,11},{9,10},{10,... | collective-permute-start | bytes 393224 | tf_op jit(solution)/shard_map/ppermute | solution.py:38
  10.4 0.0 collective-permute-start.1
  10.4 0.6 collective-permute-start.2
  11.0 0.0 copy-start
  11.0 1.6 %copy-done = bf16[4,512,512]{2,1,0:T(8,128)(2,1)S(1)} copy-done((bf16[4,512,512]{2,1,0:T(8,128)(2,1)S(1)}, bf16[4,512,512]{2,1,0:T(8,128)(2,1)}, u32[]{:S(2)}) %copy-start) | copy-done | bytes 2097176
  12.6 1.0 %copy-done.1 = f32[4,64,512]{2,1,0:T(8,128)S(1)} copy-done((f32[4,64,512]{2,1,0:T(8,128)S(1)}, f32[4,64,512]{2,1,0:T(8,128)}, u32[]{:S(2)}) %copy-start.1) | copy-done | bytes 524312
  13.7 0.9 %copy-done.4 = f32[64,512]{1,0:T(8,128)S(1)} copy-done((f32[64,512]{1,0:T(8,128)S(1)}, f32[64,512]{1,0:T(8,128)}, u32[]{:S(2)}) %copy-start.4) | copy-done | bytes 131096
  14.6 0.8 %copy-done.6 = bf16[1,1,32,512]{3,2,1,0:T(8,128)(2,1)S(1)} copy-done((bf16[1,1,32,512]{3,2,1,0:T(8,128)(2,1)S(1)}, bf16[1,1,32,512]{3,2,1,0:T(8,128)(2,1)}, u32[]{:S(2)}) %copy-start.6) | copy-done | bytes 32792
  15.3 2.6 %shard_map.95 = (bf16[4,512,512]{2,1,0:T(8,128)(2,1)S(1)}, bf16[5,320,512]{2,1,0:T(8,128)(2,1)S(1)}, bf16[640,256]{1,0:T(8,128)(2,1)S(1)}, bf16[96,512]{1,0:T(8,128)(2,1)S(1)}) custom-call(bf16[4,512,512]{2,1,0:T(8,128)(2,1)S(1)} %copy-done, f32[4,64,512]{2,1,0:T(8,128)S(1)} %copy-done.1, f32[64,512]{1,0:T(8,128)S(1)} %copy-done.4, ...), custom_call_target="tpu_custom_call" | custom-call | flops 402653184 | bytes 4194304 | tf_op jit(solution)/shard_map/pallas_call | solution.py:325
  17.9 2.7 %collective-permute-start.3 = (bf16[96,512]{1,0:T(8,128)(2,1)S(1)}, bf16[96,512]{1,0:T(8,128)(2,1)S(1)}, u32[]{:S(2)}, u32[]{:S(2)}) collective-permute-start(bf16[96,512]{1,0:T(8,128)(2,1)S(1)} %get-tuple-element.25.joined_ref.refs_0_), channel_id=1, source_target_pairs={{0,24},{4,28},{8,16},{12,20},{16,8},{20,12},{24,0},{28,4},{1,25},{... | collective-permute-start | bytes 294920 | tf_op jit(solution)/shard_map/ppermute | solution.py:38
  20.6 0.5 collective-permute-start.4
  21.1 0.0 collective-permute-done.refs_0_
  21.1 0.4 collective-permute-start.5
  21.5 0.0 collective-permute-done.1.refs_1_
  21.5 0.0 collective-permute-start.6
  21.5 0.0 collective-permute-done.2.refs_2_
  21.5 1.4 %shard_map.96 = (bf16[4,32,512]{2,1,0:T(8,128)(2,1)S(1)}, bf16[4,32,512]{2,1,0:T(8,128)(2,1)}) custom-call(bf16[4,512,512]{2,1,0:T(8,128)(2,1)S(1)} %get-tuple-element.24.l_ref, bf16[96,512]{1,0:T(8,128)(2,1)S(1)} %get-tuple-element.25.joined_ref.refs_0_, f32[4,8,512]{2,1,0:T(8,128)S(1)} %get-tuple-element.26.mask_ref, ...), custom_call_target="tpu_custom_call" | custom-call | flops 67108864 | bytes 2097152 | tf_op jit(solution)/shard_map/pallas_call | solution.py:325
  22.8 2.6 %collective-permute-start.10 = (bf16[4,32,512]{2,1,0:T(8,128)(2,1)S(1)}, bf16[4,32,512]{2,1,0:T(8,128)(2,1)S(1)}, u32[]{:S(2)}, u32[]{:S(2)}) collective-permute-start(bf16[4,32,512]{2,1,0:T(8,128)(2,1)S(1)} %get-tuple-element.36.refs_0_), channel_id=1, source_target_pairs={{0,24},{4,28},{8,16},{12,20},{16,8},{20,12},{24,0},{28,4},{1,25},{... | collective-permute-start | bytes 393224 | tf_op jit(solution)/shard_map/ppermute | solution.py:38
  25.4 0.0 collective-permute-done.3.refs_1_
  25.4 0.5 collective-permute-start.11
  25.9 0.0 collective-permute-done.4.refs_2_
  26.0 1.1 %collective-permute-start.12 = (bf16[4,32,512]{2,1,0:T(8,128)(2,1)S(1)}, bf16[4,32,512]{2,1,0:T(8,128)(2,1)S(1)}, u32[]{:S(2)}, u32[]{:S(2)}) collective-permute-start(bf16[4,32,512]{2,1,0:T(8,128)(2,1)S(1)} %get-tuple-element.36.refs_0_), channel_id=1, source_target_pairs={{0,8},{4,12},{8,0},{12,4},{16,24},{20,28},{24,16},{28,20},{1,9},{5... | collective-permute-start | bytes 393224 | tf_op jit(solution)/shard_map/ppermute | solution.py:38
  27.1 0.0 collective-permute-done.5.refs_3_
  27.1 0.0 collective-permute-start.7
  27.1 0.0 collective-permute-done.6.refs_4_
  27.1 0.5 collective-permute-start.8
  27.6 0.8 %collective-permute-done.7.refs_5_ = bf16[96,512]{1,0:T(8,128)(2,1)S(1)} collective-permute-done((bf16[96,512]{1,0:T(8,128)(2,1)S(1)}, bf16[96,512]{1,0:T(8,128)(2,1)S(1)}, u32[]{:S(2)}, u32[]{:S(2)}) %collective-permute-start.7) | collective-permute-done | bytes 98336 | tf_op jit(solution)/shard_map/ppermute | solution.py:38
  28.4 0.2 collective-permute-start.9
  28.5 0.0 collective-permute-done.8.refs_6_
  28.5 0.4 collective-permute-start.13
  28.9 0.9 %collective-permute-done.10.refs_1_ = bf16[4,32,512]{2,1,0:T(8,128)(2,1)S(1)} collective-permute-done((bf16[4,32,512]{2,1,0:T(8,128)(2,1)S(1)}, bf16[4,32,512]{2,1,0:T(8,128)(2,1)S(1)}, u32[]{:S(2)}, u32[]{:S(2)}) %collective-permute-start.10) | collective-permute-done | bytes 131104 | tf_op jit(solution)/shard_map/ppermute | solution.py:38
  29.8 0.0 collective-permute-start.14
  29.8 2.7 %collective-permute-done.11.refs_2_ = bf16[4,32,512]{2,1,0:T(8,128)(2,1)S(1)} collective-permute-done((bf16[4,32,512]{2,1,0:T(8,128)(2,1)S(1)}, bf16[4,32,512]{2,1,0:T(8,128)(2,1)S(1)}, u32[]{:S(2)}, u32[]{:S(2)}) %collective-permute-start.11) | collective-permute-done | bytes 131104 | tf_op jit(solution)/shard_map/ppermute | solution.py:38
  32.5 0.0 collective-permute-start.15
  32.5 0.2 collective-permute-done.12.refs_3_
  32.7 0.3 collective-permute-start.16
  33.0 0.0 collective-permute-done.9.refs_7_
  33.0 1.2 %shard_map.97 = (f32[320,512]{1,0:T(8,128)S(1)}, f32[320,512]{1,0:T(8,128)S(1)}) custom-call(bf16[4,512,512]{2,1,0:T(8,128)(2,1)S(1)} %get-tuple-element.24.l_ref, bf16[4,256,512]{2,1,0:T(8,128)(2,1)S(1)} %get-tuple-element.23.panel_ref, bf16[5,320,512]{2,1,0:T(8,128)(2,1)S(1)} %get-tuple-element.32.stacks_ref, ...), custom_call_target="tpu_custom_call" | custom-call | flops 503316480 | bytes 1048576 | tf_op jit(solution)/shard_map/pallas_call | solution.py:325
  34.2 0.0 collective-permute-done.13.refs_4_
  34.2 0.0 collective-permute-done.14.refs_5_
  34.2 0.0 collective-permute-done.15.refs_6_
  34.3 0.0 collective-permute-done.16.refs_7_
  34.3 0.0 copy-start.2
  34.3 1.6 %shard_map.98 = (bf16[8,16,512]{2,1,0:T(8,128)(2,1)S(1)}, bf16[8,16,512]{2,1,0:T(8,128)(2,1)S(1)}, bf16[8,16,512]{2,1,0:T(8,128)(2,1)S(1)}, bf16[8,16,512]{2,1,0:T(8,128)(2,1)S(1)}) custom-call(bf16[4,512,512]{2,1,0:T(8,128)(2,1)S(1)} %get-tuple-element.24.l_ref, bf16[4,256,512]{2,1,0:T(8,128)(2,1)S(1)} %get-tuple-element.23.panel_ref, ...), custom_call_target="tpu_custom_call" | custom-call | flops 671088640 | bytes 4194304 | tf_op jit(solution)/shard_map/pallas_call | solution.py:325
  35.8 3.8 %collective-permute-start.17 = (bf16[8,16,512]{2,1,0:T(8,128)(2,1)S(1)}, bf16[8,16,512]{2,1,0:T(8,128)(2,1)S(1)}, u32[]{:S(2)}, u32[]{:S(2)}) collective-permute-start(bf16[8,16,512]{2,1,0:T(8,128)(2,1)S(1)} %get-tuple-element.38), channel_id=1, source_target_pairs={{0,3},{1,2},{2,1},{3,0},{4,7},{5,6},{6,5},{7,4},{8,11},{9,10},{10,... | collective-permute-start | bytes 393224 | tf_op jit(solution)/shard_map/ppermute | solution.py:38
  39.7 0.0 collective-permute-start.18
  39.7 0.6 collective-permute-start.19
  40.3 3.8 %collective-permute-done.17.refs_0_ = bf16[8,16,512]{2,1,0:T(8,128)(2,1)S(1)} collective-permute-done((bf16[8,16,512]{2,1,0:T(8,128)(2,1)S(1)}, bf16[8,16,512]{2,1,0:T(8,128)(2,1)S(1)}, u32[]{:S(2)}, u32[]{:S(2)}) %collective-permute-start.17) | collective-permute-done | bytes 131104 | tf_op jit(solution)/shard_map/ppermute | solution.py:38
  44.1 6.5 %collective-permute-done.18.refs_1_ = bf16[8,16,512]{2,1,0:T(8,128)(2,1)S(1)} collective-permute-done((bf16[8,16,512]{2,1,0:T(8,128)(2,1)S(1)}, bf16[8,16,512]{2,1,0:T(8,128)(2,1)S(1)}, u32[]{:S(2)}, u32[]{:S(2)}) %collective-permute-start.18) | collective-permute-done | bytes 131104 | tf_op jit(solution)/shard_map/ppermute | solution.py:38
  50.7 0.0 collective-permute-done.19.refs_2_
  50.7 0.1 shard_map.99.refs_0_
  50.7 0.3 collective-permute-start.20
  51.0 2.8 %collective-permute-start.21 = (bf16[8,16,512]{2,1,0:T(8,128)(2,1)S(1)}, bf16[8,16,512]{2,1,0:T(8,128)(2,1)S(1)}, u32[]{:S(2)}, u32[]{:S(2)}) collective-permute-start(bf16[8,16,512]{2,1,0:T(8,128)(2,1)S(1)} %shard_map.99.refs_0_), channel_id=1, source_target_pairs={{0,2},{1,3},{2,0},{3,1},{4,6},{5,7},{6,4},{7,5},{8,10},{9,11},{10,... | collective-permute-start | bytes 393224 | tf_op jit(solution)/shard_map/ppermute | solution.py:38
  53.8 1.4 %collective-permute-start.22 = (bf16[8,16,512]{2,1,0:T(8,128)(2,1)S(1)}, bf16[8,16,512]{2,1,0:T(8,128)(2,1)S(1)}, u32[]{:S(2)}, u32[]{:S(2)}) collective-permute-start(bf16[8,16,512]{2,1,0:T(8,128)(2,1)S(1)} %shard_map.99.refs_0_), channel_id=1, source_target_pairs={{0,3},{1,2},{2,1},{3,0},{4,7},{5,6},{6,5},{7,4},{8,11},{9,10},{10,... | collective-permute-start | bytes 393224 | tf_op jit(solution)/shard_map/ppermute | solution.py:38
  55.2 2.1 %collective-permute-done.20.refs_1_ = bf16[8,16,512]{2,1,0:T(8,128)(2,1)S(1)} collective-permute-done((bf16[8,16,512]{2,1,0:T(8,128)(2,1)S(1)}, bf16[8,16,512]{2,1,0:T(8,128)(2,1)S(1)}, u32[]{:S(2)}, u32[]{:S(2)}) %collective-permute-start.20) | collective-permute-done | bytes 131104 | tf_op jit(solution)/shard_map/ppermute | solution.py:38
  57.3 6.2 %collective-permute-done.21.refs_2_ = bf16[8,16,512]{2,1,0:T(8,128)(2,1)S(1)} collective-permute-done((bf16[8,16,512]{2,1,0:T(8,128)(2,1)S(1)}, bf16[8,16,512]{2,1,0:T(8,128)(2,1)S(1)}, u32[]{:S(2)}, u32[]{:S(2)}) %collective-permute-start.21) | collective-permute-done | bytes 131104 | tf_op jit(solution)/shard_map/ppermute | solution.py:38
  63.5 0.0 collective-permute-done.22.refs_3_
  63.5 0.0 copy-done.2
  63.5 1.0 %shard_map.100 = (f32[4,64,512]{2,1,0:T(8,128)}, f32[4,64,512]{2,1,0:T(8,128)}) custom-call(f32[4,64,512]{2,1,0:T(8,128)S(1)} %copy-done.2, bf16[8,16,512]{2,1,0:T(8,128)(2,1)S(1)} %shard_map.99.refs_0_, bf16[8,16,512]{2,1,0:T(8,128)(2,1)S(1)} %collective-permute-done.20.refs_1_, bf16[8,16,512]{2,1,0:T(8,128)(2,1)S(1)} %collective-permute-done.21.refs_2_, ...), custom_call_target="tpu_custom_call" | custom-call | tf_op jit(solution)/shard_map/pallas_call | solution.py:325
  (5 shorter events, 0.0 us)
Async XLA Ops:
  0.6 1.2 %copy-start.3 = (bf16[4,1,8,32,512]{4,3,2,1,0:T(8,128)(2,1)S(1)}, bf16[4,1,8,32,512]{4,3,2,1,0:T(8,128)(2,1)}, u32[]{:S(2)}) copy-start(bf16[4,1,8,32,512]{4,3,2,1,0:T(8,128)(2,1)} %param.8) | copy-start | bytes 3145732
  1.9 0.8 %copy-start.5 = (bf16[4,1,32,256]{3,2,1,0:T(8,128)(2,1)S(1)}, bf16[4,1,32,256]{3,2,1,0:T(8,128)(2,1)}, u32[]{:S(2)}) copy-start(bf16[4,1,32,256]{3,2,1,0:T(8,128)(2,1)} %param.7) | copy-start | bytes 196612
  2.7 0.7 %copy-start.7 = (s32[4,32]{1,0:T(4,128)S(1)}, s32[4,32]{1,0:T(4,128)}, u32[]{:S(2)}) copy-start(s32[4,32]{1,0:T(4,128)} %pattern_any.1) | copy-start | bytes 1540
  5.3 15.8 %collective-permute-start = (bf16[4,32,512]{2,1,0:T(8,128)(2,1)S(1)}, bf16[4,32,512]{2,1,0:T(8,128)(2,1)S(1)}, u32[]{:S(2)}, u32[]{:S(2)}) collective-permute-start(bf16[4,32,512]{2,1,0:T(8,128)(2,1)S(1)} %get-tuple-element.28), channel_id=1, source_target_pairs={{0,3},{1,2},{2,1},{3,0},{4,7},{5,6},{6,5},{7,4},{8,11},{9,10},{10,... | collective-permute-start | bytes 393224 | tf_op jit(solution)/shard_map/ppermute | solution.py:38
  10.4 11.1 %collective-permute-start.1 = (bf16[4,32,512]{2,1,0:T(8,128)(2,1)S(1)}, bf16[4,32,512]{2,1,0:T(8,128)(2,1)S(1)}, u32[]{:S(2)}, u32[]{:S(2)}) collective-permute-start(bf16[4,32,512]{2,1,0:T(8,128)(2,1)S(1)} %get-tuple-element.29), channel_id=1, source_target_pairs={{0,2},{1,3},{2,0},{3,1},{4,6},{5,7},{6,4},{7,5},{8,10},{9,11},{10,... | collective-permute-start | bytes 393224 | tf_op jit(solution)/shard_map/ppermute | solution.py:38
  10.4 11.1 %collective-permute-start.2 = (bf16[4,32,512]{2,1,0:T(8,128)(2,1)S(1)}, bf16[4,32,512]{2,1,0:T(8,128)(2,1)S(1)}, u32[]{:S(2)}, u32[]{:S(2)}) collective-permute-start(bf16[4,32,512]{2,1,0:T(8,128)(2,1)S(1)} %get-tuple-element.30), channel_id=1, source_target_pairs={{0,1},{1,0},{2,3},{3,2},{4,5},{5,4},{6,7},{7,6},{8,9},{9,8},{10,11... | collective-permute-start | bytes 393224 | tf_op jit(solution)/shard_map/ppermute | solution.py:38
  11.0 1.6 %copy-start = (bf16[4,512,512]{2,1,0:T(8,128)(2,1)S(1)}, bf16[4,512,512]{2,1,0:T(8,128)(2,1)}, u32[]{:S(2)}) copy-start(bf16[4,512,512]{2,1,0:T(8,128)(2,1)} %l_any.1) | copy-start | bytes 6291460
  12.6 1.0 %copy-start.1 = (f32[4,64,512]{2,1,0:T(8,128)S(1)}, f32[4,64,512]{2,1,0:T(8,128)}, u32[]{:S(2)}) copy-start(f32[4,64,512]{2,1,0:T(8,128)} %diag_ref.1) | copy-start | bytes 1572868
  13.7 0.9 %copy-start.4 = (f32[64,512]{1,0:T(8,128)S(1)}, f32[64,512]{1,0:T(8,128)}, u32[]{:S(2)}) copy-start(f32[64,512]{1,0:T(8,128)} %top_any.1) | copy-start | bytes 393220
  14.6 0.8 %copy-start.6 = (bf16[1,1,32,512]{3,2,1,0:T(8,128)(2,1)S(1)}, bf16[1,1,32,512]{3,2,1,0:T(8,128)(2,1)}, u32[]{:S(2)}) copy-start(bf16[1,1,32,512]{3,2,1,0:T(8,128)(2,1)} %param.11) | copy-start | bytes 98308
  17.9 7.5 %collective-permute-start.3 = (bf16[96,512]{1,0:T(8,128)(2,1)S(1)}, bf16[96,512]{1,0:T(8,128)(2,1)S(1)}, u32[]{:S(2)}, u32[]{:S(2)}) collective-permute-start(bf16[96,512]{1,0:T(8,128)(2,1)S(1)} %get-tuple-element.25.joined_ref.refs_0_), channel_id=1, source_target_pairs={{0,24},{4,28},{8,16},{12,20},{16,8},{20,12},{24,0},{28,4},{1,25},{... | collective-permute-start | bytes 294920 | tf_op jit(solution)/shard_map/ppermute | solution.py:38
  20.6 5.4 %collective-permute-start.4 = (bf16[96,512]{1,0:T(8,128)(2,1)S(1)}, bf16[96,512]{1,0:T(8,128)(2,1)S(1)}, u32[]{:S(2)}, u32[]{:S(2)}) collective-permute-start(bf16[96,512]{1,0:T(8,128)(2,1)S(1)} %get-tuple-element.25.joined_ref.refs_0_), channel_id=1, source_target_pairs={{0,16},{4,20},{8,24},{12,28},{16,0},{20,4},{24,8},{28,12},{1,17},{... | collective-permute-start | bytes 294920 | tf_op jit(solution)/shard_map/ppermute | solution.py:38
  21.1 6.0 %collective-permute-start.5 = (bf16[96,512]{1,0:T(8,128)(2,1)S(1)}, bf16[96,512]{1,0:T(8,128)(2,1)S(1)}, u32[]{:S(2)}, u32[]{:S(2)}) collective-permute-start(bf16[96,512]{1,0:T(8,128)(2,1)S(1)} %get-tuple-element.25.joined_ref.refs_0_), channel_id=1, source_target_pairs={{0,8},{4,12},{8,0},{12,4},{16,24},{20,28},{24,16},{28,20},{1,9},{5... | collective-permute-start | bytes 294920 | tf_op jit(solution)/shard_map/ppermute | solution.py:38
  21.5 5.6 %collective-permute-start.6 = (bf16[96,512]{1,0:T(8,128)(2,1)S(1)}, bf16[96,512]{1,0:T(8,128)(2,1)S(1)}, u32[]{:S(2)}, u32[]{:S(2)}) collective-permute-start(bf16[96,512]{1,0:T(8,128)(2,1)S(1)} %get-tuple-element.25.joined_ref.refs_0_), channel_id=1, source_target_pairs={{0,4},{4,0},{8,12},{12,8},{16,20},{20,16},{24,28},{28,24},{1,5},{5... | collective-permute-start | bytes 294920 | tf_op jit(solution)/shard_map/ppermute | solution.py:38
  22.8 6.9 %collective-permute-start.10 = (bf16[4,32,512]{2,1,0:T(8,128)(2,1)S(1)}, bf16[4,32,512]{2,1,0:T(8,128)(2,1)S(1)}, u32[]{:S(2)}, u32[]{:S(2)}) collective-permute-start(bf16[4,32,512]{2,1,0:T(8,128)(2,1)S(1)} %get-tuple-element.36.refs_0_), channel_id=1, source_target_pairs={{0,24},{4,28},{8,16},{12,20},{16,8},{20,12},{24,0},{28,4},{1,25},{... | collective-permute-start | bytes 393224 | tf_op jit(solution)/shard_map/ppermute | solution.py:38
  25.4 7.0 %collective-permute-start.11 = (bf16[4,32,512]{2,1,0:T(8,128)(2,1)S(1)}, bf16[4,32,512]{2,1,0:T(8,128)(2,1)S(1)}, u32[]{:S(2)}, u32[]{:S(2)}) collective-permute-start(bf16[4,32,512]{2,1,0:T(8,128)(2,1)S(1)} %get-tuple-element.36.refs_0_), channel_id=1, source_target_pairs={{0,16},{4,20},{8,24},{12,28},{16,0},{20,4},{24,8},{28,12},{1,17},{... | collective-permute-start | bytes 393224 | tf_op jit(solution)/shard_map/ppermute | solution.py:38
  26.0 6.8 %collective-permute-start.12 = (bf16[4,32,512]{2,1,0:T(8,128)(2,1)S(1)}, bf16[4,32,512]{2,1,0:T(8,128)(2,1)S(1)}, u32[]{:S(2)}, u32[]{:S(2)}) collective-permute-start(bf16[4,32,512]{2,1,0:T(8,128)(2,1)S(1)} %get-tuple-element.36.refs_0_), channel_id=1, source_target_pairs={{0,8},{4,12},{8,0},{12,4},{16,24},{20,28},{24,16},{28,20},{1,9},{5... | collective-permute-start | bytes 393224 | tf_op jit(solution)/shard_map/ppermute | solution.py:38
  27.1 1.3 %collective-permute-start.7 = (bf16[96,512]{1,0:T(8,128)(2,1)S(1)}, bf16[96,512]{1,0:T(8,128)(2,1)S(1)}, u32[]{:S(2)}, u32[]{:S(2)}) collective-permute-start(bf16[96,512]{1,0:T(8,128)(2,1)S(1)} %collective-permute-done.3.refs_1_), channel_id=1, source_target_pairs={{0,4},{4,0},{8,12},{12,8},{16,20},{20,16},{24,28},{28,24},{1,5},{5... | collective-permute-start | bytes 294920 | tf_op jit(solution)/shard_map/ppermute | solution.py:38
  27.1 1.5 %collective-permute-start.8 = (bf16[96,512]{1,0:T(8,128)(2,1)S(1)}, bf16[96,512]{1,0:T(8,128)(2,1)S(1)}, u32[]{:S(2)}, u32[]{:S(2)}) collective-permute-start(bf16[96,512]{1,0:T(8,128)(2,1)S(1)} %collective-permute-done.4.refs_2_), channel_id=1, source_target_pairs={{0,4},{4,0},{8,12},{12,8},{16,20},{20,16},{24,28},{28,24},{1,5},{5... | collective-permute-start | bytes 294920 | tf_op jit(solution)/shard_map/ppermute | solution.py:38
  28.4 4.6 %collective-permute-start.9 = (bf16[96,512]{1,0:T(8,128)(2,1)S(1)}, bf16[96,512]{1,0:T(8,128)(2,1)S(1)}, u32[]{:S(2)}, u32[]{:S(2)}) collective-permute-start(bf16[96,512]{1,0:T(8,128)(2,1)S(1)} %collective-permute-done.5.refs_3_), channel_id=1, source_target_pairs={{0,4},{4,0},{8,12},{12,8},{16,20},{20,16},{24,28},{28,24},{1,5},{5... | collective-permute-start | bytes 294920 | tf_op jit(solution)/shard_map/ppermute | solution.py:38
  28.5 5.7 %collective-permute-start.13 = (bf16[4,32,512]{2,1,0:T(8,128)(2,1)S(1)}, bf16[4,32,512]{2,1,0:T(8,128)(2,1)S(1)}, u32[]{:S(2)}, u32[]{:S(2)}) collective-permute-start(bf16[4,32,512]{2,1,0:T(8,128)(2,1)S(1)} %get-tuple-element.36.refs_0_), channel_id=1, source_target_pairs={{0,4},{4,0},{8,12},{12,8},{16,20},{20,16},{24,28},{28,24},{1,5},{5... | collective-permute-start | bytes 393224 | tf_op jit(solution)/shard_map/ppermute | solution.py:38
  29.8 4.4 %collective-permute-start.14 = (bf16[4,32,512]{2,1,0:T(8,128)(2,1)S(1)}, bf16[4,32,512]{2,1,0:T(8,128)(2,1)S(1)}, u32[]{:S(2)}, u32[]{:S(2)}) collective-permute-start(bf16[4,32,512]{2,1,0:T(8,128)(2,1)S(1)} %collective-permute-done.10.refs_1_), channel_id=1, source_target_pairs={{0,4},{4,0},{8,12},{12,8},{16,20},{20,16},{24,28},{28,24},{1,5},{5... | collective-permute-start | bytes 393224 | tf_op jit(solution)/shard_map/ppermute | solution.py:38
  32.5 1.8 %collective-permute-start.15 = (bf16[4,32,512]{2,1,0:T(8,128)(2,1)S(1)}, bf16[4,32,512]{2,1,0:T(8,128)(2,1)S(1)}, u32[]{:S(2)}, u32[]{:S(2)}) collective-permute-start(bf16[4,32,512]{2,1,0:T(8,128)(2,1)S(1)} %collective-permute-done.11.refs_2_), channel_id=1, source_target_pairs={{0,4},{4,0},{8,12},{12,8},{16,20},{20,16},{24,28},{28,24},{1,5},{5... | collective-permute-start | bytes 393224 | tf_op jit(solution)/shard_map/ppermute | solution.py:38
  32.7 1.5 %collective-permute-start.16 = (bf16[4,32,512]{2,1,0:T(8,128)(2,1)S(1)}, bf16[4,32,512]{2,1,0:T(8,128)(2,1)S(1)}, u32[]{:S(2)}, u32[]{:S(2)}) collective-permute-start(bf16[4,32,512]{2,1,0:T(8,128)(2,1)S(1)} %collective-permute-done.12.refs_3_), channel_id=1, source_target_pairs={{0,4},{4,0},{8,12},{12,8},{16,20},{20,16},{24,28},{28,24},{1,5},{5... | collective-permute-start | bytes 393224 | tf_op jit(solution)/shard_map/ppermute | solution.py:38
  34.3 29.3 %copy-start.2 = (f32[4,64,512]{2,1,0:T(8,128)S(1)}, f32[4,64,512]{2,1,0:T(8,128)}, u32[]{:S(2)}) copy-start(f32[4,64,512]{2,1,0:T(8,128)} %diag_ref.1) | copy-start | bytes 1572868
  35.8 8.3 %collective-permute-start.17 = (bf16[8,16,512]{2,1,0:T(8,128)(2,1)S(1)}, bf16[8,16,512]{2,1,0:T(8,128)(2,1)S(1)}, u32[]{:S(2)}, u32[]{:S(2)}) collective-permute-start(bf16[8,16,512]{2,1,0:T(8,128)(2,1)S(1)} %get-tuple-element.38), channel_id=1, source_target_pairs={{0,3},{1,2},{2,1},{3,0},{4,7},{5,6},{6,5},{7,4},{8,11},{9,10},{10,... | collective-permute-start | bytes 393224 | tf_op jit(solution)/shard_map/ppermute | solution.py:38
  39.7 11.0 %collective-permute-start.18 = (bf16[8,16,512]{2,1,0:T(8,128)(2,1)S(1)}, bf16[8,16,512]{2,1,0:T(8,128)(2,1)S(1)}, u32[]{:S(2)}, u32[]{:S(2)}) collective-permute-start(bf16[8,16,512]{2,1,0:T(8,128)(2,1)S(1)} %get-tuple-element.39), channel_id=1, source_target_pairs={{0,2},{1,3},{2,0},{3,1},{4,6},{5,7},{6,4},{7,5},{8,10},{9,11},{10,... | collective-permute-start | bytes 393224 | tf_op jit(solution)/shard_map/ppermute | solution.py:38
  39.7 11.0 %collective-permute-start.19 = (bf16[8,16,512]{2,1,0:T(8,128)(2,1)S(1)}, bf16[8,16,512]{2,1,0:T(8,128)(2,1)S(1)}, u32[]{:S(2)}, u32[]{:S(2)}) collective-permute-start(bf16[8,16,512]{2,1,0:T(8,128)(2,1)S(1)} %get-tuple-element.40), channel_id=1, source_target_pairs={{0,1},{1,0},{2,3},{3,2},{4,5},{5,4},{6,7},{7,6},{8,9},{9,8},{10,11... | collective-permute-start | bytes 393224 | tf_op jit(solution)/shard_map/ppermute | solution.py:38
  50.7 6.6 %collective-permute-start.20 = (bf16[8,16,512]{2,1,0:T(8,128)(2,1)S(1)}, bf16[8,16,512]{2,1,0:T(8,128)(2,1)S(1)}, u32[]{:S(2)}, u32[]{:S(2)}) collective-permute-start(bf16[8,16,512]{2,1,0:T(8,128)(2,1)S(1)} %shard_map.99.refs_0_), channel_id=1, source_target_pairs={{0,1},{1,0},{2,3},{3,2},{4,5},{5,4},{6,7},{7,6},{8,9},{9,8},{10,11... | collective-permute-start | bytes 393224 | tf_op jit(solution)/shard_map/ppermute | solution.py:38
  51.0 12.5 %collective-permute-start.21 = (bf16[8,16,512]{2,1,0:T(8,128)(2,1)S(1)}, bf16[8,16,512]{2,1,0:T(8,128)(2,1)S(1)}, u32[]{:S(2)}, u32[]{:S(2)}) collective-permute-start(bf16[8,16,512]{2,1,0:T(8,128)(2,1)S(1)} %shard_map.99.refs_0_), channel_id=1, source_target_pairs={{0,2},{1,3},{2,0},{3,1},{4,6},{5,7},{6,4},{7,5},{8,10},{9,11},{10,... | collective-permute-start | bytes 393224 | tf_op jit(solution)/shard_map/ppermute | solution.py:38
  53.8 9.7 %collective-permute-start.22 = (bf16[8,16,512]{2,1,0:T(8,128)(2,1)S(1)}, bf16[8,16,512]{2,1,0:T(8,128)(2,1)S(1)}, u32[]{:S(2)}, u32[]{:S(2)}) collective-permute-start(bf16[8,16,512]{2,1,0:T(8,128)(2,1)S(1)} %shard_map.99.refs_0_), channel_id=1, source_target_pairs={{0,3},{1,2},{2,1},{3,0},{4,7},{5,6},{6,5},{7,4},{8,11},{9,10},{10,... | collective-permute-start | bytes 393224 | tf_op jit(solution)/shard_map/ppermute | solution.py:38

commit v4 on v3

--- a/solution.py
+++ b/solution.py
@@ -330,7 +330,7 @@
         scratch_shapes=scratch,
         compiler_params=pltpu.CompilerParams(vmem_limit_bytes=VMEM_BYTES),
         cost_estimate=pl.CostEstimate(flops=flops, bytes_accessed=moved, transcendentals=0),
-    )(*args)
+    )(*[pltpu.with_memory_space_constraint(a, pltpu.HBM) if i in away else a for i, a in enumerate(args)])
 
 
 def exchange_rows(x):

time: 65 us -> 61.7 us (0.949)
  local copies, waits for them, and re-layouts: 7.04 us -> 0.01 us
  waiting for transfers between devices: 23.3 us -> 26.1 us
  Pallas kernels: 9.73 us -> 11.5 us
    unnamed x16 -> x2, local copies, waits for them, and re-layouts: 7.04 us -> 0.01 us
    ppermute x23, waiting for transfers between devices: 23.3 us -> 26.1 us  [hop(): return lax.ppermute(x, axis, [(i, target(i, j, n)) for i in range(n)])]
    pallas_call x7, Pallas kernels: 9.73 us -> 11.5 us  [call(): pl.pallas_call(kernel, out_shape=tuple((jax.ShapeDtypeStruct(s, d) for s,...]
  transfers between devices with their start and end apart: 23 -> 23, of which waited for: 8 -> 9; matrix products, arithmetic and copies ran while one was open for 0% -> 0% of each run, Pallas kernels for 8% -> 10%
where the time goes in v4:
time: 61.7 us; the launch traced here: 61.6 us
  waiting for transfers between devices  26.1 us (42%)
  starting transfers between devices  23.2 us (38%)
  Pallas kernels  11.5 us (19%)
  between operations  0.73 us (1%)
    ppermute x23, waiting for transfers between devices, hop(): return lax.ppermute(x, axis, [(i, target(i, j, n)) for i in range(n)])  26.1 us
    ppermute x23, starting transfers between devices, hop(): return lax.ppermute(x, axis, [(i, target(i, j, n)) for i in range(n)])  23.2 us
    pallas_call x7, Pallas kernels, call(): pl.pallas_call(kernel, out_shape=tuple((jax.ShapeDtypeStruct(s, d) for s,...  11.5 us
  transfers between devices with their start and end apart: 23, of which 9 were waited for; matrix products, arithmetic and copies ran while one was open for 0% of the time, Pallas kernels for 10%

profile of v4, /device:TPU:0, one launch (start us, length us, event | category | flops | bytes accessed | tf_op | source)
XLA Modules:
  0.0 61.6 jit_solution(14483382755242152803)
XLA Ops:
  0.6 2.5 %shard_map.94 = (bf16[4,256,512]{2,1,0:T(8,128)(2,1)S(1)}, f32[4,8,512]{2,1,0:T(8,128)S(1)}, bf16[4,32,512]{2,1,0:T(8,128)(2,1)S(1)}, bf16[4,32,512]{2,1,0:T(8,1...) custom-call(bf16[4,32,256]{2,1,0:T(8,128)(2,1)} %bitcast.7, ...), custom_call_target="tpu_custom_call" | custom-call | flops 134217728 | bytes 2097152 | tf_op jit(solution)/shard_map/pallas_call | solution.py:325
  3.1 5.1 %collective-permute-start = (bf16[4,32,512]{2,1,0:T(8,128)(2,1)S(1)}, bf16[4,32,512]{2,1,0:T(8,128)(2,1)S(1)}, u32[]{:S(2)}, u32[]{:S(2)}) collective-permute-start(bf16[4,32,512]{2,1,0:T(8,128)(2,1)S(1)} %get-tuple-element.28), channel_id=1, source_target_pairs={{0,3},{1,2},{2,1},{3,0},{4,7},{5,6},{6,5},{7,4},{8,11},{9,10},{10,... | collective-permute-start | bytes 393224 | tf_op jit(solution)/shard_map/ppermute | solution.py:38
  8.2 0.0 collective-permute-start.1
  8.2 0.6 %collective-permute-start.2 = (bf16[4,32,512]{2,1,0:T(8,128)(2,1)S(1)}, bf16[4,32,512]{2,1,0:T(8,128)(2,1)S(1)}, u32[]{:S(2)}, u32[]{:S(2)}) collective-permute-start(bf16[4,32,512]{2,1,0:T(8,128)(2,1)S(1)} %get-tuple-element.30), channel_id=1, source_target_pairs={{0,1},{1,0},{2,3},{3,2},{4,5},{5,4},{6,7},{7,6},{8,9},{9,8},{10,11... | collective-permute-start | bytes 393224 | tf_op jit(solution)/shard_map/ppermute | solution.py:38
  8.9 3.8 %shard_map.95 = (bf16[4,512,512]{2,1,0:T(8,128)(2,1)S(1)}, bf16[5,320,512]{2,1,0:T(8,128)(2,1)S(1)}, bf16[640,256]{1,0:T(8,128)(2,1)S(1)}, bf16[96,512]{1,0:T(8,128)(2,1)S(1)}) custom-call(bf16[4,512,512]{2,1,0:T(8,128)(2,1)} %l_any.1, f32[4,64,512]{2,1,0:T(8,128)} %diag_ref.1, f32[64,512]{1,0:T(8,128)} %top_any.1, bf16[32,512]{1,0:T(8,128)(2,1)} %bitcast.8, ...), custom_call_target="tpu_custom_call" | custom-call | flops 402653184 | bytes 4194304 | tf_op jit(solution)/shard_map/pallas_call | solution.py:325
  12.7 2.6 %collective-permute-start.3 = (bf16[96,512]{1,0:T(8,128)(2,1)S(1)}, bf16[96,512]{1,0:T(8,128)(2,1)S(1)}, u32[]{:S(2)}, u32[]{:S(2)}) collective-permute-start(bf16[96,512]{1,0:T(8,128)(2,1)S(1)} %get-tuple-element.25.joined_ref.refs_0_), channel_id=1, source_target_pairs={{0,24},{4,28},{8,16},{12,20},{16,8},{20,12},{24,0},{28,4},{1,25},{... | collective-permute-start | bytes 294920 | tf_op jit(solution)/shard_map/ppermute | solution.py:38
  15.3 0.5 collective-permute-start.4
  15.8 0.0 collective-permute-done.refs_0_
  15.8 0.4 collective-permute-start.5
  16.2 3.1 %collective-permute-done.1.refs_1_ = bf16[4,32,512]{2,1,0:T(8,128)(2,1)S(1)} collective-permute-done((bf16[4,32,512]{2,1,0:T(8,128)(2,1)S(1)}, bf16[4,32,512]{2,1,0:T(8,128)(2,1)S(1)}, u32[]{:S(2)}, u32[]{:S(2)}) %collective-permute-start.1) | collective-permute-done | bytes 131104 | tf_op jit(solution)/shard_map/ppermute | solution.py:38
  19.3 0.0 collective-permute-start.6
  19.3 0.0 collective-permute-done.2.refs_2_
  19.3 1.4 %shard_map.96 = (bf16[4,32,512]{2,1,0:T(8,128)(2,1)S(1)}, bf16[4,32,512]{2,1,0:T(8,128)(2,1)}) custom-call(bf16[4,512,512]{2,1,0:T(8,128)(2,1)S(1)} %get-tuple-element.24.l_ref, bf16[96,512]{1,0:T(8,128)(2,1)S(1)} %get-tuple-element.25.joined_ref.refs_0_, f32[4,8,512]{2,1,0:T(8,128)S(1)} %get-tuple-element.26.mask_ref, ...), custom_call_target="tpu_custom_call" | custom-call | flops 67108864 | bytes 2097152 | tf_op jit(solution)/shard_map/pallas_call | solution.py:325
  20.7 2.4 %collective-permute-start.10 = (bf16[4,32,512]{2,1,0:T(8,128)(2,1)S(1)}, bf16[4,32,512]{2,1,0:T(8,128)(2,1)S(1)}, u32[]{:S(2)}, u32[]{:S(2)}) collective-permute-start(bf16[4,32,512]{2,1,0:T(8,128)(2,1)S(1)} %get-tuple-element.36.refs_0_), channel_id=1, source_target_pairs={{0,24},{4,28},{8,16},{12,20},{16,8},{20,12},{24,0},{28,4},{1,25},{... | collective-permute-start | bytes 393224 | tf_op jit(solution)/shard_map/ppermute | solution.py:38
  23.1 0.0 collective-permute-done.3.refs_1_
  23.1 0.5 collective-permute-start.11
  23.6 0.0 collective-permute-done.4.refs_2_
  23.6 0.5 collective-permute-start.12
  24.1 0.0 collective-permute-done.5.refs_3_
  24.2 0.0 collective-permute-start.7
  24.2 0.0 collective-permute-done.6.refs_4_
  24.2 0.5 collective-permute-start.8
  24.7 0.8 %collective-permute-done.7.refs_5_ = bf16[96,512]{1,0:T(8,128)(2,1)S(1)} collective-permute-done((bf16[96,512]{1,0:T(8,128)(2,1)S(1)}, bf16[96,512]{1,0:T(8,128)(2,1)S(1)}, u32[]{:S(2)}, u32[]{:S(2)}) %collective-permute-start.7) | collective-permute-done | bytes 98336 | tf_op jit(solution)/shard_map/ppermute | solution.py:38
  25.5 0.2 collective-permute-start.9
  25.6 0.0 collective-permute-done.8.refs_6_
  25.6 0.4 collective-permute-start.13
  26.0 1.8 %collective-permute-done.10.refs_1_ = bf16[4,32,512]{2,1,0:T(8,128)(2,1)S(1)} collective-permute-done((bf16[4,32,512]{2,1,0:T(8,128)(2,1)S(1)}, bf16[4,32,512]{2,1,0:T(8,128)(2,1)S(1)}, u32[]{:S(2)}, u32[]{:S(2)}) %collective-permute-start.10) | collective-permute-done | bytes 131104 | tf_op jit(solution)/shard_map/ppermute | solution.py:38
  27.7 0.0 collective-permute-start.14
  27.7 2.5 %collective-permute-done.11.refs_2_ = bf16[4,32,512]{2,1,0:T(8,128)(2,1)S(1)} collective-permute-done((bf16[4,32,512]{2,1,0:T(8,128)(2,1)S(1)}, bf16[4,32,512]{2,1,0:T(8,128)(2,1)S(1)}, u32[]{:S(2)}, u32[]{:S(2)}) %collective-permute-start.11) | collective-permute-done | bytes 131104 | tf_op jit(solution)/shard_map/ppermute | solution.py:38
  30.3 0.0 collective-permute-start.15
  30.3 0.1 collective-permute-done.12.refs_3_
  30.4 0.4 collective-permute-start.16
  30.8 0.0 collective-permute-done.9.refs_7_
  30.8 1.2 %shard_map.97 = (f32[320,512]{1,0:T(8,128)S(1)}, f32[320,512]{1,0:T(8,128)S(1)}) custom-call(bf16[4,512,512]{2,1,0:T(8,128)(2,1)S(1)} %get-tuple-element.24.l_ref, bf16[4,256,512]{2,1,0:T(8,128)(2,1)S(1)} %get-tuple-element.23.panel_ref, bf16[5,320,512]{2,1,0:T(8,128)(2,1)S(1)} %get-tuple-element.32.stacks_ref, ...), custom_call_target="tpu_custom_call" | custom-call | flops 503316480 | bytes 1048576 | tf_op jit(solution)/shard_map/pallas_call | solution.py:325
  32.0 0.0 collective-permute-done.13.refs_4_
  32.0 0.0 collective-permute-done.14.refs_5_
  32.1 0.0 collective-permute-done.15.refs_6_
  32.1 0.0 collective-permute-done.16.refs_7_
  32.1 0.0 copy-start
  32.1 1.6 %shard_map.98 = (bf16[8,16,512]{2,1,0:T(8,128)(2,1)S(1)}, bf16[8,16,512]{2,1,0:T(8,128)(2,1)S(1)}, bf16[8,16,512]{2,1,0:T(8,128)(2,1)S(1)}, bf16[8,16,512]{2,1,0:T(8,128)(2,1)S(1)}) custom-call(bf16[4,512,512]{2,1,0:T(8,128)(2,1)S(1)} %get-tuple-element.24.l_ref, bf16[4,256,512]{2,1,0:T(8,128)(2,1)S(1)} %get-tuple-element.23.panel_ref, ...), custom_call_target="tpu_custom_call" | custom-call | flops 671088640 | bytes 4194304 | tf_op jit(solution)/shard_map/pallas_call | solution.py:325
  33.7 2.5 %collective-permute-start.17 = (bf16[8,16,512]{2,1,0:T(8,128)(2,1)S(1)}, bf16[8,16,512]{2,1,0:T(8,128)(2,1)S(1)}, u32[]{:S(2)}, u32[]{:S(2)}) collective-permute-start(bf16[8,16,512]{2,1,0:T(8,128)(2,1)S(1)} %get-tuple-element.38), channel_id=1, source_target_pairs={{0,3},{1,2},{2,1},{3,0},{4,7},{5,6},{6,5},{7,4},{8,11},{9,10},{10,... | collective-permute-start | bytes 393224 | tf_op jit(solution)/shard_map/ppermute | solution.py:38
  36.2 0.0 collective-permute-start.18
  36.2 1.9 %collective-permute-start.19 = (bf16[8,16,512]{2,1,0:T(8,128)(2,1)S(1)}, bf16[8,16,512]{2,1,0:T(8,128)(2,1)S(1)}, u32[]{:S(2)}, u32[]{:S(2)}) collective-permute-start(bf16[8,16,512]{2,1,0:T(8,128)(2,1)S(1)} %get-tuple-element.40), channel_id=1, source_target_pairs={{0,1},{1,0},{2,3},{3,2},{4,5},{5,4},{6,7},{7,6},{8,9},{9,8},{10,11... | collective-permute-start | bytes 393224 | tf_op jit(solution)/shard_map/ppermute | solution.py:38
  38.1 3.9 %collective-permute-done.17.refs_0_ = bf16[8,16,512]{2,1,0:T(8,128)(2,1)S(1)} collective-permute-done((bf16[8,16,512]{2,1,0:T(8,128)(2,1)S(1)}, bf16[8,16,512]{2,1,0:T(8,128)(2,1)S(1)}, u32[]{:S(2)}, u32[]{:S(2)}) %collective-permute-start.17) | collective-permute-done | bytes 131104 | tf_op jit(solution)/shard_map/ppermute | solution.py:38
  42.0 5.3 %collective-permute-done.18.refs_1_ = bf16[8,16,512]{2,1,0:T(8,128)(2,1)S(1)} collective-permute-done((bf16[8,16,512]{2,1,0:T(8,128)(2,1)S(1)}, bf16[8,16,512]{2,1,0:T(8,128)(2,1)S(1)}, u32[]{:S(2)}, u32[]{:S(2)}) %collective-permute-start.18) | collective-permute-done | bytes 131104 | tf_op jit(solution)/shard_map/ppermute | solution.py:38
  47.3 0.0 collective-permute-done.19.refs_2_
  47.3 0.1 shard_map.99.refs_0_
  47.4 0.1 collective-permute-start.20
  47.5 3.1 %collective-permute-start.21 = (bf16[8,16,512]{2,1,0:T(8,128)(2,1)S(1)}, bf16[8,16,512]{2,1,0:T(8,128)(2,1)S(1)}, u32[]{:S(2)}, u32[]{:S(2)}) collective-permute-start(bf16[8,16,512]{2,1,0:T(8,128)(2,1)S(1)} %shard_map.99.refs_0_), channel_id=1, source_target_pairs={{0,2},{1,3},{2,0},{3,1},{4,6},{5,7},{6,4},{7,5},{8,10},{9,11},{10,... | collective-permute-start | bytes 393224 | tf_op jit(solution)/shard_map/ppermute | solution.py:38
  50.7 1.2 %collective-permute-start.22 = (bf16[8,16,512]{2,1,0:T(8,128)(2,1)S(1)}, bf16[8,16,512]{2,1,0:T(8,128)(2,1)S(1)}, u32[]{:S(2)}, u32[]{:S(2)}) collective-permute-start(bf16[8,16,512]{2,1,0:T(8,128)(2,1)S(1)} %shard_map.99.refs_0_), channel_id=1, source_target_pairs={{0,3},{1,2},{2,1},{3,0},{4,7},{5,6},{6,5},{7,4},{8,11},{9,10},{10,... | collective-permute-start | bytes 393224 | tf_op jit(solution)/shard_map/ppermute | solution.py:38
  51.9 2.5 %collective-permute-done.20.refs_1_ = bf16[8,16,512]{2,1,0:T(8,128)(2,1)S(1)} collective-permute-done((bf16[8,16,512]{2,1,0:T(8,128)(2,1)S(1)}, bf16[8,16,512]{2,1,0:T(8,128)(2,1)S(1)}, u32[]{:S(2)}, u32[]{:S(2)}) %collective-permute-start.20) | collective-permute-done | bytes 131104 | tf_op jit(solution)/shard_map/ppermute | solution.py:38
  54.4 6.1 %collective-permute-done.21.refs_2_ = bf16[8,16,512]{2,1,0:T(8,128)(2,1)S(1)} collective-permute-done((bf16[8,16,512]{2,1,0:T(8,128)(2,1)S(1)}, bf16[8,16,512]{2,1,0:T(8,128)(2,1)S(1)}, u32[]{:S(2)}, u32[]{:S(2)}) %collective-permute-start.21) | collective-permute-done | bytes 131104 | tf_op jit(solution)/shard_map/ppermute | solution.py:38
  60.5 0.0 collective-permute-done.22.refs_3_
  60.5 0.0 copy-done
  60.5 1.0 %shard_map.100 = (f32[4,64,512]{2,1,0:T(8,128)}, f32[4,64,512]{2,1,0:T(8,128)}) custom-call(f32[4,64,512]{2,1,0:T(8,128)S(1)} %copy-done, bf16[8,16,512]{2,1,0:T(8,128)(2,1)S(1)} %shard_map.99.refs_0_, bf16[8,16,512]{2,1,0:T(8,128)(2,1)S(1)} %collective-permute-done.20.refs_1_, bf16[8,16,512]{2,1,0:T(8,128)(2,1)S(1)} %collective-permute-done.21.refs_2_, ...), custom_call_target="tpu_custom_call" | custom-call | tf_op jit(solution)/shard_map/pallas_call | solution.py:325
Async XLA Ops:
  3.1 12.7 %collective-permute-start = (bf16[4,32,512]{2,1,0:T(8,128)(2,1)S(1)}, bf16[4,32,512]{2,1,0:T(8,128)(2,1)S(1)}, u32[]{:S(2)}, u32[]{:S(2)}) collective-permute-start(bf16[4,32,512]{2,1,0:T(8,128)(2,1)S(1)} %get-tuple-element.28), channel_id=1, source_target_pairs={{0,3},{1,2},{2,1},{3,0},{4,7},{5,6},{6,5},{7,4},{8,11},{9,10},{10,... | collective-permute-start | bytes 393224 | tf_op jit(solution)/shard_map/ppermute | solution.py:38
  8.2 11.1 %collective-permute-start.1 = (bf16[4,32,512]{2,1,0:T(8,128)(2,1)S(1)}, bf16[4,32,512]{2,1,0:T(8,128)(2,1)S(1)}, u32[]{:S(2)}, u32[]{:S(2)}) collective-permute-start(bf16[4,32,512]{2,1,0:T(8,128)(2,1)S(1)} %get-tuple-element.29), channel_id=1, source_target_pairs={{0,2},{1,3},{2,0},{3,1},{4,6},{5,7},{6,4},{7,5},{8,10},{9,11},{10,... | collective-permute-start | bytes 393224 | tf_op jit(solution)/shard_map/ppermute | solution.py:38
  8.2 11.1 %collective-permute-start.2 = (bf16[4,32,512]{2,1,0:T(8,128)(2,1)S(1)}, bf16[4,32,512]{2,1,0:T(8,128)(2,1)S(1)}, u32[]{:S(2)}, u32[]{:S(2)}) collective-permute-start(bf16[4,32,512]{2,1,0:T(8,128)(2,1)S(1)} %get-tuple-element.30), channel_id=1, source_target_pairs={{0,1},{1,0},{2,3},{3,2},{4,5},{5,4},{6,7},{7,6},{8,9},{9,8},{10,11... | collective-permute-start | bytes 393224 | tf_op jit(solution)/shard_map/ppermute | solution.py:38
  12.7 10.4 %collective-permute-start.3 = (bf16[96,512]{1,0:T(8,128)(2,1)S(1)}, bf16[96,512]{1,0:T(8,128)(2,1)S(1)}, u32[]{:S(2)}, u32[]{:S(2)}) collective-permute-start(bf16[96,512]{1,0:T(8,128)(2,1)S(1)} %get-tuple-element.25.joined_ref.refs_0_), channel_id=1, source_target_pairs={{0,24},{4,28},{8,16},{12,20},{16,8},{20,12},{24,0},{28,4},{1,25},{... | collective-permute-start | bytes 294920 | tf_op jit(solution)/shard_map/ppermute | solution.py:38
  15.3 8.3 %collective-permute-start.4 = (bf16[96,512]{1,0:T(8,128)(2,1)S(1)}, bf16[96,512]{1,0:T(8,128)(2,1)S(1)}, u32[]{:S(2)}, u32[]{:S(2)}) collective-permute-start(bf16[96,512]{1,0:T(8,128)(2,1)S(1)} %get-tuple-element.25.joined_ref.refs_0_), channel_id=1, source_target_pairs={{0,16},{4,20},{8,24},{12,28},{16,0},{20,4},{24,8},{28,12},{1,17},{... | collective-permute-start | bytes 294920 | tf_op jit(solution)/shard_map/ppermute | solution.py:38
  15.8 8.3 %collective-permute-start.5 = (bf16[96,512]{1,0:T(8,128)(2,1)S(1)}, bf16[96,512]{1,0:T(8,128)(2,1)S(1)}, u32[]{:S(2)}, u32[]{:S(2)}) collective-permute-start(bf16[96,512]{1,0:T(8,128)(2,1)S(1)} %get-tuple-element.25.joined_ref.refs_0_), channel_id=1, source_target_pairs={{0,8},{4,12},{8,0},{12,4},{16,24},{20,28},{24,16},{28,20},{1,9},{5... | collective-permute-start | bytes 294920 | tf_op jit(solution)/shard_map/ppermute | solution.py:38
  19.3 4.9 %collective-permute-start.6 = (bf16[96,512]{1,0:T(8,128)(2,1)S(1)}, bf16[96,512]{1,0:T(8,128)(2,1)S(1)}, u32[]{:S(2)}, u32[]{:S(2)}) collective-permute-start(bf16[96,512]{1,0:T(8,128)(2,1)S(1)} %get-tuple-element.25.joined_ref.refs_0_), channel_id=1, source_target_pairs={{0,4},{4,0},{8,12},{12,8},{16,20},{20,16},{24,28},{28,24},{1,5},{5... | collective-permute-start | bytes 294920 | tf_op jit(solution)/shard_map/ppermute | solution.py:38
  20.7 7.1 %collective-permute-start.10 = (bf16[4,32,512]{2,1,0:T(8,128)(2,1)S(1)}, bf16[4,32,512]{2,1,0:T(8,128)(2,1)S(1)}, u32[]{:S(2)}, u32[]{:S(2)}) collective-permute-start(bf16[4,32,512]{2,1,0:T(8,128)(2,1)S(1)} %get-tuple-element.36.refs_0_), channel_id=1, source_target_pairs={{0,24},{4,28},{8,16},{12,20},{16,8},{20,12},{24,0},{28,4},{1,25},{... | collective-permute-start | bytes 393224 | tf_op jit(solution)/shard_map/ppermute | solution.py:38
  23.1 7.2 %collective-permute-start.11 = (bf16[4,32,512]{2,1,0:T(8,128)(2,1)S(1)}, bf16[4,32,512]{2,1,0:T(8,128)(2,1)S(1)}, u32[]{:S(2)}, u32[]{:S(2)}) collective-permute-start(bf16[4,32,512]{2,1,0:T(8,128)(2,1)S(1)} %get-tuple-element.36.refs_0_), channel_id=1, source_target_pairs={{0,16},{4,20},{8,24},{12,28},{16,0},{20,4},{24,8},{28,12},{1,17},{... | collective-permute-start | bytes 393224 | tf_op jit(solution)/shard_map/ppermute | solution.py:38
  23.6 6.8 %collective-permute-start.12 = (bf16[4,32,512]{2,1,0:T(8,128)(2,1)S(1)}, bf16[4,32,512]{2,1,0:T(8,128)(2,1)S(1)}, u32[]{:S(2)}, u32[]{:S(2)}) collective-permute-start(bf16[4,32,512]{2,1,0:T(8,128)(2,1)S(1)} %get-tuple-element.36.refs_0_), channel_id=1, source_target_pairs={{0,8},{4,12},{8,0},{12,4},{16,24},{20,28},{24,16},{28,20},{1,9},{5... | collective-permute-start | bytes 393224 | tf_op jit(solution)/shard_map/ppermute | solution.py:38
  24.2 1.3 %collective-permute-start.7 = (bf16[96,512]{1,0:T(8,128)(2,1)S(1)}, bf16[96,512]{1,0:T(8,128)(2,1)S(1)}, u32[]{:S(2)}, u32[]{:S(2)}) collective-permute-start(bf16[96,512]{1,0:T(8,128)(2,1)S(1)} %collective-permute-done.3.refs_1_), channel_id=1, source_target_pairs={{0,4},{4,0},{8,12},{12,8},{16,20},{20,16},{24,28},{28,24},{1,5},{5... | collective-permute-start | bytes 294920 | tf_op jit(solution)/shard_map/ppermute | solution.py:38
  24.2 1.5 %collective-permute-start.8 = (bf16[96,512]{1,0:T(8,128)(2,1)S(1)}, bf16[96,512]{1,0:T(8,128)(2,1)S(1)}, u32[]{:S(2)}, u32[]{:S(2)}) collective-permute-start(bf16[96,512]{1,0:T(8,128)(2,1)S(1)} %collective-permute-done.4.refs_2_), channel_id=1, source_target_pairs={{0,4},{4,0},{8,12},{12,8},{16,20},{20,16},{24,28},{28,24},{1,5},{5... | collective-permute-start | bytes 294920 | tf_op jit(solution)/shard_map/ppermute | solution.py:38
  25.5 5.3 %collective-permute-start.9 = (bf16[96,512]{1,0:T(8,128)(2,1)S(1)}, bf16[96,512]{1,0:T(8,128)(2,1)S(1)}, u32[]{:S(2)}, u32[]{:S(2)}) collective-permute-start(bf16[96,512]{1,0:T(8,128)(2,1)S(1)} %collective-permute-done.5.refs_3_), channel_id=1, source_target_pairs={{0,4},{4,0},{8,12},{12,8},{16,20},{20,16},{24,28},{28,24},{1,5},{5... | collective-permute-start | bytes 294920 | tf_op jit(solution)/shard_map/ppermute | solution.py:38
  25.6 6.4 %collective-permute-start.13 = (bf16[4,32,512]{2,1,0:T(8,128)(2,1)S(1)}, bf16[4,32,512]{2,1,0:T(8,128)(2,1)S(1)}, u32[]{:S(2)}, u32[]{:S(2)}) collective-permute-start(bf16[4,32,512]{2,1,0:T(8,128)(2,1)S(1)} %get-tuple-element.36.refs_0_), channel_id=1, source_target_pairs={{0,4},{4,0},{8,12},{12,8},{16,20},{20,16},{24,28},{28,24},{1,5},{5... | collective-permute-start | bytes 393224 | tf_op jit(solution)/shard_map/ppermute | solution.py:38
  27.7 4.3 %collective-permute-start.14 = (bf16[4,32,512]{2,1,0:T(8,128)(2,1)S(1)}, bf16[4,32,512]{2,1,0:T(8,128)(2,1)S(1)}, u32[]{:S(2)}, u32[]{:S(2)}) collective-permute-start(bf16[4,32,512]{2,1,0:T(8,128)(2,1)S(1)} %collective-permute-done.10.refs_1_), channel_id=1, source_target_pairs={{0,4},{4,0},{8,12},{12,8},{16,20},{20,16},{24,28},{28,24},{1,5},{5... | collective-permute-start | bytes 393224 | tf_op jit(solution)/shard_map/ppermute | solution.py:38
  30.3 1.8 %collective-permute-start.15 = (bf16[4,32,512]{2,1,0:T(8,128)(2,1)S(1)}, bf16[4,32,512]{2,1,0:T(8,128)(2,1)S(1)}, u32[]{:S(2)}, u32[]{:S(2)}) collective-permute-start(bf16[4,32,512]{2,1,0:T(8,128)(2,1)S(1)} %collective-permute-done.11.refs_2_), channel_id=1, source_target_pairs={{0,4},{4,0},{8,12},{12,8},{16,20},{20,16},{24,28},{28,24},{1,5},{5... | collective-permute-start | bytes 393224 | tf_op jit(solution)/shard_map/ppermute | solution.py:38
  30.4 1.7 %collective-permute-start.16 = (bf16[4,32,512]{2,1,0:T(8,128)(2,1)S(1)}, bf16[4,32,512]{2,1,0:T(8,128)(2,1)S(1)}, u32[]{:S(2)}, u32[]{:S(2)}) collective-permute-start(bf16[4,32,512]{2,1,0:T(8,128)(2,1)S(1)} %collective-permute-done.12.refs_3_), channel_id=1, source_target_pairs={{0,4},{4,0},{8,12},{12,8},{16,20},{20,16},{24,28},{28,24},{1,5},{5... | collective-permute-start | bytes 393224 | tf_op jit(solution)/shard_map/ppermute | solution.py:38
  32.1 28.4 %copy-start = (f32[4,64,512]{2,1,0:T(8,128)S(1)}, f32[4,64,512]{2,1,0:T(8,128)}, u32[]{:S(2)}) copy-start(f32[4,64,512]{2,1,0:T(8,128)} %diag_ref.1) | copy-start | bytes 1572868
  33.7 8.3 %collective-permute-start.17 = (bf16[8,16,512]{2,1,0:T(8,128)(2,1)S(1)}, bf16[8,16,512]{2,1,0:T(8,128)(2,1)S(1)}, u32[]{:S(2)}, u32[]{:S(2)}) collective-permute-start(bf16[8,16,512]{2,1,0:T(8,128)(2,1)S(1)} %get-tuple-element.38), channel_id=1, source_target_pairs={{0,3},{1,2},{2,1},{3,0},{4,7},{5,6},{6,5},{7,4},{8,11},{9,10},{10,... | collective-permute-start | bytes 393224 | tf_op jit(solution)/shard_map/ppermute | solution.py:38
  36.2 11.1 %collective-permute-start.18 = (bf16[8,16,512]{2,1,0:T(8,128)(2,1)S(1)}, bf16[8,16,512]{2,1,0:T(8,128)(2,1)S(1)}, u32[]{:S(2)}, u32[]{:S(2)}) collective-permute-start(bf16[8,16,512]{2,1,0:T(8,128)(2,1)S(1)} %get-tuple-element.39), channel_id=1, source_target_pairs={{0,2},{1,3},{2,0},{3,1},{4,6},{5,7},{6,4},{7,5},{8,10},{9,11},{10,... | collective-permute-start | bytes 393224 | tf_op jit(solution)/shard_map/ppermute | solution.py:38
  36.2 11.1 %collective-permute-start.19 = (bf16[8,16,512]{2,1,0:T(8,128)(2,1)S(1)}, bf16[8,16,512]{2,1,0:T(8,128)(2,1)S(1)}, u32[]{:S(2)}, u32[]{:S(2)}) collective-permute-start(bf16[8,16,512]{2,1,0:T(8,128)(2,1)S(1)} %get-tuple-element.40), channel_id=1, source_target_pairs={{0,1},{1,0},{2,3},{3,2},{4,5},{5,4},{6,7},{7,6},{8,9},{9,8},{10,11... | collective-permute-start | bytes 393224 | tf_op jit(solution)/shard_map/ppermute | solution.py:38
  47.4 7.0 %collective-permute-start.20 = (bf16[8,16,512]{2,1,0:T(8,128)(2,1)S(1)}, bf16[8,16,512]{2,1,0:T(8,128)(2,1)S(1)}, u32[]{:S(2)}, u32[]{:S(2)}) collective-permute-start(bf16[8,16,512]{2,1,0:T(8,128)(2,1)S(1)} %shard_map.99.refs_0_), channel_id=1, source_target_pairs={{0,1},{1,0},{2,3},{3,2},{4,5},{5,4},{6,7},{7,6},{8,9},{9,8},{10,11... | collective-permute-start | bytes 393224 | tf_op jit(solution)/shard_map/ppermute | solution.py:38
  47.5 13.0 %collective-permute-start.21 = (bf16[8,16,512]{2,1,0:T(8,128)(2,1)S(1)}, bf16[8,16,512]{2,1,0:T(8,128)(2,1)S(1)}, u32[]{:S(2)}, u32[]{:S(2)}) collective-permute-start(bf16[8,16,512]{2,1,0:T(8,128)(2,1)S(1)} %shard_map.99.refs_0_), channel_id=1, source_target_pairs={{0,2},{1,3},{2,0},{3,1},{4,6},{5,7},{6,4},{7,5},{8,10},{9,11},{10,... | collective-permute-start | bytes 393224 | tf_op jit(solution)/shard_map/ppermute | solution.py:38
  50.7 9.8 %collective-permute-start.22 = (bf16[8,16,512]{2,1,0:T(8,128)(2,1)S(1)}, bf16[8,16,512]{2,1,0:T(8,128)(2,1)S(1)}, u32[]{:S(2)}, u32[]{:S(2)}) collective-permute-start(bf16[8,16,512]{2,1,0:T(8,128)(2,1)S(1)} %shard_map.99.refs_0_), channel_id=1, source_target_pairs={{0,3},{1,2},{2,1},{3,0},{4,7},{5,6},{6,5},{7,4},{8,11},{9,10},{10,... | collective-permute-start | bytes 393224 | tf_op jit(solution)/shard_map/ppermute | solution.py:38

commit v5 on v4

--- a/solution.py
+++ b/solution.py
@@ -11,6 +11,7 @@
 F32 = jnp.float32
 ROW_ORDER = (0, 6, 4, 2, 1, 7, 5, 3)
 VMEM_BYTES = 32 << 20
+AG_ORDER = (1, 2, 3)
 
 
 def dot(a, b):
@@ -168,19 +169,20 @@
     col, row = lax.axis_index("cols"), lax.axis_index("rows")
     supers, _, piece, _ = m_ref.shape
     pattern_copy = fetch(pattern_any, pattern_ref, sems.at[0])
+    g_copies = [fetch(g_any.at[col ^ j], g_ref.at[pl.ds(j * piece, piece)], sems.at[1 + supers + j]) for j in range(n_cols)]
     panel_copies = [fetch(m_any.at[k], m_ref.at[k], sems.at[1 + k]) for k in range(supers)]
-    g_copy = fetch(g_any, g_ref, sems.at[1 + supers])
     pattern_copy.wait()
+    for copy in g_copies:
+        copy.wait()
     for k in range(supers):
         mask_ref[k] = jnp.full(mask_ref.shape[1:], pattern_ref[k, col * n_rows + row].astype(F32))
         panel_copies[k].wait()
-        if k == 0:
-            g_copy.wait()
         for r in range(n_rows):
-            on = pattern_ref[k, col * n_rows + r].astype(F32)
-            panel_ref[k, pl.ds(r * piece, piece)] = (m_ref[k, r].astype(F32) * on).astype(BF)
+            on = pattern_ref[k, col * n_rows + r] != 0
+            panel_ref[k, pl.ds(r * piece, piece)] = jnp.where(on, m_ref[k, r], jnp.zeros_like(m_ref[k, r]))
+        product = dot(g_ref[...], panel_ref[k]).astype(BF)
         for j, out in enumerate(piece_refs):
-            out[k] = dot(g_ref[col ^ j], panel_ref[k]).astype(BF)
+            out[k] = product[j * piece : (j + 1) * piece]
 
 
 def chain_kernel(l_ref, joined_ref, mask_ref, own_ref, *refs):
@@ -265,38 +267,39 @@
     ahead_ref[...] = dot(first, l_ref[supers - 1]) + dot(across, panel_ref[supers - 1])
 
 
-def rows_kernel(n_cols, n_rows, order, l_ref, panel_ref, stacks_ref, reach_ref, begin_ref, ahead_ref, *refs):
-    got = refs[: len(order)]
-    pieces = refs[len(order) : len(order) + n_cols]
-    y_ref, done_ref = refs[len(order) + n_cols :]
+def rows_kernel(n_cols, n_rows, order, levels, last, l_ref, panel_ref, stacks_ref, reach_ref, begin_ref, from_ref, *refs):
+    got, refs = refs[: len(order)], refs[len(order) :]
+    pieces, refs = refs[:n_cols], refs[n_cols:]
+    *acc_refs, y_ref, done_ref = refs
     supers, width, _ = l_ref.shape
     share = width // n_rows
     piece = y_ref.shape[1] // n_rows
     part = share // n_cols
     col = lax.axis_index("cols")
+    top = levels[0] == supers - 1
 
     def write(at, ref):
-        for k in range(supers):
+        for k in range(levels[-1], levels[0] + (1 if top else 2)):
             y_ref[k, pl.ds(pl.multiple_of(at * piece, piece), piece)] = ref[k]
 
     place(got, order, write)
-    full = ahead_ref[...]
-    reach_at = sum((k + 1) * share for k in range(supers))
-    for k in reversed(range(supers)):
+    acc = from_ref[...]
+    for i, k in enumerate(levels):
         here = (k + 1) * share
-        if k < supers - 1:
+        if k == supers - 1:
+            full = acc
+        else:
             across = dot_nt(stacks_ref[k + 1, pl.ds(0, here + share)], y_ref[k + 1]).astype(BF)
             full = dot(acc.astype(BF), l_ref[k]) + dot(across, panel_ref[k])
-        reach_at -= here
-        acc = full[:here] - dot(reach_ref[pl.ds(reach_at, here)], y_ref[k])
-        done_ref[supers + k] = -full[here:]
-        done_ref[k] = acc[k * share :]
+        acc = full[:here] - dot(reach_ref[pl.ds(sum((j + 1) * share for j in range(k)), here)], y_ref[k])
+        done_ref[2 * i] = acc[k * share :].astype(BF)
+        done_ref[2 * i + 1] = (-full[here:]).astype(BF)
         if k:
             acc = acc + jnp.where(col == supers - k, begin_ref[pl.ds(0, here)], 0.0)
+    if not last:
+        acc_refs[0][...] = acc
     for j, out in enumerate(pieces):
-        at = pl.multiple_of((col ^ j) * part, part)
-        for i in range(2 * supers):
-            out[i] = done_ref[i, pl.ds(at, part)].astype(BF)
+        out[...] = done_ref[:, pl.ds(pl.multiple_of((col ^ j) * part, part), part)]
 
 
 def sum_kernel(own_ref, *refs):
@@ -308,25 +311,31 @@
         out_ref[i] = total.astype(BF)
 
 
-def last_kernel(n_cols, diag_ref, *refs):
-    *got_refs, diag_out, sub_out = refs
-    supers = diag_ref.shape[0]
+def last_kernel(n_cols, offsets, levels, diag_ref, *refs):
+    got_refs = refs[:n_cols]
+    diag_out, sub_out, done_ref, sems = refs[-4:]
     part = got_refs[0].shape[1]
     col = lax.axis_index("cols")
-    for j, got in enumerate(got_refs):
-        rows = pl.ds(pl.multiple_of((col ^ j) * part, part), part)
-        for k in range(supers):
-            diag_out[k, rows] = diag_ref[k, rows] + got[k].astype(F32)
-            sub_out[k, rows] = got[supers + k].astype(F32)
-
-
-def call(kernel, outs, *args, scratch=(), away=(), flops=0, moved=0):
+    copies = []
+    for i, k in enumerate(levels):
+        for j, got in zip(offsets, got_refs):
+            rows = pl.ds(pl.multiple_of((col ^ j) * part, part), part)
+            done_ref[2 * i, rows] = diag_ref[k, rows] + got[2 * i].astype(F32)
+            done_ref[2 * i + 1, rows] = got[2 * i + 1].astype(F32)
+        copies.append(fetch(done_ref.at[2 * i], diag_out.at[k], sems.at[2 * i]))
+        copies.append(fetch(done_ref.at[2 * i + 1], sub_out.at[k], sems.at[2 * i + 1]))
+    for copy in copies:
+        copy.wait()
+
+
+def call(kernel, outs, *args, scratch=(), away=(), out_away=False, aliases=None, flops=0, moved=0):
     vmem, hbm = pl.BlockSpec(memory_space=pltpu.VMEM), pl.BlockSpec(memory_space=pltpu.HBM)
     return pl.pallas_call(
         kernel,
         out_shape=tuple(jax.ShapeDtypeStruct(s, d) for s, d in outs),
         in_specs=[hbm if i in away else vmem for i in range(len(args))],
-        out_specs=tuple(vmem for _ in outs),
+        out_specs=tuple(hbm if out_away else vmem for _ in outs),
+        input_output_aliases=aliases or {},
         scratch_shapes=scratch,
         compiler_params=pltpu.CompilerParams(vmem_limit_bytes=VMEM_BYTES),
         cost_estimate=pl.CostEstimate(flops=flops, bytes_accessed=moved, transcendentals=0),
@@ -357,8 +366,8 @@
         [((supers, block, width), BF), ((supers, 8, width), F32)] + [((supers, piece, width), BF)] * n_cols,
         known, lower_panel[:, 0], pattern, away=range(3),
         scratch=[
-            pltpu.VMEM(known.shape, BF), pltpu.VMEM((supers, n_rows, piece, width), BF),
-            pltpu.SMEM(pattern.shape, jnp.int32), pltpu.SemaphoreType.DMA((2 + supers,)),
+            pltpu.VMEM((n_cols * piece, block), BF), pltpu.VMEM((supers, n_rows, piece, width), BF),
+            pltpu.SMEM(pattern.shape, jnp.int32), pltpu.SemaphoreType.DMA((1 + supers + n_cols,)),
         ],
         flops=2 * known.size * supers * width, moved=4 * block * width * supers,
     )
@@ -383,21 +392,37 @@
         links, joined, mask, own, *got,
         flops=2 * piece * width * width * supers, moved=2 * width * width * supers,
     )
-    pieces = call(
-        functools.partial(rows_kernel, n_cols, n_rows, ROW_ORDER),
-        [((2 * supers, share // n_cols, width), BF)] * n_cols,
-        links, panel, stacks, reach, begin, ahead, *exchange_rows(cols),
-        scratch=[pltpu.VMEM((supers, block, width), BF), pltpu.VMEM((2 * supers, share, width), F32)],
-        flops=2 * 20 * share * width * width, moved=4 * width * width * supers,
-    )
-    got = [hop(pieces[j], "cols", j) for j in reversed(ways)]
-    (summed,) = call(sum_kernel, [(pieces[0].shape, BF)], pieces[0], *got)
-    there = {j: hop(summed, "cols", j) for j in reversed(ways)}
-    diag, sub = call(
-        functools.partial(last_kernel, n_cols),
-        [(diag_inverse.shape, F32)] * 2,
-        diag_inverse, summed, *[there[j] for j in ways],
-    )
+    arrived = exchange_rows(cols)
+    split = supers // 2
+    groups = [tuple(reversed(range(split, supers))), tuple(reversed(range(split)))]
+    state, parts = ahead, []
+    for levels in groups:
+        last = levels[-1] == 0
+        count = 2 * len(levels)
+        *pieces, state = call(
+            functools.partial(rows_kernel, n_cols, n_rows, ROW_ORDER, levels, last),
+            [((count, share // n_cols, width), BF)] * n_cols + ([] if last else [((levels[-1] * share + share, width), F32)]),
+            links, panel, stacks, reach, begin, state, *arrived,
+            scratch=[pltpu.VMEM((supers, block, width), BF), pltpu.VMEM((count, share, width), BF)],
+            flops=2 * 10 * share * width * width, moved=4 * width * width * supers,
+        ) + ((None,) if last else ())
+        parts.append((levels, pieces))
+    sums = []
+    for levels, pieces in parts:
+        got = [hop(pieces[j], "cols", j) for j in reversed(ways)]
+        sums.append((levels, call(sum_kernel, [(pieces[0].shape, BF)], pieces[0], *got)[0]))
+    filled = ()
+    for levels, summed in sums:
+        offsets = [0] + [j for j in AG_ORDER if j < n_cols]
+        got = [summed] + [hop(summed, "cols", j) for j in offsets[1:]]
+        filled = call(
+            functools.partial(last_kernel, n_cols, offsets, levels),
+            [(diag_inverse.shape, F32)] * 2,
+            diag_inverse, *got, *filled, away=range(1 + n_cols, 1 + n_cols + len(filled)), out_away=True,
+            aliases={1 + n_cols + i: i for i in range(len(filled))},
+            scratch=[pltpu.VMEM((2 * len(levels), share, width), F32), pltpu.SemaphoreType.DMA((2 * len(levels),))],
+        )
+    diag, sub = filled
     return cols_out.reshape(supers, 1, 1, piece, width), diag, sub
 
 

time: 61.7 us -> 58.2 us (0.943)
  waiting for transfers between devices: 26.1 us -> 12.6 us
  starting transfers between devices: 23.2 us -> 32.5 us
    ppermute x23 -> x29, waiting for transfers between devices: 26.1 us -> 12.6 us  [hop(): return lax.ppermute(x, axis, [(i, target(i, j, n)) for i in range(n)])]
    ppermute x23 -> x29, starting transfers between devices: 23.2 us -> 32.5 us  [hop(): return lax.ppermute(x, axis, [(i, target(i, j, n)) for i in range(n)])]
    pallas_call x7 -> x10, Pallas kernels: 11.5 us -> 12.1 us  [call(): pl.pallas_call(kernel, out_shape=tuple((jax.ShapeDtypeStruct(s, d) for s,...]
  transfers between devices with their start and end apart: 23 -> 29, of which waited for: 9 -> 9; matrix products, arithmetic and copies ran while one was open for 0% -> 0% of each run, Pallas kernels for 10% -> 14%
where the time goes in v5:
time: 58.2 us; the launch traced here: 58 us
  starting transfers between devices  32.5 us (56%)
  waiting for transfers between devices  12.6 us (22%)
  Pallas kernels  12.1 us (21%)
  between operations  0.76 us (1%)
    ppermute x29, starting transfers between devices, hop(): return lax.ppermute(x, axis, [(i, target(i, j, n)) for i in range(n)])  32.5 us
    ppermute x29, waiting for transfers between devices, hop(): return lax.ppermute(x, axis, [(i, target(i, j, n)) for i in range(n)])  12.6 us
    pallas_call x10, Pallas kernels, call(): pl.pallas_call(kernel, out_shape=tuple((jax.ShapeDtypeStruct(s, d) for s,...  12.1 us
  transfers between devices with their start and end apart: 29, of which 9 were waited for; matrix products, arithmetic and copies ran while one was open for 0% of the time, Pallas kernels for 14%

profile of v5, /device:TPU:0, one launch (start us, length us, event | category | flops | bytes accessed | tf_op | source)
XLA Modules:
  0.0 58.0 jit_solution(4069065437293368845)
XLA Ops:
  0.6 1.9 %shard_map.94 = (bf16[4,256,512]{2,1,0:T(8,128)(2,1)S(1)}, f32[4,8,512]{2,1,0:T(8,128)S(1)}, bf16[4,32,512]{2,1,0:T(8,128)(2,1)S(1)}, bf16[4,32,512]{2,1,0:T(8,1...) custom-call(bf16[4,32,256]{2,1,0:T(8,128)(2,1)} %bitcast.7, ...), custom_call_target="tpu_custom_call" | custom-call | flops 134217728 | bytes 2097152 | tf_op jit(solution)/shard_map/pallas_call | solution.py:333
  2.5 5.1 %collective-permute-start = (bf16[4,32,512]{2,1,0:T(8,128)(2,1)S(1)}, bf16[4,32,512]{2,1,0:T(8,128)(2,1)S(1)}, u32[]{:S(2)}, u32[]{:S(2)}) collective-permute-start(bf16[4,32,512]{2,1,0:T(8,128)(2,1)S(1)} %get-tuple-element.35), channel_id=1, source_target_pairs={{0,3},{1,2},{2,1},{3,0},{4,7},{5,6},{6,5},{7,4},{8,11},{9,10},{10,... | collective-permute-start | bytes 393224 | tf_op jit(solution)/shard_map/ppermute | solution.py:39
  7.6 0.0 collective-permute-start.1
  7.6 0.6 %collective-permute-start.2 = (bf16[4,32,512]{2,1,0:T(8,128)(2,1)S(1)}, bf16[4,32,512]{2,1,0:T(8,128)(2,1)S(1)}, u32[]{:S(2)}, u32[]{:S(2)}) collective-permute-start(bf16[4,32,512]{2,1,0:T(8,128)(2,1)S(1)} %get-tuple-element.37), channel_id=1, source_target_pairs={{0,1},{1,0},{2,3},{3,2},{4,5},{5,4},{6,7},{7,6},{8,9},{9,8},{10,11... | collective-permute-start | bytes 393224 | tf_op jit(solution)/shard_map/ppermute | solution.py:39
  8.3 3.8 %shard_map.95 = (bf16[4,512,512]{2,1,0:T(8,128)(2,1)S(1)}, bf16[5,320,512]{2,1,0:T(8,128)(2,1)S(1)}, bf16[640,256]{1,0:T(8,128)(2,1)S(1)}, bf16[96,512]{1,0:T(8,128)(2,1)S(1)}) custom-call(bf16[4,512,512]{2,1,0:T(8,128)(2,1)} %l_any.1, f32[4,64,512]{2,1,0:T(8,128)} %diag_ref.3, f32[64,512]{1,0:T(8,128)} %top_any.1, bf16[32,512]{1,0:T(8,128)(2,1)} %bitcast.8, ...), custom_call_target="tpu_custom_call" | custom-call | flops 402653184 | bytes 4194304 | tf_op jit(solution)/shard_map/pallas_call | solution.py:333
  12.1 2.7 %collective-permute-start.3 = (bf16[96,512]{1,0:T(8,128)(2,1)S(1)}, bf16[96,512]{1,0:T(8,128)(2,1)S(1)}, u32[]{:S(2)}, u32[]{:S(2)}) collective-permute-start(bf16[96,512]{1,0:T(8,128)(2,1)S(1)} %get-tuple-element.32.joined_ref.refs_0_), channel_id=1, source_target_pairs={{0,24},{4,28},{8,16},{12,20},{16,8},{20,12},{24,0},{28,4},{1,25},{... | collective-permute-start | bytes 294920 | tf_op jit(solution)/shard_map/ppermute | solution.py:39
  14.7 0.5 collective-permute-start.4
  15.2 0.0 collective-permute-done.refs_0_
  15.2 0.4 collective-permute-start.5
  15.6 3.1 %collective-permute-done.1.refs_1_ = bf16[4,32,512]{2,1,0:T(8,128)(2,1)S(1)} collective-permute-done((bf16[4,32,512]{2,1,0:T(8,128)(2,1)S(1)}, bf16[4,32,512]{2,1,0:T(8,128)(2,1)S(1)}, u32[]{:S(2)}, u32[]{:S(2)}) %collective-permute-start.1) | collective-permute-done | bytes 131104 | tf_op jit(solution)/shard_map/ppermute | solution.py:39
  18.7 0.0 collective-permute-start.6
  18.7 0.0 collective-permute-done.2.refs_2_
  18.7 1.4 %shard_map.96 = (bf16[4,32,512]{2,1,0:T(8,128)(2,1)S(1)}, bf16[4,32,512]{2,1,0:T(8,128)(2,1)}) custom-call(bf16[4,512,512]{2,1,0:T(8,128)(2,1)S(1)} %get-tuple-element.31.l_ref, bf16[96,512]{1,0:T(8,128)(2,1)S(1)} %get-tuple-element.32.joined_ref.refs_0_, f32[4,8,512]{2,1,0:T(8,128)S(1)} %get-tuple-element.33.mask_ref, ...), custom_call_target="tpu_custom_call" | custom-call | flops 67108864 | bytes 2097152 | tf_op jit(solution)/shard_map/pallas_call | solution.py:333
  20.1 2.5 %collective-permute-start.10 = (bf16[4,32,512]{2,1,0:T(8,128)(2,1)S(1)}, bf16[4,32,512]{2,1,0:T(8,128)(2,1)S(1)}, u32[]{:S(2)}, u32[]{:S(2)}) collective-permute-start(bf16[4,32,512]{2,1,0:T(8,128)(2,1)S(1)} %get-tuple-element.43.refs_0_), channel_id=1, source_target_pairs={{0,24},{4,28},{8,16},{12,20},{16,8},{20,12},{24,0},{28,4},{1,25},{... | collective-permute-start | bytes 393224 | tf_op jit(solution)/shard_map/ppermute | solution.py:39
  22.5 0.0 collective-permute-done.3.refs_1_
  22.5 0.5 collective-permute-start.11
  23.0 0.0 collective-permute-done.4.refs_2_
  23.0 0.5 collective-permute-start.12
  23.6 0.0 collective-permute-done.5.refs_3_
  23.6 0.0 collective-permute-start.7
  23.6 0.0 collective-permute-done.6.refs_4_
  23.6 0.5 collective-permute-start.8
  24.1 0.8 %collective-permute-done.7.refs_5_ = bf16[96,512]{1,0:T(8,128)(2,1)S(1)} collective-permute-done((bf16[96,512]{1,0:T(8,128)(2,1)S(1)}, bf16[96,512]{1,0:T(8,128)(2,1)S(1)}, u32[]{:S(2)}, u32[]{:S(2)}) %collective-permute-start.7) | collective-permute-done | bytes 98336 | tf_op jit(solution)/shard_map/ppermute | solution.py:39
  24.9 0.2 collective-permute-start.9
  25.0 0.0 collective-permute-done.8.refs_6_
  25.0 0.4 collective-permute-start.13
  25.4 1.8 %collective-permute-done.10.refs_1_ = bf16[4,32,512]{2,1,0:T(8,128)(2,1)S(1)} collective-permute-done((bf16[4,32,512]{2,1,0:T(8,128)(2,1)S(1)}, bf16[4,32,512]{2,1,0:T(8,128)(2,1)S(1)}, u32[]{:S(2)}, u32[]{:S(2)}) %collective-permute-start.10) | collective-permute-done | bytes 131104 | tf_op jit(solution)/shard_map/ppermute | solution.py:39
  27.2 0.0 collective-permute-start.14
  27.2 2.5 %collective-permute-done.11.refs_2_ = bf16[4,32,512]{2,1,0:T(8,128)(2,1)S(1)} collective-permute-done((bf16[4,32,512]{2,1,0:T(8,128)(2,1)S(1)}, bf16[4,32,512]{2,1,0:T(8,128)(2,1)S(1)}, u32[]{:S(2)}, u32[]{:S(2)}) %collective-permute-start.11) | collective-permute-done | bytes 131104 | tf_op jit(solution)/shard_map/ppermute | solution.py:39
  29.7 0.0 collective-permute-start.15
  29.7 0.1 collective-permute-done.12.refs_3_
  29.8 0.4 collective-permute-start.16
  30.2 0.0 collective-permute-done.9.refs_7_
  30.2 1.2 %shard_map.97 = (f32[320,512]{1,0:T(8,128)S(1)}, f32[320,512]{1,0:T(8,128)S(1)}) custom-call(bf16[4,512,512]{2,1,0:T(8,128)(2,1)S(1)} %get-tuple-element.31.l_ref, bf16[4,256,512]{2,1,0:T(8,128)(2,1)S(1)} %get-tuple-element.30.panel_ref, bf16[5,320,512]{2,1,0:T(8,128)(2,1)S(1)} %get-tuple-element.39.stacks_ref, ...), custom_call_target="tpu_custom_call" | custom-call | flops 503316480 | bytes 1048576 | tf_op jit(solution)/shard_map/pallas_call | solution.py:333
  31.5 0.0 collective-permute-done.13.refs_4_
  31.5 0.0 collective-permute-done.14.refs_5_
  31.5 0.0 collective-permute-done.15.refs_6_
  31.5 0.0 collective-permute-done.16.refs_7_
  31.5 1.0 %shard_map.98 = (bf16[4,16,512]{2,1,0:T(8,128)(2,1)S(1)}, bf16[4,16,512]{2,1,0:T(8,128)(2,1)S(1)}, bf16[4,16,512]{2,1,0:T(8,128)(2,1)S(1)}, bf16[4,16,512]{2,1,0:T(8,128)(2,1)S(1)}, f32[192,512]{1,0:T(8,128)S(1)}) custom-call(bf16[4,512,512]{2,1,0:T(8,128)(2,1)S(1)} %get-tuple-element.31.l_ref, bf16[4,256,512]{2,1,0:T(8,128)(2,1)S(1)} %get-tuple-element.30.panel_ref, ...), custom_call_target="tpu_custom_call" | custom-call | flops 335544320 | bytes 4194304 | tf_op jit(solution)/shard_map/pallas_call | solution.py:333
  32.5 2.6 %collective-permute-start.23 = (bf16[4,16,512]{2,1,0:T(8,128)(2,1)S(1)}, bf16[4,16,512]{2,1,0:T(8,128)(2,1)S(1)}, u32[]{:S(2)}, u32[]{:S(2)}) collective-permute-start(bf16[4,16,512]{2,1,0:T(8,128)(2,1)S(1)} %get-tuple-element.50), channel_id=1, source_target_pairs={{0,3},{1,2},{2,1},{3,0},{4,7},{5,6},{6,5},{7,4},{8,11},{9,10},{10,... | collective-permute-start | bytes 196616 | tf_op jit(solution)/shard_map/ppermute | solution.py:39
  35.0 0.0 collective-permute-start.24
  35.0 1.9 %collective-permute-start.25 = (bf16[4,16,512]{2,1,0:T(8,128)(2,1)S(1)}, bf16[4,16,512]{2,1,0:T(8,128)(2,1)S(1)}, u32[]{:S(2)}, u32[]{:S(2)}) collective-permute-start(bf16[4,16,512]{2,1,0:T(8,128)(2,1)S(1)} %get-tuple-element.52), channel_id=1, source_target_pairs={{0,1},{1,0},{2,3},{3,2},{4,5},{5,4},{6,7},{7,6},{8,9},{9,8},{10,11... | collective-permute-start | bytes 196616 | tf_op jit(solution)/shard_map/ppermute | solution.py:39
  36.9 1.0 %shard_map.99 = (bf16[4,16,512]{2,1,0:T(8,128)(2,1)S(1)}, bf16[4,16,512]{2,1,0:T(8,128)(2,1)S(1)}, bf16[4,16,512]{2,1,0:T(8,128)(2,1)S(1)}, bf16[4,16,512]{2,1,0:T(8,128)(2,1)S(1)}) custom-call(bf16[4,512,512]{2,1,0:T(8,128)(2,1)S(1)} %get-tuple-element.31.l_ref, bf16[4,256,512]{2,1,0:T(8,128)(2,1)S(1)} %get-tuple-element.30.panel_ref, ...), custom_call_target="tpu_custom_call" | custom-call | flops 335544320 | bytes 4194304 | tf_op jit(solution)/shard_map/pallas_call | solution.py:333
  38.0 2.6 %collective-permute-start.17 = (bf16[4,16,512]{2,1,0:T(8,128)(2,1)S(1)}, bf16[4,16,512]{2,1,0:T(8,128)(2,1)S(1)}, u32[]{:S(2)}, u32[]{:S(2)}) collective-permute-start(bf16[4,16,512]{2,1,0:T(8,128)(2,1)S(1)} %get-tuple-element.46), channel_id=1, source_target_pairs={{0,3},{1,2},{2,1},{3,0},{4,7},{5,6},{6,5},{7,4},{8,11},{9,10},{10,... | collective-permute-start | bytes 196616 | tf_op jit(solution)/shard_map/ppermute | solution.py:39
  40.5 0.0 collective-permute-start.18
  40.5 0.0 collective-permute-done.23.refs_0_
  40.5 1.9 %collective-permute-start.19 = (bf16[4,16,512]{2,1,0:T(8,128)(2,1)S(1)}, bf16[4,16,512]{2,1,0:T(8,128)(2,1)S(1)}, u32[]{:S(2)}, u32[]{:S(2)}) collective-permute-start(bf16[4,16,512]{2,1,0:T(8,128)(2,1)S(1)} %get-tuple-element.48), channel_id=1, source_target_pairs={{0,1},{1,0},{2,3},{3,2},{4,5},{5,4},{6,7},{7,6},{8,9},{9,8},{10,11... | collective-permute-start | bytes 196616 | tf_op jit(solution)/shard_map/ppermute | solution.py:39
  42.4 0.0 collective-permute-done.24.refs_1_
  42.4 0.0 collective-permute-done.25.refs_2_
  42.5 0.2 collective-permute-start.26
  42.7 2.9 %collective-permute-start.27 = (bf16[4,16,512]{2,1,0:T(8,128)(2,1)S(1)}, bf16[4,16,512]{2,1,0:T(8,128)(2,1)S(1)}, u32[]{:S(2)}, u32[]{:S(2)}) collective-permute-start(bf16[4,16,512]{2,1,0:T(8,128)(2,1)S(1)} %shard_map.101.refs_0_), channel_id=1, source_target_pairs={{0,2},{1,3},{2,0},{3,1},{4,6},{5,7},{6,4},{7,5},{8,10},{9,11},{10,... | collective-permute-start | bytes 196616 | tf_op jit(solution)/shard_map/ppermute | solution.py:39
  45.6 0.0 collective-permute-done.17.refs_0_
  45.6 1.8 %collective-permute-start.28 = (bf16[4,16,512]{2,1,0:T(8,128)(2,1)S(1)}, bf16[4,16,512]{2,1,0:T(8,128)(2,1)S(1)}, u32[]{:S(2)}, u32[]{:S(2)}) collective-permute-start(bf16[4,16,512]{2,1,0:T(8,128)(2,1)S(1)} %shard_map.101.refs_0_), channel_id=1, source_target_pairs={{0,3},{1,2},{2,1},{3,0},{4,7},{5,6},{6,5},{7,4},{8,11},{9,10},{10,... | collective-permute-start | bytes 196616 | tf_op jit(solution)/shard_map/ppermute | solution.py:39
  47.4 0.3 collective-permute-done.18.refs_1_
  47.7 0.3 collective-permute-start.20
  48.0 3.0 %collective-permute-start.21 = (bf16[4,16,512]{2,1,0:T(8,128)(2,1)S(1)}, bf16[4,16,512]{2,1,0:T(8,128)(2,1)S(1)}, u32[]{:S(2)}, u32[]{:S(2)}) collective-permute-start(bf16[4,16,512]{2,1,0:T(8,128)(2,1)S(1)} %shard_map.100.refs_0_), channel_id=1, source_target_pairs={{0,2},{1,3},{2,0},{3,1},{4,6},{5,7},{6,4},{7,5},{8,10},{9,11},{10,... | collective-permute-start | bytes 196616 | tf_op jit(solution)/shard_map/ppermute | solution.py:39
  51.0 0.0 collective-permute-done.26.refs_1_
  51.0 1.2 %collective-permute-start.22 = (bf16[4,16,512]{2,1,0:T(8,128)(2,1)S(1)}, bf16[4,16,512]{2,1,0:T(8,128)(2,1)S(1)}, u32[]{:S(2)}, u32[]{:S(2)}) collective-permute-start(bf16[4,16,512]{2,1,0:T(8,128)(2,1)S(1)} %shard_map.100.refs_0_), channel_id=1, source_target_pairs={{0,3},{1,2},{2,1},{3,0},{4,7},{5,6},{6,5},{7,4},{8,11},{9,10},{10,... | collective-permute-start | bytes 196616 | tf_op jit(solution)/shard_map/ppermute | solution.py:39
  52.2 0.2 collective-permute-done.28.refs_3_
  52.4 0.9 %shard_map.102 = (f32[4,64,512]{2,1,0:T(8,128)}, f32[4,64,512]{2,1,0:T(8,128)}) custom-call(f32[4,64,512]{2,1,0:T(8,128)S(1)} %copy-done, bf16[4,16,512]{2,1,0:T(8,128)(2,1)S(1)} %shard_map.101.refs_0_, bf16[4,16,512]{2,1,0:T(8,128)(2,1)S(1)} %collective-permute-done.26.refs_1_, bf16[4,16,512]{2,1,0:T(8,128)(2,1)S(1)} %collective-permute-done.27.refs_2_, ...), custom_call_target="tpu_custom_call" | custom-call | tf_op jit(solution)/shard_map/pallas_call | solution.py:333
  53.2 0.0 collective-permute-done.20.refs_1_
  53.2 2.8 %collective-permute-done.21.refs_2_ = bf16[4,16,512]{2,1,0:T(8,128)(2,1)S(1)} collective-permute-done((bf16[4,16,512]{2,1,0:T(8,128)(2,1)S(1)}, bf16[4,16,512]{2,1,0:T(8,128)(2,1)S(1)}, u32[]{:S(2)}, u32[]{:S(2)}) %collective-permute-start.21) | collective-permute-done | bytes 65568 | tf_op jit(solution)/shard_map/ppermute | solution.py:39
  56.1 1.1 %collective-permute-done.22.refs_3_ = bf16[4,16,512]{2,1,0:T(8,128)(2,1)S(1)} collective-permute-done((bf16[4,16,512]{2,1,0:T(8,128)(2,1)S(1)}, bf16[4,16,512]{2,1,0:T(8,128)(2,1)S(1)}, u32[]{:S(2)}, u32[]{:S(2)}) %collective-permute-start.22) | collective-permute-done | bytes 65568 | tf_op jit(solution)/shard_map/ppermute | solution.py:39
  57.1 0.9 %shard_map.103 = (f32[4,64,512]{2,1,0:T(8,128)}, f32[4,64,512]{2,1,0:T(8,128)}) custom-call(f32[4,64,512]{2,1,0:T(8,128)S(1)} %copy-done, bf16[4,16,512]{2,1,0:T(8,128)(2,1)S(1)} %shard_map.100.refs_0_, bf16[4,16,512]{2,1,0:T(8,128)(2,1)S(1)} %collective-permute-done.20.refs_1_, ...), custom_call_target="tpu_custom_call", output_to_operand_aliasing={{0}: (5, {}), {1}: (6, {})} | custom-call | tf_op jit(solution)/shard_map/pallas_call | solution.py:333
  (6 shorter events, 0.1 us)
Async XLA Ops:
  2.5 12.7 %collective-permute-start = (bf16[4,32,512]{2,1,0:T(8,128)(2,1)S(1)}, bf16[4,32,512]{2,1,0:T(8,128)(2,1)S(1)}, u32[]{:S(2)}, u32[]{:S(2)}) collective-permute-start(bf16[4,32,512]{2,1,0:T(8,128)(2,1)S(1)} %get-tuple-element.35), channel_id=1, source_target_pairs={{0,3},{1,2},{2,1},{3,0},{4,7},{5,6},{6,5},{7,4},{8,11},{9,10},{10,... | collective-permute-start | bytes 393224 | tf_op jit(solution)/shard_map/ppermute | solution.py:39
  7.6 11.1 %collective-permute-start.1 = (bf16[4,32,512]{2,1,0:T(8,128)(2,1)S(1)}, bf16[4,32,512]{2,1,0:T(8,128)(2,1)S(1)}, u32[]{:S(2)}, u32[]{:S(2)}) collective-permute-start(bf16[4,32,512]{2,1,0:T(8,128)(2,1)S(1)} %get-tuple-element.36), channel_id=1, source_target_pairs={{0,2},{1,3},{2,0},{3,1},{4,6},{5,7},{6,4},{7,5},{8,10},{9,11},{10,... | collective-permute-start | bytes 393224 | tf_op jit(solution)/shard_map/ppermute | solution.py:39
  7.6 11.1 %collective-permute-start.2 = (bf16[4,32,512]{2,1,0:T(8,128)(2,1)S(1)}, bf16[4,32,512]{2,1,0:T(8,128)(2,1)S(1)}, u32[]{:S(2)}, u32[]{:S(2)}) collective-permute-start(bf16[4,32,512]{2,1,0:T(8,128)(2,1)S(1)} %get-tuple-element.37), channel_id=1, source_target_pairs={{0,1},{1,0},{2,3},{3,2},{4,5},{5,4},{6,7},{7,6},{8,9},{9,8},{10,11... | collective-permute-start | bytes 393224 | tf_op jit(solution)/shard_map/ppermute | solution.py:39
  12.1 10.5 %collective-permute-start.3 = (bf16[96,512]{1,0:T(8,128)(2,1)S(1)}, bf16[96,512]{1,0:T(8,128)(2,1)S(1)}, u32[]{:S(2)}, u32[]{:S(2)}) collective-permute-start(bf16[96,512]{1,0:T(8,128)(2,1)S(1)} %get-tuple-element.32.joined_ref.refs_0_), channel_id=1, source_target_pairs={{0,24},{4,28},{8,16},{12,20},{16,8},{20,12},{24,0},{28,4},{1,25},{... | collective-permute-start | bytes 294920 | tf_op jit(solution)/shard_map/ppermute | solution.py:39
  14.7 8.3 %collective-permute-start.4 = (bf16[96,512]{1,0:T(8,128)(2,1)S(1)}, bf16[96,512]{1,0:T(8,128)(2,1)S(1)}, u32[]{:S(2)}, u32[]{:S(2)}) collective-permute-start(bf16[96,512]{1,0:T(8,128)(2,1)S(1)} %get-tuple-element.32.joined_ref.refs_0_), channel_id=1, source_target_pairs={{0,16},{4,20},{8,24},{12,28},{16,0},{20,4},{24,8},{28,12},{1,17},{... | collective-permute-start | bytes 294920 | tf_op jit(solution)/shard_map/ppermute | solution.py:39
  15.2 8.3 %collective-permute-start.5 = (bf16[96,512]{1,0:T(8,128)(2,1)S(1)}, bf16[96,512]{1,0:T(8,128)(2,1)S(1)}, u32[]{:S(2)}, u32[]{:S(2)}) collective-permute-start(bf16[96,512]{1,0:T(8,128)(2,1)S(1)} %get-tuple-element.32.joined_ref.refs_0_), channel_id=1, source_target_pairs={{0,8},{4,12},{8,0},{12,4},{16,24},{20,28},{24,16},{28,20},{1,9},{5... | collective-permute-start | bytes 294920 | tf_op jit(solution)/shard_map/ppermute | solution.py:39
  18.7 4.9 %collective-permute-start.6 = (bf16[96,512]{1,0:T(8,128)(2,1)S(1)}, bf16[96,512]{1,0:T(8,128)(2,1)S(1)}, u32[]{:S(2)}, u32[]{:S(2)}) collective-permute-start(bf16[96,512]{1,0:T(8,128)(2,1)S(1)} %get-tuple-element.32.joined_ref.refs_0_), channel_id=1, source_target_pairs={{0,4},{4,0},{8,12},{12,8},{16,20},{20,16},{24,28},{28,24},{1,5},{5... | collective-permute-start | bytes 294920 | tf_op jit(solution)/shard_map/ppermute | solution.py:39
  20.1 7.1 %collective-permute-start.10 = (bf16[4,32,512]{2,1,0:T(8,128)(2,1)S(1)}, bf16[4,32,512]{2,1,0:T(8,128)(2,1)S(1)}, u32[]{:S(2)}, u32[]{:S(2)}) collective-permute-start(bf16[4,32,512]{2,1,0:T(8,128)(2,1)S(1)} %get-tuple-element.43.refs_0_), channel_id=1, source_target_pairs={{0,24},{4,28},{8,16},{12,20},{16,8},{20,12},{24,0},{28,4},{1,25},{... | collective-permute-start | bytes 393224 | tf_op jit(solution)/shard_map/ppermute | solution.py:39
  22.5 7.2 %collective-permute-start.11 = (bf16[4,32,512]{2,1,0:T(8,128)(2,1)S(1)}, bf16[4,32,512]{2,1,0:T(8,128)(2,1)S(1)}, u32[]{:S(2)}, u32[]{:S(2)}) collective-permute-start(bf16[4,32,512]{2,1,0:T(8,128)(2,1)S(1)} %get-tuple-element.43.refs_0_), channel_id=1, source_target_pairs={{0,16},{4,20},{8,24},{12,28},{16,0},{20,4},{24,8},{28,12},{1,17},{... | collective-permute-start | bytes 393224 | tf_op jit(solution)/shard_map/ppermute | solution.py:39
  23.0 6.8 %collective-permute-start.12 = (bf16[4,32,512]{2,1,0:T(8,128)(2,1)S(1)}, bf16[4,32,512]{2,1,0:T(8,128)(2,1)S(1)}, u32[]{:S(2)}, u32[]{:S(2)}) collective-permute-start(bf16[4,32,512]{2,1,0:T(8,128)(2,1)S(1)} %get-tuple-element.43.refs_0_), channel_id=1, source_target_pairs={{0,8},{4,12},{8,0},{12,4},{16,24},{20,28},{24,16},{28,20},{1,9},{5... | collective-permute-start | bytes 393224 | tf_op jit(solution)/shard_map/ppermute | solution.py:39
  23.6 1.3 %collective-permute-start.7 = (bf16[96,512]{1,0:T(8,128)(2,1)S(1)}, bf16[96,512]{1,0:T(8,128)(2,1)S(1)}, u32[]{:S(2)}, u32[]{:S(2)}) collective-permute-start(bf16[96,512]{1,0:T(8,128)(2,1)S(1)} %collective-permute-done.3.refs_1_), channel_id=1, source_target_pairs={{0,4},{4,0},{8,12},{12,8},{16,20},{20,16},{24,28},{28,24},{1,5},{5... | collective-permute-start | bytes 294920 | tf_op jit(solution)/shard_map/ppermute | solution.py:39
  23.6 1.5 %collective-permute-start.8 = (bf16[96,512]{1,0:T(8,128)(2,1)S(1)}, bf16[96,512]{1,0:T(8,128)(2,1)S(1)}, u32[]{:S(2)}, u32[]{:S(2)}) collective-permute-start(bf16[96,512]{1,0:T(8,128)(2,1)S(1)} %collective-permute-done.4.refs_2_), channel_id=1, source_target_pairs={{0,4},{4,0},{8,12},{12,8},{16,20},{20,16},{24,28},{28,24},{1,5},{5... | collective-permute-start | bytes 294920 | tf_op jit(solution)/shard_map/ppermute | solution.py:39
  24.9 5.3 %collective-permute-start.9 = (bf16[96,512]{1,0:T(8,128)(2,1)S(1)}, bf16[96,512]{1,0:T(8,128)(2,1)S(1)}, u32[]{:S(2)}, u32[]{:S(2)}) collective-permute-start(bf16[96,512]{1,0:T(8,128)(2,1)S(1)} %collective-permute-done.5.refs_3_), channel_id=1, source_target_pairs={{0,4},{4,0},{8,12},{12,8},{16,20},{20,16},{24,28},{28,24},{1,5},{5... | collective-permute-start | bytes 294920 | tf_op jit(solution)/shard_map/ppermute | solution.py:39
  25.0 6.4 %collective-permute-start.13 = (bf16[4,32,512]{2,1,0:T(8,128)(2,1)S(1)}, bf16[4,32,512]{2,1,0:T(8,128)(2,1)S(1)}, u32[]{:S(2)}, u32[]{:S(2)}) collective-permute-start(bf16[4,32,512]{2,1,0:T(8,128)(2,1)S(1)} %get-tuple-element.43.refs_0_), channel_id=1, source_target_pairs={{0,4},{4,0},{8,12},{12,8},{16,20},{20,16},{24,28},{28,24},{1,5},{5... | collective-permute-start | bytes 393224 | tf_op jit(solution)/shard_map/ppermute | solution.py:39
  27.2 4.3 %collective-permute-start.14 = (bf16[4,32,512]{2,1,0:T(8,128)(2,1)S(1)}, bf16[4,32,512]{2,1,0:T(8,128)(2,1)S(1)}, u32[]{:S(2)}, u32[]{:S(2)}) collective-permute-start(bf16[4,32,512]{2,1,0:T(8,128)(2,1)S(1)} %collective-permute-done.10.refs_1_), channel_id=1, source_target_pairs={{0,4},{4,0},{8,12},{12,8},{16,20},{20,16},{24,28},{28,24},{1,5},{5... | collective-permute-start | bytes 393224 | tf_op jit(solution)/shard_map/ppermute | solution.py:39
  29.7 1.8 %collective-permute-start.15 = (bf16[4,32,512]{2,1,0:T(8,128)(2,1)S(1)}, bf16[4,32,512]{2,1,0:T(8,128)(2,1)S(1)}, u32[]{:S(2)}, u32[]{:S(2)}) collective-permute-start(bf16[4,32,512]{2,1,0:T(8,128)(2,1)S(1)} %collective-permute-done.11.refs_2_), channel_id=1, source_target_pairs={{0,4},{4,0},{8,12},{12,8},{16,20},{20,16},{24,28},{28,24},{1,5},{5... | collective-permute-start | bytes 393224 | tf_op jit(solution)/shard_map/ppermute | solution.py:39
  29.8 1.7 %collective-permute-start.16 = (bf16[4,32,512]{2,1,0:T(8,128)(2,1)S(1)}, bf16[4,32,512]{2,1,0:T(8,128)(2,1)S(1)}, u32[]{:S(2)}, u32[]{:S(2)}) collective-permute-start(bf16[4,32,512]{2,1,0:T(8,128)(2,1)S(1)} %collective-permute-done.12.refs_3_), channel_id=1, source_target_pairs={{0,4},{4,0},{8,12},{12,8},{16,20},{20,16},{24,28},{28,24},{1,5},{5... | collective-permute-start | bytes 393224 | tf_op jit(solution)/shard_map/ppermute | solution.py:39
  32.5 8.1 %collective-permute-start.23 = (bf16[4,16,512]{2,1,0:T(8,128)(2,1)S(1)}, bf16[4,16,512]{2,1,0:T(8,128)(2,1)S(1)}, u32[]{:S(2)}, u32[]{:S(2)}) collective-permute-start(bf16[4,16,512]{2,1,0:T(8,128)(2,1)S(1)} %get-tuple-element.50), channel_id=1, source_target_pairs={{0,3},{1,2},{2,1},{3,0},{4,7},{5,6},{6,5},{7,4},{8,11},{9,10},{10,... | collective-permute-start | bytes 196616 | tf_op jit(solution)/shard_map/ppermute | solution.py:39
  35.0 7.4 %collective-permute-start.24 = (bf16[4,16,512]{2,1,0:T(8,128)(2,1)S(1)}, bf16[4,16,512]{2,1,0:T(8,128)(2,1)S(1)}, u32[]{:S(2)}, u32[]{:S(2)}) collective-permute-start(bf16[4,16,512]{2,1,0:T(8,128)(2,1)S(1)} %get-tuple-element.51), channel_id=1, source_target_pairs={{0,2},{1,3},{2,0},{3,1},{4,6},{5,7},{6,4},{7,5},{8,10},{9,11},{10,... | collective-permute-start | bytes 196616 | tf_op jit(solution)/shard_map/ppermute | solution.py:39
  35.0 7.4 %collective-permute-start.25 = (bf16[4,16,512]{2,1,0:T(8,128)(2,1)S(1)}, bf16[4,16,512]{2,1,0:T(8,128)(2,1)S(1)}, u32[]{:S(2)}, u32[]{:S(2)}) collective-permute-start(bf16[4,16,512]{2,1,0:T(8,128)(2,1)S(1)} %get-tuple-element.52), channel_id=1, source_target_pairs={{0,1},{1,0},{2,3},{3,2},{4,5},{5,4},{6,7},{7,6},{8,9},{9,8},{10,11... | collective-permute-start | bytes 196616 | tf_op jit(solution)/shard_map/ppermute | solution.py:39
  36.9 15.5 %copy-start = (f32[4,64,512]{2,1,0:T(8,128)S(1)}, f32[4,64,512]{2,1,0:T(8,128)}, u32[]{:S(2)}) copy-start(f32[4,64,512]{2,1,0:T(8,128)} %diag_ref.3) | copy-start | bytes 1572868
  38.0 7.6 %collective-permute-start.17 = (bf16[4,16,512]{2,1,0:T(8,128)(2,1)S(1)}, bf16[4,16,512]{2,1,0:T(8,128)(2,1)S(1)}, u32[]{:S(2)}, u32[]{:S(2)}) collective-permute-start(bf16[4,16,512]{2,1,0:T(8,128)(2,1)S(1)} %get-tuple-element.46), channel_id=1, source_target_pairs={{0,3},{1,2},{2,1},{3,0},{4,7},{5,6},{6,5},{7,4},{8,11},{9,10},{10,... | collective-permute-start | bytes 196616 | tf_op jit(solution)/shard_map/ppermute | solution.py:39
  40.5 7.2 %collective-permute-start.18 = (bf16[4,16,512]{2,1,0:T(8,128)(2,1)S(1)}, bf16[4,16,512]{2,1,0:T(8,128)(2,1)S(1)}, u32[]{:S(2)}, u32[]{:S(2)}) collective-permute-start(bf16[4,16,512]{2,1,0:T(8,128)(2,1)S(1)} %get-tuple-element.47), channel_id=1, source_target_pairs={{0,2},{1,3},{2,0},{3,1},{4,6},{5,7},{6,4},{7,5},{8,10},{9,11},{10,... | collective-permute-start | bytes 196616 | tf_op jit(solution)/shard_map/ppermute | solution.py:39
  40.5 7.1 %collective-permute-start.19 = (bf16[4,16,512]{2,1,0:T(8,128)(2,1)S(1)}, bf16[4,16,512]{2,1,0:T(8,128)(2,1)S(1)}, u32[]{:S(2)}, u32[]{:S(2)}) collective-permute-start(bf16[4,16,512]{2,1,0:T(8,128)(2,1)S(1)} %get-tuple-element.48), channel_id=1, source_target_pairs={{0,1},{1,0},{2,3},{3,2},{4,5},{5,4},{6,7},{7,6},{8,9},{9,8},{10,11... | collective-permute-start | bytes 196616 | tf_op jit(solution)/shard_map/ppermute | solution.py:39
  42.5 8.5 %collective-permute-start.26 = (bf16[4,16,512]{2,1,0:T(8,128)(2,1)S(1)}, bf16[4,16,512]{2,1,0:T(8,128)(2,1)S(1)}, u32[]{:S(2)}, u32[]{:S(2)}) collective-permute-start(bf16[4,16,512]{2,1,0:T(8,128)(2,1)S(1)} %shard_map.101.refs_0_), channel_id=1, source_target_pairs={{0,1},{1,0},{2,3},{3,2},{4,5},{5,4},{6,7},{7,6},{8,9},{9,8},{10,11... | collective-permute-start | bytes 196616 | tf_op jit(solution)/shard_map/ppermute | solution.py:39
  42.7 9.5 %collective-permute-start.27 = (bf16[4,16,512]{2,1,0:T(8,128)(2,1)S(1)}, bf16[4,16,512]{2,1,0:T(8,128)(2,1)S(1)}, u32[]{:S(2)}, u32[]{:S(2)}) collective-permute-start(bf16[4,16,512]{2,1,0:T(8,128)(2,1)S(1)} %shard_map.101.refs_0_), channel_id=1, source_target_pairs={{0,2},{1,3},{2,0},{3,1},{4,6},{5,7},{6,4},{7,5},{8,10},{9,11},{10,... | collective-permute-start | bytes 196616 | tf_op jit(solution)/shard_map/ppermute | solution.py:39
  45.6 6.8 %collective-permute-start.28 = (bf16[4,16,512]{2,1,0:T(8,128)(2,1)S(1)}, bf16[4,16,512]{2,1,0:T(8,128)(2,1)S(1)}, u32[]{:S(2)}, u32[]{:S(2)}) collective-permute-start(bf16[4,16,512]{2,1,0:T(8,128)(2,1)S(1)} %shard_map.101.refs_0_), channel_id=1, source_target_pairs={{0,3},{1,2},{2,1},{3,0},{4,7},{5,6},{6,5},{7,4},{8,11},{9,10},{10,... | collective-permute-start | bytes 196616 | tf_op jit(solution)/shard_map/ppermute | solution.py:39
  47.7 5.5 %collective-permute-start.20 = (bf16[4,16,512]{2,1,0:T(8,128)(2,1)S(1)}, bf16[4,16,512]{2,1,0:T(8,128)(2,1)S(1)}, u32[]{:S(2)}, u32[]{:S(2)}) collective-permute-start(bf16[4,16,512]{2,1,0:T(8,128)(2,1)S(1)} %shard_map.100.refs_0_), channel_id=1, source_target_pairs={{0,1},{1,0},{2,3},{3,2},{4,5},{5,4},{6,7},{7,6},{8,9},{9,8},{10,11... | collective-permute-start | bytes 196616 | tf_op jit(solution)/shard_map/ppermute | solution.py:39
  48.0 8.1 %collective-permute-start.21 = (bf16[4,16,512]{2,1,0:T(8,128)(2,1)S(1)}, bf16[4,16,512]{2,1,0:T(8,128)(2,1)S(1)}, u32[]{:S(2)}, u32[]{:S(2)}) collective-permute-start(bf16[4,16,512]{2,1,0:T(8,128)(2,1)S(1)} %shard_map.100.refs_0_), channel_id=1, source_target_pairs={{0,2},{1,3},{2,0},{3,1},{4,6},{5,7},{6,4},{7,5},{8,10},{9,11},{10,... | collective-permute-start | bytes 196616 | tf_op jit(solution)/shard_map/ppermute | solution.py:39
  51.0 6.2 %collective-permute-start.22 = (bf16[4,16,512]{2,1,0:T(8,128)(2,1)S(1)}, bf16[4,16,512]{2,1,0:T(8,128)(2,1)S(1)}, u32[]{:S(2)}, u32[]{:S(2)}) collective-permute-start(bf16[4,16,512]{2,1,0:T(8,128)(2,1)S(1)} %shard_map.100.refs_0_), channel_id=1, source_target_pairs={{0,3},{1,2},{2,1},{3,0},{4,7},{5,6},{6,5},{7,4},{8,11},{9,10},{10,... | collective-permute-start | bytes 196616 | tf_op jit(solution)/shard_map/ppermute | solution.py:39

commit v6 on v5

--- a/solution.py
+++ b/solution.py
@@ -11,7 +11,9 @@
 F32 = jnp.float32
 ROW_ORDER = (0, 6, 4, 2, 1, 7, 5, 3)
 VMEM_BYTES = 32 << 20
-AG_ORDER = (1, 2, 3)
+FIRST_ORDER = (3, 1, 2)
+SUM_ORDER = (3, 2, 1)
+LAST_ORDER = (1, 2, 3)
 
 
 def dot(a, b):
@@ -354,7 +356,7 @@
     piece = known_inverse.shape[2]
     width = lower_panel.shape[-1]
     share = width // n_rows
-    if n_rows != len(ROW_ORDER) or not pow2(n_cols) or n_cols < supers or share % (16 * n_cols) or piece % 16:
+    if n_rows != len(ROW_ORDER) or n_cols != 1 + len(FIRST_ORDER) or n_cols < supers or share % (16 * n_cols) or piece % 16:
         return general(known_inverse, lower_panel, chain_panel, diag_inverse, top_cols, top_diag, pattern)
     known = known_inverse[:, 0]
     tops = top_cols[0, 0]
@@ -371,7 +373,7 @@
         ],
         flops=2 * known.size * supers * width, moved=4 * block * width * supers,
     )
-    got = [hop(sent[j - 1], "cols", j) for j in reversed(ways)]
+    got = [hop(sent[j - 1], "cols", j) for j in FIRST_ORDER]
     links, stacks, reach, joined = call(
         functools.partial(ready_kernel, n_cols, n_rows),
         [(chain_panel.shape, BF), ((supers + 1, rows_of[supers], width), BF), ((sum(rows_of[:supers]), block), BF), ((share + piece, width), BF)],
@@ -409,11 +411,11 @@
         parts.append((levels, pieces))
     sums = []
     for levels, pieces in parts:
-        got = [hop(pieces[j], "cols", j) for j in reversed(ways)]
+        got = [hop(pieces[j], "cols", j) for j in SUM_ORDER]
         sums.append((levels, call(sum_kernel, [(pieces[0].shape, BF)], pieces[0], *got)[0]))
     filled = ()
     for levels, summed in sums:
-        offsets = [0] + [j for j in AG_ORDER if j < n_cols]
+        offsets = (0,) + LAST_ORDER
         got = [summed] + [hop(summed, "cols", j) for j in offsets[1:]]
         filled = call(
             functools.partial(last_kernel, n_cols, offsets, levels),

time: 58.2 us -> 56.4 us (0.969)
  waiting for transfers between devices: 12.6 us -> 11.3 us
    ppermute x29, waiting for transfers between devices: 12.6 us -> 11.3 us  [hop(): return lax.ppermute(x, axis, [(i, target(i, j, n)) for i in range(n)])]
  transfers between devices with their start and end apart: 29 -> 29, of which waited for: 9 -> 7; matrix products, arithmetic and copies ran while one was open for 0% -> 0% of each run, Pallas kernels for 14% -> 15%
where the time goes in v6:
time: 56.4 us; the launch traced here: 56.3 us
  starting transfers between devices  32.1 us (57%)
  Pallas kernels  12.1 us (21%)
  waiting for transfers between devices  11.3 us (20%)
  between operations  0.76 us (1%)
    ppermute x29, starting transfers between devices, hop(): return lax.ppermute(x, axis, [(i, target(i, j, n)) for i in range(n)])  32.1 us
    pallas_call x10, Pallas kernels, call(): pl.pallas_call(kernel, out_shape=tuple((jax.ShapeDtypeStruct(s, d) for s,...  12.1 us
    ppermute x29, waiting for transfers between devices, hop(): return lax.ppermute(x, axis, [(i, target(i, j, n)) for i in range(n)])  11.3 us
  transfers between devices with their start and end apart: 29, of which 7 were waited for; matrix products, arithmetic and copies ran while one was open for 0% of the time, Pallas kernels for 15%

profile of v6, /device:TPU:0, one launch (start us, length us, event | category | flops | bytes accessed | tf_op | source)
XLA Modules:
  0.0 56.3 jit_solution(169688998600996065)
XLA Ops:
  0.6 1.9 %shard_map.94 = (bf16[4,256,512]{2,1,0:T(8,128)(2,1)S(1)}, f32[4,8,512]{2,1,0:T(8,128)S(1)}, bf16[4,32,512]{2,1,0:T(8,128)(2,1)S(1)}, bf16[4,32,512]{2,1,0:T(8,1...) custom-call(bf16[4,32,256]{2,1,0:T(8,128)(2,1)} %bitcast.7, ...), custom_call_target="tpu_custom_call" | custom-call | flops 134217728 | bytes 2097152 | tf_op jit(solution)/shard_map/pallas_call | solution.py:335
  2.5 5.1 %collective-permute-start = (bf16[4,32,512]{2,1,0:T(8,128)(2,1)S(1)}, bf16[4,32,512]{2,1,0:T(8,128)(2,1)S(1)}, u32[]{:S(2)}, u32[]{:S(2)}) collective-permute-start(bf16[4,32,512]{2,1,0:T(8,128)(2,1)S(1)} %get-tuple-element.35), channel_id=1, source_target_pairs={{0,3},{1,2},{2,1},{3,0},{4,7},{5,6},{6,5},{7,4},{8,11},{9,10},{10,... | collective-permute-start | bytes 393224 | tf_op jit(solution)/shard_map/ppermute | solution.py:41
  7.6 0.0 collective-permute-start.1
  7.6 0.6 %collective-permute-start.2 = (bf16[4,32,512]{2,1,0:T(8,128)(2,1)S(1)}, bf16[4,32,512]{2,1,0:T(8,128)(2,1)S(1)}, u32[]{:S(2)}, u32[]{:S(2)}) collective-permute-start(bf16[4,32,512]{2,1,0:T(8,128)(2,1)S(1)} %get-tuple-element.37), channel_id=1, source_target_pairs={{0,2},{1,3},{2,0},{3,1},{4,6},{5,7},{6,4},{7,5},{8,10},{9,11},{10,... | collective-permute-start | bytes 393224 | tf_op jit(solution)/shard_map/ppermute | solution.py:41
  8.3 3.8 %shard_map.95 = (bf16[4,512,512]{2,1,0:T(8,128)(2,1)S(1)}, bf16[5,320,512]{2,1,0:T(8,128)(2,1)S(1)}, bf16[640,256]{1,0:T(8,128)(2,1)S(1)}, bf16[96,512]{1,0:T(8,128)(2,1)S(1)}) custom-call(bf16[4,512,512]{2,1,0:T(8,128)(2,1)} %l_any.1, f32[4,64,512]{2,1,0:T(8,128)} %diag_ref.3, f32[64,512]{1,0:T(8,128)} %top_any.1, bf16[32,512]{1,0:T(8,128)(2,1)} %bitcast.8, ...), custom_call_target="tpu_custom_call" | custom-call | flops 402653184 | bytes 4194304 | tf_op jit(solution)/shard_map/pallas_call | solution.py:335
  12.1 2.7 %collective-permute-start.3 = (bf16[96,512]{1,0:T(8,128)(2,1)S(1)}, bf16[96,512]{1,0:T(8,128)(2,1)S(1)}, u32[]{:S(2)}, u32[]{:S(2)}) collective-permute-start(bf16[96,512]{1,0:T(8,128)(2,1)S(1)} %get-tuple-element.32.joined_ref.refs_0_), channel_id=1, source_target_pairs={{0,24},{4,28},{8,16},{12,20},{16,8},{20,12},{24,0},{28,4},{1,25},{... | collective-permute-start | bytes 294920 | tf_op jit(solution)/shard_map/ppermute | solution.py:41
  14.7 0.5 collective-permute-start.4
  15.2 0.0 collective-permute-done.refs_0_
  15.2 0.4 collective-permute-start.5
  15.6 0.0 collective-permute-done.1.refs_1_
  15.6 0.0 collective-permute-start.6
  15.6 3.1 %collective-permute-done.2.refs_2_ = bf16[4,32,512]{2,1,0:T(8,128)(2,1)S(1)} collective-permute-done((bf16[4,32,512]{2,1,0:T(8,128)(2,1)S(1)}, bf16[4,32,512]{2,1,0:T(8,128)(2,1)S(1)}, u32[]{:S(2)}, u32[]{:S(2)}) %collective-permute-start.2) | collective-permute-done | bytes 131104 | tf_op jit(solution)/shard_map/ppermute | solution.py:41
  18.7 1.4 %shard_map.96 = (bf16[4,32,512]{2,1,0:T(8,128)(2,1)S(1)}, bf16[4,32,512]{2,1,0:T(8,128)(2,1)}) custom-call(bf16[4,512,512]{2,1,0:T(8,128)(2,1)S(1)} %get-tuple-element.31.l_ref, bf16[96,512]{1,0:T(8,128)(2,1)S(1)} %get-tuple-element.32.joined_ref.refs_0_, f32[4,8,512]{2,1,0:T(8,128)S(1)} %get-tuple-element.33.mask_ref, ...), custom_call_target="tpu_custom_call" | custom-call | flops 67108864 | bytes 2097152 | tf_op jit(solution)/shard_map/pallas_call | solution.py:335
  20.1 2.5 %collective-permute-start.10 = (bf16[4,32,512]{2,1,0:T(8,128)(2,1)S(1)}, bf16[4,32,512]{2,1,0:T(8,128)(2,1)S(1)}, u32[]{:S(2)}, u32[]{:S(2)}) collective-permute-start(bf16[4,32,512]{2,1,0:T(8,128)(2,1)S(1)} %get-tuple-element.43.refs_0_), channel_id=1, source_target_pairs={{0,24},{4,28},{8,16},{12,20},{16,8},{20,12},{24,0},{28,4},{1,25},{... | collective-permute-start | bytes 393224 | tf_op jit(solution)/shard_map/ppermute | solution.py:41
  22.5 0.0 collective-permute-done.3.refs_1_
  22.5 0.5 collective-permute-start.11
  23.0 0.0 collective-permute-done.4.refs_2_
  23.0 0.5 collective-permute-start.12
  23.6 0.0 collective-permute-done.5.refs_3_
  23.6 0.0 collective-permute-start.7
  23.6 0.0 collective-permute-done.6.refs_4_
  23.6 0.5 collective-permute-start.8
  24.1 0.8 %collective-permute-done.7.refs_5_ = bf16[96,512]{1,0:T(8,128)(2,1)S(1)} collective-permute-done((bf16[96,512]{1,0:T(8,128)(2,1)S(1)}, bf16[96,512]{1,0:T(8,128)(2,1)S(1)}, u32[]{:S(2)}, u32[]{:S(2)}) %collective-permute-start.7) | collective-permute-done | bytes 98336 | tf_op jit(solution)/shard_map/ppermute | solution.py:41
  24.9 0.2 collective-permute-start.9
  25.0 0.0 collective-permute-done.8.refs_6_
  25.0 0.4 collective-permute-start.13
  25.4 1.4 %collective-permute-done.10.refs_1_ = bf16[4,32,512]{2,1,0:T(8,128)(2,1)S(1)} collective-permute-done((bf16[4,32,512]{2,1,0:T(8,128)(2,1)S(1)}, bf16[4,32,512]{2,1,0:T(8,128)(2,1)S(1)}, u32[]{:S(2)}, u32[]{:S(2)}) %collective-permute-start.10) | collective-permute-done | bytes 131104 | tf_op jit(solution)/shard_map/ppermute | solution.py:41
  26.7 0.0 collective-permute-start.14
  26.7 1.6 %collective-permute-done.11.refs_2_ = bf16[4,32,512]{2,1,0:T(8,128)(2,1)S(1)} collective-permute-done((bf16[4,32,512]{2,1,0:T(8,128)(2,1)S(1)}, bf16[4,32,512]{2,1,0:T(8,128)(2,1)S(1)}, u32[]{:S(2)}, u32[]{:S(2)}) %collective-permute-start.11) | collective-permute-done | bytes 131104 | tf_op jit(solution)/shard_map/ppermute | solution.py:41
  28.3 0.0 collective-permute-start.15
  28.3 0.1 collective-permute-done.12.refs_3_
  28.4 0.4 collective-permute-start.16
  28.8 0.0 collective-permute-done.9.refs_7_
  28.8 1.2 %shard_map.97 = (f32[320,512]{1,0:T(8,128)S(1)}, f32[320,512]{1,0:T(8,128)S(1)}) custom-call(bf16[4,512,512]{2,1,0:T(8,128)(2,1)S(1)} %get-tuple-element.31.l_ref, bf16[4,256,512]{2,1,0:T(8,128)(2,1)S(1)} %get-tuple-element.30.panel_ref, bf16[5,320,512]{2,1,0:T(8,128)(2,1)S(1)} %get-tuple-element.39.stacks_ref, ...), custom_call_target="tpu_custom_call" | custom-call | flops 503316480 | bytes 1048576 | tf_op jit(solution)/shard_map/pallas_call | solution.py:335
  30.1 0.0 collective-permute-done.13.refs_4_
  30.1 0.0 collective-permute-done.14.refs_5_
  30.1 0.0 collective-permute-done.15.refs_6_
  30.1 0.0 collective-permute-done.16.refs_7_
  30.1 1.0 %shard_map.98 = (bf16[4,16,512]{2,1,0:T(8,128)(2,1)S(1)}, bf16[4,16,512]{2,1,0:T(8,128)(2,1)S(1)}, bf16[4,16,512]{2,1,0:T(8,128)(2,1)S(1)}, bf16[4,16,512]{2,1,0:T(8,128)(2,1)S(1)}, f32[192,512]{1,0:T(8,128)S(1)}) custom-call(bf16[4,512,512]{2,1,0:T(8,128)(2,1)S(1)} %get-tuple-element.31.l_ref, bf16[4,256,512]{2,1,0:T(8,128)(2,1)S(1)} %get-tuple-element.30.panel_ref, ...), custom_call_target="tpu_custom_call" | custom-call | flops 335544320 | bytes 4194304 | tf_op jit(solution)/shard_map/pallas_call | solution.py:335
  31.1 2.2 %collective-permute-start.23 = (bf16[4,16,512]{2,1,0:T(8,128)(2,1)S(1)}, bf16[4,16,512]{2,1,0:T(8,128)(2,1)S(1)}, u32[]{:S(2)}, u32[]{:S(2)}) collective-permute-start(bf16[4,16,512]{2,1,0:T(8,128)(2,1)S(1)} %get-tuple-element.50), channel_id=1, source_target_pairs={{0,3},{1,2},{2,1},{3,0},{4,7},{5,6},{6,5},{7,4},{8,11},{9,10},{10,... | collective-permute-start | bytes 196616 | tf_op jit(solution)/shard_map/ppermute | solution.py:41
  33.3 0.0 collective-permute-start.24
  33.3 2.2 %collective-permute-start.25 = (bf16[4,16,512]{2,1,0:T(8,128)(2,1)S(1)}, bf16[4,16,512]{2,1,0:T(8,128)(2,1)S(1)}, u32[]{:S(2)}, u32[]{:S(2)}) collective-permute-start(bf16[4,16,512]{2,1,0:T(8,128)(2,1)S(1)} %get-tuple-element.52), channel_id=1, source_target_pairs={{0,1},{1,0},{2,3},{3,2},{4,5},{5,4},{6,7},{7,6},{8,9},{9,8},{10,11... | collective-permute-start | bytes 196616 | tf_op jit(solution)/shard_map/ppermute | solution.py:41
  35.5 1.0 %shard_map.99 = (bf16[4,16,512]{2,1,0:T(8,128)(2,1)S(1)}, bf16[4,16,512]{2,1,0:T(8,128)(2,1)S(1)}, bf16[4,16,512]{2,1,0:T(8,128)(2,1)S(1)}, bf16[4,16,512]{2,1,0:T(8,128)(2,1)S(1)}) custom-call(bf16[4,512,512]{2,1,0:T(8,128)(2,1)S(1)} %get-tuple-element.31.l_ref, bf16[4,256,512]{2,1,0:T(8,128)(2,1)S(1)} %get-tuple-element.30.panel_ref, ...), custom_call_target="tpu_custom_call" | custom-call | flops 335544320 | bytes 4194304 | tf_op jit(solution)/shard_map/pallas_call | solution.py:335
  36.6 2.3 %collective-permute-start.17 = (bf16[4,16,512]{2,1,0:T(8,128)(2,1)S(1)}, bf16[4,16,512]{2,1,0:T(8,128)(2,1)S(1)}, u32[]{:S(2)}, u32[]{:S(2)}) collective-permute-start(bf16[4,16,512]{2,1,0:T(8,128)(2,1)S(1)} %get-tuple-element.46), channel_id=1, source_target_pairs={{0,3},{1,2},{2,1},{3,0},{4,7},{5,6},{6,5},{7,4},{8,11},{9,10},{10,... | collective-permute-start | bytes 196616 | tf_op jit(solution)/shard_map/ppermute | solution.py:41
  38.8 0.0 collective-permute-start.18
  38.9 0.0 collective-permute-done.23.refs_0_
  38.9 2.2 %collective-permute-start.19 = (bf16[4,16,512]{2,1,0:T(8,128)(2,1)S(1)}, bf16[4,16,512]{2,1,0:T(8,128)(2,1)S(1)}, u32[]{:S(2)}, u32[]{:S(2)}) collective-permute-start(bf16[4,16,512]{2,1,0:T(8,128)(2,1)S(1)} %get-tuple-element.48), channel_id=1, source_target_pairs={{0,1},{1,0},{2,3},{3,2},{4,5},{5,4},{6,7},{7,6},{8,9},{9,8},{10,11... | collective-permute-start | bytes 196616 | tf_op jit(solution)/shard_map/ppermute | solution.py:41
  41.1 0.0 collective-permute-done.24.refs_1_
  41.1 0.0 collective-permute-done.25.refs_2_
  41.1 0.1 collective-permute-start.26
  41.2 2.7 %collective-permute-start.27 = (bf16[4,16,512]{2,1,0:T(8,128)(2,1)S(1)}, bf16[4,16,512]{2,1,0:T(8,128)(2,1)S(1)}, u32[]{:S(2)}, u32[]{:S(2)}) collective-permute-start(bf16[4,16,512]{2,1,0:T(8,128)(2,1)S(1)} %shard_map.101.refs_0_), channel_id=1, source_target_pairs={{0,2},{1,3},{2,0},{3,1},{4,6},{5,7},{6,4},{7,5},{8,10},{9,11},{10,... | collective-permute-start | bytes 196616 | tf_op jit(solution)/shard_map/ppermute | solution.py:41
  43.9 0.0 collective-permute-done.17.refs_0_
  43.9 1.7 %collective-permute-start.28 = (bf16[4,16,512]{2,1,0:T(8,128)(2,1)S(1)}, bf16[4,16,512]{2,1,0:T(8,128)(2,1)S(1)}, u32[]{:S(2)}, u32[]{:S(2)}) collective-permute-start(bf16[4,16,512]{2,1,0:T(8,128)(2,1)S(1)} %shard_map.101.refs_0_), channel_id=1, source_target_pairs={{0,3},{1,2},{2,1},{3,0},{4,7},{5,6},{6,5},{7,4},{8,11},{9,10},{10,... | collective-permute-start | bytes 196616 | tf_op jit(solution)/shard_map/ppermute | solution.py:41
  45.6 0.6 %collective-permute-done.18.refs_1_ = bf16[4,16,512]{2,1,0:T(8,128)(2,1)S(1)} collective-permute-done((bf16[4,16,512]{2,1,0:T(8,128)(2,1)S(1)}, bf16[4,16,512]{2,1,0:T(8,128)(2,1)S(1)}, u32[]{:S(2)}, u32[]{:S(2)}) %collective-permute-start.18) | collective-permute-done | bytes 65568 | tf_op jit(solution)/shard_map/ppermute | solution.py:41
  46.3 0.0 collective-permute-done.19.refs_2_
  46.3 0.4 collective-permute-start.20
  46.7 2.5 %collective-permute-start.21 = (bf16[4,16,512]{2,1,0:T(8,128)(2,1)S(1)}, bf16[4,16,512]{2,1,0:T(8,128)(2,1)S(1)}, u32[]{:S(2)}, u32[]{:S(2)}) collective-permute-start(bf16[4,16,512]{2,1,0:T(8,128)(2,1)S(1)} %shard_map.100.refs_0_), channel_id=1, source_target_pairs={{0,2},{1,3},{2,0},{3,1},{4,6},{5,7},{6,4},{7,5},{8,10},{9,11},{10,... | collective-permute-start | bytes 196616 | tf_op jit(solution)/shard_map/ppermute | solution.py:41
  49.2 0.0 collective-permute-done.26.refs_1_
  49.2 1.6 %collective-permute-start.22 = (bf16[4,16,512]{2,1,0:T(8,128)(2,1)S(1)}, bf16[4,16,512]{2,1,0:T(8,128)(2,1)S(1)}, u32[]{:S(2)}, u32[]{:S(2)}) collective-permute-start(bf16[4,16,512]{2,1,0:T(8,128)(2,1)S(1)} %shard_map.100.refs_0_), channel_id=1, source_target_pairs={{0,3},{1,2},{2,1},{3,0},{4,7},{5,6},{6,5},{7,4},{8,11},{9,10},{10,... | collective-permute-start | bytes 196616 | tf_op jit(solution)/shard_map/ppermute | solution.py:41
  50.8 0.0 collective-permute-done.27.refs_2_
  50.8 0.9 %shard_map.102 = (f32[4,64,512]{2,1,0:T(8,128)}, f32[4,64,512]{2,1,0:T(8,128)}) custom-call(f32[4,64,512]{2,1,0:T(8,128)S(1)} %copy-done, bf16[4,16,512]{2,1,0:T(8,128)(2,1)S(1)} %shard_map.101.refs_0_, bf16[4,16,512]{2,1,0:T(8,128)(2,1)S(1)} %collective-permute-done.26.refs_1_, bf16[4,16,512]{2,1,0:T(8,128)(2,1)S(1)} %collective-permute-done.27.refs_2_, ...), custom_call_target="tpu_custom_call" | custom-call | tf_op jit(solution)/shard_map/pallas_call | solution.py:335
  51.7 0.0 collective-permute-done.20.refs_1_
  51.7 3.7 %collective-permute-done.21.refs_2_ = bf16[4,16,512]{2,1,0:T(8,128)(2,1)S(1)} collective-permute-done((bf16[4,16,512]{2,1,0:T(8,128)(2,1)S(1)}, bf16[4,16,512]{2,1,0:T(8,128)(2,1)S(1)}, u32[]{:S(2)}, u32[]{:S(2)}) %collective-permute-start.21) | collective-permute-done | bytes 65568 | tf_op jit(solution)/shard_map/ppermute | solution.py:41
  55.4 0.9 %shard_map.103 = (f32[4,64,512]{2,1,0:T(8,128)}, f32[4,64,512]{2,1,0:T(8,128)}) custom-call(f32[4,64,512]{2,1,0:T(8,128)S(1)} %copy-done, bf16[4,16,512]{2,1,0:T(8,128)(2,1)S(1)} %shard_map.100.refs_0_, bf16[4,16,512]{2,1,0:T(8,128)(2,1)S(1)} %collective-permute-done.20.refs_1_, ...), custom_call_target="tpu_custom_call", output_to_operand_aliasing={{0}: (5, {}), {1}: (6, {})} | custom-call | tf_op jit(solution)/shard_map/pallas_call | solution.py:335
  (6 shorter events, 0.1 us)
Async XLA Ops:
  2.5 12.7 %collective-permute-start = (bf16[4,32,512]{2,1,0:T(8,128)(2,1)S(1)}, bf16[4,32,512]{2,1,0:T(8,128)(2,1)S(1)}, u32[]{:S(2)}, u32[]{:S(2)}) collective-permute-start(bf16[4,32,512]{2,1,0:T(8,128)(2,1)S(1)} %get-tuple-element.35), channel_id=1, source_target_pairs={{0,3},{1,2},{2,1},{3,0},{4,7},{5,6},{6,5},{7,4},{8,11},{9,10},{10,... | collective-permute-start | bytes 393224 | tf_op jit(solution)/shard_map/ppermute | solution.py:41
  7.6 8.0 %collective-permute-start.1 = (bf16[4,32,512]{2,1,0:T(8,128)(2,1)S(1)}, bf16[4,32,512]{2,1,0:T(8,128)(2,1)S(1)}, u32[]{:S(2)}, u32[]{:S(2)}) collective-permute-start(bf16[4,32,512]{2,1,0:T(8,128)(2,1)S(1)} %get-tuple-element.36), channel_id=1, source_target_pairs={{0,1},{1,0},{2,3},{3,2},{4,5},{5,4},{6,7},{7,6},{8,9},{9,8},{10,11... | collective-permute-start | bytes 393224 | tf_op jit(solution)/shard_map/ppermute | solution.py:41
  7.6 11.1 %collective-permute-start.2 = (bf16[4,32,512]{2,1,0:T(8,128)(2,1)S(1)}, bf16[4,32,512]{2,1,0:T(8,128)(2,1)S(1)}, u32[]{:S(2)}, u32[]{:S(2)}) collective-permute-start(bf16[4,32,512]{2,1,0:T(8,128)(2,1)S(1)} %get-tuple-element.37), channel_id=1, source_target_pairs={{0,2},{1,3},{2,0},{3,1},{4,6},{5,7},{6,4},{7,5},{8,10},{9,11},{10,... | collective-permute-start | bytes 393224 | tf_op jit(solution)/shard_map/ppermute | solution.py:41
  12.1 10.5 %collective-permute-start.3 = (bf16[96,512]{1,0:T(8,128)(2,1)S(1)}, bf16[96,512]{1,0:T(8,128)(2,1)S(1)}, u32[]{:S(2)}, u32[]{:S(2)}) collective-permute-start(bf16[96,512]{1,0:T(8,128)(2,1)S(1)} %get-tuple-element.32.joined_ref.refs_0_), channel_id=1, source_target_pairs={{0,24},{4,28},{8,16},{12,20},{16,8},{20,12},{24,0},{28,4},{1,25},{... | collective-permute-start | bytes 294920 | tf_op jit(solution)/shard_map/ppermute | solution.py:41
  14.7 8.3 %collective-permute-start.4 = (bf16[96,512]{1,0:T(8,128)(2,1)S(1)}, bf16[96,512]{1,0:T(8,128)(2,1)S(1)}, u32[]{:S(2)}, u32[]{:S(2)}) collective-permute-start(bf16[96,512]{1,0:T(8,128)(2,1)S(1)} %get-tuple-element.32.joined_ref.refs_0_), channel_id=1, source_target_pairs={{0,16},{4,20},{8,24},{12,28},{16,0},{20,4},{24,8},{28,12},{1,17},{... | collective-permute-start | bytes 294920 | tf_op jit(solution)/shard_map/ppermute | solution.py:41
  15.2 8.3 %collective-permute-start.5 = (bf16[96,512]{1,0:T(8,128)(2,1)S(1)}, bf16[96,512]{1,0:T(8,128)(2,1)S(1)}, u32[]{:S(2)}, u32[]{:S(2)}) collective-permute-start(bf16[96,512]{1,0:T(8,128)(2,1)S(1)} %get-tuple-element.32.joined_ref.refs_0_), channel_id=1, source_target_pairs={{0,8},{4,12},{8,0},{12,4},{16,24},{20,28},{24,16},{28,20},{1,9},{5... | collective-permute-start | bytes 294920 | tf_op jit(solution)/shard_map/ppermute | solution.py:41
  15.6 7.9 %collective-permute-start.6 = (bf16[96,512]{1,0:T(8,128)(2,1)S(1)}, bf16[96,512]{1,0:T(8,128)(2,1)S(1)}, u32[]{:S(2)}, u32[]{:S(2)}) collective-permute-start(bf16[96,512]{1,0:T(8,128)(2,1)S(1)} %get-tuple-element.32.joined_ref.refs_0_), channel_id=1, source_target_pairs={{0,4},{4,0},{8,12},{12,8},{16,20},{20,16},{24,28},{28,24},{1,5},{5... | collective-permute-start | bytes 294920 | tf_op jit(solution)/shard_map/ppermute | solution.py:41
  20.1 6.7 %collective-permute-start.10 = (bf16[4,32,512]{2,1,0:T(8,128)(2,1)S(1)}, bf16[4,32,512]{2,1,0:T(8,128)(2,1)S(1)}, u32[]{:S(2)}, u32[]{:S(2)}) collective-permute-start(bf16[4,32,512]{2,1,0:T(8,128)(2,1)S(1)} %get-tuple-element.43.refs_0_), channel_id=1, source_target_pairs={{0,24},{4,28},{8,16},{12,20},{16,8},{20,12},{24,0},{28,4},{1,25},{... | collective-permute-start | bytes 393224 | tf_op jit(solution)/shard_map/ppermute | solution.py:41
  22.5 5.8 %collective-permute-start.11 = (bf16[4,32,512]{2,1,0:T(8,128)(2,1)S(1)}, bf16[4,32,512]{2,1,0:T(8,128)(2,1)S(1)}, u32[]{:S(2)}, u32[]{:S(2)}) collective-permute-start(bf16[4,32,512]{2,1,0:T(8,128)(2,1)S(1)} %get-tuple-element.43.refs_0_), channel_id=1, source_target_pairs={{0,16},{4,20},{8,24},{12,28},{16,0},{20,4},{24,8},{28,12},{1,17},{... | collective-permute-start | bytes 393224 | tf_op jit(solution)/shard_map/ppermute | solution.py:41
  23.0 5.4 %collective-permute-start.12 = (bf16[4,32,512]{2,1,0:T(8,128)(2,1)S(1)}, bf16[4,32,512]{2,1,0:T(8,128)(2,1)S(1)}, u32[]{:S(2)}, u32[]{:S(2)}) collective-permute-start(bf16[4,32,512]{2,1,0:T(8,128)(2,1)S(1)} %get-tuple-element.43.refs_0_), channel_id=1, source_target_pairs={{0,8},{4,12},{8,0},{12,4},{16,24},{20,28},{24,16},{28,20},{1,9},{5... | collective-permute-start | bytes 393224 | tf_op jit(solution)/shard_map/ppermute | solution.py:41
  23.6 1.3 %collective-permute-start.7 = (bf16[96,512]{1,0:T(8,128)(2,1)S(1)}, bf16[96,512]{1,0:T(8,128)(2,1)S(1)}, u32[]{:S(2)}, u32[]{:S(2)}) collective-permute-start(bf16[96,512]{1,0:T(8,128)(2,1)S(1)} %collective-permute-done.3.refs_1_), channel_id=1, source_target_pairs={{0,4},{4,0},{8,12},{12,8},{16,20},{20,16},{24,28},{28,24},{1,5},{5... | collective-permute-start | bytes 294920 | tf_op jit(solution)/shard_map/ppermute | solution.py:41
  23.6 1.5 %collective-permute-start.8 = (bf16[96,512]{1,0:T(8,128)(2,1)S(1)}, bf16[96,512]{1,0:T(8,128)(2,1)S(1)}, u32[]{:S(2)}, u32[]{:S(2)}) collective-permute-start(bf16[96,512]{1,0:T(8,128)(2,1)S(1)} %collective-permute-done.4.refs_2_), channel_id=1, source_target_pairs={{0,4},{4,0},{8,12},{12,8},{16,20},{20,16},{24,28},{28,24},{1,5},{5... | collective-permute-start | bytes 294920 | tf_op jit(solution)/shard_map/ppermute | solution.py:41
  24.9 4.0 %collective-permute-start.9 = (bf16[96,512]{1,0:T(8,128)(2,1)S(1)}, bf16[96,512]{1,0:T(8,128)(2,1)S(1)}, u32[]{:S(2)}, u32[]{:S(2)}) collective-permute-start(bf16[96,512]{1,0:T(8,128)(2,1)S(1)} %collective-permute-done.5.refs_3_), channel_id=1, source_target_pairs={{0,4},{4,0},{8,12},{12,8},{16,20},{20,16},{24,28},{28,24},{1,5},{5... | collective-permute-start | bytes 294920 | tf_op jit(solution)/shard_map/ppermute | solution.py:41
  25.0 5.1 %collective-permute-start.13 = (bf16[4,32,512]{2,1,0:T(8,128)(2,1)S(1)}, bf16[4,32,512]{2,1,0:T(8,128)(2,1)S(1)}, u32[]{:S(2)}, u32[]{:S(2)}) collective-permute-start(bf16[4,32,512]{2,1,0:T(8,128)(2,1)S(1)} %get-tuple-element.43.refs_0_), channel_id=1, source_target_pairs={{0,4},{4,0},{8,12},{12,8},{16,20},{20,16},{24,28},{28,24},{1,5},{5... | collective-permute-start | bytes 393224 | tf_op jit(solution)/shard_map/ppermute | solution.py:41
  26.7 3.4 %collective-permute-start.14 = (bf16[4,32,512]{2,1,0:T(8,128)(2,1)S(1)}, bf16[4,32,512]{2,1,0:T(8,128)(2,1)S(1)}, u32[]{:S(2)}, u32[]{:S(2)}) collective-permute-start(bf16[4,32,512]{2,1,0:T(8,128)(2,1)S(1)} %collective-permute-done.10.refs_1_), channel_id=1, source_target_pairs={{0,4},{4,0},{8,12},{12,8},{16,20},{20,16},{24,28},{28,24},{1,5},{5... | collective-permute-start | bytes 393224 | tf_op jit(solution)/shard_map/ppermute | solution.py:41
  28.3 1.8 %collective-permute-start.15 = (bf16[4,32,512]{2,1,0:T(8,128)(2,1)S(1)}, bf16[4,32,512]{2,1,0:T(8,128)(2,1)S(1)}, u32[]{:S(2)}, u32[]{:S(2)}) collective-permute-start(bf16[4,32,512]{2,1,0:T(8,128)(2,1)S(1)} %collective-permute-done.11.refs_2_), channel_id=1, source_target_pairs={{0,4},{4,0},{8,12},{12,8},{16,20},{20,16},{24,28},{28,24},{1,5},{5... | collective-permute-start | bytes 393224 | tf_op jit(solution)/shard_map/ppermute | solution.py:41
  28.4 1.7 %collective-permute-start.16 = (bf16[4,32,512]{2,1,0:T(8,128)(2,1)S(1)}, bf16[4,32,512]{2,1,0:T(8,128)(2,1)S(1)}, u32[]{:S(2)}, u32[]{:S(2)}) collective-permute-start(bf16[4,32,512]{2,1,0:T(8,128)(2,1)S(1)} %collective-permute-done.12.refs_3_), channel_id=1, source_target_pairs={{0,4},{4,0},{8,12},{12,8},{16,20},{20,16},{24,28},{28,24},{1,5},{5... | collective-permute-start | bytes 393224 | tf_op jit(solution)/shard_map/ppermute | solution.py:41
  31.1 7.8 %collective-permute-start.23 = (bf16[4,16,512]{2,1,0:T(8,128)(2,1)S(1)}, bf16[4,16,512]{2,1,0:T(8,128)(2,1)S(1)}, u32[]{:S(2)}, u32[]{:S(2)}) collective-permute-start(bf16[4,16,512]{2,1,0:T(8,128)(2,1)S(1)} %get-tuple-element.50), channel_id=1, source_target_pairs={{0,3},{1,2},{2,1},{3,0},{4,7},{5,6},{6,5},{7,4},{8,11},{9,10},{10,... | collective-permute-start | bytes 196616 | tf_op jit(solution)/shard_map/ppermute | solution.py:41
  33.3 7.7 %collective-permute-start.24 = (bf16[4,16,512]{2,1,0:T(8,128)(2,1)S(1)}, bf16[4,16,512]{2,1,0:T(8,128)(2,1)S(1)}, u32[]{:S(2)}, u32[]{:S(2)}) collective-permute-start(bf16[4,16,512]{2,1,0:T(8,128)(2,1)S(1)} %get-tuple-element.51), channel_id=1, source_target_pairs={{0,2},{1,3},{2,0},{3,1},{4,6},{5,7},{6,4},{7,5},{8,10},{9,11},{10,... | collective-permute-start | bytes 196616 | tf_op jit(solution)/shard_map/ppermute | solution.py:41
  33.3 7.7 %collective-permute-start.25 = (bf16[4,16,512]{2,1,0:T(8,128)(2,1)S(1)}, bf16[4,16,512]{2,1,0:T(8,128)(2,1)S(1)}, u32[]{:S(2)}, u32[]{:S(2)}) collective-permute-start(bf16[4,16,512]{2,1,0:T(8,128)(2,1)S(1)} %get-tuple-element.52), channel_id=1, source_target_pairs={{0,1},{1,0},{2,3},{3,2},{4,5},{5,4},{6,7},{7,6},{8,9},{9,8},{10,11... | collective-permute-start | bytes 196616 | tf_op jit(solution)/shard_map/ppermute | solution.py:41
  35.5 15.2 %copy-start = (f32[4,64,512]{2,1,0:T(8,128)S(1)}, f32[4,64,512]{2,1,0:T(8,128)}, u32[]{:S(2)}) copy-start(f32[4,64,512]{2,1,0:T(8,128)} %diag_ref.3) | copy-start | bytes 1572868
  36.6 7.3 %collective-permute-start.17 = (bf16[4,16,512]{2,1,0:T(8,128)(2,1)S(1)}, bf16[4,16,512]{2,1,0:T(8,128)(2,1)S(1)}, u32[]{:S(2)}, u32[]{:S(2)}) collective-permute-start(bf16[4,16,512]{2,1,0:T(8,128)(2,1)S(1)} %get-tuple-element.46), channel_id=1, source_target_pairs={{0,3},{1,2},{2,1},{3,0},{4,7},{5,6},{6,5},{7,4},{8,11},{9,10},{10,... | collective-permute-start | bytes 196616 | tf_op jit(solution)/shard_map/ppermute | solution.py:41
  38.8 7.4 %collective-permute-start.18 = (bf16[4,16,512]{2,1,0:T(8,128)(2,1)S(1)}, bf16[4,16,512]{2,1,0:T(8,128)(2,1)S(1)}, u32[]{:S(2)}, u32[]{:S(2)}) collective-permute-start(bf16[4,16,512]{2,1,0:T(8,128)(2,1)S(1)} %get-tuple-element.47), channel_id=1, source_target_pairs={{0,2},{1,3},{2,0},{3,1},{4,6},{5,7},{6,4},{7,5},{8,10},{9,11},{10,... | collective-permute-start | bytes 196616 | tf_op jit(solution)/shard_map/ppermute | solution.py:41
  38.9 7.4 %collective-permute-start.19 = (bf16[4,16,512]{2,1,0:T(8,128)(2,1)S(1)}, bf16[4,16,512]{2,1,0:T(8,128)(2,1)S(1)}, u32[]{:S(2)}, u32[]{:S(2)}) collective-permute-start(bf16[4,16,512]{2,1,0:T(8,128)(2,1)S(1)} %get-tuple-element.48), channel_id=1, source_target_pairs={{0,1},{1,0},{2,3},{3,2},{4,5},{5,4},{6,7},{7,6},{8,9},{9,8},{10,11... | collective-permute-start | bytes 196616 | tf_op jit(solution)/shard_map/ppermute | solution.py:41
  41.1 8.1 %collective-permute-start.26 = (bf16[4,16,512]{2,1,0:T(8,128)(2,1)S(1)}, bf16[4,16,512]{2,1,0:T(8,128)(2,1)S(1)}, u32[]{:S(2)}, u32[]{:S(2)}) collective-permute-start(bf16[4,16,512]{2,1,0:T(8,128)(2,1)S(1)} %shard_map.101.refs_0_), channel_id=1, source_target_pairs={{0,1},{1,0},{2,3},{3,2},{4,5},{5,4},{6,7},{7,6},{8,9},{9,8},{10,11... | collective-permute-start | bytes 196616 | tf_op jit(solution)/shard_map/ppermute | solution.py:41
  41.2 9.6 %collective-permute-start.27 = (bf16[4,16,512]{2,1,0:T(8,128)(2,1)S(1)}, bf16[4,16,512]{2,1,0:T(8,128)(2,1)S(1)}, u32[]{:S(2)}, u32[]{:S(2)}) collective-permute-start(bf16[4,16,512]{2,1,0:T(8,128)(2,1)S(1)} %shard_map.101.refs_0_), channel_id=1, source_target_pairs={{0,2},{1,3},{2,0},{3,1},{4,6},{5,7},{6,4},{7,5},{8,10},{9,11},{10,... | collective-permute-start | bytes 196616 | tf_op jit(solution)/shard_map/ppermute | solution.py:41
  43.9 6.9 %collective-permute-start.28 = (bf16[4,16,512]{2,1,0:T(8,128)(2,1)S(1)}, bf16[4,16,512]{2,1,0:T(8,128)(2,1)S(1)}, u32[]{:S(2)}, u32[]{:S(2)}) collective-permute-start(bf16[4,16,512]{2,1,0:T(8,128)(2,1)S(1)} %shard_map.101.refs_0_), channel_id=1, source_target_pairs={{0,3},{1,2},{2,1},{3,0},{4,7},{5,6},{6,5},{7,4},{8,11},{9,10},{10,... | collective-permute-start | bytes 196616 | tf_op jit(solution)/shard_map/ppermute | solution.py:41
  46.3 5.3 %collective-permute-start.20 = (bf16[4,16,512]{2,1,0:T(8,128)(2,1)S(1)}, bf16[4,16,512]{2,1,0:T(8,128)(2,1)S(1)}, u32[]{:S(2)}, u32[]{:S(2)}) collective-permute-start(bf16[4,16,512]{2,1,0:T(8,128)(2,1)S(1)} %shard_map.100.refs_0_), channel_id=1, source_target_pairs={{0,1},{1,0},{2,3},{3,2},{4,5},{5,4},{6,7},{7,6},{8,9},{9,8},{10,11... | collective-permute-start | bytes 196616 | tf_op jit(solution)/shard_map/ppermute | solution.py:41
  46.7 8.7 %collective-permute-start.21 = (bf16[4,16,512]{2,1,0:T(8,128)(2,1)S(1)}, bf16[4,16,512]{2,1,0:T(8,128)(2,1)S(1)}, u32[]{:S(2)}, u32[]{:S(2)}) collective-permute-start(bf16[4,16,512]{2,1,0:T(8,128)(2,1)S(1)} %shard_map.100.refs_0_), channel_id=1, source_target_pairs={{0,2},{1,3},{2,0},{3,1},{4,6},{5,7},{6,4},{7,5},{8,10},{9,11},{10,... | collective-permute-start | bytes 196616 | tf_op jit(solution)/shard_map/ppermute | solution.py:41
  49.2 6.2 %collective-permute-start.22 = (bf16[4,16,512]{2,1,0:T(8,128)(2,1)S(1)}, bf16[4,16,512]{2,1,0:T(8,128)(2,1)S(1)}, u32[]{:S(2)}, u32[]{:S(2)}) collective-permute-start(bf16[4,16,512]{2,1,0:T(8,128)(2,1)S(1)} %shard_map.100.refs_0_), channel_id=1, source_target_pairs={{0,3},{1,2},{2,1},{3,0},{4,7},{5,6},{6,5},{7,4},{8,11},{9,10},{10,... | collective-permute-start | bytes 196616 | tf_op jit(solution)/shard_map/ppermute | solution.py:41

commit v7 on v6

--- a/solution.py
+++ b/solution.py
@@ -167,35 +167,36 @@
 def first_kernel(n_cols, n_rows, g_any, m_any, pattern_any, *refs):
     panel_ref, mask_ref = refs[:2]
     piece_refs = refs[2 : 2 + n_cols]
-    g_ref, m_ref, pattern_ref, sems = refs[2 + n_cols :]
+    g_ref, order_ref, m_ref, pattern_ref, sems = refs[2 + n_cols :]
     col, row = lax.axis_index("cols"), lax.axis_index("rows")
     supers, _, piece, _ = m_ref.shape
     pattern_copy = fetch(pattern_any, pattern_ref, sems.at[0])
-    g_copies = [fetch(g_any.at[col ^ j], g_ref.at[pl.ds(j * piece, piece)], sems.at[1 + supers + j]) for j in range(n_cols)]
-    panel_copies = [fetch(m_any.at[k], m_ref.at[k], sems.at[1 + k]) for k in range(supers)]
+    panel_copy = fetch(m_any, m_ref, sems.at[1])
+    g_copy = fetch(g_any, g_ref, sems.at[2])
+    g_copy.wait()
+    for j in range(n_cols):
+        order_ref[pl.ds(j * piece, piece)] = g_ref[col ^ j]
     pattern_copy.wait()
-    for copy in g_copies:
-        copy.wait()
+    panel_copy.wait()
     for k in range(supers):
         mask_ref[k] = jnp.full(mask_ref.shape[1:], pattern_ref[k, col * n_rows + row].astype(F32))
-        panel_copies[k].wait()
         for r in range(n_rows):
             on = pattern_ref[k, col * n_rows + r] != 0
             panel_ref[k, pl.ds(r * piece, piece)] = jnp.where(on, m_ref[k, r], jnp.zeros_like(m_ref[k, r]))
-        product = dot(g_ref[...], panel_ref[k]).astype(BF)
+        product = dot(order_ref[...], panel_ref[k]).astype(BF)
         for j, out in enumerate(piece_refs):
             out[k] = product[j * piece : (j + 1) * piece]
 
 
-def chain_kernel(l_ref, joined_ref, mask_ref, own_ref, *refs):
+def chain_kernel(l_ref, carry_ref, mask_ref, own_ref, *refs):
     *got_refs, cols_ref, copy_ref = refs
     supers, piece, _ = own_ref.shape
-    prev = joined_ref[pl.ds(joined_ref.shape[0] - piece, piece)]
+    carried = carry_ref[...]
     for k in reversed(range(supers)):
         total = own_ref[k].astype(F32)
         for got in got_refs:
             total = total + got[k].astype(F32)
-        total = total + dot(prev, l_ref[k])
+        total = total + (carried if k == supers - 1 else dot(prev, l_ref[k]))
         prev = (-(total * mask_ref[k, pl.ds(0, 1)])).astype(BF)
         cols_ref[k] = prev
         copy_ref[k] = prev
@@ -208,7 +209,7 @@
 
 
 def ready_kernel(n_cols, n_rows, l_any, diag_any, top_any, tops_any, panel_ref, *refs):
-    l_ref, stacks_ref, reach_ref, joined_ref, begin_ref, tops_ref, sems = refs
+    l_ref, stacks_ref, reach_ref, joined_ref, carry_ref, begin_ref, tops_ref, sems = refs
     supers, width, _ = l_ref.shape
     share, piece = width // n_rows, tops_ref.shape[0]
     col, row = lax.axis_index("cols"), lax.axis_index("rows")
@@ -242,6 +243,7 @@
         copies[k].wait()
         stack = jnp.concatenate([dot_nt(stack, l_ref[k]).astype(BF), unit], 0)
         stacks_ref[k + 1, pl.ds(0, (k + 2) * share)] = stack
+    carry_ref[...] = dot(tops_ref[...], l_ref[supers - 1])
 
 
 def place(refs, order, write):
@@ -368,15 +370,15 @@
         [((supers, block, width), BF), ((supers, 8, width), F32)] + [((supers, piece, width), BF)] * n_cols,
         known, lower_panel[:, 0], pattern, away=range(3),
         scratch=[
-            pltpu.VMEM((n_cols * piece, block), BF), pltpu.VMEM((supers, n_rows, piece, width), BF),
-            pltpu.SMEM(pattern.shape, jnp.int32), pltpu.SemaphoreType.DMA((1 + supers + n_cols,)),
+            pltpu.VMEM(known.shape, BF), pltpu.VMEM((n_cols * piece, block), BF), pltpu.VMEM((supers, n_rows, piece, width), BF),
+            pltpu.SMEM(pattern.shape, jnp.int32), pltpu.SemaphoreType.DMA((3,)),
         ],
         flops=2 * known.size * supers * width, moved=4 * block * width * supers,
     )
     got = [hop(sent[j - 1], "cols", j) for j in FIRST_ORDER]
-    links, stacks, reach, joined = call(
+    links, stacks, reach, joined, carry = call(
         functools.partial(ready_kernel, n_cols, n_rows),
-        [(chain_panel.shape, BF), ((supers + 1, rows_of[supers], width), BF), ((sum(rows_of[:supers]), block), BF), ((share + piece, width), BF)],
+        [(chain_panel.shape, BF), ((supers + 1, rows_of[supers], width), BF), ((sum(rows_of[:supers]), block), BF), ((share + piece, width), BF), ((piece, width), F32)],
         chain_panel, diag_inverse, top_diag, tops, panel, away=range(4),
         scratch=[pltpu.VMEM((share, width), F32), pltpu.VMEM((piece, width), BF), pltpu.SemaphoreType.DMA((supers + 2,))],
         flops=2 * 12 * share * width * width, moved=4 * width * width * supers,
@@ -391,7 +393,7 @@
     cols, cols_out = call(
         chain_kernel,
         [((supers, piece, width), BF)] * 2,
-        links, joined, mask, own, *got,
+        links, carry, mask, own, *got,
         flops=2 * piece * width * width * supers, moved=2 * width * width * supers,
     )
     arrived = exchange_rows(cols)

time: 56.4 us -> 56 us (level)
  no operation moved by 1% of the time
where the time goes in v7:
time: 56 us; the launch traced here: 55.8 us
  starting transfers between devices  32.1 us (57%)
  Pallas kernels  11.7 us (21%)
  waiting for transfers between devices  11.3 us (20%)
  between operations  0.76 us (1%)
    ppermute x29, starting transfers between devices, hop(): return lax.ppermute(x, axis, [(i, target(i, j, n)) for i in range(n)])  32.1 us
    pallas_call x10, Pallas kernels, call(): pl.pallas_call(kernel, out_shape=tuple((jax.ShapeDtypeStruct(s, d) for s,...  11.7 us
    ppermute x29, waiting for transfers between devices, hop(): return lax.ppermute(x, axis, [(i, target(i, j, n)) for i in range(n)])  11.3 us
  transfers between devices with their start and end apart: 29, of which 7 were waited for; matrix products, arithmetic and copies ran while one was open for 0% of the time, Pallas kernels for 15%

profile of v7, /device:TPU:0, one launch (start us, length us, event | category | flops | bytes accessed | tf_op | source)
XLA Modules:
  0.0 55.8 jit_solution(10939405021696649549)
XLA Ops:
  0.6 1.6 %shard_map.94 = (bf16[4,256,512]{2,1,0:T(8,128)(2,1)S(1)}, f32[4,8,512]{2,1,0:T(8,128)S(1)}, bf16[4,32,512]{2,1,0:T(8,128)(2,1)S(1)}, bf16[4,32,512]{2,1,0:T(8,1...) custom-call(bf16[4,32,256]{2,1,0:T(8,128)(2,1)} %bitcast.7, ...), custom_call_target="tpu_custom_call" | custom-call | flops 134217728 | bytes 2097152 | tf_op jit(solution)/shard_map/pallas_call | solution.py:337
  2.3 5.1 %collective-permute-start = (bf16[4,32,512]{2,1,0:T(8,128)(2,1)S(1)}, bf16[4,32,512]{2,1,0:T(8,128)(2,1)S(1)}, u32[]{:S(2)}, u32[]{:S(2)}) collective-permute-start(bf16[4,32,512]{2,1,0:T(8,128)(2,1)S(1)} %get-tuple-element.36), channel_id=1, source_target_pairs={{0,3},{1,2},{2,1},{3,0},{4,7},{5,6},{6,5},{7,4},{8,11},{9,10},{10,... | collective-permute-start | bytes 393224 | tf_op jit(solution)/shard_map/ppermute | solution.py:41
  7.4 0.0 collective-permute-start.1
  7.4 0.6 %collective-permute-start.2 = (bf16[4,32,512]{2,1,0:T(8,128)(2,1)S(1)}, bf16[4,32,512]{2,1,0:T(8,128)(2,1)S(1)}, u32[]{:S(2)}, u32[]{:S(2)}) collective-permute-start(bf16[4,32,512]{2,1,0:T(8,128)(2,1)S(1)} %get-tuple-element.38), channel_id=1, source_target_pairs={{0,2},{1,3},{2,0},{3,1},{4,6},{5,7},{6,4},{7,5},{8,10},{9,11},{10,... | collective-permute-start | bytes 393224 | tf_op jit(solution)/shard_map/ppermute | solution.py:41
  8.0 3.8 %shard_map.95 = (bf16[4,512,512]{2,1,0:T(8,128)(2,1)S(1)}, bf16[5,320,512]{2,1,0:T(8,128)(2,1)S(1)}, bf16[640,256]{1,0:T(8,128)(2,1)S(1)}, bf16[96,512]{1,0:T(8,128)(2,1)S(1)}, f32[32,512]{1,0:T(8,128)S(1)}) custom-call(bf16[4,512,512]{2,1,0:T(8,128)(2,1)} %l_any.1, f32[4,64,512]{2,1,0:T(8,128)} %diag_ref.3, f32[64,512]{1,0:T(8,128)} %top_any.1, ...), custom_call_target="tpu_custom_call" | custom-call | flops 402653184 | bytes 4194304 | tf_op jit(solution)/shard_map/pallas_call | solution.py:337
  11.9 2.7 %collective-permute-start.3 = (bf16[96,512]{1,0:T(8,128)(2,1)S(1)}, bf16[96,512]{1,0:T(8,128)(2,1)S(1)}, u32[]{:S(2)}, u32[]{:S(2)}) collective-permute-start(bf16[96,512]{1,0:T(8,128)(2,1)S(1)} %get-tuple-element.42.refs_0_), channel_id=1, source_target_pairs={{0,24},{4,28},{8,16},{12,20},{16,8},{20,12},{24,0},{28,4},{1,25},{... | collective-permute-start | bytes 294920 | tf_op jit(solution)/shard_map/ppermute | solution.py:41
  14.5 0.5 collective-permute-start.4
  15.0 0.0 collective-permute-done.refs_0_
  15.0 0.4 collective-permute-start.5
  15.4 0.0 collective-permute-done.1.refs_1_
  15.4 0.0 collective-permute-start.6
  15.4 3.0 %collective-permute-done.2.refs_2_ = bf16[4,32,512]{2,1,0:T(8,128)(2,1)S(1)} collective-permute-done((bf16[4,32,512]{2,1,0:T(8,128)(2,1)S(1)}, bf16[4,32,512]{2,1,0:T(8,128)(2,1)S(1)}, u32[]{:S(2)}, u32[]{:S(2)}) %collective-permute-start.2) | collective-permute-done | bytes 131104 | tf_op jit(solution)/shard_map/ppermute | solution.py:41
  18.5 1.2 %shard_map.96 = (bf16[4,32,512]{2,1,0:T(8,128)(2,1)S(1)}, bf16[4,32,512]{2,1,0:T(8,128)(2,1)}) custom-call(bf16[4,512,512]{2,1,0:T(8,128)(2,1)S(1)} %get-tuple-element.32.l_ref, f32[32,512]{1,0:T(8,128)S(1)} %get-tuple-element.33.carry_ref, f32[4,8,512]{2,1,0:T(8,128)S(1)} %get-tuple-element.34.mask_ref, bf16[4,32,512]{2,1,0:T(8,128)(2,1)S(1)} %get-tuple-element.35.own_ref, ...), custom_call_target="tpu_custom_call" | custom-call | flops 67108864 | bytes 2097152 | tf_op jit(solution)/shard_map/pallas_call | solution.py:337
  19.6 2.4 %collective-permute-start.10 = (bf16[4,32,512]{2,1,0:T(8,128)(2,1)S(1)}, bf16[4,32,512]{2,1,0:T(8,128)(2,1)S(1)}, u32[]{:S(2)}, u32[]{:S(2)}) collective-permute-start(bf16[4,32,512]{2,1,0:T(8,128)(2,1)S(1)} %get-tuple-element.45.refs_0_), channel_id=1, source_target_pairs={{0,24},{4,28},{8,16},{12,20},{16,8},{20,12},{24,0},{28,4},{1,25},{... | collective-permute-start | bytes 393224 | tf_op jit(solution)/shard_map/ppermute | solution.py:41
  22.1 0.0 collective-permute-done.3.refs_1_
  22.1 0.5 collective-permute-start.11
  22.6 0.0 collective-permute-done.4.refs_2_
  22.6 0.5 collective-permute-start.12
  23.1 0.0 collective-permute-done.5.refs_3_
  23.1 0.0 collective-permute-start.7
  23.1 0.0 collective-permute-done.6.refs_4_
  23.1 0.5 collective-permute-start.8
  23.6 0.8 %collective-permute-done.7.refs_5_ = bf16[96,512]{1,0:T(8,128)(2,1)S(1)} collective-permute-done((bf16[96,512]{1,0:T(8,128)(2,1)S(1)}, bf16[96,512]{1,0:T(8,128)(2,1)S(1)}, u32[]{:S(2)}, u32[]{:S(2)}) %collective-permute-start.7) | collective-permute-done | bytes 98336 | tf_op jit(solution)/shard_map/ppermute | solution.py:41
  24.4 0.2 collective-permute-start.9
  24.6 0.0 collective-permute-done.8.refs_6_
  24.6 0.4 collective-permute-start.13
  25.0 1.4 %collective-permute-done.10.refs_1_ = bf16[4,32,512]{2,1,0:T(8,128)(2,1)S(1)} collective-permute-done((bf16[4,32,512]{2,1,0:T(8,128)(2,1)S(1)}, bf16[4,32,512]{2,1,0:T(8,128)(2,1)S(1)}, u32[]{:S(2)}, u32[]{:S(2)}) %collective-permute-start.10) | collective-permute-done | bytes 131104 | tf_op jit(solution)/shard_map/ppermute | solution.py:41
  26.3 0.0 collective-permute-start.14
  26.3 1.6 %collective-permute-done.11.refs_2_ = bf16[4,32,512]{2,1,0:T(8,128)(2,1)S(1)} collective-permute-done((bf16[4,32,512]{2,1,0:T(8,128)(2,1)S(1)}, bf16[4,32,512]{2,1,0:T(8,128)(2,1)S(1)}, u32[]{:S(2)}, u32[]{:S(2)}) %collective-permute-start.11) | collective-permute-done | bytes 131104 | tf_op jit(solution)/shard_map/ppermute | solution.py:41
  27.9 0.0 collective-permute-start.15
  27.9 0.1 collective-permute-done.12.refs_3_
  28.0 0.4 collective-permute-start.16
  28.4 0.0 collective-permute-done.9.refs_7_
  28.4 1.2 %shard_map.97 = (f32[320,512]{1,0:T(8,128)S(1)}, f32[320,512]{1,0:T(8,128)S(1)}) custom-call(bf16[4,512,512]{2,1,0:T(8,128)(2,1)S(1)} %get-tuple-element.32.l_ref, bf16[4,256,512]{2,1,0:T(8,128)(2,1)S(1)} %get-tuple-element.31.panel_ref, bf16[5,320,512]{2,1,0:T(8,128)(2,1)S(1)} %get-tuple-element.40.stacks_ref, ...), custom_call_target="tpu_custom_call" | custom-call | flops 503316480 | bytes 1048576 | tf_op jit(solution)/shard_map/pallas_call | solution.py:337
  29.7 0.0 collective-permute-done.13.refs_4_
  29.7 0.0 collective-permute-done.14.refs_5_
  29.7 0.0 collective-permute-done.15.refs_6_
  29.7 0.0 collective-permute-done.16.refs_7_
  29.7 1.0 %shard_map.98 = (bf16[4,16,512]{2,1,0:T(8,128)(2,1)S(1)}, bf16[4,16,512]{2,1,0:T(8,128)(2,1)S(1)}, bf16[4,16,512]{2,1,0:T(8,128)(2,1)S(1)}, bf16[4,16,512]{2,1,0:T(8,128)(2,1)S(1)}, f32[192,512]{1,0:T(8,128)S(1)}) custom-call(bf16[4,512,512]{2,1,0:T(8,128)(2,1)S(1)} %get-tuple-element.32.l_ref, bf16[4,256,512]{2,1,0:T(8,128)(2,1)S(1)} %get-tuple-element.31.panel_ref, ...), custom_call_target="tpu_custom_call" | custom-call | flops 335544320 | bytes 4194304 | tf_op jit(solution)/shard_map/pallas_call | solution.py:337
  30.7 2.2 %collective-permute-start.23 = (bf16[4,16,512]{2,1,0:T(8,128)(2,1)S(1)}, bf16[4,16,512]{2,1,0:T(8,128)(2,1)S(1)}, u32[]{:S(2)}, u32[]{:S(2)}) collective-permute-start(bf16[4,16,512]{2,1,0:T(8,128)(2,1)S(1)} %get-tuple-element.52), channel_id=1, source_target_pairs={{0,3},{1,2},{2,1},{3,0},{4,7},{5,6},{6,5},{7,4},{8,11},{9,10},{10,... | collective-permute-start | bytes 196616 | tf_op jit(solution)/shard_map/ppermute | solution.py:41
  32.9 0.0 collective-permute-start.24
  32.9 2.2 %collective-permute-start.25 = (bf16[4,16,512]{2,1,0:T(8,128)(2,1)S(1)}, bf16[4,16,512]{2,1,0:T(8,128)(2,1)S(1)}, u32[]{:S(2)}, u32[]{:S(2)}) collective-permute-start(bf16[4,16,512]{2,1,0:T(8,128)(2,1)S(1)} %get-tuple-element.54), channel_id=1, source_target_pairs={{0,1},{1,0},{2,3},{3,2},{4,5},{5,4},{6,7},{7,6},{8,9},{9,8},{10,11... | collective-permute-start | bytes 196616 | tf_op jit(solution)/shard_map/ppermute | solution.py:41
  35.1 1.0 %shard_map.99 = (bf16[4,16,512]{2,1,0:T(8,128)(2,1)S(1)}, bf16[4,16,512]{2,1,0:T(8,128)(2,1)S(1)}, bf16[4,16,512]{2,1,0:T(8,128)(2,1)S(1)}, bf16[4,16,512]{2,1,0:T(8,128)(2,1)S(1)}) custom-call(bf16[4,512,512]{2,1,0:T(8,128)(2,1)S(1)} %get-tuple-element.32.l_ref, bf16[4,256,512]{2,1,0:T(8,128)(2,1)S(1)} %get-tuple-element.31.panel_ref, ...), custom_call_target="tpu_custom_call" | custom-call | flops 335544320 | bytes 4194304 | tf_op jit(solution)/shard_map/pallas_call | solution.py:337
  36.2 2.2 %collective-permute-start.17 = (bf16[4,16,512]{2,1,0:T(8,128)(2,1)S(1)}, bf16[4,16,512]{2,1,0:T(8,128)(2,1)S(1)}, u32[]{:S(2)}, u32[]{:S(2)}) collective-permute-start(bf16[4,16,512]{2,1,0:T(8,128)(2,1)S(1)} %get-tuple-element.48), channel_id=1, source_target_pairs={{0,3},{1,2},{2,1},{3,0},{4,7},{5,6},{6,5},{7,4},{8,11},{9,10},{10,... | collective-permute-start | bytes 196616 | tf_op jit(solution)/shard_map/ppermute | solution.py:41
  38.4 0.0 collective-permute-start.18
  38.4 0.0 collective-permute-done.23.refs_0_
  38.4 2.2 %collective-permute-start.19 = (bf16[4,16,512]{2,1,0:T(8,128)(2,1)S(1)}, bf16[4,16,512]{2,1,0:T(8,128)(2,1)S(1)}, u32[]{:S(2)}, u32[]{:S(2)}) collective-permute-start(bf16[4,16,512]{2,1,0:T(8,128)(2,1)S(1)} %get-tuple-element.50), channel_id=1, source_target_pairs={{0,1},{1,0},{2,3},{3,2},{4,5},{5,4},{6,7},{7,6},{8,9},{9,8},{10,11... | collective-permute-start | bytes 196616 | tf_op jit(solution)/shard_map/ppermute | solution.py:41
  40.6 0.0 collective-permute-done.24.refs_1_
  40.6 0.0 collective-permute-done.25.refs_2_
  40.7 0.1 collective-permute-start.26
  40.7 2.7 %collective-permute-start.27 = (bf16[4,16,512]{2,1,0:T(8,128)(2,1)S(1)}, bf16[4,16,512]{2,1,0:T(8,128)(2,1)S(1)}, u32[]{:S(2)}, u32[]{:S(2)}) collective-permute-start(bf16[4,16,512]{2,1,0:T(8,128)(2,1)S(1)} %shard_map.101.refs_0_), channel_id=1, source_target_pairs={{0,2},{1,3},{2,0},{3,1},{4,6},{5,7},{6,4},{7,5},{8,10},{9,11},{10,... | collective-permute-start | bytes 196616 | tf_op jit(solution)/shard_map/ppermute | solution.py:41
  43.5 0.0 collective-permute-done.17.refs_0_
  43.5 1.7 %collective-permute-start.28 = (bf16[4,16,512]{2,1,0:T(8,128)(2,1)S(1)}, bf16[4,16,512]{2,1,0:T(8,128)(2,1)S(1)}, u32[]{:S(2)}, u32[]{:S(2)}) collective-permute-start(bf16[4,16,512]{2,1,0:T(8,128)(2,1)S(1)} %shard_map.101.refs_0_), channel_id=1, source_target_pairs={{0,3},{1,2},{2,1},{3,0},{4,7},{5,6},{6,5},{7,4},{8,11},{9,10},{10,... | collective-permute-start | bytes 196616 | tf_op jit(solution)/shard_map/ppermute | solution.py:41
  45.2 0.7 %collective-permute-done.18.refs_1_ = bf16[4,16,512]{2,1,0:T(8,128)(2,1)S(1)} collective-permute-done((bf16[4,16,512]{2,1,0:T(8,128)(2,1)S(1)}, bf16[4,16,512]{2,1,0:T(8,128)(2,1)S(1)}, u32[]{:S(2)}, u32[]{:S(2)}) %collective-permute-start.18) | collective-permute-done | bytes 65568 | tf_op jit(solution)/shard_map/ppermute | solution.py:41
  45.8 0.0 collective-permute-done.19.refs_2_
  45.9 0.4 collective-permute-start.20
  46.3 2.4 %collective-permute-start.21 = (bf16[4,16,512]{2,1,0:T(8,128)(2,1)S(1)}, bf16[4,16,512]{2,1,0:T(8,128)(2,1)S(1)}, u32[]{:S(2)}, u32[]{:S(2)}) collective-permute-start(bf16[4,16,512]{2,1,0:T(8,128)(2,1)S(1)} %shard_map.100.refs_0_), channel_id=1, source_target_pairs={{0,2},{1,3},{2,0},{3,1},{4,6},{5,7},{6,4},{7,5},{8,10},{9,11},{10,... | collective-permute-start | bytes 196616 | tf_op jit(solution)/shard_map/ppermute | solution.py:41
  48.7 1.6 %collective-permute-start.22 = (bf16[4,16,512]{2,1,0:T(8,128)(2,1)S(1)}, bf16[4,16,512]{2,1,0:T(8,128)(2,1)S(1)}, u32[]{:S(2)}, u32[]{:S(2)}) collective-permute-start(bf16[4,16,512]{2,1,0:T(8,128)(2,1)S(1)} %shard_map.100.refs_0_), channel_id=1, source_target_pairs={{0,3},{1,2},{2,1},{3,0},{4,7},{5,6},{6,5},{7,4},{8,11},{9,10},{10,... | collective-permute-start | bytes 196616 | tf_op jit(solution)/shard_map/ppermute | solution.py:41
  50.3 0.0 collective-permute-done.28.refs_3_
  50.3 0.9 %shard_map.102 = (f32[4,64,512]{2,1,0:T(8,128)}, f32[4,64,512]{2,1,0:T(8,128)}) custom-call(f32[4,64,512]{2,1,0:T(8,128)S(1)} %copy-done, bf16[4,16,512]{2,1,0:T(8,128)(2,1)S(1)} %shard_map.101.refs_0_, bf16[4,16,512]{2,1,0:T(8,128)(2,1)S(1)} %collective-permute-done.26.refs_1_, bf16[4,16,512]{2,1,0:T(8,128)(2,1)S(1)} %collective-permute-done.27.refs_2_, ...), custom_call_target="tpu_custom_call" | custom-call | tf_op jit(solution)/shard_map/pallas_call | solution.py:337
  51.2 0.0 collective-permute-done.20.refs_1_
  51.2 3.7 %collective-permute-done.21.refs_2_ = bf16[4,16,512]{2,1,0:T(8,128)(2,1)S(1)} collective-permute-done((bf16[4,16,512]{2,1,0:T(8,128)(2,1)S(1)}, bf16[4,16,512]{2,1,0:T(8,128)(2,1)S(1)}, u32[]{:S(2)}, u32[]{:S(2)}) %collective-permute-start.21) | collective-permute-done | bytes 65568 | tf_op jit(solution)/shard_map/ppermute | solution.py:41
  55.0 0.0 collective-permute-done.22.refs_3_
  55.0 0.9 %shard_map.103 = (f32[4,64,512]{2,1,0:T(8,128)}, f32[4,64,512]{2,1,0:T(8,128)}) custom-call(f32[4,64,512]{2,1,0:T(8,128)S(1)} %copy-done, bf16[4,16,512]{2,1,0:T(8,128)(2,1)S(1)} %shard_map.100.refs_0_, bf16[4,16,512]{2,1,0:T(8,128)(2,1)S(1)} %collective-permute-done.20.refs_1_, ...), custom_call_target="tpu_custom_call", output_to_operand_aliasing={{0}: (5, {}), {1}: (6, {})} | custom-call | tf_op jit(solution)/shard_map/pallas_call | solution.py:337
  (6 shorter events, 0.1 us)
Async XLA Ops:
  2.3 12.7 %collective-permute-start = (bf16[4,32,512]{2,1,0:T(8,128)(2,1)S(1)}, bf16[4,32,512]{2,1,0:T(8,128)(2,1)S(1)}, u32[]{:S(2)}, u32[]{:S(2)}) collective-permute-start(bf16[4,32,512]{2,1,0:T(8,128)(2,1)S(1)} %get-tuple-element.36), channel_id=1, source_target_pairs={{0,3},{1,2},{2,1},{3,0},{4,7},{5,6},{6,5},{7,4},{8,11},{9,10},{10,... | collective-permute-start | bytes 393224 | tf_op jit(solution)/shard_map/ppermute | solution.py:41
  7.4 8.0 %collective-permute-start.1 = (bf16[4,32,512]{2,1,0:T(8,128)(2,1)S(1)}, bf16[4,32,512]{2,1,0:T(8,128)(2,1)S(1)}, u32[]{:S(2)}, u32[]{:S(2)}) collective-permute-start(bf16[4,32,512]{2,1,0:T(8,128)(2,1)S(1)} %get-tuple-element.37), channel_id=1, source_target_pairs={{0,1},{1,0},{2,3},{3,2},{4,5},{5,4},{6,7},{7,6},{8,9},{9,8},{10,11... | collective-permute-start | bytes 393224 | tf_op jit(solution)/shard_map/ppermute | solution.py:41
  7.4 11.1 %collective-permute-start.2 = (bf16[4,32,512]{2,1,0:T(8,128)(2,1)S(1)}, bf16[4,32,512]{2,1,0:T(8,128)(2,1)S(1)}, u32[]{:S(2)}, u32[]{:S(2)}) collective-permute-start(bf16[4,32,512]{2,1,0:T(8,128)(2,1)S(1)} %get-tuple-element.38), channel_id=1, source_target_pairs={{0,2},{1,3},{2,0},{3,1},{4,6},{5,7},{6,4},{7,5},{8,10},{9,11},{10,... | collective-permute-start | bytes 393224 | tf_op jit(solution)/shard_map/ppermute | solution.py:41
  11.9 10.2 %collective-permute-start.3 = (bf16[96,512]{1,0:T(8,128)(2,1)S(1)}, bf16[96,512]{1,0:T(8,128)(2,1)S(1)}, u32[]{:S(2)}, u32[]{:S(2)}) collective-permute-start(bf16[96,512]{1,0:T(8,128)(2,1)S(1)} %get-tuple-element.42.refs_0_), channel_id=1, source_target_pairs={{0,24},{4,28},{8,16},{12,20},{16,8},{20,12},{24,0},{28,4},{1,25},{... | collective-permute-start | bytes 294920 | tf_op jit(solution)/shard_map/ppermute | solution.py:41
  14.5 8.1 %collective-permute-start.4 = (bf16[96,512]{1,0:T(8,128)(2,1)S(1)}, bf16[96,512]{1,0:T(8,128)(2,1)S(1)}, u32[]{:S(2)}, u32[]{:S(2)}) collective-permute-start(bf16[96,512]{1,0:T(8,128)(2,1)S(1)} %get-tuple-element.42.refs_0_), channel_id=1, source_target_pairs={{0,16},{4,20},{8,24},{12,28},{16,0},{20,4},{24,8},{28,12},{1,17},{... | collective-permute-start | bytes 294920 | tf_op jit(solution)/shard_map/ppermute | solution.py:41
  15.0 8.1 %collective-permute-start.5 = (bf16[96,512]{1,0:T(8,128)(2,1)S(1)}, bf16[96,512]{1,0:T(8,128)(2,1)S(1)}, u32[]{:S(2)}, u32[]{:S(2)}) collective-permute-start(bf16[96,512]{1,0:T(8,128)(2,1)S(1)} %get-tuple-element.42.refs_0_), channel_id=1, source_target_pairs={{0,8},{4,12},{8,0},{12,4},{16,24},{20,28},{24,16},{28,20},{1,9},{5... | collective-permute-start | bytes 294920 | tf_op jit(solution)/shard_map/ppermute | solution.py:41
  15.4 7.7 %collective-permute-start.6 = (bf16[96,512]{1,0:T(8,128)(2,1)S(1)}, bf16[96,512]{1,0:T(8,128)(2,1)S(1)}, u32[]{:S(2)}, u32[]{:S(2)}) collective-permute-start(bf16[96,512]{1,0:T(8,128)(2,1)S(1)} %get-tuple-element.42.refs_0_), channel_id=1, source_target_pairs={{0,4},{4,0},{8,12},{12,8},{16,20},{20,16},{24,28},{28,24},{1,5},{5... | collective-permute-start | bytes 294920 | tf_op jit(solution)/shard_map/ppermute | solution.py:41
  19.6 6.7 %collective-permute-start.10 = (bf16[4,32,512]{2,1,0:T(8,128)(2,1)S(1)}, bf16[4,32,512]{2,1,0:T(8,128)(2,1)S(1)}, u32[]{:S(2)}, u32[]{:S(2)}) collective-permute-start(bf16[4,32,512]{2,1,0:T(8,128)(2,1)S(1)} %get-tuple-element.45.refs_0_), channel_id=1, source_target_pairs={{0,24},{4,28},{8,16},{12,20},{16,8},{20,12},{24,0},{28,4},{1,25},{... | collective-permute-start | bytes 393224 | tf_op jit(solution)/shard_map/ppermute | solution.py:41
  22.1 5.8 %collective-permute-start.11 = (bf16[4,32,512]{2,1,0:T(8,128)(2,1)S(1)}, bf16[4,32,512]{2,1,0:T(8,128)(2,1)S(1)}, u32[]{:S(2)}, u32[]{:S(2)}) collective-permute-start(bf16[4,32,512]{2,1,0:T(8,128)(2,1)S(1)} %get-tuple-element.45.refs_0_), channel_id=1, source_target_pairs={{0,16},{4,20},{8,24},{12,28},{16,0},{20,4},{24,8},{28,12},{1,17},{... | collective-permute-start | bytes 393224 | tf_op jit(solution)/shard_map/ppermute | solution.py:41
  22.6 5.4 %collective-permute-start.12 = (bf16[4,32,512]{2,1,0:T(8,128)(2,1)S(1)}, bf16[4,32,512]{2,1,0:T(8,128)(2,1)S(1)}, u32[]{:S(2)}, u32[]{:S(2)}) collective-permute-start(bf16[4,32,512]{2,1,0:T(8,128)(2,1)S(1)} %get-tuple-element.45.refs_0_), channel_id=1, source_target_pairs={{0,8},{4,12},{8,0},{12,4},{16,24},{20,28},{24,16},{28,20},{1,9},{5... | collective-permute-start | bytes 393224 | tf_op jit(solution)/shard_map/ppermute | solution.py:41
  23.1 1.3 %collective-permute-start.7 = (bf16[96,512]{1,0:T(8,128)(2,1)S(1)}, bf16[96,512]{1,0:T(8,128)(2,1)S(1)}, u32[]{:S(2)}, u32[]{:S(2)}) collective-permute-start(bf16[96,512]{1,0:T(8,128)(2,1)S(1)} %collective-permute-done.3.refs_1_), channel_id=1, source_target_pairs={{0,4},{4,0},{8,12},{12,8},{16,20},{20,16},{24,28},{28,24},{1,5},{5... | collective-permute-start | bytes 294920 | tf_op jit(solution)/shard_map/ppermute | solution.py:41
  23.1 1.5 %collective-permute-start.8 = (bf16[96,512]{1,0:T(8,128)(2,1)S(1)}, bf16[96,512]{1,0:T(8,128)(2,1)S(1)}, u32[]{:S(2)}, u32[]{:S(2)}) collective-permute-start(bf16[96,512]{1,0:T(8,128)(2,1)S(1)} %collective-permute-done.4.refs_2_), channel_id=1, source_target_pairs={{0,4},{4,0},{8,12},{12,8},{16,20},{20,16},{24,28},{28,24},{1,5},{5... | collective-permute-start | bytes 294920 | tf_op jit(solution)/shard_map/ppermute | solution.py:41
  24.4 4.0 %collective-permute-start.9 = (bf16[96,512]{1,0:T(8,128)(2,1)S(1)}, bf16[96,512]{1,0:T(8,128)(2,1)S(1)}, u32[]{:S(2)}, u32[]{:S(2)}) collective-permute-start(bf16[96,512]{1,0:T(8,128)(2,1)S(1)} %collective-permute-done.5.refs_3_), channel_id=1, source_target_pairs={{0,4},{4,0},{8,12},{12,8},{16,20},{20,16},{24,28},{28,24},{1,5},{5... | collective-permute-start | bytes 294920 | tf_op jit(solution)/shard_map/ppermute | solution.py:41
  24.6 5.1 %collective-permute-start.13 = (bf16[4,32,512]{2,1,0:T(8,128)(2,1)S(1)}, bf16[4,32,512]{2,1,0:T(8,128)(2,1)S(1)}, u32[]{:S(2)}, u32[]{:S(2)}) collective-permute-start(bf16[4,32,512]{2,1,0:T(8,128)(2,1)S(1)} %get-tuple-element.45.refs_0_), channel_id=1, source_target_pairs={{0,4},{4,0},{8,12},{12,8},{16,20},{20,16},{24,28},{28,24},{1,5},{5... | collective-permute-start | bytes 393224 | tf_op jit(solution)/shard_map/ppermute | solution.py:41
  26.3 3.4 %collective-permute-start.14 = (bf16[4,32,512]{2,1,0:T(8,128)(2,1)S(1)}, bf16[4,32,512]{2,1,0:T(8,128)(2,1)S(1)}, u32[]{:S(2)}, u32[]{:S(2)}) collective-permute-start(bf16[4,32,512]{2,1,0:T(8,128)(2,1)S(1)} %collective-permute-done.10.refs_1_), channel_id=1, source_target_pairs={{0,4},{4,0},{8,12},{12,8},{16,20},{20,16},{24,28},{28,24},{1,5},{5... | collective-permute-start | bytes 393224 | tf_op jit(solution)/shard_map/ppermute | solution.py:41
  27.9 1.8 %collective-permute-start.15 = (bf16[4,32,512]{2,1,0:T(8,128)(2,1)S(1)}, bf16[4,32,512]{2,1,0:T(8,128)(2,1)S(1)}, u32[]{:S(2)}, u32[]{:S(2)}) collective-permute-start(bf16[4,32,512]{2,1,0:T(8,128)(2,1)S(1)} %collective-permute-done.11.refs_2_), channel_id=1, source_target_pairs={{0,4},{4,0},{8,12},{12,8},{16,20},{20,16},{24,28},{28,24},{1,5},{5... | collective-permute-start | bytes 393224 | tf_op jit(solution)/shard_map/ppermute | solution.py:41
  28.0 1.7 %collective-permute-start.16 = (bf16[4,32,512]{2,1,0:T(8,128)(2,1)S(1)}, bf16[4,32,512]{2,1,0:T(8,128)(2,1)S(1)}, u32[]{:S(2)}, u32[]{:S(2)}) collective-permute-start(bf16[4,32,512]{2,1,0:T(8,128)(2,1)S(1)} %collective-permute-done.12.refs_3_), channel_id=1, source_target_pairs={{0,4},{4,0},{8,12},{12,8},{16,20},{20,16},{24,28},{28,24},{1,5},{5... | collective-permute-start | bytes 393224 | tf_op jit(solution)/shard_map/ppermute | solution.py:41
  30.7 7.7 %collective-permute-start.23 = (bf16[4,16,512]{2,1,0:T(8,128)(2,1)S(1)}, bf16[4,16,512]{2,1,0:T(8,128)(2,1)S(1)}, u32[]{:S(2)}, u32[]{:S(2)}) collective-permute-start(bf16[4,16,512]{2,1,0:T(8,128)(2,1)S(1)} %get-tuple-element.52), channel_id=1, source_target_pairs={{0,3},{1,2},{2,1},{3,0},{4,7},{5,6},{6,5},{7,4},{8,11},{9,10},{10,... | collective-permute-start | bytes 196616 | tf_op jit(solution)/shard_map/ppermute | solution.py:41
  32.9 7.7 %collective-permute-start.24 = (bf16[4,16,512]{2,1,0:T(8,128)(2,1)S(1)}, bf16[4,16,512]{2,1,0:T(8,128)(2,1)S(1)}, u32[]{:S(2)}, u32[]{:S(2)}) collective-permute-start(bf16[4,16,512]{2,1,0:T(8,128)(2,1)S(1)} %get-tuple-element.53), channel_id=1, source_target_pairs={{0,2},{1,3},{2,0},{3,1},{4,6},{5,7},{6,4},{7,5},{8,10},{9,11},{10,... | collective-permute-start | bytes 196616 | tf_op jit(solution)/shard_map/ppermute | solution.py:41
  32.9 7.7 %collective-permute-start.25 = (bf16[4,16,512]{2,1,0:T(8,128)(2,1)S(1)}, bf16[4,16,512]{2,1,0:T(8,128)(2,1)S(1)}, u32[]{:S(2)}, u32[]{:S(2)}) collective-permute-start(bf16[4,16,512]{2,1,0:T(8,128)(2,1)S(1)} %get-tuple-element.54), channel_id=1, source_target_pairs={{0,1},{1,0},{2,3},{3,2},{4,5},{5,4},{6,7},{7,6},{8,9},{9,8},{10,11... | collective-permute-start | bytes 196616 | tf_op jit(solution)/shard_map/ppermute | solution.py:41
  35.1 15.2 %copy-start = (f32[4,64,512]{2,1,0:T(8,128)S(1)}, f32[4,64,512]{2,1,0:T(8,128)}, u32[]{:S(2)}) copy-start(f32[4,64,512]{2,1,0:T(8,128)} %diag_ref.3) | copy-start | bytes 1572868
  36.2 7.3 %collective-permute-start.17 = (bf16[4,16,512]{2,1,0:T(8,128)(2,1)S(1)}, bf16[4,16,512]{2,1,0:T(8,128)(2,1)S(1)}, u32[]{:S(2)}, u32[]{:S(2)}) collective-permute-start(bf16[4,16,512]{2,1,0:T(8,128)(2,1)S(1)} %get-tuple-element.48), channel_id=1, source_target_pairs={{0,3},{1,2},{2,1},{3,0},{4,7},{5,6},{6,5},{7,4},{8,11},{9,10},{10,... | collective-permute-start | bytes 196616 | tf_op jit(solution)/shard_map/ppermute | solution.py:41
  38.4 7.5 %collective-permute-start.18 = (bf16[4,16,512]{2,1,0:T(8,128)(2,1)S(1)}, bf16[4,16,512]{2,1,0:T(8,128)(2,1)S(1)}, u32[]{:S(2)}, u32[]{:S(2)}) collective-permute-start(bf16[4,16,512]{2,1,0:T(8,128)(2,1)S(1)} %get-tuple-element.49), channel_id=1, source_target_pairs={{0,2},{1,3},{2,0},{3,1},{4,6},{5,7},{6,4},{7,5},{8,10},{9,11},{10,... | collective-permute-start | bytes 196616 | tf_op jit(solution)/shard_map/ppermute | solution.py:41
  38.4 7.4 %collective-permute-start.19 = (bf16[4,16,512]{2,1,0:T(8,128)(2,1)S(1)}, bf16[4,16,512]{2,1,0:T(8,128)(2,1)S(1)}, u32[]{:S(2)}, u32[]{:S(2)}) collective-permute-start(bf16[4,16,512]{2,1,0:T(8,128)(2,1)S(1)} %get-tuple-element.50), channel_id=1, source_target_pairs={{0,1},{1,0},{2,3},{3,2},{4,5},{5,4},{6,7},{7,6},{8,9},{9,8},{10,11... | collective-permute-start | bytes 196616 | tf_op jit(solution)/shard_map/ppermute | solution.py:41
  40.7 8.0 %collective-permute-start.26 = (bf16[4,16,512]{2,1,0:T(8,128)(2,1)S(1)}, bf16[4,16,512]{2,1,0:T(8,128)(2,1)S(1)}, u32[]{:S(2)}, u32[]{:S(2)}) collective-permute-start(bf16[4,16,512]{2,1,0:T(8,128)(2,1)S(1)} %shard_map.101.refs_0_), channel_id=1, source_target_pairs={{0,1},{1,0},{2,3},{3,2},{4,5},{5,4},{6,7},{7,6},{8,9},{9,8},{10,11... | collective-permute-start | bytes 196616 | tf_op jit(solution)/shard_map/ppermute | solution.py:41
  40.7 9.6 %collective-permute-start.27 = (bf16[4,16,512]{2,1,0:T(8,128)(2,1)S(1)}, bf16[4,16,512]{2,1,0:T(8,128)(2,1)S(1)}, u32[]{:S(2)}, u32[]{:S(2)}) collective-permute-start(bf16[4,16,512]{2,1,0:T(8,128)(2,1)S(1)} %shard_map.101.refs_0_), channel_id=1, source_target_pairs={{0,2},{1,3},{2,0},{3,1},{4,6},{5,7},{6,4},{7,5},{8,10},{9,11},{10,... | collective-permute-start | bytes 196616 | tf_op jit(solution)/shard_map/ppermute | solution.py:41
  43.5 6.9 %collective-permute-start.28 = (bf16[4,16,512]{2,1,0:T(8,128)(2,1)S(1)}, bf16[4,16,512]{2,1,0:T(8,128)(2,1)S(1)}, u32[]{:S(2)}, u32[]{:S(2)}) collective-permute-start(bf16[4,16,512]{2,1,0:T(8,128)(2,1)S(1)} %shard_map.101.refs_0_), channel_id=1, source_target_pairs={{0,3},{1,2},{2,1},{3,0},{4,7},{5,6},{6,5},{7,4},{8,11},{9,10},{10,... | collective-permute-start | bytes 196616 | tf_op jit(solution)/shard_map/ppermute | solution.py:41
  45.9 5.3 %collective-permute-start.20 = (bf16[4,16,512]{2,1,0:T(8,128)(2,1)S(1)}, bf16[4,16,512]{2,1,0:T(8,128)(2,1)S(1)}, u32[]{:S(2)}, u32[]{:S(2)}) collective-permute-start(bf16[4,16,512]{2,1,0:T(8,128)(2,1)S(1)} %shard_map.100.refs_0_), channel_id=1, source_target_pairs={{0,1},{1,0},{2,3},{3,2},{4,5},{5,4},{6,7},{7,6},{8,9},{9,8},{10,11... | collective-permute-start | bytes 196616 | tf_op jit(solution)/shard_map/ppermute | solution.py:41
  46.3 8.7 %collective-permute-start.21 = (bf16[4,16,512]{2,1,0:T(8,128)(2,1)S(1)}, bf16[4,16,512]{2,1,0:T(8,128)(2,1)S(1)}, u32[]{:S(2)}, u32[]{:S(2)}) collective-permute-start(bf16[4,16,512]{2,1,0:T(8,128)(2,1)S(1)} %shard_map.100.refs_0_), channel_id=1, source_target_pairs={{0,2},{1,3},{2,0},{3,1},{4,6},{5,7},{6,4},{7,5},{8,10},{9,11},{10,... | collective-permute-start | bytes 196616 | tf_op jit(solution)/shard_map/ppermute | solution.py:41
  48.7 6.3 %collective-permute-start.22 = (bf16[4,16,512]{2,1,0:T(8,128)(2,1)S(1)}, bf16[4,16,512]{2,1,0:T(8,128)(2,1)S(1)}, u32[]{:S(2)}, u32[]{:S(2)}) collective-permute-start(bf16[4,16,512]{2,1,0:T(8,128)(2,1)S(1)} %shard_map.100.refs_0_), channel_id=1, source_target_pairs={{0,3},{1,2},{2,1},{3,0},{4,7},{5,6},{6,5},{7,4},{8,11},{9,10},{10,... | collective-permute-start | bytes 196616 | tf_op jit(solution)/shard_map/ppermute | solution.py:41

commit v8 on v7

--- a/solution.py
+++ b/solution.py
@@ -213,24 +213,21 @@
     supers, width, _ = l_ref.shape
     share, piece = width // n_rows, tops_ref.shape[0]
     col, row = lax.axis_index("cols"), lax.axis_index("rows")
-    copies = [fetch(l_any.at[k], l_ref.at[k], sems.at[k]) for k in range(supers)]
+    copies = [fetch(l_any.at[0], l_ref.at[0], sems.at[0]), fetch(l_any.at[pl.ds(1, supers - 1)], l_ref.at[pl.ds(1, supers - 1)], sems.at[1])]
     tops_copy = fetch(tops_any, tops_ref, sems.at[supers])
 
     @pl.when(col == 0)
     def _():
-        fetch(top_any, begin_ref, sems.at[supers + 1]).wait()
+        fetch(top_any, begin_ref, sems.at[supers + 1])
 
     @pl.when(jnp.logical_and(col > 0, col < supers))
     def _():
-        fetch(diag_any.at[jnp.clip(supers - col, 1, supers - 1)], begin_ref, sems.at[supers + 1]).wait()
+        fetch(diag_any.at[jnp.clip(supers - col, 1, supers - 1)], begin_ref, sems.at[supers + 1])
 
     @pl.when(col >= supers)
     def _():
         begin_ref[...] = jnp.zeros_like(begin_ref)
 
-    tops_copy.wait()
-    joined_ref[pl.ds(0, share)] = begin_ref[...].astype(BF)
-    joined_ref[pl.ds(share, piece)] = tops_ref[...]
     lane = lax.broadcasted_iota(jnp.int32, (share, width), 1)
     sub = lax.broadcasted_iota(jnp.int32, (share, width), 0)
     unit = jnp.where(lane == row * share + sub, 1.0, 0.0).astype(BF)
@@ -240,10 +237,19 @@
     for k in range(supers):
         reach_ref[pl.ds(at, (k + 1) * share)] = dot_nt(stack, panel_ref[k]).astype(BF)
         at += (k + 1) * share
-        copies[k].wait()
+        if k < 2:
+            copies[k].wait()
         stack = jnp.concatenate([dot_nt(stack, l_ref[k]).astype(BF), unit], 0)
         stacks_ref[k + 1, pl.ds(0, (k + 2) * share)] = stack
+    tops_copy.wait()
     carry_ref[...] = dot(tops_ref[...], l_ref[supers - 1])
+
+    @pl.when(col < supers)
+    def _():
+        pltpu.make_async_copy(top_any, begin_ref, sems.at[supers + 1]).wait()
+
+    joined_ref[pl.ds(0, share)] = begin_ref[...].astype(BF)
+    joined_ref[pl.ds(share, piece)] = tops_ref[...]
 
 
 def place(refs, order, write):
@@ -266,9 +272,12 @@
     place(got, order, write)
     begin = dot(stacks_ref[jnp.maximum(supers - col, 0)], x_ref[...])
     begin_ref[...] = begin
-    first = jnp.where(col == 0, begin, 0.0).astype(BF)
     across = dot_nt(stacks_ref[supers], y_ref[...]).astype(BF)
-    ahead_ref[...] = dot(first, l_ref[supers - 1]) + dot(across, panel_ref[supers - 1])
+    ahead_ref[...] = dot(across, panel_ref[supers - 1])
+
+    @pl.when(col == 0)
+    def _():
+        ahead_ref[...] += dot(begin.astype(BF), l_ref[supers - 1])
 
 
 def rows_kernel(n_cols, n_rows, order, levels, last, l_ref, panel_ref, stacks_ref, reach_ref, begin_ref, from_ref, *refs):
@@ -317,19 +326,21 @@
 
 def last_kernel(n_cols, offsets, levels, diag_ref, *refs):
     got_refs = refs[:n_cols]
-    diag_out, sub_out, done_ref, sems = refs[-4:]
+    diag_out, sub_out, done_ref, sub_ref, sems = refs[-5:]
     part = got_refs[0].shape[1]
     col = lax.axis_index("cols")
-    copies = []
+    span = pl.ds(levels[-1], len(levels))
+    places = [pl.ds(pl.multiple_of((col ^ j) * part, part), part) for j in offsets]
     for i, k in enumerate(levels):
-        for j, got in zip(offsets, got_refs):
-            rows = pl.ds(pl.multiple_of((col ^ j) * part, part), part)
-            done_ref[2 * i, rows] = diag_ref[k, rows] + got[2 * i].astype(F32)
-            done_ref[2 * i + 1, rows] = got[2 * i + 1].astype(F32)
-        copies.append(fetch(done_ref.at[2 * i], diag_out.at[k], sems.at[2 * i]))
-        copies.append(fetch(done_ref.at[2 * i + 1], sub_out.at[k], sems.at[2 * i + 1]))
-    for copy in copies:
-        copy.wait()
+        for rows, got in zip(places, got_refs):
+            sub_ref[k - levels[-1], rows] = got[2 * i + 1].astype(F32)
+    sub_copy = fetch(sub_ref, sub_out.at[span], sems.at[0])
+    for i, k in enumerate(levels):
+        for rows, got in zip(places, got_refs):
+            done_ref[k - levels[-1], rows] = diag_ref[k, rows] + got[2 * i].astype(F32)
+    diag_copy = fetch(done_ref, diag_out.at[span], sems.at[1])
+    sub_copy.wait()
+    diag_copy.wait()
 
 
 def call(kernel, outs, *args, scratch=(), away=(), out_away=False, aliases=None, flops=0, moved=0):
@@ -424,7 +435,7 @@
             [(diag_inverse.shape, F32)] * 2,
             diag_inverse, *got, *filled, away=range(1 + n_cols, 1 + n_cols + len(filled)), out_away=True,
             aliases={1 + n_cols + i: i for i in range(len(filled))},
-            scratch=[pltpu.VMEM((2 * len(levels), share, width), F32), pltpu.SemaphoreType.DMA((2 * len(levels),))],
+            scratch=[pltpu.VMEM((len(levels), share, width), F32)] * 2 + [pltpu.SemaphoreType.DMA((2,))],
         )
     diag, sub = filled
     return cols_out.reshape(supers, 1, 1, piece, width), diag, sub

time: 56 us -> 55.9 us (level)
  Pallas kernels: 11.7 us -> 10.4 us
  waiting for transfers between devices: 11.3 us -> 12.5 us
    pallas_call x10, Pallas kernels: 11.7 us -> 10.4 us  [call(): pl.pallas_call(kernel, out_shape=tuple((jax.ShapeDtypeStruct(s, d) for s,...]
    ppermute x29, waiting for transfers between devices: 11.3 us -> 12.5 us  [hop(): return lax.ppermute(x, axis, [(i, target(i, j, n)) for i in range(n)])]
  transfers between devices with their start and end apart: 29 -> 29, of which waited for: 7 -> 8; matrix products, arithmetic and copies ran while one was open for 0% -> 0% of each run, Pallas kernels for 15% -> 13%
where the time goes in v8:
time: 55.9 us; the launch traced here: 55.8 us
  starting transfers between devices  32 us (57%)
  waiting for transfers between devices  12.5 us (22%)
  Pallas kernels  10.4 us (19%)
  between operations  0.77 us (1%)
    ppermute x29, starting transfers between devices, hop(): return lax.ppermute(x, axis, [(i, target(i, j, n)) for i in range(n)])  32 us
    ppermute x29, waiting for transfers between devices, hop(): return lax.ppermute(x, axis, [(i, target(i, j, n)) for i in range(n)])  12.5 us
    pallas_call x10, Pallas kernels, call(): pl.pallas_call(kernel, out_shape=tuple((jax.ShapeDtypeStruct(s, d) for s,...  10.4 us
  transfers between devices with their start and end apart: 29, of which 8 were waited for; matrix products, arithmetic and copies ran while one was open for 0% of the time, Pallas kernels for 13%

profile of v8, /device:TPU:0, one launch (start us, length us, event | category | flops | bytes accessed | tf_op | source)
XLA Modules:
  0.0 55.8 jit_solution(6438348995936428341)
XLA Ops:
  0.6 1.6 %shard_map.94 = (bf16[4,256,512]{2,1,0:T(8,128)(2,1)S(1)}, f32[4,8,512]{2,1,0:T(8,128)S(1)}, bf16[4,32,512]{2,1,0:T(8,128)(2,1)S(1)}, bf16[4,32,512]{2,1,0:T(8,1...) custom-call(bf16[4,32,256]{2,1,0:T(8,128)(2,1)} %bitcast.7, ...), custom_call_target="tpu_custom_call" | custom-call | flops 134217728 | bytes 2097152 | tf_op jit(solution)/shard_map/pallas_call | solution.py:348
  2.3 5.1 %collective-permute-start = (bf16[4,32,512]{2,1,0:T(8,128)(2,1)S(1)}, bf16[4,32,512]{2,1,0:T(8,128)(2,1)S(1)}, u32[]{:S(2)}, u32[]{:S(2)}) collective-permute-start(bf16[4,32,512]{2,1,0:T(8,128)(2,1)S(1)} %get-tuple-element.36), channel_id=1, source_target_pairs={{0,3},{1,2},{2,1},{3,0},{4,7},{5,6},{6,5},{7,4},{8,11},{9,10},{10,... | collective-permute-start | bytes 393224 | tf_op jit(solution)/shard_map/ppermute | solution.py:41
  7.4 0.0 collective-permute-start.1
  7.4 0.6 %collective-permute-start.2 = (bf16[4,32,512]{2,1,0:T(8,128)(2,1)S(1)}, bf16[4,32,512]{2,1,0:T(8,128)(2,1)S(1)}, u32[]{:S(2)}, u32[]{:S(2)}) collective-permute-start(bf16[4,32,512]{2,1,0:T(8,128)(2,1)S(1)} %get-tuple-element.38), channel_id=1, source_target_pairs={{0,2},{1,3},{2,0},{3,1},{4,6},{5,7},{6,4},{7,5},{8,10},{9,11},{10,... | collective-permute-start | bytes 393224 | tf_op jit(solution)/shard_map/ppermute | solution.py:41
  8.0 2.8 %shard_map.95 = (bf16[4,512,512]{2,1,0:T(8,128)(2,1)S(1)}, bf16[5,320,512]{2,1,0:T(8,128)(2,1)S(1)}, bf16[640,256]{1,0:T(8,128)(2,1)S(1)}, bf16[96,512]{1,0:T(8,128)(2,1)S(1)}, f32[32,512]{1,0:T(8,128)S(1)}) custom-call(bf16[4,512,512]{2,1,0:T(8,128)(2,1)} %l_any.1, f32[4,64,512]{2,1,0:T(8,128)} %diag_ref.3, f32[64,512]{1,0:T(8,128)} %top_any.1, ...), custom_call_target="tpu_custom_call" | custom-call | flops 402653184 | bytes 4194304 | tf_op jit(solution)/shard_map/pallas_call | solution.py:348
  10.8 2.7 %collective-permute-start.3 = (bf16[96,512]{1,0:T(8,128)(2,1)S(1)}, bf16[96,512]{1,0:T(8,128)(2,1)S(1)}, u32[]{:S(2)}, u32[]{:S(2)}) collective-permute-start(bf16[96,512]{1,0:T(8,128)(2,1)S(1)} %get-tuple-element.42.refs_0_), channel_id=1, source_target_pairs={{0,24},{4,28},{8,16},{12,20},{16,8},{20,12},{24,0},{28,4},{1,25},{... | collective-permute-start | bytes 294920 | tf_op jit(solution)/shard_map/ppermute | solution.py:41
  13.5 0.5 collective-permute-start.4
  14.0 0.0 collective-permute-done.refs_0_
  14.0 0.4 collective-permute-start.5
  14.4 0.4 collective-permute-done.1.refs_1_
  14.8 0.0 collective-permute-start.6
  14.8 3.7 %collective-permute-done.2.refs_2_ = bf16[4,32,512]{2,1,0:T(8,128)(2,1)S(1)} collective-permute-done((bf16[4,32,512]{2,1,0:T(8,128)(2,1)S(1)}, bf16[4,32,512]{2,1,0:T(8,128)(2,1)S(1)}, u32[]{:S(2)}, u32[]{:S(2)}) %collective-permute-start.2) | collective-permute-done | bytes 131104 | tf_op jit(solution)/shard_map/ppermute | solution.py:41
  18.5 1.2 %shard_map.96 = (bf16[4,32,512]{2,1,0:T(8,128)(2,1)S(1)}, bf16[4,32,512]{2,1,0:T(8,128)(2,1)}) custom-call(bf16[4,512,512]{2,1,0:T(8,128)(2,1)S(1)} %get-tuple-element.32.l_ref, f32[32,512]{1,0:T(8,128)S(1)} %get-tuple-element.33.carry_ref, f32[4,8,512]{2,1,0:T(8,128)S(1)} %get-tuple-element.34.mask_ref, bf16[4,32,512]{2,1,0:T(8,128)(2,1)S(1)} %get-tuple-element.35.own_ref, ...), custom_call_target="tpu_custom_call" | custom-call | flops 67108864 | bytes 2097152 | tf_op jit(solution)/shard_map/pallas_call | solution.py:348
  19.6 2.4 %collective-permute-start.10 = (bf16[4,32,512]{2,1,0:T(8,128)(2,1)S(1)}, bf16[4,32,512]{2,1,0:T(8,128)(2,1)S(1)}, u32[]{:S(2)}, u32[]{:S(2)}) collective-permute-start(bf16[4,32,512]{2,1,0:T(8,128)(2,1)S(1)} %get-tuple-element.45.refs_0_), channel_id=1, source_target_pairs={{0,24},{4,28},{8,16},{12,20},{16,8},{20,12},{24,0},{28,4},{1,25},{... | collective-permute-start | bytes 393224 | tf_op jit(solution)/shard_map/ppermute | solution.py:41
  22.1 0.0 collective-permute-done.3.refs_1_
  22.1 0.5 collective-permute-start.11
  22.6 0.0 collective-permute-done.4.refs_2_
  22.6 0.5 collective-permute-start.12
  23.1 0.0 collective-permute-done.5.refs_3_
  23.1 0.0 collective-permute-start.7
  23.1 0.0 collective-permute-done.6.refs_4_
  23.1 0.5 collective-permute-start.8
  23.6 0.8 %collective-permute-done.7.refs_5_ = bf16[96,512]{1,0:T(8,128)(2,1)S(1)} collective-permute-done((bf16[96,512]{1,0:T(8,128)(2,1)S(1)}, bf16[96,512]{1,0:T(8,128)(2,1)S(1)}, u32[]{:S(2)}, u32[]{:S(2)}) %collective-permute-start.7) | collective-permute-done | bytes 98336 | tf_op jit(solution)/shard_map/ppermute | solution.py:41
  24.4 0.2 collective-permute-start.9
  24.6 0.0 collective-permute-done.8.refs_6_
  24.6 0.4 collective-permute-start.13
  25.0 1.4 %collective-permute-done.10.refs_1_ = bf16[4,32,512]{2,1,0:T(8,128)(2,1)S(1)} collective-permute-done((bf16[4,32,512]{2,1,0:T(8,128)(2,1)S(1)}, bf16[4,32,512]{2,1,0:T(8,128)(2,1)S(1)}, u32[]{:S(2)}, u32[]{:S(2)}) %collective-permute-start.10) | collective-permute-done | bytes 131104 | tf_op jit(solution)/shard_map/ppermute | solution.py:41
  26.3 0.0 collective-permute-start.14
  26.3 1.6 %collective-permute-done.11.refs_2_ = bf16[4,32,512]{2,1,0:T(8,128)(2,1)S(1)} collective-permute-done((bf16[4,32,512]{2,1,0:T(8,128)(2,1)S(1)}, bf16[4,32,512]{2,1,0:T(8,128)(2,1)S(1)}, u32[]{:S(2)}, u32[]{:S(2)}) %collective-permute-start.11) | collective-permute-done | bytes 131104 | tf_op jit(solution)/shard_map/ppermute | solution.py:41
  27.9 0.0 collective-permute-start.15
  27.9 0.1 collective-permute-done.12.refs_3_
  28.0 0.4 collective-permute-start.16
  28.4 0.0 collective-permute-done.9.refs_7_
  28.4 1.1 %shard_map.97 = (f32[320,512]{1,0:T(8,128)S(1)}, f32[320,512]{1,0:T(8,128)S(1)}) custom-call(bf16[4,512,512]{2,1,0:T(8,128)(2,1)S(1)} %get-tuple-element.32.l_ref, bf16[4,256,512]{2,1,0:T(8,128)(2,1)S(1)} %get-tuple-element.31.panel_ref, bf16[5,320,512]{2,1,0:T(8,128)(2,1)S(1)} %get-tuple-element.40.stacks_ref, ...), custom_call_target="tpu_custom_call" | custom-call | flops 503316480 | bytes 1048576 | tf_op jit(solution)/shard_map/pallas_call | solution.py:348
  29.5 0.0 collective-permute-done.13.refs_4_
  29.5 0.0 collective-permute-done.14.refs_5_
  29.5 0.0 collective-permute-done.15.refs_6_
  29.5 0.0 collective-permute-done.16.refs_7_
  29.5 1.0 %shard_map.98 = (bf16[4,16,512]{2,1,0:T(8,128)(2,1)S(1)}, bf16[4,16,512]{2,1,0:T(8,128)(2,1)S(1)}, bf16[4,16,512]{2,1,0:T(8,128)(2,1)S(1)}, bf16[4,16,512]{2,1,0:T(8,128)(2,1)S(1)}, f32[192,512]{1,0:T(8,128)S(1)}) custom-call(bf16[4,512,512]{2,1,0:T(8,128)(2,1)S(1)} %get-tuple-element.32.l_ref, bf16[4,256,512]{2,1,0:T(8,128)(2,1)S(1)} %get-tuple-element.31.panel_ref, ...), custom_call_target="tpu_custom_call" | custom-call | flops 335544320 | bytes 4194304 | tf_op jit(solution)/shard_map/pallas_call | solution.py:348
  30.5 2.1 %collective-permute-start.23 = (bf16[4,16,512]{2,1,0:T(8,128)(2,1)S(1)}, bf16[4,16,512]{2,1,0:T(8,128)(2,1)S(1)}, u32[]{:S(2)}, u32[]{:S(2)}) collective-permute-start(bf16[4,16,512]{2,1,0:T(8,128)(2,1)S(1)} %get-tuple-element.52), channel_id=1, source_target_pairs={{0,3},{1,2},{2,1},{3,0},{4,7},{5,6},{6,5},{7,4},{8,11},{9,10},{10,... | collective-permute-start | bytes 196616 | tf_op jit(solution)/shard_map/ppermute | solution.py:41
  32.6 0.0 collective-permute-start.24
  32.6 2.4 %collective-permute-start.25 = (bf16[4,16,512]{2,1,0:T(8,128)(2,1)S(1)}, bf16[4,16,512]{2,1,0:T(8,128)(2,1)S(1)}, u32[]{:S(2)}, u32[]{:S(2)}) collective-permute-start(bf16[4,16,512]{2,1,0:T(8,128)(2,1)S(1)} %get-tuple-element.54), channel_id=1, source_target_pairs={{0,1},{1,0},{2,3},{3,2},{4,5},{5,4},{6,7},{7,6},{8,9},{9,8},{10,11... | collective-permute-start | bytes 196616 | tf_op jit(solution)/shard_map/ppermute | solution.py:41
  34.9 1.0 %shard_map.99 = (bf16[4,16,512]{2,1,0:T(8,128)(2,1)S(1)}, bf16[4,16,512]{2,1,0:T(8,128)(2,1)S(1)}, bf16[4,16,512]{2,1,0:T(8,128)(2,1)S(1)}, bf16[4,16,512]{2,1,0:T(8,128)(2,1)S(1)}) custom-call(bf16[4,512,512]{2,1,0:T(8,128)(2,1)S(1)} %get-tuple-element.32.l_ref, bf16[4,256,512]{2,1,0:T(8,128)(2,1)S(1)} %get-tuple-element.31.panel_ref, ...), custom_call_target="tpu_custom_call" | custom-call | flops 335544320 | bytes 4194304 | tf_op jit(solution)/shard_map/pallas_call | solution.py:348
  36.0 2.1 %collective-permute-start.17 = (bf16[4,16,512]{2,1,0:T(8,128)(2,1)S(1)}, bf16[4,16,512]{2,1,0:T(8,128)(2,1)S(1)}, u32[]{:S(2)}, u32[]{:S(2)}) collective-permute-start(bf16[4,16,512]{2,1,0:T(8,128)(2,1)S(1)} %get-tuple-element.48), channel_id=1, source_target_pairs={{0,3},{1,2},{2,1},{3,0},{4,7},{5,6},{6,5},{7,4},{8,11},{9,10},{10,... | collective-permute-start | bytes 196616 | tf_op jit(solution)/shard_map/ppermute | solution.py:41
  38.1 0.0 collective-permute-start.18
  38.1 0.0 collective-permute-done.23.refs_0_
  38.1 2.4 %collective-permute-start.19 = (bf16[4,16,512]{2,1,0:T(8,128)(2,1)S(1)}, bf16[4,16,512]{2,1,0:T(8,128)(2,1)S(1)}, u32[]{:S(2)}, u32[]{:S(2)}) collective-permute-start(bf16[4,16,512]{2,1,0:T(8,128)(2,1)S(1)} %get-tuple-element.50), channel_id=1, source_target_pairs={{0,1},{1,0},{2,3},{3,2},{4,5},{5,4},{6,7},{7,6},{8,9},{9,8},{10,11... | collective-permute-start | bytes 196616 | tf_op jit(solution)/shard_map/ppermute | solution.py:41
  40.4 0.0 collective-permute-done.24.refs_1_
  40.4 0.0 collective-permute-done.25.refs_2_
  40.5 0.1 collective-permute-start.26
  40.6 2.6 %collective-permute-start.27 = (bf16[4,16,512]{2,1,0:T(8,128)(2,1)S(1)}, bf16[4,16,512]{2,1,0:T(8,128)(2,1)S(1)}, u32[]{:S(2)}, u32[]{:S(2)}) collective-permute-start(bf16[4,16,512]{2,1,0:T(8,128)(2,1)S(1)} %shard_map.101.refs_0_), channel_id=1, source_target_pairs={{0,2},{1,3},{2,0},{3,1},{4,6},{5,7},{6,4},{7,5},{8,10},{9,11},{10,... | collective-permute-start | bytes 196616 | tf_op jit(solution)/shard_map/ppermute | solution.py:41
  43.1 0.0 collective-permute-done.17.refs_0_
  43.1 1.8 %collective-permute-start.28 = (bf16[4,16,512]{2,1,0:T(8,128)(2,1)S(1)}, bf16[4,16,512]{2,1,0:T(8,128)(2,1)S(1)}, u32[]{:S(2)}, u32[]{:S(2)}) collective-permute-start(bf16[4,16,512]{2,1,0:T(8,128)(2,1)S(1)} %shard_map.101.refs_0_), channel_id=1, source_target_pairs={{0,3},{1,2},{2,1},{3,0},{4,7},{5,6},{6,5},{7,4},{8,11},{9,10},{10,... | collective-permute-start | bytes 196616 | tf_op jit(solution)/shard_map/ppermute | solution.py:41
  44.9 0.8 %collective-permute-done.18.refs_1_ = bf16[4,16,512]{2,1,0:T(8,128)(2,1)S(1)} collective-permute-done((bf16[4,16,512]{2,1,0:T(8,128)(2,1)S(1)}, bf16[4,16,512]{2,1,0:T(8,128)(2,1)S(1)}, u32[]{:S(2)}, u32[]{:S(2)}) %collective-permute-start.18) | collective-permute-done | bytes 65568 | tf_op jit(solution)/shard_map/ppermute | solution.py:41
  45.8 0.0 collective-permute-done.19.refs_2_
  45.8 0.1 collective-permute-start.20
  45.9 2.7 %collective-permute-start.21 = (bf16[4,16,512]{2,1,0:T(8,128)(2,1)S(1)}, bf16[4,16,512]{2,1,0:T(8,128)(2,1)S(1)}, u32[]{:S(2)}, u32[]{:S(2)}) collective-permute-start(bf16[4,16,512]{2,1,0:T(8,128)(2,1)S(1)} %shard_map.100.refs_0_), channel_id=1, source_target_pairs={{0,2},{1,3},{2,0},{3,1},{4,6},{5,7},{6,4},{7,5},{8,10},{9,11},{10,... | collective-permute-start | bytes 196616 | tf_op jit(solution)/shard_map/ppermute | solution.py:41
  48.6 0.0 collective-permute-done.26.refs_1_
  48.6 1.7 %collective-permute-start.22 = (bf16[4,16,512]{2,1,0:T(8,128)(2,1)S(1)}, bf16[4,16,512]{2,1,0:T(8,128)(2,1)S(1)}, u32[]{:S(2)}, u32[]{:S(2)}) collective-permute-start(bf16[4,16,512]{2,1,0:T(8,128)(2,1)S(1)} %shard_map.100.refs_0_), channel_id=1, source_target_pairs={{0,3},{1,2},{2,1},{3,0},{4,7},{5,6},{6,5},{7,4},{8,11},{9,10},{10,... | collective-permute-start | bytes 196616 | tf_op jit(solution)/shard_map/ppermute | solution.py:41
  50.3 0.0 collective-permute-done.27.refs_2_
  50.3 0.8 %shard_map.102 = (f32[4,64,512]{2,1,0:T(8,128)}, f32[4,64,512]{2,1,0:T(8,128)}) custom-call(f32[4,64,512]{2,1,0:T(8,128)S(1)} %copy-done, bf16[4,16,512]{2,1,0:T(8,128)(2,1)S(1)} %shard_map.101.refs_0_, bf16[4,16,512]{2,1,0:T(8,128)(2,1)S(1)} %collective-permute-done.26.refs_1_, bf16[4,16,512]{2,1,0:T(8,128)(2,1)S(1)} %collective-permute-done.27.refs_2_, ...), custom_call_target="tpu_custom_call" | custom-call | tf_op jit(solution)/shard_map/pallas_call | solution.py:348
  51.2 0.0 collective-permute-done.20.refs_1_
  51.2 3.7 %collective-permute-done.21.refs_2_ = bf16[4,16,512]{2,1,0:T(8,128)(2,1)S(1)} collective-permute-done((bf16[4,16,512]{2,1,0:T(8,128)(2,1)S(1)}, bf16[4,16,512]{2,1,0:T(8,128)(2,1)S(1)}, u32[]{:S(2)}, u32[]{:S(2)}) %collective-permute-start.21) | collective-permute-done | bytes 65568 | tf_op jit(solution)/shard_map/ppermute | solution.py:41
  54.9 0.8 %shard_map.103 = (f32[4,64,512]{2,1,0:T(8,128)}, f32[4,64,512]{2,1,0:T(8,128)}) custom-call(f32[4,64,512]{2,1,0:T(8,128)S(1)} %copy-done, bf16[4,16,512]{2,1,0:T(8,128)(2,1)S(1)} %shard_map.100.refs_0_, bf16[4,16,512]{2,1,0:T(8,128)(2,1)S(1)} %collective-permute-done.20.refs_1_, ...), custom_call_target="tpu_custom_call", output_to_operand_aliasing={{0}: (5, {}), {1}: (6, {})} | custom-call | tf_op jit(solution)/shard_map/pallas_call | solution.py:348
  (6 shorter events, 0.1 us)
Async XLA Ops:
  2.3 11.7 %collective-permute-start = (bf16[4,32,512]{2,1,0:T(8,128)(2,1)S(1)}, bf16[4,32,512]{2,1,0:T(8,128)(2,1)S(1)}, u32[]{:S(2)}, u32[]{:S(2)}) collective-permute-start(bf16[4,32,512]{2,1,0:T(8,128)(2,1)S(1)} %get-tuple-element.36), channel_id=1, source_target_pairs={{0,3},{1,2},{2,1},{3,0},{4,7},{5,6},{6,5},{7,4},{8,11},{9,10},{10,... | collective-permute-start | bytes 393224 | tf_op jit(solution)/shard_map/ppermute | solution.py:41
  7.4 7.4 %collective-permute-start.1 = (bf16[4,32,512]{2,1,0:T(8,128)(2,1)S(1)}, bf16[4,32,512]{2,1,0:T(8,128)(2,1)S(1)}, u32[]{:S(2)}, u32[]{:S(2)}) collective-permute-start(bf16[4,32,512]{2,1,0:T(8,128)(2,1)S(1)} %get-tuple-element.37), channel_id=1, source_target_pairs={{0,1},{1,0},{2,3},{3,2},{4,5},{5,4},{6,7},{7,6},{8,9},{9,8},{10,11... | collective-permute-start | bytes 393224 | tf_op jit(solution)/shard_map/ppermute | solution.py:41
  7.4 11.1 %collective-permute-start.2 = (bf16[4,32,512]{2,1,0:T(8,128)(2,1)S(1)}, bf16[4,32,512]{2,1,0:T(8,128)(2,1)S(1)}, u32[]{:S(2)}, u32[]{:S(2)}) collective-permute-start(bf16[4,32,512]{2,1,0:T(8,128)(2,1)S(1)} %get-tuple-element.38), channel_id=1, source_target_pairs={{0,2},{1,3},{2,0},{3,1},{4,6},{5,7},{6,4},{7,5},{8,10},{9,11},{10,... | collective-permute-start | bytes 393224 | tf_op jit(solution)/shard_map/ppermute | solution.py:41
  10.8 11.3 %collective-permute-start.3 = (bf16[96,512]{1,0:T(8,128)(2,1)S(1)}, bf16[96,512]{1,0:T(8,128)(2,1)S(1)}, u32[]{:S(2)}, u32[]{:S(2)}) collective-permute-start(bf16[96,512]{1,0:T(8,128)(2,1)S(1)} %get-tuple-element.42.refs_0_), channel_id=1, source_target_pairs={{0,24},{4,28},{8,16},{12,20},{16,8},{20,12},{24,0},{28,4},{1,25},{... | collective-permute-start | bytes 294920 | tf_op jit(solution)/shard_map/ppermute | solution.py:41
  13.5 9.1 %collective-permute-start.4 = (bf16[96,512]{1,0:T(8,128)(2,1)S(1)}, bf16[96,512]{1,0:T(8,128)(2,1)S(1)}, u32[]{:S(2)}, u32[]{:S(2)}) collective-permute-start(bf16[96,512]{1,0:T(8,128)(2,1)S(1)} %get-tuple-element.42.refs_0_), channel_id=1, source_target_pairs={{0,16},{4,20},{8,24},{12,28},{16,0},{20,4},{24,8},{28,12},{1,17},{... | collective-permute-start | bytes 294920 | tf_op jit(solution)/shard_map/ppermute | solution.py:41
  14.0 9.1 %collective-permute-start.5 = (bf16[96,512]{1,0:T(8,128)(2,1)S(1)}, bf16[96,512]{1,0:T(8,128)(2,1)S(1)}, u32[]{:S(2)}, u32[]{:S(2)}) collective-permute-start(bf16[96,512]{1,0:T(8,128)(2,1)S(1)} %get-tuple-element.42.refs_0_), channel_id=1, source_target_pairs={{0,8},{4,12},{8,0},{12,4},{16,24},{20,28},{24,16},{28,20},{1,9},{5... | collective-permute-start | bytes 294920 | tf_op jit(solution)/shard_map/ppermute | solution.py:41
  14.8 8.4 %collective-permute-start.6 = (bf16[96,512]{1,0:T(8,128)(2,1)S(1)}, bf16[96,512]{1,0:T(8,128)(2,1)S(1)}, u32[]{:S(2)}, u32[]{:S(2)}) collective-permute-start(bf16[96,512]{1,0:T(8,128)(2,1)S(1)} %get-tuple-element.42.refs_0_), channel_id=1, source_target_pairs={{0,4},{4,0},{8,12},{12,8},{16,20},{20,16},{24,28},{28,24},{1,5},{5... | collective-permute-start | bytes 294920 | tf_op jit(solution)/shard_map/ppermute | solution.py:41
  19.6 6.7 %collective-permute-start.10 = (bf16[4,32,512]{2,1,0:T(8,128)(2,1)S(1)}, bf16[4,32,512]{2,1,0:T(8,128)(2,1)S(1)}, u32[]{:S(2)}, u32[]{:S(2)}) collective-permute-start(bf16[4,32,512]{2,1,0:T(8,128)(2,1)S(1)} %get-tuple-element.45.refs_0_), channel_id=1, source_target_pairs={{0,24},{4,28},{8,16},{12,20},{16,8},{20,12},{24,0},{28,4},{1,25},{... | collective-permute-start | bytes 393224 | tf_op jit(solution)/shard_map/ppermute | solution.py:41
  22.1 5.8 %collective-permute-start.11 = (bf16[4,32,512]{2,1,0:T(8,128)(2,1)S(1)}, bf16[4,32,512]{2,1,0:T(8,128)(2,1)S(1)}, u32[]{:S(2)}, u32[]{:S(2)}) collective-permute-start(bf16[4,32,512]{2,1,0:T(8,128)(2,1)S(1)} %get-tuple-element.45.refs_0_), channel_id=1, source_target_pairs={{0,16},{4,20},{8,24},{12,28},{16,0},{20,4},{24,8},{28,12},{1,17},{... | collective-permute-start | bytes 393224 | tf_op jit(solution)/shard_map/ppermute | solution.py:41
  22.6 5.4 %collective-permute-start.12 = (bf16[4,32,512]{2,1,0:T(8,128)(2,1)S(1)}, bf16[4,32,512]{2,1,0:T(8,128)(2,1)S(1)}, u32[]{:S(2)}, u32[]{:S(2)}) collective-permute-start(bf16[4,32,512]{2,1,0:T(8,128)(2,1)S(1)} %get-tuple-element.45.refs_0_), channel_id=1, source_target_pairs={{0,8},{4,12},{8,0},{12,4},{16,24},{20,28},{24,16},{28,20},{1,9},{5... | collective-permute-start | bytes 393224 | tf_op jit(solution)/shard_map/ppermute | solution.py:41
  23.1 1.3 %collective-permute-start.7 = (bf16[96,512]{1,0:T(8,128)(2,1)S(1)}, bf16[96,512]{1,0:T(8,128)(2,1)S(1)}, u32[]{:S(2)}, u32[]{:S(2)}) collective-permute-start(bf16[96,512]{1,0:T(8,128)(2,1)S(1)} %collective-permute-done.3.refs_1_), channel_id=1, source_target_pairs={{0,4},{4,0},{8,12},{12,8},{16,20},{20,16},{24,28},{28,24},{1,5},{5... | collective-permute-start | bytes 294920 | tf_op jit(solution)/shard_map/ppermute | solution.py:41
  23.1 1.5 %collective-permute-start.8 = (bf16[96,512]{1,0:T(8,128)(2,1)S(1)}, bf16[96,512]{1,0:T(8,128)(2,1)S(1)}, u32[]{:S(2)}, u32[]{:S(2)}) collective-permute-start(bf16[96,512]{1,0:T(8,128)(2,1)S(1)} %collective-permute-done.4.refs_2_), channel_id=1, source_target_pairs={{0,4},{4,0},{8,12},{12,8},{16,20},{20,16},{24,28},{28,24},{1,5},{5... | collective-permute-start | bytes 294920 | tf_op jit(solution)/shard_map/ppermute | solution.py:41
  24.4 4.0 %collective-permute-start.9 = (bf16[96,512]{1,0:T(8,128)(2,1)S(1)}, bf16[96,512]{1,0:T(8,128)(2,1)S(1)}, u32[]{:S(2)}, u32[]{:S(2)}) collective-permute-start(bf16[96,512]{1,0:T(8,128)(2,1)S(1)} %collective-permute-done.5.refs_3_), channel_id=1, source_target_pairs={{0,4},{4,0},{8,12},{12,8},{16,20},{20,16},{24,28},{28,24},{1,5},{5... | collective-permute-start | bytes 294920 | tf_op jit(solution)/shard_map/ppermute | solution.py:41
  24.6 4.9 %collective-permute-start.13 = (bf16[4,32,512]{2,1,0:T(8,128)(2,1)S(1)}, bf16[4,32,512]{2,1,0:T(8,128)(2,1)S(1)}, u32[]{:S(2)}, u32[]{:S(2)}) collective-permute-start(bf16[4,32,512]{2,1,0:T(8,128)(2,1)S(1)} %get-tuple-element.45.refs_0_), channel_id=1, source_target_pairs={{0,4},{4,0},{8,12},{12,8},{16,20},{20,16},{24,28},{28,24},{1,5},{5... | collective-permute-start | bytes 393224 | tf_op jit(solution)/shard_map/ppermute | solution.py:41
  26.3 3.2 %collective-permute-start.14 = (bf16[4,32,512]{2,1,0:T(8,128)(2,1)S(1)}, bf16[4,32,512]{2,1,0:T(8,128)(2,1)S(1)}, u32[]{:S(2)}, u32[]{:S(2)}) collective-permute-start(bf16[4,32,512]{2,1,0:T(8,128)(2,1)S(1)} %collective-permute-done.10.refs_1_), channel_id=1, source_target_pairs={{0,4},{4,0},{8,12},{12,8},{16,20},{20,16},{24,28},{28,24},{1,5},{5... | collective-permute-start | bytes 393224 | tf_op jit(solution)/shard_map/ppermute | solution.py:41
  27.9 1.6 %collective-permute-start.15 = (bf16[4,32,512]{2,1,0:T(8,128)(2,1)S(1)}, bf16[4,32,512]{2,1,0:T(8,128)(2,1)S(1)}, u32[]{:S(2)}, u32[]{:S(2)}) collective-permute-start(bf16[4,32,512]{2,1,0:T(8,128)(2,1)S(1)} %collective-permute-done.11.refs_2_), channel_id=1, source_target_pairs={{0,4},{4,0},{8,12},{12,8},{16,20},{20,16},{24,28},{28,24},{1,5},{5... | collective-permute-start | bytes 393224 | tf_op jit(solution)/shard_map/ppermute | solution.py:41
  28.0 1.5 %collective-permute-start.16 = (bf16[4,32,512]{2,1,0:T(8,128)(2,1)S(1)}, bf16[4,32,512]{2,1,0:T(8,128)(2,1)S(1)}, u32[]{:S(2)}, u32[]{:S(2)}) collective-permute-start(bf16[4,32,512]{2,1,0:T(8,128)(2,1)S(1)} %collective-permute-done.12.refs_3_), channel_id=1, source_target_pairs={{0,4},{4,0},{8,12},{12,8},{16,20},{20,16},{24,28},{28,24},{1,5},{5... | collective-permute-start | bytes 393224 | tf_op jit(solution)/shard_map/ppermute | solution.py:41
  30.5 7.6 %collective-permute-start.23 = (bf16[4,16,512]{2,1,0:T(8,128)(2,1)S(1)}, bf16[4,16,512]{2,1,0:T(8,128)(2,1)S(1)}, u32[]{:S(2)}, u32[]{:S(2)}) collective-permute-start(bf16[4,16,512]{2,1,0:T(8,128)(2,1)S(1)} %get-tuple-element.52), channel_id=1, source_target_pairs={{0,3},{1,2},{2,1},{3,0},{4,7},{5,6},{6,5},{7,4},{8,11},{9,10},{10,... | collective-permute-start | bytes 196616 | tf_op jit(solution)/shard_map/ppermute | solution.py:41
  32.6 7.9 %collective-permute-start.24 = (bf16[4,16,512]{2,1,0:T(8,128)(2,1)S(1)}, bf16[4,16,512]{2,1,0:T(8,128)(2,1)S(1)}, u32[]{:S(2)}, u32[]{:S(2)}) collective-permute-start(bf16[4,16,512]{2,1,0:T(8,128)(2,1)S(1)} %get-tuple-element.53), channel_id=1, source_target_pairs={{0,2},{1,3},{2,0},{3,1},{4,6},{5,7},{6,4},{7,5},{8,10},{9,11},{10,... | collective-permute-start | bytes 196616 | tf_op jit(solution)/shard_map/ppermute | solution.py:41
  32.6 7.9 %collective-permute-start.25 = (bf16[4,16,512]{2,1,0:T(8,128)(2,1)S(1)}, bf16[4,16,512]{2,1,0:T(8,128)(2,1)S(1)}, u32[]{:S(2)}, u32[]{:S(2)}) collective-permute-start(bf16[4,16,512]{2,1,0:T(8,128)(2,1)S(1)} %get-tuple-element.54), channel_id=1, source_target_pairs={{0,1},{1,0},{2,3},{3,2},{4,5},{5,4},{6,7},{7,6},{8,9},{9,8},{10,11... | collective-permute-start | bytes 196616 | tf_op jit(solution)/shard_map/ppermute | solution.py:41
  34.9 15.4 %copy-start = (f32[4,64,512]{2,1,0:T(8,128)S(1)}, f32[4,64,512]{2,1,0:T(8,128)}, u32[]{:S(2)}) copy-start(f32[4,64,512]{2,1,0:T(8,128)} %diag_ref.3) | copy-start | bytes 1572868
  36.0 7.2 %collective-permute-start.17 = (bf16[4,16,512]{2,1,0:T(8,128)(2,1)S(1)}, bf16[4,16,512]{2,1,0:T(8,128)(2,1)S(1)}, u32[]{:S(2)}, u32[]{:S(2)}) collective-permute-start(bf16[4,16,512]{2,1,0:T(8,128)(2,1)S(1)} %get-tuple-element.48), channel_id=1, source_target_pairs={{0,3},{1,2},{2,1},{3,0},{4,7},{5,6},{6,5},{7,4},{8,11},{9,10},{10,... | collective-permute-start | bytes 196616 | tf_op jit(solution)/shard_map/ppermute | solution.py:41
  38.1 7.7 %collective-permute-start.18 = (bf16[4,16,512]{2,1,0:T(8,128)(2,1)S(1)}, bf16[4,16,512]{2,1,0:T(8,128)(2,1)S(1)}, u32[]{:S(2)}, u32[]{:S(2)}) collective-permute-start(bf16[4,16,512]{2,1,0:T(8,128)(2,1)S(1)} %get-tuple-element.49), channel_id=1, source_target_pairs={{0,2},{1,3},{2,0},{3,1},{4,6},{5,7},{6,4},{7,5},{8,10},{9,11},{10,... | collective-permute-start | bytes 196616 | tf_op jit(solution)/shard_map/ppermute | solution.py:41
  38.1 7.7 %collective-permute-start.19 = (bf16[4,16,512]{2,1,0:T(8,128)(2,1)S(1)}, bf16[4,16,512]{2,1,0:T(8,128)(2,1)S(1)}, u32[]{:S(2)}, u32[]{:S(2)}) collective-permute-start(bf16[4,16,512]{2,1,0:T(8,128)(2,1)S(1)} %get-tuple-element.50), channel_id=1, source_target_pairs={{0,1},{1,0},{2,3},{3,2},{4,5},{5,4},{6,7},{7,6},{8,9},{9,8},{10,11... | collective-permute-start | bytes 196616 | tf_op jit(solution)/shard_map/ppermute | solution.py:41
  40.5 8.1 %collective-permute-start.26 = (bf16[4,16,512]{2,1,0:T(8,128)(2,1)S(1)}, bf16[4,16,512]{2,1,0:T(8,128)(2,1)S(1)}, u32[]{:S(2)}, u32[]{:S(2)}) collective-permute-start(bf16[4,16,512]{2,1,0:T(8,128)(2,1)S(1)} %shard_map.101.refs_0_), channel_id=1, source_target_pairs={{0,1},{1,0},{2,3},{3,2},{4,5},{5,4},{6,7},{7,6},{8,9},{9,8},{10,11... | collective-permute-start | bytes 196616 | tf_op jit(solution)/shard_map/ppermute | solution.py:41
  40.6 9.7 %collective-permute-start.27 = (bf16[4,16,512]{2,1,0:T(8,128)(2,1)S(1)}, bf16[4,16,512]{2,1,0:T(8,128)(2,1)S(1)}, u32[]{:S(2)}, u32[]{:S(2)}) collective-permute-start(bf16[4,16,512]{2,1,0:T(8,128)(2,1)S(1)} %shard_map.101.refs_0_), channel_id=1, source_target_pairs={{0,2},{1,3},{2,0},{3,1},{4,6},{5,7},{6,4},{7,5},{8,10},{9,11},{10,... | collective-permute-start | bytes 196616 | tf_op jit(solution)/shard_map/ppermute | solution.py:41
  43.1 7.2 %collective-permute-start.28 = (bf16[4,16,512]{2,1,0:T(8,128)(2,1)S(1)}, bf16[4,16,512]{2,1,0:T(8,128)(2,1)S(1)}, u32[]{:S(2)}, u32[]{:S(2)}) collective-permute-start(bf16[4,16,512]{2,1,0:T(8,128)(2,1)S(1)} %shard_map.101.refs_0_), channel_id=1, source_target_pairs={{0,3},{1,2},{2,1},{3,0},{4,7},{5,6},{6,5},{7,4},{8,11},{9,10},{10,... | collective-permute-start | bytes 196616 | tf_op jit(solution)/shard_map/ppermute | solution.py:41
  45.8 5.3 %collective-permute-start.20 = (bf16[4,16,512]{2,1,0:T(8,128)(2,1)S(1)}, bf16[4,16,512]{2,1,0:T(8,128)(2,1)S(1)}, u32[]{:S(2)}, u32[]{:S(2)}) collective-permute-start(bf16[4,16,512]{2,1,0:T(8,128)(2,1)S(1)} %shard_map.100.refs_0_), channel_id=1, source_target_pairs={{0,1},{1,0},{2,3},{3,2},{4,5},{5,4},{6,7},{7,6},{8,9},{9,8},{10,11... | collective-permute-start | bytes 196616 | tf_op jit(solution)/shard_map/ppermute | solution.py:41
  45.9 9.0 %collective-permute-start.21 = (bf16[4,16,512]{2,1,0:T(8,128)(2,1)S(1)}, bf16[4,16,512]{2,1,0:T(8,128)(2,1)S(1)}, u32[]{:S(2)}, u32[]{:S(2)}) collective-permute-start(bf16[4,16,512]{2,1,0:T(8,128)(2,1)S(1)} %shard_map.100.refs_0_), channel_id=1, source_target_pairs={{0,2},{1,3},{2,0},{3,1},{4,6},{5,7},{6,4},{7,5},{8,10},{9,11},{10,... | collective-permute-start | bytes 196616 | tf_op jit(solution)/shard_map/ppermute | solution.py:41
  48.6 6.3 %collective-permute-start.22 = (bf16[4,16,512]{2,1,0:T(8,128)(2,1)S(1)}, bf16[4,16,512]{2,1,0:T(8,128)(2,1)S(1)}, u32[]{:S(2)}, u32[]{:S(2)}) collective-permute-start(bf16[4,16,512]{2,1,0:T(8,128)(2,1)S(1)} %shard_map.100.refs_0_), channel_id=1, source_target_pairs={{0,3},{1,2},{2,1},{3,0},{4,7},{5,6},{6,5},{7,4},{8,11},{9,10},{10,... | collective-permute-start | bytes 196616 | tf_op jit(solution)/shard_map/ppermute | solution.py:41

commit v9 on v8

--- a/solution.py
+++ b/solution.py
@@ -192,11 +192,14 @@
     *got_refs, cols_ref, copy_ref = refs
     supers, piece, _ = own_ref.shape
     carried = carry_ref[...]
-    for k in reversed(range(supers)):
+    totals = []
+    for k in range(supers):
         total = own_ref[k].astype(F32)
         for got in got_refs:
             total = total + got[k].astype(F32)
-        total = total + (carried if k == supers - 1 else dot(prev, l_ref[k]))
+        totals.append(total)
+    for k in reversed(range(supers)):
+        total = totals[k] + (carried if k == supers - 1 else dot(prev, l_ref[k]))
         prev = (-(total * mask_ref[k, pl.ds(0, 1)])).astype(BF)
         cols_ref[k] = prev
         copy_ref[k] = prev
@@ -329,18 +332,17 @@
     diag_out, sub_out, done_ref, sub_ref, sems = refs[-5:]
     part = got_refs[0].shape[1]
     col = lax.axis_index("cols")
-    span = pl.ds(levels[-1], len(levels))
     places = [pl.ds(pl.multiple_of((col ^ j) * part, part), part) for j in offsets]
+    copies = []
     for i, k in enumerate(levels):
+        at = k - levels[-1]
         for rows, got in zip(places, got_refs):
-            sub_ref[k - levels[-1], rows] = got[2 * i + 1].astype(F32)
-    sub_copy = fetch(sub_ref, sub_out.at[span], sems.at[0])
-    for i, k in enumerate(levels):
-        for rows, got in zip(places, got_refs):
-            done_ref[k - levels[-1], rows] = diag_ref[k, rows] + got[2 * i].astype(F32)
-    diag_copy = fetch(done_ref, diag_out.at[span], sems.at[1])
-    sub_copy.wait()
-    diag_copy.wait()
+            sub_ref[at, rows] = got[2 * i + 1].astype(F32)
+            done_ref[at, rows] = diag_ref[k, rows] + got[2 * i].astype(F32)
+        copies.append(fetch(sub_ref.at[at], sub_out.at[k], sems.at[2 * i]))
+        copies.append(fetch(done_ref.at[at], diag_out.at[k], sems.at[2 * i + 1]))
+    for copy in copies:
+        copy.wait()
 
 
 def call(kernel, outs, *args, scratch=(), away=(), out_away=False, aliases=None, flops=0, moved=0):
@@ -435,7 +437,7 @@
             [(diag_inverse.shape, F32)] * 2,
             diag_inverse, *got, *filled, away=range(1 + n_cols, 1 + n_cols + len(filled)), out_away=True,
             aliases={1 + n_cols + i: i for i in range(len(filled))},
-            scratch=[pltpu.VMEM((len(levels), share, width), F32)] * 2 + [pltpu.SemaphoreType.DMA((2,))],
+            scratch=[pltpu.VMEM((len(levels), share, width), F32)] * 2 + [pltpu.SemaphoreType.DMA((2 * len(levels),))],
         )
     diag, sub = filled
     return cols_out.reshape(supers, 1, 1, piece, width), diag, sub

time: 55.9 us -> 55.9 us (level)
  no operation moved by 1% of the time
where the time goes in v9:
time: 55.9 us; the launch traced here: 55.8 us
  starting transfers between devices  32 us (57%)
  waiting for transfers between devices  12.5 us (22%)
  Pallas kernels  10.4 us (19%)
  between operations  0.77 us (1%)
    ppermute x29, starting transfers between devices, hop(): return lax.ppermute(x, axis, [(i, target(i, j, n)) for i in range(n)])  32 us
    ppermute x29, waiting for transfers between devices, hop(): return lax.ppermute(x, axis, [(i, target(i, j, n)) for i in range(n)])  12.5 us
    pallas_call x10, Pallas kernels, call(): pl.pallas_call(kernel, out_shape=tuple((jax.ShapeDtypeStruct(s, d) for s,...  10.4 us
  transfers between devices with their start and end apart: 29, of which 8 were waited for; matrix products, arithmetic and copies ran while one was open for 0% of the time, Pallas kernels for 13%

profile of v9, /device:TPU:0, one launch (start us, length us, event | category | flops | bytes accessed | tf_op | source)
XLA Modules:
  0.0 55.8 jit_solution(8260584053911529453)
XLA Ops:
  0.6 1.6 %shard_map.94 = (bf16[4,256,512]{2,1,0:T(8,128)(2,1)S(1)}, f32[4,8,512]{2,1,0:T(8,128)S(1)}, bf16[4,32,512]{2,1,0:T(8,128)(2,1)S(1)}, bf16[4,32,512]{2,1,0:T(8,1...) custom-call(bf16[4,32,256]{2,1,0:T(8,128)(2,1)} %bitcast.7, ...), custom_call_target="tpu_custom_call" | custom-call | flops 134217728 | bytes 2097152 | tf_op jit(solution)/shard_map/pallas_call | solution.py:350
  2.3 5.1 %collective-permute-start = (bf16[4,32,512]{2,1,0:T(8,128)(2,1)S(1)}, bf16[4,32,512]{2,1,0:T(8,128)(2,1)S(1)}, u32[]{:S(2)}, u32[]{:S(2)}) collective-permute-start(bf16[4,32,512]{2,1,0:T(8,128)(2,1)S(1)} %get-tuple-element.36), channel_id=1, source_target_pairs={{0,3},{1,2},{2,1},{3,0},{4,7},{5,6},{6,5},{7,4},{8,11},{9,10},{10,... | collective-permute-start | bytes 393224 | tf_op jit(solution)/shard_map/ppermute | solution.py:41
  7.4 0.0 collective-permute-start.1
  7.4 0.6 %collective-permute-start.2 = (bf16[4,32,512]{2,1,0:T(8,128)(2,1)S(1)}, bf16[4,32,512]{2,1,0:T(8,128)(2,1)S(1)}, u32[]{:S(2)}, u32[]{:S(2)}) collective-permute-start(bf16[4,32,512]{2,1,0:T(8,128)(2,1)S(1)} %get-tuple-element.38), channel_id=1, source_target_pairs={{0,2},{1,3},{2,0},{3,1},{4,6},{5,7},{6,4},{7,5},{8,10},{9,11},{10,... | collective-permute-start | bytes 393224 | tf_op jit(solution)/shard_map/ppermute | solution.py:41
  8.0 2.8 %shard_map.95 = (bf16[4,512,512]{2,1,0:T(8,128)(2,1)S(1)}, bf16[5,320,512]{2,1,0:T(8,128)(2,1)S(1)}, bf16[640,256]{1,0:T(8,128)(2,1)S(1)}, bf16[96,512]{1,0:T(8,128)(2,1)S(1)}, f32[32,512]{1,0:T(8,128)S(1)}) custom-call(bf16[4,512,512]{2,1,0:T(8,128)(2,1)} %l_any.1, f32[4,64,512]{2,1,0:T(8,128)} %diag_ref.3, f32[64,512]{1,0:T(8,128)} %top_any.1, ...), custom_call_target="tpu_custom_call" | custom-call | flops 402653184 | bytes 4194304 | tf_op jit(solution)/shard_map/pallas_call | solution.py:350
  10.8 2.7 %collective-permute-start.3 = (bf16[96,512]{1,0:T(8,128)(2,1)S(1)}, bf16[96,512]{1,0:T(8,128)(2,1)S(1)}, u32[]{:S(2)}, u32[]{:S(2)}) collective-permute-start(bf16[96,512]{1,0:T(8,128)(2,1)S(1)} %get-tuple-element.42.refs_0_), channel_id=1, source_target_pairs={{0,24},{4,28},{8,16},{12,20},{16,8},{20,12},{24,0},{28,4},{1,25},{... | collective-permute-start | bytes 294920 | tf_op jit(solution)/shard_map/ppermute | solution.py:41
  13.5 0.5 collective-permute-start.4
  14.0 0.0 collective-permute-done.refs_0_
  14.0 0.4 collective-permute-start.5
  14.4 0.4 collective-permute-done.1.refs_1_
  14.8 0.0 collective-permute-start.6
  14.8 3.7 %collective-permute-done.2.refs_2_ = bf16[4,32,512]{2,1,0:T(8,128)(2,1)S(1)} collective-permute-done((bf16[4,32,512]{2,1,0:T(8,128)(2,1)S(1)}, bf16[4,32,512]{2,1,0:T(8,128)(2,1)S(1)}, u32[]{:S(2)}, u32[]{:S(2)}) %collective-permute-start.2) | collective-permute-done | bytes 131104 | tf_op jit(solution)/shard_map/ppermute | solution.py:41
  18.5 1.2 %shard_map.96 = (bf16[4,32,512]{2,1,0:T(8,128)(2,1)S(1)}, bf16[4,32,512]{2,1,0:T(8,128)(2,1)}) custom-call(bf16[4,512,512]{2,1,0:T(8,128)(2,1)S(1)} %get-tuple-element.32.l_ref, f32[32,512]{1,0:T(8,128)S(1)} %get-tuple-element.33.carry_ref, f32[4,8,512]{2,1,0:T(8,128)S(1)} %get-tuple-element.34.mask_ref, bf16[4,32,512]{2,1,0:T(8,128)(2,1)S(1)} %get-tuple-element.35.own_ref, ...), custom_call_target="tpu_custom_call" | custom-call | flops 67108864 | bytes 2097152 | tf_op jit(solution)/shard_map/pallas_call | solution.py:350
  19.6 2.4 %collective-permute-start.10 = (bf16[4,32,512]{2,1,0:T(8,128)(2,1)S(1)}, bf16[4,32,512]{2,1,0:T(8,128)(2,1)S(1)}, u32[]{:S(2)}, u32[]{:S(2)}) collective-permute-start(bf16[4,32,512]{2,1,0:T(8,128)(2,1)S(1)} %get-tuple-element.45.refs_0_), channel_id=1, source_target_pairs={{0,24},{4,28},{8,16},{12,20},{16,8},{20,12},{24,0},{28,4},{1,25},{... | collective-permute-start | bytes 393224 | tf_op jit(solution)/shard_map/ppermute | solution.py:41
  22.1 0.0 collective-permute-done.3.refs_1_
  22.1 0.5 collective-permute-start.11
  22.6 0.0 collective-permute-done.4.refs_2_
  22.6 0.5 collective-permute-start.12
  23.1 0.0 collective-permute-done.5.refs_3_
  23.1 0.0 collective-permute-start.7
  23.1 0.0 collective-permute-done.6.refs_4_
  23.1 0.5 collective-permute-start.8
  23.6 0.8 %collective-permute-done.7.refs_5_ = bf16[96,512]{1,0:T(8,128)(2,1)S(1)} collective-permute-done((bf16[96,512]{1,0:T(8,128)(2,1)S(1)}, bf16[96,512]{1,0:T(8,128)(2,1)S(1)}, u32[]{:S(2)}, u32[]{:S(2)}) %collective-permute-start.7) | collective-permute-done | bytes 98336 | tf_op jit(solution)/shard_map/ppermute | solution.py:41
  24.4 0.2 collective-permute-start.9
  24.6 0.0 collective-permute-done.8.refs_6_
  24.6 0.4 collective-permute-start.13
  25.0 1.4 %collective-permute-done.10.refs_1_ = bf16[4,32,512]{2,1,0:T(8,128)(2,1)S(1)} collective-permute-done((bf16[4,32,512]{2,1,0:T(8,128)(2,1)S(1)}, bf16[4,32,512]{2,1,0:T(8,128)(2,1)S(1)}, u32[]{:S(2)}, u32[]{:S(2)}) %collective-permute-start.10) | collective-permute-done | bytes 131104 | tf_op jit(solution)/shard_map/ppermute | solution.py:41
  26.3 0.0 collective-permute-start.14
  26.3 1.6 %collective-permute-done.11.refs_2_ = bf16[4,32,512]{2,1,0:T(8,128)(2,1)S(1)} collective-permute-done((bf16[4,32,512]{2,1,0:T(8,128)(2,1)S(1)}, bf16[4,32,512]{2,1,0:T(8,128)(2,1)S(1)}, u32[]{:S(2)}, u32[]{:S(2)}) %collective-permute-start.11) | collective-permute-done | bytes 131104 | tf_op jit(solution)/shard_map/ppermute | solution.py:41
  27.9 0.0 collective-permute-start.15
  27.9 0.1 collective-permute-done.12.refs_3_
  28.0 0.4 collective-permute-start.16
  28.4 0.0 collective-permute-done.9.refs_7_
  28.4 1.1 %shard_map.97 = (f32[320,512]{1,0:T(8,128)S(1)}, f32[320,512]{1,0:T(8,128)S(1)}) custom-call(bf16[4,512,512]{2,1,0:T(8,128)(2,1)S(1)} %get-tuple-element.32.l_ref, bf16[4,256,512]{2,1,0:T(8,128)(2,1)S(1)} %get-tuple-element.31.panel_ref, bf16[5,320,512]{2,1,0:T(8,128)(2,1)S(1)} %get-tuple-element.40.stacks_ref, ...), custom_call_target="tpu_custom_call" | custom-call | flops 503316480 | bytes 1048576 | tf_op jit(solution)/shard_map/pallas_call | solution.py:350
  29.5 0.0 collective-permute-done.13.refs_4_
  29.5 0.0 collective-permute-done.14.refs_5_
  29.5 0.0 collective-permute-done.15.refs_6_
  29.5 0.0 collective-permute-done.16.refs_7_
  29.5 1.0 %shard_map.98 = (bf16[4,16,512]{2,1,0:T(8,128)(2,1)S(1)}, bf16[4,16,512]{2,1,0:T(8,128)(2,1)S(1)}, bf16[4,16,512]{2,1,0:T(8,128)(2,1)S(1)}, bf16[4,16,512]{2,1,0:T(8,128)(2,1)S(1)}, f32[192,512]{1,0:T(8,128)S(1)}) custom-call(bf16[4,512,512]{2,1,0:T(8,128)(2,1)S(1)} %get-tuple-element.32.l_ref, bf16[4,256,512]{2,1,0:T(8,128)(2,1)S(1)} %get-tuple-element.31.panel_ref, ...), custom_call_target="tpu_custom_call" | custom-call | flops 335544320 | bytes 4194304 | tf_op jit(solution)/shard_map/pallas_call | solution.py:350
  30.5 2.1 %collective-permute-start.23 = (bf16[4,16,512]{2,1,0:T(8,128)(2,1)S(1)}, bf16[4,16,512]{2,1,0:T(8,128)(2,1)S(1)}, u32[]{:S(2)}, u32[]{:S(2)}) collective-permute-start(bf16[4,16,512]{2,1,0:T(8,128)(2,1)S(1)} %get-tuple-element.52), channel_id=1, source_target_pairs={{0,3},{1,2},{2,1},{3,0},{4,7},{5,6},{6,5},{7,4},{8,11},{9,10},{10,... | collective-permute-start | bytes 196616 | tf_op jit(solution)/shard_map/ppermute | solution.py:41
  32.6 0.0 collective-permute-start.24
  32.6 2.4 %collective-permute-start.25 = (bf16[4,16,512]{2,1,0:T(8,128)(2,1)S(1)}, bf16[4,16,512]{2,1,0:T(8,128)(2,1)S(1)}, u32[]{:S(2)}, u32[]{:S(2)}) collective-permute-start(bf16[4,16,512]{2,1,0:T(8,128)(2,1)S(1)} %get-tuple-element.54), channel_id=1, source_target_pairs={{0,1},{1,0},{2,3},{3,2},{4,5},{5,4},{6,7},{7,6},{8,9},{9,8},{10,11... | collective-permute-start | bytes 196616 | tf_op jit(solution)/shard_map/ppermute | solution.py:41
  34.9 1.0 %shard_map.99 = (bf16[4,16,512]{2,1,0:T(8,128)(2,1)S(1)}, bf16[4,16,512]{2,1,0:T(8,128)(2,1)S(1)}, bf16[4,16,512]{2,1,0:T(8,128)(2,1)S(1)}, bf16[4,16,512]{2,1,0:T(8,128)(2,1)S(1)}) custom-call(bf16[4,512,512]{2,1,0:T(8,128)(2,1)S(1)} %get-tuple-element.32.l_ref, bf16[4,256,512]{2,1,0:T(8,128)(2,1)S(1)} %get-tuple-element.31.panel_ref, ...), custom_call_target="tpu_custom_call" | custom-call | flops 335544320 | bytes 4194304 | tf_op jit(solution)/shard_map/pallas_call | solution.py:350
  36.0 2.1 %collective-permute-start.17 = (bf16[4,16,512]{2,1,0:T(8,128)(2,1)S(1)}, bf16[4,16,512]{2,1,0:T(8,128)(2,1)S(1)}, u32[]{:S(2)}, u32[]{:S(2)}) collective-permute-start(bf16[4,16,512]{2,1,0:T(8,128)(2,1)S(1)} %get-tuple-element.48), channel_id=1, source_target_pairs={{0,3},{1,2},{2,1},{3,0},{4,7},{5,6},{6,5},{7,4},{8,11},{9,10},{10,... | collective-permute-start | bytes 196616 | tf_op jit(solution)/shard_map/ppermute | solution.py:41
  38.1 0.0 collective-permute-start.18
  38.1 0.0 collective-permute-done.23.refs_0_
  38.1 2.4 %collective-permute-start.19 = (bf16[4,16,512]{2,1,0:T(8,128)(2,1)S(1)}, bf16[4,16,512]{2,1,0:T(8,128)(2,1)S(1)}, u32[]{:S(2)}, u32[]{:S(2)}) collective-permute-start(bf16[4,16,512]{2,1,0:T(8,128)(2,1)S(1)} %get-tuple-element.50), channel_id=1, source_target_pairs={{0,1},{1,0},{2,3},{3,2},{4,5},{5,4},{6,7},{7,6},{8,9},{9,8},{10,11... | collective-permute-start | bytes 196616 | tf_op jit(solution)/shard_map/ppermute | solution.py:41
  40.4 0.0 collective-permute-done.24.refs_1_
  40.4 0.0 collective-permute-done.25.refs_2_
  40.5 0.1 collective-permute-start.26
  40.6 2.6 %collective-permute-start.27 = (bf16[4,16,512]{2,1,0:T(8,128)(2,1)S(1)}, bf16[4,16,512]{2,1,0:T(8,128)(2,1)S(1)}, u32[]{:S(2)}, u32[]{:S(2)}) collective-permute-start(bf16[4,16,512]{2,1,0:T(8,128)(2,1)S(1)} %shard_map.101.refs_0_), channel_id=1, source_target_pairs={{0,2},{1,3},{2,0},{3,1},{4,6},{5,7},{6,4},{7,5},{8,10},{9,11},{10,... | collective-permute-start | bytes 196616 | tf_op jit(solution)/shard_map/ppermute | solution.py:41
  43.1 0.0 collective-permute-done.17.refs_0_
  43.1 1.8 %collective-permute-start.28 = (bf16[4,16,512]{2,1,0:T(8,128)(2,1)S(1)}, bf16[4,16,512]{2,1,0:T(8,128)(2,1)S(1)}, u32[]{:S(2)}, u32[]{:S(2)}) collective-permute-start(bf16[4,16,512]{2,1,0:T(8,128)(2,1)S(1)} %shard_map.101.refs_0_), channel_id=1, source_target_pairs={{0,3},{1,2},{2,1},{3,0},{4,7},{5,6},{6,5},{7,4},{8,11},{9,10},{10,... | collective-permute-start | bytes 196616 | tf_op jit(solution)/shard_map/ppermute | solution.py:41
  44.9 0.8 %collective-permute-done.18.refs_1_ = bf16[4,16,512]{2,1,0:T(8,128)(2,1)S(1)} collective-permute-done((bf16[4,16,512]{2,1,0:T(8,128)(2,1)S(1)}, bf16[4,16,512]{2,1,0:T(8,128)(2,1)S(1)}, u32[]{:S(2)}, u32[]{:S(2)}) %collective-permute-start.18) | collective-permute-done | bytes 65568 | tf_op jit(solution)/shard_map/ppermute | solution.py:41
  45.8 0.0 collective-permute-done.19.refs_2_
  45.8 0.1 collective-permute-start.20
  45.9 2.7 %collective-permute-start.21 = (bf16[4,16,512]{2,1,0:T(8,128)(2,1)S(1)}, bf16[4,16,512]{2,1,0:T(8,128)(2,1)S(1)}, u32[]{:S(2)}, u32[]{:S(2)}) collective-permute-start(bf16[4,16,512]{2,1,0:T(8,128)(2,1)S(1)} %shard_map.100.refs_0_), channel_id=1, source_target_pairs={{0,2},{1,3},{2,0},{3,1},{4,6},{5,7},{6,4},{7,5},{8,10},{9,11},{10,... | collective-permute-start | bytes 196616 | tf_op jit(solution)/shard_map/ppermute | solution.py:41
  48.6 0.0 collective-permute-done.26.refs_1_
  48.6 1.7 %collective-permute-start.22 = (bf16[4,16,512]{2,1,0:T(8,128)(2,1)S(1)}, bf16[4,16,512]{2,1,0:T(8,128)(2,1)S(1)}, u32[]{:S(2)}, u32[]{:S(2)}) collective-permute-start(bf16[4,16,512]{2,1,0:T(8,128)(2,1)S(1)} %shard_map.100.refs_0_), channel_id=1, source_target_pairs={{0,3},{1,2},{2,1},{3,0},{4,7},{5,6},{6,5},{7,4},{8,11},{9,10},{10,... | collective-permute-start | bytes 196616 | tf_op jit(solution)/shard_map/ppermute | solution.py:41
  50.3 0.0 collective-permute-done.27.refs_2_
  50.3 0.9 %shard_map.102 = (f32[4,64,512]{2,1,0:T(8,128)}, f32[4,64,512]{2,1,0:T(8,128)}) custom-call(f32[4,64,512]{2,1,0:T(8,128)S(1)} %copy-done, bf16[4,16,512]{2,1,0:T(8,128)(2,1)S(1)} %shard_map.101.refs_0_, bf16[4,16,512]{2,1,0:T(8,128)(2,1)S(1)} %collective-permute-done.26.refs_1_, bf16[4,16,512]{2,1,0:T(8,128)(2,1)S(1)} %collective-permute-done.27.refs_2_, ...), custom_call_target="tpu_custom_call" | custom-call | tf_op jit(solution)/shard_map/pallas_call | solution.py:350
  51.2 0.0 collective-permute-done.20.refs_1_
  51.2 3.7 %collective-permute-done.21.refs_2_ = bf16[4,16,512]{2,1,0:T(8,128)(2,1)S(1)} collective-permute-done((bf16[4,16,512]{2,1,0:T(8,128)(2,1)S(1)}, bf16[4,16,512]{2,1,0:T(8,128)(2,1)S(1)}, u32[]{:S(2)}, u32[]{:S(2)}) %collective-permute-start.21) | collective-permute-done | bytes 65568 | tf_op jit(solution)/shard_map/ppermute | solution.py:41
  54.9 0.9 %shard_map.103 = (f32[4,64,512]{2,1,0:T(8,128)}, f32[4,64,512]{2,1,0:T(8,128)}) custom-call(f32[4,64,512]{2,1,0:T(8,128)S(1)} %copy-done, bf16[4,16,512]{2,1,0:T(8,128)(2,1)S(1)} %shard_map.100.refs_0_, bf16[4,16,512]{2,1,0:T(8,128)(2,1)S(1)} %collective-permute-done.20.refs_1_, ...), custom_call_target="tpu_custom_call", output_to_operand_aliasing={{0}: (5, {}), {1}: (6, {})} | custom-call | tf_op jit(solution)/shard_map/pallas_call | solution.py:350
  (6 shorter events, 0.1 us)
Async XLA Ops:
  2.3 11.7 %collective-permute-start = (bf16[4,32,512]{2,1,0:T(8,128)(2,1)S(1)}, bf16[4,32,512]{2,1,0:T(8,128)(2,1)S(1)}, u32[]{:S(2)}, u32[]{:S(2)}) collective-permute-start(bf16[4,32,512]{2,1,0:T(8,128)(2,1)S(1)} %get-tuple-element.36), channel_id=1, source_target_pairs={{0,3},{1,2},{2,1},{3,0},{4,7},{5,6},{6,5},{7,4},{8,11},{9,10},{10,... | collective-permute-start | bytes 393224 | tf_op jit(solution)/shard_map/ppermute | solution.py:41
  7.4 7.4 %collective-permute-start.1 = (bf16[4,32,512]{2,1,0:T(8,128)(2,1)S(1)}, bf16[4,32,512]{2,1,0:T(8,128)(2,1)S(1)}, u32[]{:S(2)}, u32[]{:S(2)}) collective-permute-start(bf16[4,32,512]{2,1,0:T(8,128)(2,1)S(1)} %get-tuple-element.37), channel_id=1, source_target_pairs={{0,1},{1,0},{2,3},{3,2},{4,5},{5,4},{6,7},{7,6},{8,9},{9,8},{10,11... | collective-permute-start | bytes 393224 | tf_op jit(solution)/shard_map/ppermute | solution.py:41
  7.4 11.1 %collective-permute-start.2 = (bf16[4,32,512]{2,1,0:T(8,128)(2,1)S(1)}, bf16[4,32,512]{2,1,0:T(8,128)(2,1)S(1)}, u32[]{:S(2)}, u32[]{:S(2)}) collective-permute-start(bf16[4,32,512]{2,1,0:T(8,128)(2,1)S(1)} %get-tuple-element.38), channel_id=1, source_target_pairs={{0,2},{1,3},{2,0},{3,1},{4,6},{5,7},{6,4},{7,5},{8,10},{9,11},{10,... | collective-permute-start | bytes 393224 | tf_op jit(solution)/shard_map/ppermute | solution.py:41
  10.8 11.3 %collective-permute-start.3 = (bf16[96,512]{1,0:T(8,128)(2,1)S(1)}, bf16[96,512]{1,0:T(8,128)(2,1)S(1)}, u32[]{:S(2)}, u32[]{:S(2)}) collective-permute-start(bf16[96,512]{1,0:T(8,128)(2,1)S(1)} %get-tuple-element.42.refs_0_), channel_id=1, source_target_pairs={{0,24},{4,28},{8,16},{12,20},{16,8},{20,12},{24,0},{28,4},{1,25},{... | collective-permute-start | bytes 294920 | tf_op jit(solution)/shard_map/ppermute | solution.py:41
  13.5 9.1 %collective-permute-start.4 = (bf16[96,512]{1,0:T(8,128)(2,1)S(1)}, bf16[96,512]{1,0:T(8,128)(2,1)S(1)}, u32[]{:S(2)}, u32[]{:S(2)}) collective-permute-start(bf16[96,512]{1,0:T(8,128)(2,1)S(1)} %get-tuple-element.42.refs_0_), channel_id=1, source_target_pairs={{0,16},{4,20},{8,24},{12,28},{16,0},{20,4},{24,8},{28,12},{1,17},{... | collective-permute-start | bytes 294920 | tf_op jit(solution)/shard_map/ppermute | solution.py:41
  14.0 9.1 %collective-permute-start.5 = (bf16[96,512]{1,0:T(8,128)(2,1)S(1)}, bf16[96,512]{1,0:T(8,128)(2,1)S(1)}, u32[]{:S(2)}, u32[]{:S(2)}) collective-permute-start(bf16[96,512]{1,0:T(8,128)(2,1)S(1)} %get-tuple-element.42.refs_0_), channel_id=1, source_target_pairs={{0,8},{4,12},{8,0},{12,4},{16,24},{20,28},{24,16},{28,20},{1,9},{5... | collective-permute-start | bytes 294920 | tf_op jit(solution)/shard_map/ppermute | solution.py:41
  14.8 8.4 %collective-permute-start.6 = (bf16[96,512]{1,0:T(8,128)(2,1)S(1)}, bf16[96,512]{1,0:T(8,128)(2,1)S(1)}, u32[]{:S(2)}, u32[]{:S(2)}) collective-permute-start(bf16[96,512]{1,0:T(8,128)(2,1)S(1)} %get-tuple-element.42.refs_0_), channel_id=1, source_target_pairs={{0,4},{4,0},{8,12},{12,8},{16,20},{20,16},{24,28},{28,24},{1,5},{5... | collective-permute-start | bytes 294920 | tf_op jit(solution)/shard_map/ppermute | solution.py:41
  19.6 6.7 %collective-permute-start.10 = (bf16[4,32,512]{2,1,0:T(8,128)(2,1)S(1)}, bf16[4,32,512]{2,1,0:T(8,128)(2,1)S(1)}, u32[]{:S(2)}, u32[]{:S(2)}) collective-permute-start(bf16[4,32,512]{2,1,0:T(8,128)(2,1)S(1)} %get-tuple-element.45.refs_0_), channel_id=1, source_target_pairs={{0,24},{4,28},{8,16},{12,20},{16,8},{20,12},{24,0},{28,4},{1,25},{... | collective-permute-start | bytes 393224 | tf_op jit(solution)/shard_map/ppermute | solution.py:41
  22.1 5.8 %collective-permute-start.11 = (bf16[4,32,512]{2,1,0:T(8,128)(2,1)S(1)}, bf16[4,32,512]{2,1,0:T(8,128)(2,1)S(1)}, u32[]{:S(2)}, u32[]{:S(2)}) collective-permute-start(bf16[4,32,512]{2,1,0:T(8,128)(2,1)S(1)} %get-tuple-element.45.refs_0_), channel_id=1, source_target_pairs={{0,16},{4,20},{8,24},{12,28},{16,0},{20,4},{24,8},{28,12},{1,17},{... | collective-permute-start | bytes 393224 | tf_op jit(solution)/shard_map/ppermute | solution.py:41
  22.6 5.4 %collective-permute-start.12 = (bf16[4,32,512]{2,1,0:T(8,128)(2,1)S(1)}, bf16[4,32,512]{2,1,0:T(8,128)(2,1)S(1)}, u32[]{:S(2)}, u32[]{:S(2)}) collective-permute-start(bf16[4,32,512]{2,1,0:T(8,128)(2,1)S(1)} %get-tuple-element.45.refs_0_), channel_id=1, source_target_pairs={{0,8},{4,12},{8,0},{12,4},{16,24},{20,28},{24,16},{28,20},{1,9},{5... | collective-permute-start | bytes 393224 | tf_op jit(solution)/shard_map/ppermute | solution.py:41
  23.1 1.3 %collective-permute-start.7 = (bf16[96,512]{1,0:T(8,128)(2,1)S(1)}, bf16[96,512]{1,0:T(8,128)(2,1)S(1)}, u32[]{:S(2)}, u32[]{:S(2)}) collective-permute-start(bf16[96,512]{1,0:T(8,128)(2,1)S(1)} %collective-permute-done.3.refs_1_), channel_id=1, source_target_pairs={{0,4},{4,0},{8,12},{12,8},{16,20},{20,16},{24,28},{28,24},{1,5},{5... | collective-permute-start | bytes 294920 | tf_op jit(solution)/shard_map/ppermute | solution.py:41
  23.1 1.5 %collective-permute-start.8 = (bf16[96,512]{1,0:T(8,128)(2,1)S(1)}, bf16[96,512]{1,0:T(8,128)(2,1)S(1)}, u32[]{:S(2)}, u32[]{:S(2)}) collective-permute-start(bf16[96,512]{1,0:T(8,128)(2,1)S(1)} %collective-permute-done.4.refs_2_), channel_id=1, source_target_pairs={{0,4},{4,0},{8,12},{12,8},{16,20},{20,16},{24,28},{28,24},{1,5},{5... | collective-permute-start | bytes 294920 | tf_op jit(solution)/shard_map/ppermute | solution.py:41
  24.4 4.0 %collective-permute-start.9 = (bf16[96,512]{1,0:T(8,128)(2,1)S(1)}, bf16[96,512]{1,0:T(8,128)(2,1)S(1)}, u32[]{:S(2)}, u32[]{:S(2)}) collective-permute-start(bf16[96,512]{1,0:T(8,128)(2,1)S(1)} %collective-permute-done.5.refs_3_), channel_id=1, source_target_pairs={{0,4},{4,0},{8,12},{12,8},{16,20},{20,16},{24,28},{28,24},{1,5},{5... | collective-permute-start | bytes 294920 | tf_op jit(solution)/shard_map/ppermute | solution.py:41
  24.6 4.9 %collective-permute-start.13 = (bf16[4,32,512]{2,1,0:T(8,128)(2,1)S(1)}, bf16[4,32,512]{2,1,0:T(8,128)(2,1)S(1)}, u32[]{:S(2)}, u32[]{:S(2)}) collective-permute-start(bf16[4,32,512]{2,1,0:T(8,128)(2,1)S(1)} %get-tuple-element.45.refs_0_), channel_id=1, source_target_pairs={{0,4},{4,0},{8,12},{12,8},{16,20},{20,16},{24,28},{28,24},{1,5},{5... | collective-permute-start | bytes 393224 | tf_op jit(solution)/shard_map/ppermute | solution.py:41
  26.3 3.2 %collective-permute-start.14 = (bf16[4,32,512]{2,1,0:T(8,128)(2,1)S(1)}, bf16[4,32,512]{2,1,0:T(8,128)(2,1)S(1)}, u32[]{:S(2)}, u32[]{:S(2)}) collective-permute-start(bf16[4,32,512]{2,1,0:T(8,128)(2,1)S(1)} %collective-permute-done.10.refs_1_), channel_id=1, source_target_pairs={{0,4},{4,0},{8,12},{12,8},{16,20},{20,16},{24,28},{28,24},{1,5},{5... | collective-permute-start | bytes 393224 | tf_op jit(solution)/shard_map/ppermute | solution.py:41
  27.9 1.6 %collective-permute-start.15 = (bf16[4,32,512]{2,1,0:T(8,128)(2,1)S(1)}, bf16[4,32,512]{2,1,0:T(8,128)(2,1)S(1)}, u32[]{:S(2)}, u32[]{:S(2)}) collective-permute-start(bf16[4,32,512]{2,1,0:T(8,128)(2,1)S(1)} %collective-permute-done.11.refs_2_), channel_id=1, source_target_pairs={{0,4},{4,0},{8,12},{12,8},{16,20},{20,16},{24,28},{28,24},{1,5},{5... | collective-permute-start | bytes 393224 | tf_op jit(solution)/shard_map/ppermute | solution.py:41
  28.0 1.5 %collective-permute-start.16 = (bf16[4,32,512]{2,1,0:T(8,128)(2,1)S(1)}, bf16[4,32,512]{2,1,0:T(8,128)(2,1)S(1)}, u32[]{:S(2)}, u32[]{:S(2)}) collective-permute-start(bf16[4,32,512]{2,1,0:T(8,128)(2,1)S(1)} %collective-permute-done.12.refs_3_), channel_id=1, source_target_pairs={{0,4},{4,0},{8,12},{12,8},{16,20},{20,16},{24,28},{28,24},{1,5},{5... | collective-permute-start | bytes 393224 | tf_op jit(solution)/shard_map/ppermute | solution.py:41
  30.5 7.6 %collective-permute-start.23 = (bf16[4,16,512]{2,1,0:T(8,128)(2,1)S(1)}, bf16[4,16,512]{2,1,0:T(8,128)(2,1)S(1)}, u32[]{:S(2)}, u32[]{:S(2)}) collective-permute-start(bf16[4,16,512]{2,1,0:T(8,128)(2,1)S(1)} %get-tuple-element.52), channel_id=1, source_target_pairs={{0,3},{1,2},{2,1},{3,0},{4,7},{5,6},{6,5},{7,4},{8,11},{9,10},{10,... | collective-permute-start | bytes 196616 | tf_op jit(solution)/shard_map/ppermute | solution.py:41
  32.6 7.9 %collective-permute-start.24 = (bf16[4,16,512]{2,1,0:T(8,128)(2,1)S(1)}, bf16[4,16,512]{2,1,0:T(8,128)(2,1)S(1)}, u32[]{:S(2)}, u32[]{:S(2)}) collective-permute-start(bf16[4,16,512]{2,1,0:T(8,128)(2,1)S(1)} %get-tuple-element.53), channel_id=1, source_target_pairs={{0,2},{1,3},{2,0},{3,1},{4,6},{5,7},{6,4},{7,5},{8,10},{9,11},{10,... | collective-permute-start | bytes 196616 | tf_op jit(solution)/shard_map/ppermute | solution.py:41
  32.6 7.9 %collective-permute-start.25 = (bf16[4,16,512]{2,1,0:T(8,128)(2,1)S(1)}, bf16[4,16,512]{2,1,0:T(8,128)(2,1)S(1)}, u32[]{:S(2)}, u32[]{:S(2)}) collective-permute-start(bf16[4,16,512]{2,1,0:T(8,128)(2,1)S(1)} %get-tuple-element.54), channel_id=1, source_target_pairs={{0,1},{1,0},{2,3},{3,2},{4,5},{5,4},{6,7},{7,6},{8,9},{9,8},{10,11... | collective-permute-start | bytes 196616 | tf_op jit(solution)/shard_map/ppermute | solution.py:41
  34.9 15.4 %copy-start = (f32[4,64,512]{2,1,0:T(8,128)S(1)}, f32[4,64,512]{2,1,0:T(8,128)}, u32[]{:S(2)}) copy-start(f32[4,64,512]{2,1,0:T(8,128)} %diag_ref.3) | copy-start | bytes 1572868
  36.0 7.2 %collective-permute-start.17 = (bf16[4,16,512]{2,1,0:T(8,128)(2,1)S(1)}, bf16[4,16,512]{2,1,0:T(8,128)(2,1)S(1)}, u32[]{:S(2)}, u32[]{:S(2)}) collective-permute-start(bf16[4,16,512]{2,1,0:T(8,128)(2,1)S(1)} %get-tuple-element.48), channel_id=1, source_target_pairs={{0,3},{1,2},{2,1},{3,0},{4,7},{5,6},{6,5},{7,4},{8,11},{9,10},{10,... | collective-permute-start | bytes 196616 | tf_op jit(solution)/shard_map/ppermute | solution.py:41
  38.1 7.7 %collective-permute-start.18 = (bf16[4,16,512]{2,1,0:T(8,128)(2,1)S(1)}, bf16[4,16,512]{2,1,0:T(8,128)(2,1)S(1)}, u32[]{:S(2)}, u32[]{:S(2)}) collective-permute-start(bf16[4,16,512]{2,1,0:T(8,128)(2,1)S(1)} %get-tuple-element.49), channel_id=1, source_target_pairs={{0,2},{1,3},{2,0},{3,1},{4,6},{5,7},{6,4},{7,5},{8,10},{9,11},{10,... | collective-permute-start | bytes 196616 | tf_op jit(solution)/shard_map/ppermute | solution.py:41
  38.1 7.7 %collective-permute-start.19 = (bf16[4,16,512]{2,1,0:T(8,128)(2,1)S(1)}, bf16[4,16,512]{2,1,0:T(8,128)(2,1)S(1)}, u32[]{:S(2)}, u32[]{:S(2)}) collective-permute-start(bf16[4,16,512]{2,1,0:T(8,128)(2,1)S(1)} %get-tuple-element.50), channel_id=1, source_target_pairs={{0,1},{1,0},{2,3},{3,2},{4,5},{5,4},{6,7},{7,6},{8,9},{9,8},{10,11... | collective-permute-start | bytes 196616 | tf_op jit(solution)/shard_map/ppermute | solution.py:41
  40.5 8.1 %collective-permute-start.26 = (bf16[4,16,512]{2,1,0:T(8,128)(2,1)S(1)}, bf16[4,16,512]{2,1,0:T(8,128)(2,1)S(1)}, u32[]{:S(2)}, u32[]{:S(2)}) collective-permute-start(bf16[4,16,512]{2,1,0:T(8,128)(2,1)S(1)} %shard_map.101.refs_0_), channel_id=1, source_target_pairs={{0,1},{1,0},{2,3},{3,2},{4,5},{5,4},{6,7},{7,6},{8,9},{9,8},{10,11... | collective-permute-start | bytes 196616 | tf_op jit(solution)/shard_map/ppermute | solution.py:41
  40.6 9.7 %collective-permute-start.27 = (bf16[4,16,512]{2,1,0:T(8,128)(2,1)S(1)}, bf16[4,16,512]{2,1,0:T(8,128)(2,1)S(1)}, u32[]{:S(2)}, u32[]{:S(2)}) collective-permute-start(bf16[4,16,512]{2,1,0:T(8,128)(2,1)S(1)} %shard_map.101.refs_0_), channel_id=1, source_target_pairs={{0,2},{1,3},{2,0},{3,1},{4,6},{5,7},{6,4},{7,5},{8,10},{9,11},{10,... | collective-permute-start | bytes 196616 | tf_op jit(solution)/shard_map/ppermute | solution.py:41
  43.1 7.2 %collective-permute-start.28 = (bf16[4,16,512]{2,1,0:T(8,128)(2,1)S(1)}, bf16[4,16,512]{2,1,0:T(8,128)(2,1)S(1)}, u32[]{:S(2)}, u32[]{:S(2)}) collective-permute-start(bf16[4,16,512]{2,1,0:T(8,128)(2,1)S(1)} %shard_map.101.refs_0_), channel_id=1, source_target_pairs={{0,3},{1,2},{2,1},{3,0},{4,7},{5,6},{6,5},{7,4},{8,11},{9,10},{10,... | collective-permute-start | bytes 196616 | tf_op jit(solution)/shard_map/ppermute | solution.py:41
  45.8 5.3 %collective-permute-start.20 = (bf16[4,16,512]{2,1,0:T(8,128)(2,1)S(1)}, bf16[4,16,512]{2,1,0:T(8,128)(2,1)S(1)}, u32[]{:S(2)}, u32[]{:S(2)}) collective-permute-start(bf16[4,16,512]{2,1,0:T(8,128)(2,1)S(1)} %shard_map.100.refs_0_), channel_id=1, source_target_pairs={{0,1},{1,0},{2,3},{3,2},{4,5},{5,4},{6,7},{7,6},{8,9},{9,8},{10,11... | collective-permute-start | bytes 196616 | tf_op jit(solution)/shard_map/ppermute | solution.py:41
  45.9 9.0 %collective-permute-start.21 = (bf16[4,16,512]{2,1,0:T(8,128)(2,1)S(1)}, bf16[4,16,512]{2,1,0:T(8,128)(2,1)S(1)}, u32[]{:S(2)}, u32[]{:S(2)}) collective-permute-start(bf16[4,16,512]{2,1,0:T(8,128)(2,1)S(1)} %shard_map.100.refs_0_), channel_id=1, source_target_pairs={{0,2},{1,3},{2,0},{3,1},{4,6},{5,7},{6,4},{7,5},{8,10},{9,11},{10,... | collective-permute-start | bytes 196616 | tf_op jit(solution)/shard_map/ppermute | solution.py:41
  48.6 6.3 %collective-permute-start.22 = (bf16[4,16,512]{2,1,0:T(8,128)(2,1)S(1)}, bf16[4,16,512]{2,1,0:T(8,128)(2,1)S(1)}, u32[]{:S(2)}, u32[]{:S(2)}) collective-permute-start(bf16[4,16,512]{2,1,0:T(8,128)(2,1)S(1)} %shard_map.100.refs_0_), channel_id=1, source_target_pairs={{0,3},{1,2},{2,1},{3,0},{4,7},{5,6},{6,5},{7,4},{8,11},{9,10},{10,... | collective-permute-start | bytes 196616 | tf_op jit(solution)/shard_map/ppermute | solution.py:41
